TPU v7x, 32 devices: a whole 2x2x4 slice. The times are simulated.
32 devices in a mesh: band: 4 (over y, x), plane: 8 (over z, core).
Axes of the slice: x: 2, y: 2, z: 4, core: 2. Of those that a mesh axis runs over, the one named last changes fastest.
Arguments:
- orbitals: float32 [32, 96, 9216], P('band', 'plane'), may hold values from -6 to 6
Outputs:
- exchange_action: float32 [32, 96, 9216], P('band', 'plane')
All inputs are finite; a program needn't handle non-finite values.
Results may differ from a plain program's by a relative error of at most 0.0001.
Values sent between devices are 32-bit elements; how exact they have to be, the bound alone decides.
No kernel may reach another device: no remote copies, remote signals or barrier semaphores. Data moves between devices by JAX's collectives and lax.ppermute only.
A program may use at most 192 MiB of HBM per device.

v0:
```python
import math

import jax
import jax.numpy as jnp
from jax import lax
from jax.sharding import PartitionSpec as P

PAIR = 2
ROUNDS = 4


OMEGA = 0.106
CELL = 41.05
ALPHA = 0.25
HIGHEST = lax.Precision.HIGHEST


def from_root(value, axis, source):
    kept = jnp.where(lax.axis_index(axis) == source, value, 0).astype(value.dtype)
    return lax.psum(kept, axis)


def hartley_table(count):
    index = jnp.arange(count, dtype=jnp.int32)
    product = index[:, None] * index[None, :] % count
    angle = product.astype(jnp.float32) * (2.0 * math.pi / count)
    return jnp.cos(angle) + jnp.sin(angle)


def frequencies(count):
    index = jnp.arange(count, dtype=jnp.int32)
    return jnp.where(index <= count // 2, index, index - count).astype(jnp.float32)


def screened_kernel(count, first, width):
    freq = frequencies(count)
    square = freq * freq
    middle = lax.dynamic_slice_in_dim(square, first, width)
    scale = (2.0 * math.pi / CELL) ** 2
    g_two = scale * (square[:, None, None] + middle[None, :, None] + square[None, None, :])
    positive = g_two > 0
    safe = jnp.where(positive, g_two, 1.0)
    value = 4.0 * math.pi / safe * -jnp.expm1(-safe / (4.0 * OMEGA * OMEGA))
    value = jnp.where(positive, value, math.pi / (OMEGA * OMEGA))
    return value / float(count**3)


def coulomb_solve(density, table, kernel):
    field = jnp.einsum("pxyz,zw->pxyw", density, table, precision=HIGHEST)
    field = jnp.einsum("pxyz,yv->pxvz", field, table, precision=HIGHEST)
    field = lax.all_to_all(field, "plane", split_axis=2, concat_axis=1, tiled=True)
    field = jnp.einsum("pxyz,xu->puyz", field, table, precision=HIGHEST) * kernel
    field = jnp.einsum("pxyz,xu->puyz", field, table, precision=HIGHEST)
    field = lax.all_to_all(field, "plane", split_axis=1, concat_axis=2, tiled=True)
    field = jnp.einsum("pxyz,zw->pxyw", field, table, precision=HIGHEST)
    return jnp.einsum("pxyz,yv->pxvz", field, table, precision=HIGHEST)


def fetch_pair(fields, turn):
    return from_root(fields[0:PAIR], "band", turn)


def local(orbitals):
    local_bands, planes, flat = orbitals.shape
    count = planes * lax.axis_size("plane")
    fields = orbitals.reshape(local_bands, planes, count, count)
    table = hartley_table(count)
    kernel = screened_kernel(count, lax.axis_index("plane") * planes, planes)
    shape_tail = (planes, count, count)
    local_sum = jnp.zeros_like(fields)
    owner_list = []
    for turn in range(ROUNDS):
        received = fetch_pair(fields, turn)
        density = (fields[:, None] * received[None]).reshape((local_bands * PAIR,) + shape_tail)
        potential = coulomb_solve(density, table, kernel).reshape((local_bands, PAIR) + shape_tail)
        local_sum = local_sum + jnp.sum(received[None] * potential, axis=1)
        owner_list.append(jnp.sum(fields[:, None] * potential, axis=0))
    owner_terms = jnp.stack(owner_list)
    own_extra = jnp.zeros((PAIR,) + shape_tail, jnp.float32)
    for turn in range(ROUNDS):
        summed = lax.psum(owner_terms[turn], "band")
        owner_flag = (lax.axis_index("band") == turn).astype(jnp.float32)
        own_extra = own_extra + owner_flag * summed
    local_sum = local_sum.at[0:PAIR].add(own_extra)
    return (-ALPHA * local_sum).reshape(local_bands, planes, count * count)


def solution(mesh):
    placed = (P("band", "plane", None),)
    return jax.shard_map(
        local, mesh=mesh, in_specs=placed, out_specs=P("band", "plane", None), check_vma=False
    )
```

profile of v0, /device:TPU:17, one launch (start us, length us, event | category | flops | bytes accessed | tf_op | source)
XLA Modules:
  0.0 2119.4 jit_solution(14304185071652825598)
XLA Ops:
  27.0 111.2 %all-reduce.7.cloned.1.call-done = (f32[2,12,96,96]{3,2,0,1:T(8,128)}, f32[2,12,96,96]{3,2,0,1:T(8,128)}, f32[2,12,96,96]{3,2,0,1:T(8,128)}, f32[2,12,96,96]{3,2,0,1:T(8,128)}) async-done(((f32[2,12,96,96]{3,2,0,1:T(8,128)}, f32[2,12,96,96]{3,2,0,1:T(8,128)}, f32[2,12,96,96]{3,2,0,1:T(8,128)}, f32[2,12,96,96]{3,2,0,1:T(8,128)}), (f32[2,12,96,96]{3,2,0,1:T(8,128)}, f32[2,12,96,96]{3,2,0,1:T(8,128)}, ...) | async-done | bytes 3538960 | tf_op jit(solution)/shard_map/psum | solution.py:20
  138.2 13.3 broadcast_multiply_fusion.2
  151.5 9.0 fusion.52
  160.6 9.6 convolution_bitcast_fusion.1
  170.2 9.4 copy.143
  179.6 5.8 all-to-all-start.4
  185.4 10.9 fusion.55
  196.3 9.6 convolution_bitcast_fusion.2
  205.9 9.3 copy.133
  215.2 172.7 %all-to-all-done.4 = f32[16,12,96,96]{3,0,1,2:T(8,128)} async-done(((f32[16,12,96,96]{3,0,1,2:T(8,128)}), f32[16,12,96,96]{3,0,1,2:T(8,128)}, u32[]{:S(2)}, u32[]{:S(2)}) %all-to-all-start.4) | async-done | bytes 7077920 | tf_op jit(solution)/shard_map/all_to_all | solution.py:51
  388.0 8.9 all-to-all-start.2
  396.8 11.2 fusion.49
  408.0 9.6 convolution_bitcast_fusion
  417.6 9.3 copy.153
  426.9 172.5 %all-to-all-done.2 = f32[16,12,96,96]{3,0,1,2:T(8,128)} async-done(((f32[16,12,96,96]{3,0,1,2:T(8,128)}), f32[16,12,96,96]{3,0,1,2:T(8,128)}, u32[]{:S(2)}, u32[]{:S(2)}) %all-to-all-start.2) | async-done | bytes 7077920 | tf_op jit(solution)/shard_map/all_to_all | solution.py:51
  599.4 8.8 all-to-all-start.6
  608.3 11.0 fusion.58
  619.2 9.6 convolution_bitcast_fusion.3
  628.8 9.5 copy.123
  638.3 172.5 %all-to-all-done.6 = f32[16,12,96,96]{3,0,1,2:T(8,128)} async-done(((f32[16,12,96,96]{3,0,1,2:T(8,128)}), f32[16,12,96,96]{3,0,1,2:T(8,128)}, u32[]{:S(2)}, u32[]{:S(2)}) %all-to-all-start.6) | async-done | bytes 7077920 | tf_op jit(solution)/shard_map/all_to_all | solution.py:51
  810.8 8.8 all-to-all-start
  820.3 5.1 copy.145
  825.4 15.3 fusion.14
  840.7 10.0 fusion.38
  850.8 9.1 copy.147
  859.9 162.4 %all-to-all-done = f32[16,12,96,96]{3,0,1,2:T(8,128)} async-done(((f32[16,12,96,96]{3,0,1,2:T(8,128)}), f32[16,12,96,96]{3,0,1,2:T(8,128)}, u32[]{:S(2)}, u32[]{:S(2)}) %all-to-all-start) | async-done | bytes 7077920 | tf_op jit(solution)/shard_map/all_to_all | solution.py:51
  1022.2 9.2 all-to-all-start.5
  1031.5 5.1 copy.135
  1036.6 15.4 fusion.18
  1052.0 10.2 fusion.35
  1062.2 9.1 copy.137
  1071.3 162.4 %all-to-all-done.5 = f32[16,96,12,96]{3,0,2,1:T(8,128)} async-done(((f32[16,96,12,96]{3,0,2,1:T(8,128)}), f32[16,96,12,96]{3,0,2,1:T(8,128)}, u32[]{:S(2)}, u32[]{:S(2)}) %all-to-all-start.5) | async-done | bytes 7077920 | tf_op jit(solution)/shard_map/all_to_all | solution.py:54
  1233.7 8.9 all-to-all-start.3
  1242.5 5.1 copy.155
  1247.7 15.3 fusion.10
  1263.0 10.2 fusion.41
  1273.2 9.0 copy.157
  1282.2 162.9 %all-to-all-done.3 = f32[16,96,12,96]{3,0,2,1:T(8,128)} async-done(((f32[16,96,12,96]{3,0,2,1:T(8,128)}), f32[16,96,12,96]{3,0,2,1:T(8,128)}, u32[]{:S(2)}, u32[]{:S(2)}) %all-to-all-start.3) | async-done | bytes 7077920 | tf_op jit(solution)/shard_map/all_to_all | solution.py:54
  1445.1 8.8 all-to-all-start.7
  1454.0 5.1 copy.125
  1459.1 15.3 fusion.22
  1474.4 10.0 fusion.32
  1484.5 9.1 copy.127
  1493.6 163.0 %all-to-all-done.7 = f32[16,96,12,96]{3,0,2,1:T(8,128)} async-done(((f32[16,96,12,96]{3,0,2,1:T(8,128)}), f32[16,96,12,96]{3,0,2,1:T(8,128)}, u32[]{:S(2)}, u32[]{:S(2)}) %all-to-all-start.7) | async-done | bytes 7077920 | tf_op jit(solution)/shard_map/all_to_all | solution.py:54
  1656.6 8.8 all-to-all-start.1
  1671.1 4.8 copy.148
  1675.9 4.8 copy.138
  1680.7 8.5 copy.158
  1689.2 13.1 fusion.12
  1702.4 12.6 fusion.16
  1715.0 12.9 fusion.8
  1727.9 140.0 %all-to-all-done.1 = f32[16,96,12,96]{3,0,2,1:T(8,128)} async-done(((f32[16,96,12,96]{3,0,2,1:T(8,128)}), f32[16,96,12,96]{3,0,2,1:T(8,128)}, u32[]{:S(2)}, u32[]{:S(2)}) %all-to-all-start.1) | async-done | bytes 7077920 | tf_op jit(solution)/shard_map/all_to_all | solution.py:54
  1868.0 8.5 copy.128
  1876.5 15.0 fusion.20
  1891.5 18.1 multiply_reduce_fusion.6
  1909.7 16.4 multiply_reduce_fusion.5
  1926.1 17.1 multiply_reduce_fusion.4
  1943.2 15.2 multiply_reduce_fusion.7
  1958.4 17.3 multiply_reduce_fusion.3
  1975.7 10.8 add_add_fusion
  1986.5 103.9 %all-reduce.5.cloned.1.call-done = (f32[2,12,96,96]{3,2,1,0:T(8,128)}, f32[2,12,96,96]{3,2,1,0:T(8,128)}, f32[2,12,96,96]{3,2,1,0:T(8,128)}, f32[2,12,96,96]{3,2,1,0:T(8,128)}) async-done(((f32[2,12,96,96]{3,2,1,0:T(8,128)}, f32[2,12,96,96]{3,2,1,0:T(8,128)}, f32[2,12,96,96]{3,2,1,0:T(8,128)}, f32[2,12,96,96]{3,2,1,0:T(8,128)}), (f32[2,12,96,96]{3,2,1,0:T(8,128)}, f32[2,12,96,96]{3,2,1,0:T(8,128)}, ...) | async-done | bytes 3538960 | tf_op jit(solution)/shard_map/psum | solution.py:81
  2094.7 5.2 broadcast_multiply_fusion.4
  2099.9 6.3 reshape.164
  2106.2 6.2 copy.183
  (64 shorter events, 31.1 us)
Async XLA Ops:
  6.5 16.9 copy-start
  6.5 131.7 %all-reduce.7.cloned.1.call-start = ((), (), s32[]{:S(2)}) async-start(), calls=%async_computation.9 | async-start | bytes 9437184 | tf_op jit(solution)/shard_map/psum | solution.py:20
  179.6 208.4 %all-to-all-start.4 = ((f32[16,12,96,96]{3,0,1,2:T(8,128)}), f32[16,12,96,96]{3,0,1,2:T(8,128)}, u32[]{:S(2)}, u32[]{:S(2)}) async-start(f32[16,12,96,96]{3,0,1,2:T(8,128)} %copy.143), calls=%async_computation.4 | async-start | bytes 18874368 | tf_op jit(solution)/shard_map/all_to_all | solution.py:51
  388.0 211.5 %all-to-all-start.2 = ((f32[16,12,96,96]{3,0,1,2:T(8,128)}), f32[16,12,96,96]{3,0,1,2:T(8,128)}, u32[]{:S(2)}, u32[]{:S(2)}) async-start(f32[16,12,96,96]{3,0,1,2:T(8,128)} %copy.133), calls=%async_computation.2 | async-start | bytes 18874368 | tf_op jit(solution)/shard_map/all_to_all | solution.py:51
  599.4 211.4 %all-to-all-start.6 = ((f32[16,12,96,96]{3,0,1,2:T(8,128)}), f32[16,12,96,96]{3,0,1,2:T(8,128)}, u32[]{:S(2)}, u32[]{:S(2)}) async-start(f32[16,12,96,96]{3,0,1,2:T(8,128)} %copy.153), calls=%async_computation.6 | async-start | bytes 18874368 | tf_op jit(solution)/shard_map/all_to_all | solution.py:51
  810.8 211.4 %all-to-all-start = ((f32[16,12,96,96]{3,0,1,2:T(8,128)}), f32[16,12,96,96]{3,0,1,2:T(8,128)}, u32[]{:S(2)}, u32[]{:S(2)}) async-start(f32[16,12,96,96]{3,0,1,2:T(8,128)} %copy.123), calls=%async_computation | async-start | bytes 18874368 | tf_op jit(solution)/shard_map/all_to_all | solution.py:51
  1022.2 211.4 %all-to-all-start.5 = ((f32[16,96,12,96]{3,0,2,1:T(8,128)}), f32[16,96,12,96]{3,0,2,1:T(8,128)}, u32[]{:S(2)}, u32[]{:S(2)}) async-start(f32[16,96,12,96]{3,0,2,1:T(8,128)} %copy.147), calls=%async_computation.5 | async-start | bytes 18874368 | tf_op jit(solution)/shard_map/all_to_all | solution.py:54
  1233.7 211.5 %all-to-all-start.3 = ((f32[16,96,12,96]{3,0,2,1:T(8,128)}), f32[16,96,12,96]{3,0,2,1:T(8,128)}, u32[]{:S(2)}, u32[]{:S(2)}) async-start(f32[16,96,12,96]{3,0,2,1:T(8,128)} %copy.137), calls=%async_computation.3 | async-start | bytes 18874368 | tf_op jit(solution)/shard_map/all_to_all | solution.py:54
  1445.1 211.4 %all-to-all-start.7 = ((f32[16,96,12,96]{3,0,2,1:T(8,128)}), f32[16,96,12,96]{3,0,2,1:T(8,128)}, u32[]{:S(2)}, u32[]{:S(2)}) async-start(f32[16,96,12,96]{3,0,2,1:T(8,128)} %copy.157), calls=%async_computation.7 | async-start | bytes 18874368 | tf_op jit(solution)/shard_map/all_to_all | solution.py:54
  1493.6 174.2 %copy-start.3 = (f32[2,12,96,96]{3,2,0,1:T(8,128)S(1)}, f32[2,12,96,96]{3,2,0,1:T(8,128)}, u32[]{:S(2)}) copy-start(f32[2,12,96,96]{3,2,0,1:T(8,128)} %get-tuple-element.26) | copy-start | bytes 2654212
  1493.6 175.3 %copy-start.2 = (f32[2,12,96,96]{3,2,0,1:T(8,128)S(1)}, f32[2,12,96,96]{3,2,0,1:T(8,128)}, u32[]{:S(2)}) copy-start(f32[2,12,96,96]{3,2,0,1:T(8,128)} %get-tuple-element.27) | copy-start | bytes 2654212
  1493.6 176.4 %copy-start.1 = (f32[2,12,96,96]{3,2,0,1:T(8,128)S(1)}, f32[2,12,96,96]{3,2,0,1:T(8,128)}, u32[]{:S(2)}) copy-start(f32[2,12,96,96]{3,2,0,1:T(8,128)} %get-tuple-element.28) | copy-start | bytes 2654212
  1656.6 211.4 %all-to-all-start.1 = ((f32[16,96,12,96]{3,0,2,1:T(8,128)}), f32[16,96,12,96]{3,0,2,1:T(8,128)}, u32[]{:S(2)}, u32[]{:S(2)}) async-start(f32[16,96,12,96]{3,0,2,1:T(8,128)} %copy.127), calls=%async_computation.1 | async-start | bytes 18874368 | tf_op jit(solution)/shard_map/all_to_all | solution.py:54
  1665.4 425.0 %all-reduce.5.cloned.1.call-start = ((), (), s32[]{:S(2)}) async-start(), calls=%async_computation.8 | async-start | bytes 9437184 | tf_op jit(solution)/shard_map/psum | solution.py:81
  1689.2 25.8 %slice-start.9 = ((s8[9437184]{0:T(1024)(128)(4,1)}), s8[4194304]{0:T(1024)(128)(4,1)S(1)}, s32[]{:S(2)}) async-start(s8[9437184]{0:T(1024)(128)(4,1)} %bitcast.191), calls=%async_computation.19 | async-start | bytes 8388608
  1689.2 25.8 %slice-start.10 = ((s8[9437184]{0:T(1024)(128)(4,1)}), s8[4194304]{0:T(1024)(128)(4,1)S(1)}, s32[]{:S(2)}) async-start(s8[9437184]{0:T(1024)(128)(4,1)} %bitcast.191), calls=%async_computation.20 | async-start | bytes 8388608
  1702.4 12.6 slice-start.11
  1876.5 15.0 copy-start.5
  1876.5 33.1 %slice-start.3 = ((s8[9437184]{0:T(1024)(128)(4,1)}), s8[4194304]{0:T(1024)(128)(4,1)S(1)}, s32[]{:S(2)}) async-start(s8[9437184]{0:T(1024)(128)(4,1)} %bitcast.185), calls=%async_computation.13 | async-start | bytes 8388608
  1876.5 33.1 %slice-start.4 = ((s8[9437184]{0:T(1024)(128)(4,1)}), s8[4194304]{0:T(1024)(128)(4,1)S(1)}, s32[]{:S(2)}) async-start(s8[9437184]{0:T(1024)(128)(4,1)} %bitcast.185), calls=%async_computation.14 | async-start | bytes 8388608
  1891.5 18.2 slice-start.5
  1891.5 34.6 %slice-start = ((s8[9437184]{0:T(1024)(128)(4,1)}), s8[4194304]{0:T(1024)(128)(4,1)S(1)}, s32[]{:S(2)}) async-start(s8[9437184]{0:T(1024)(128)(4,1)} %bitcast.183), calls=%async_computation.10 | async-start | bytes 8388608
  1891.5 34.5 %slice-start.1 = ((s8[9437184]{0:T(1024)(128)(4,1)}), s8[4194304]{0:T(1024)(128)(4,1)S(1)}, s32[]{:S(2)}) async-start(s8[9437184]{0:T(1024)(128)(4,1)} %bitcast.183), calls=%async_computation.11 | async-start | bytes 8388608
  1909.7 16.4 slice-start.2
  1909.7 33.5 %slice-start.6 = ((s8[9437184]{0:T(1024)(128)(4,1)}), s8[4194304]{0:T(1024)(128)(4,1)S(1)}, s32[]{:S(2)}) async-start(s8[9437184]{0:T(1024)(128)(4,1)} %bitcast.187), calls=%async_computation.16 | async-start | bytes 8388608
  1909.7 33.5 %slice-start.7 = ((s8[9437184]{0:T(1024)(128)(4,1)}), s8[1048576]{0:T(1024)(128)(4,1)S(1)}, s32[]{:S(2)}) async-start(s8[9437184]{0:T(1024)(128)(4,1)} %bitcast.187), calls=%async_computation.17 | async-start | bytes 2097152
  1926.1 17.1 slice-start.8
  1926.1 17.1 copy-start.4
  1926.1 32.3 %slice-start.12 = ((s8[4718592]{0:T(1024)(128)(4,1)}), s8[524288]{0:T(1024)(128)(4,1)S(1)}, s32[]{:S(2)}) async-start(s8[4718592]{0:T(1024)(128)(4,1)} %bitcast.195), calls=%async_computation.22 | async-start | bytes 1048576
  1943.2 15.2 slice-start.13
Sparse Core Ops, SparseCore 0:
  23.6 114.6 all-reduce.6
  1975.8 114.5 all-reduce.4
where the time goes:
time: 2130 us; the launch traced here: 2120 us
  waiting for transfers between devices  1520 us (71%)
  matrix products  303 us (14%)
  local copies, waits for them, and re-layouts  155 us (7%)
  starting transfers between devices  68.1 us (3%)
  other arithmetic  56.1 us (3%)
    all_to_all x4, waiting for transfers between devices, coulomb_solve(): lax.all_to_all(field, 'plane', split_axis=2, concat_axis=1, tiled=True)  680 us
    all_to_all x4, waiting for transfers between devices, coulomb_solve(): lax.all_to_all(field, 'plane', split_axis=1, concat_axis=2, tiled=True)  628 us
    psum x1, waiting for transfers between devices, from_root(): return lax.psum(kept, axis)  111 us
    psum x1, waiting for transfers between devices, local(): summed = lax.psum(owner_terms[turn], 'band')  104 us
    dot_general x4, matrix products, coulomb_solve(): return jnp.einsum('pxyz,yv->pxvz', field, table, precision=HIGHEST)  66.8 us
    dot_general x4, matrix products, coulomb_solve(): jnp.einsum('pxyz,xu->puyz', field, table, precision=HIGHEST) * kernel  61.4 us
    dot_general x4, matrix products, coulomb_solve(): field = jnp.einsum('pxyz,zw->pxyw', field, table, precision=HIGHEST)  53.7 us
  transfers between devices with their start and end apart: 10, of which 10 were waited for; matrix products, arithmetic and copies ran while one was open for 15% of the time, Pallas kernels for 0%

commit v1 on v0

v1 whole, which is shorter than its diff:
```python
import functools
import math

import jax
import jax.numpy as jnp
import numpy as np
from jax import lax
from jax.experimental import pallas as pl
from jax.experimental.pallas import tpu as pltpu
from jax.sharding import Mesh, PartitionSpec as P

PAIR = 2
ROUNDS = 4
OMEGA = 0.106
CELL = 41.05
ALPHA = 0.25
LANES = 128
F32 = jnp.float32
BF16 = jnp.bfloat16


def hartley_table(count):
    index = np.arange(count)
    angle = (index[:, None] * index[None, :] % count).astype(np.float64) * (2.0 * math.pi / count)
    return (np.cos(angle) + np.sin(angle)).astype(np.float32)


def halves(value):
    high = value.astype(BF16)
    return high, (value - high.astype(F32)).astype(BF16)


def np_halves(value):
    high = value.astype(BF16)
    return high, (value - high.astype(np.float32)).astype(BF16)


def row_order(count):
    return np.arange(count).reshape(count // 4, 4).T.reshape(-1)


def lane_table(count):
    table = np.zeros((LANES, LANES), np.float32)
    table[:count, :count] = hartley_table(count)
    high, low = np_halves(table)
    top = np.concatenate([high, low], axis=1)
    return np.concatenate([top, np.concatenate([high, np.zeros_like(low)], axis=1)], axis=0)


def row_table(table):
    high, low = np_halves(table)
    top = np.concatenate([high, high], axis=1)
    return np.concatenate([top, np.concatenate([low, np.zeros_like(low)], axis=1)], axis=0)


def frequencies(count):
    index = jnp.arange(count, dtype=jnp.int32)
    return jnp.where(index <= count // 2, index, index - count).astype(F32)


def screened_kernel(count):
    freq = frequencies(count)
    square = freq * freq
    scale = (2.0 * math.pi / CELL) ** 2
    wide = jnp.pad(square, (0, LANES - count))
    g_two = scale * (
        square.reshape(count // 2, 1, 2, 1) + square[None, :, None, None] + wide[None, None, None, :]
    )
    positive = g_two > 0
    safe = jnp.where(positive, g_two, 1.0)
    value = 4.0 * math.pi / safe * -jnp.expm1(-safe / (4.0 * OMEGA * OMEGA))
    value = jnp.where(positive, value, math.pi / (OMEGA * OMEGA))
    return (value / float(count**3)).reshape(count // 2, count, 2 * LANES)


def to_rows(parts):
    first, second, third = parts
    lane = lax.broadcasted_iota(jnp.int32, first.shape, 1)
    row1 = jnp.where(lane < 32, pltpu.roll(first, 32, 1), pltpu.roll(second, 32, 1))
    row2 = jnp.where(lane < 64, pltpu.roll(second, 64, 1), pltpu.roll(third, 64, 1))
    row3 = pltpu.roll(third, 96, 1)
    return jnp.concatenate([first, row1, row2, row3], axis=0)


def from_rows(plane):
    step = plane.shape[0] // 4
    row0, row1, row2, row3 = (plane[k * step : (k + 1) * step] for k in range(4))
    lane = lax.broadcasted_iota(jnp.int32, row0.shape, 1)
    first = jnp.where(lane < 96, row0, pltpu.roll(row1, 96, 1))
    second = jnp.where(lane < 64, pltpu.roll(row1, 96, 1), pltpu.roll(row2, 64, 1))
    third = jnp.where(lane < 32, pltpu.roll(row2, 64, 1), pltpu.roll(row3, 32, 1))
    return first, second, third


def dot(a, b):
    return jnp.dot(a, b, preferred_element_type=F32)


def along_lanes(value, table):
    out = dot(jnp.concatenate(halves(value), axis=1), table)
    return out[:, :LANES] + out[:, LANES:]


def along_rows(table, value):
    out = dot(table, jnp.concatenate(halves(value), axis=0))
    half = out.shape[0] // 2
    return out[:half] + out[half:]


def pair_kernel(
    count, partner, orbital, acc_in, lanes, rows_in, rows_mid, rows_out, coulomb, acc, owner, field
):
    third = count // 4

    def density(x):
        parts = []
        for r in range(3):
            place = pl.ds(r * third, third)
            parts.append(orbital[0, x, place, :] * partner[0, x, place, :])
        return to_rows(parts)

    def forward(step, carry):
        x = 2 * step
        both = jnp.concatenate([density(x), density(x + 1)], axis=0)
        both = along_lanes(both, lanes[...])
        both = jnp.concatenate([both[:count], both[count:]], axis=1)
        both = along_rows(rows_in[...], both)
        start = pl.multiple_of(x * count, 2 * count)
        field[pl.ds(start, count), :] = both[:, :LANES]
        field[pl.ds(start + count, count), :] = both[:, LANES:]
        return carry

    lax.fori_loop(0, count // 2, forward, 0)

    def middle(step, carry):
        v = 2 * step
        both = jnp.concatenate(
            [field[pl.ds(v, count, stride=count), :], field[pl.ds(v + 1, count, stride=count), :]], axis=1
        )
        both = along_rows(rows_mid[...], both) * coulomb[step]
        both = along_rows(rows_mid[...], both)
        field[pl.ds(v, count, stride=count), :] = both[:, :LANES]
        field[pl.ds(v + 1, count, stride=count), :] = both[:, LANES:]
        return carry

    lax.fori_loop(0, count // 2, middle, 0)

    first = pl.program_id(0) == 0

    def backward(step, carry):
        x = 2 * step
        start = pl.multiple_of(x * count, 2 * count)
        both = jnp.concatenate([field[pl.ds(start, count), :], field[pl.ds(start + count, count), :]], axis=1)
        both = along_rows(rows_out[...], both)
        both = along_lanes(jnp.concatenate([both[:, :LANES], both[:, LANES:]], axis=0), lanes[...])
        for k in range(2):
            for r, part in enumerate(from_rows(both[k * count : (k + 1) * count])):
                place = pl.ds(r * third, third)
                acc[0, x + k, place, :] = acc_in[0, x + k, place, :] + partner[0, x + k, place, :] * part
                term = orbital[0, x + k, place, :] * part
                owner[0, x + k, place, :] = jnp.where(first, 0.0, owner[0, x + k, place, :]) + term
        return carry

    lax.fori_loop(0, count // 2, backward, 0)


def pair_solve(partner, orbitals, acc, tables):
    lanes, rows_in, rows_mid, rows_out, coulomb = tables
    number, count, rows, _ = orbitals.shape
    block = (1, count, rows, LANES)
    one = pl.BlockSpec(block, lambda i: (0, 0, 0, 0), pipeline_mode=pl.Buffered(1))
    each = pl.BlockSpec(block, lambda i: (i, 0, 0, 0))
    whole = lambda a: pl.BlockSpec(a.shape, lambda i: (0,) * a.ndim, pipeline_mode=pl.Buffered(1))
    return pl.pallas_call(
        functools.partial(pair_kernel, count),
        grid=(number,),
        in_specs=[one, each, each] + [whole(t) for t in tables],
        out_specs=[each, pl.BlockSpec(block, lambda i: (0, 0, 0, 0))],
        out_shape=[jax.ShapeDtypeStruct(orbitals.shape, F32), jax.ShapeDtypeStruct(partner.shape, F32)],
        scratch_shapes=[pltpu.VMEM((count * count, LANES), F32)],
        input_output_aliases={2: 0},
        cost_estimate=pl.CostEstimate(
            flops=number * 36 * count**3 * LANES, bytes_accessed=16 * number * count * rows * LANES, transcendentals=0
        ),
        compiler_params=pltpu.CompilerParams(vmem_limit_bytes=60 * 1024 * 1024),
    )(partner, orbitals, acc, lanes, rows_in, rows_mid, rows_out, coulomb)


def make_tables(count):
    table = hartley_table(count)
    order = row_order(count)
    return (
        jnp.asarray(lane_table(count)),
        jnp.asarray(row_table(table[:, order])),
        jnp.asarray(row_table(table)),
        jnp.asarray(row_table(table[order, :])),
        screened_kernel(count),
    )


def pack(fields):
    number, planes, flat = fields.shape
    return fields.reshape(number, planes, flat // 384, 3, LANES).swapaxes(2, 3).reshape(number, planes, flat // LANES, LANES)


def unpack(fields):
    number, planes, rows, _ = fields.shape
    return fields.reshape(number, planes, 3, rows // 3, LANES).swapaxes(2, 3).reshape(number, planes, rows * LANES)


def local(orbitals):
    packed = pack(orbitals)
    n_local, planes, rows, _ = packed.shape
    zs = lax.axis_size("z")
    count = planes * zs * 2
    tables = make_tables(count)
    tail = (rows, LANES)
    core = lax.axis_index("core")

    mine = lax.all_to_all(packed[0:PAIR], "core", split_axis=0, concat_axis=1, tiled=True)
    partners = lax.all_gather(mine, ("band", "z"), axis=0, tiled=False)
    bands = lax.axis_size("band")
    partners = partners.reshape((bands, count) + tail)

    split = lax.all_to_all(packed, "z", split_axis=0, concat_axis=1, tiled=True)
    own = n_local // zs
    whole = lax.all_gather(split.reshape((own, zs, planes) + tail), "core", axis=2, tiled=False)
    whole = whole.reshape((own, count) + tail)

    acc = jnp.zeros_like(whole)
    terms = []
    for turn in range(ROUNDS):
        acc, term = pair_solve(partners[turn : turn + 1], whole, acc, tables)
        terms.append(term)
    terms += [jnp.zeros_like(terms[0])] * (bands - ROUNDS)
    owner = jnp.concatenate(terms, axis=0).reshape((bands * zs, 2 * planes) + tail)
    owner = lax.psum_scatter(owner, ("band", "z"), scatter_dimension=0, tiled=True)
    owner = lax.all_to_all(owner.reshape((1, 2 * planes) + tail), "core", split_axis=1, concat_axis=0, tiled=True)

    acc = acc.reshape((own, zs, 2, planes) + tail)
    acc = lax.psum_scatter(acc, "core", scatter_dimension=2, tiled=False)
    acc = acc.reshape((own, zs * planes) + tail)
    acc = lax.all_to_all(acc, "z", split_axis=1, concat_axis=0, tiled=True)
    acc = acc.at[0:PAIR].add(owner)
    return -ALPHA * unpack(acc)


def solution(mesh):
    bands, planes = mesh.devices.shape
    inner = Mesh(mesh.devices.reshape(bands, planes // 2, 2), ("band", "z", "core"))
    placed = P("band", ("z", "core"), None)
    return jax.shard_map(local, mesh=inner, in_specs=(placed,), out_specs=placed, check_vma=False)
```

time: 2130 us -> 1370 us (0.64)
  waiting for transfers between devices: 1520 us -> 620 us
  Pallas kernels: 0 us -> 531 us
  matrix products: 303 us -> 0 us
  blocking collectives: 0 us -> 92 us
  local copies, waits for them, and re-layouts: 155 us -> 82.4 us
  starting transfers between devices: 68.1 us -> 4.99 us
  other arithmetic: 56.1 us -> 22.6 us
    all_to_all x8 -> x1, waiting for transfers between devices: 1310 us -> 149 us  [local(): acc = lax.all_to_all(acc, 'z', split_axis=1, concat_axis=0, tiled=True)]
    pallas_call x0 -> x4, Pallas kernels: none -> 531 us  [pair_solve(): pl.pallas_call(functools.partial(pair_kernel, count), grid=(number,), in_...]
    unnamed x2 -> x6, waiting for transfers between devices: 0.03 us -> 317 us
    dot_general x24 -> x0, matrix products: 303 us -> none  [the longest x4 66.8 us: coulomb_solve(): return jnp.einsum('pxyz,yv->pxvz', field, table, precision=HIGHEST)]
    psum x2 -> x0, waiting for transfers between devices: 215 us -> none  [the longest x1 111 us: from_root(): return lax.psum(kept, axis)]
    all_gather x0 -> x2, waiting for transfers between devices: none -> 154 us  [the longest x1 154 us: local(): partners = lax.all_gather(mine, ('band', 'z'), axis=0, tiled=False)]
    all_to_all x0 -> x3, blocking collectives: none -> 92 us  [the longest x1 80.9 us: local(): split = lax.all_to_all(packed, 'z', split_axis=0, concat_axis=1, tiled=True)]
    transpose x8 -> x1, local copies, waits for them, and re-layouts: 73.8 us -> 2.61 us  [pack(): fields.reshape(number, planes, flat // 384, 3, LANES).swapaxes(2, 3)]
  transfers between devices with their start and end apart: 10 -> 5, of which waited for: 10 -> 4; matrix products, arithmetic and copies ran while one was open for 15% -> 5% of each run, Pallas kernels for 0% -> 0%
where the time goes in v1:
time: 1370 us
  waiting for transfers between devices  620 us (45%)
  Pallas kernels  531 us (39%)
  blocking collectives  92 us (7%)
  local copies, waits for them, and re-layouts  82.4 us (6%)
  other arithmetic  22.6 us (2%)
    pallas_call x4, Pallas kernels, pair_solve(): pl.pallas_call(functools.partial(pair_kernel, count), grid=(number,), in_...  531 us
    unnamed x6, waiting for transfers between devices  317 us
    all_gather x1, waiting for transfers between devices, local(): partners = lax.all_gather(mine, ('band', 'z'), axis=0, tiled=False)  154 us
    all_to_all x1, waiting for transfers between devices, local(): acc = lax.all_to_all(acc, 'z', split_axis=1, concat_axis=0, tiled=True)  149 us
    all_to_all x1, blocking collectives, local(): split = lax.all_to_all(packed, 'z', split_axis=0, concat_axis=1, tiled=True)  80.9 us
  transfers between devices with their start and end apart: 5, of which 4 were waited for; matrix products, arithmetic and copies ran while one was open for 5% of the time, Pallas kernels for 0%

profile of v1, /device:TPU:17, one launch (start us, length us, event | category | flops | bytes accessed | tf_op | source)
XLA Modules:
  0.0 1366.0 jit_solution(4536985697339559354)
XLA Ops:
  6.5 0.0 all-gather.6.cloned.1.call-start
  6.5 6.7 reshape.112
  13.2 2.6 copy.27
  15.8 80.9 %all_to_all.51 = f32[8,12,72,128]{3,2,1,0:T(8,128)} all-to-all(f32[8,12,72,128]{3,2,1,0:T(8,128)S(1)} %bitcast.55), channel_id=1, replica_groups=mesh['band'=4,'z'=4,'core'=2] {'z'}, dimensions={0} | all-to-all | bytes 7077888 | tf_op jit(solution)/shard_map/all_to_all | solution.py:225
  96.7 0.0 all-gather.6.cloned.1.call-update
  96.7 0.0 all-gather.4.cloned.1.call-start
  96.8 1.5 slice.71
  98.3 0.1 copy.26
  98.4 6.3 all_to_all.52
  104.7 0.0 all-gather.4.cloned.1.call-update
  104.7 0.0 all-reduce.6.cloned.1.call-start
  104.8 0.3 broadcast_add_fusion
  105.2 6.4 add.72
  111.6 7.3 add.73
  118.9 7.4 fusion.coulomb
  126.3 0.0 all-gather.6.cloned.1.call-done
  126.3 6.4 copy.28
  132.7 153.8 %all-gather.4.cloned.1.call-done = f32[16,1,24,72,128]{4,3,2,1,0:T(8,128)} async-done(((f32[1,1,24,72,128]{4,3,2,1,0:T(8,128)}), f32[16,1,24,72,128]{4,3,2,1,0:T(8,128)}) %all-gather.4.cloned.1.call-update) | async-done | bytes 14155792 | tf_op jit(solution)/shard_map/all_gather | solution.py:221
  286.5 10.5 fusion.7
  297.0 3.3 broadcast_in_dim.12.acc_in
  300.3 132.8 %shard_map.55 = (f32[2,96,72,128]{3,2,1,0:T(8,128)}, f32[1,96,72,128]{3,2,1,0:T(8,128)}) custom-call(f32[1,96,72,128]{3,2,1,0:T(8,128)} %bitcast.64, f32[2,96,72,128]{3,2,1,0:T(8,128)} %bitcast.56, f32[2,96,72,128]{3,2,1,0:T(8,128)} %broadcast_in_dim.12.acc_in, bf16[256,256]{1,0:T(8,128)(2,1)} %constant.71.clone.lanes, ...), custom_call_target="tpu_custom_call", output_to_operand_aliasing={{0}: (2, {})} | custom-call | flops 8153726976 | bytes 28311552 | tf_op jit(solution)/shard_map/pallas_call | solution.py:174
  433.2 132.9 %shard_map.56 = (f32[2,96,72,128]{3,2,1,0:T(8,128)}, f32[1,96,72,128]{3,2,1,0:T(8,128)}) custom-call(f32[1,96,72,128]{3,2,1,0:T(8,128)} %bitcast.63, f32[2,96,72,128]{3,2,1,0:T(8,128)} %bitcast.57, f32[2,96,72,128]{3,2,1,0:T(8,128)} %get-tuple-element.25.acc_in, bf16[256,256]{1,0:T(8,128)(2,1)} %constant.71.clone.lanes, ...), custom_call_target="tpu_custom_call", output_to_operand_aliasing={{0}: (2, {})} | custom-call | flops 8153726976 | bytes 28311552 | tf_op jit(solution)/shard_map/pallas_call | solution.py:174
  566.0 132.8 %shard_map.57 = (f32[2,96,72,128]{3,2,1,0:T(8,128)}, f32[1,96,72,128]{3,2,1,0:T(8,128)}) custom-call(f32[1,96,72,128]{3,2,1,0:T(8,128)} %bitcast.62, f32[2,96,72,128]{3,2,1,0:T(8,128)} %bitcast.58, f32[2,96,72,128]{3,2,1,0:T(8,128)} %get-tuple-element.26.acc_in, bf16[256,256]{1,0:T(8,128)(2,1)} %constant.71.clone.lanes, ...), custom_call_target="tpu_custom_call", output_to_operand_aliasing={{0}: (2, {})} | custom-call | flops 8153726976 | bytes 28311552 | tf_op jit(solution)/shard_map/pallas_call | solution.py:174
  698.9 132.7 %shard_map.58 = (f32[2,96,72,128]{3,2,1,0:T(8,128)}, f32[1,96,72,128]{3,2,1,0:T(8,128)}) custom-call(f32[1,96,72,128]{3,2,1,0:T(8,128)} %bitcast.61, f32[2,96,72,128]{3,2,1,0:T(8,128)} %bitcast.59, f32[2,96,72,128]{3,2,1,0:T(8,128)} %get-tuple-element.27.acc_in, bf16[256,256]{1,0:T(8,128)(2,1)} %constant.71.clone.lanes, ...), custom_call_target="tpu_custom_call", output_to_operand_aliasing={{0}: (2, {})} | custom-call | flops 8153726976 | bytes 28311552 | tf_op jit(solution)/shard_map/pallas_call | solution.py:174
  831.6 0.0 copy-start
  831.6 0.0 all-reduce.6.cloned.1.call-update
  831.6 0.2 all-reduce.8.cloned.1.call-start
  831.8 1.7 copy-done
  833.6 10.3 pad_maximum_fusion
  843.9 13.3 copy.32
  857.2 0.0 copy-start.2
  857.2 0.0 all-reduce.8.cloned.1.call-update
  857.2 0.6 copy-done.2
  857.8 0.6 dynamic-slice.7
  858.4 7.1 all-reduce.6.cloned.1.call-done
  865.6 2.9 constant_dynamic-slice_fusion.1
  868.5 2.1 copy.29
  870.5 0.0 copy-start.1
  870.5 4.7 all-to-all-start.2
  875.2 0.0 copy-done.1
  875.2 0.6 dynamic-slice.9
  875.8 149.3 %all-to-all-done.2 = f32[2,48,72,128]{3,2,0,1:T(8,128)S(1)} async-done(((f32[2,48,72,128]{3,2,0,1:T(8,128)}), f32[2,48,72,128]{3,2,0,1:T(8,128)S(1)}, u32[]{:S(2)}, u32[]{:S(2)}) %all-to-all-start.2) | async-done | bytes 3538976 | tf_op jit(solution)/shard_map/all_to_all | solution.py:243
  1025.1 2.1 copy.31
  1027.1 2.0 copy.30
  1029.1 309.4 %all-reduce.8.cloned.1.call-done = f32[16,24,72,128]{3,2,0,1:T(8,128)} async-done(((f32[16,24,72,128]{3,2,0,1:T(8,128)}), f32[16,24,72,128]{3,2,0,1:T(8,128)}) %all-reduce.8.cloned.1.call-update) | async-done | bytes 14155792
  1338.5 1.8 constant_dynamic-slice_fusion
  1340.3 4.7 all_to_all.53
  1345.0 2.2 fusion.2
  1347.2 2.3 broadcast_multiply_fusion
  1349.5 3.5 copy.33
  1353.0 6.5 mul.50
  (4 shorter events, 0.0 us)
Async XLA Ops:
  6.5 119.7 %all-gather.6.cloned.1.call-start = ((), (), s32[]{:S(2)}) async-start(), calls=%async_computation.5 | async-start | bytes 10616832 | tf_op jit(solution)/shard_map/all_gather | solution.py:227
  96.7 189.7 %all-gather.4.cloned.1.call-start = ((), (), s32[]{:S(2)}) async-start(), calls=%async_computation.4 | async-start | bytes 15040512 | tf_op jit(solution)/shard_map/all_gather | solution.py:221
  104.7 760.8 %all-reduce.6.cloned.1.call-start = ((), (), s32[]{:S(2)}) async-start(), calls=%async_computation.6 | async-start | bytes 14155776
  831.6 2.0 copy-start
  831.6 506.9 %all-reduce.8.cloned.1.call-start = ((), (), s32[]{:S(2)}) async-start(), calls=%async_computation.7 | async-start | bytes 28311552
  857.2 0.7 copy-start.2
  870.5 4.7 copy-start.1
  870.5 154.5 %all-to-all-start.2 = ((f32[2,48,72,128]{3,2,0,1:T(8,128)}), f32[2,48,72,128]{3,2,0,1:T(8,128)S(1)}, u32[]{:S(2)}, u32[]{:S(2)}) async-start(f32[2,48,72,128]{3,2,0,1:T(8,128)} %copy.29), calls=%async_computation.2 | async-start | bytes 7077888 | tf_op jit(solution)/shard_map/all_to_all | solution.py:243
Sparse Core Ops, SparseCore 0:
  96.9 20.7 all-gather.5
  120.4 165.9 all-gather.3
  831.7 33.7 all-reduce.5
  873.0 465.4 all-reduce.7

commit v2 on v1

v2 whole, which is shorter than its diff:
```python
import functools
import math

import jax
import jax.numpy as jnp
import numpy as np
from jax import lax
from jax.experimental import pallas as pl
from jax.experimental.pallas import tpu as pltpu
from jax.sharding import Mesh, PartitionSpec as P

PAIR = 2
ROUNDS = 4
OMEGA = 0.106
CELL = 41.05
ALPHA = 0.25
LANES = 128
F32 = jnp.float32
BF16 = jnp.bfloat16
GROUP = 8


def hartley_table(count):
    index = np.arange(count)
    angle = (index[:, None] * index[None, :] % count).astype(np.float64) * (2.0 * math.pi / count)
    return (np.cos(angle) + np.sin(angle)).astype(np.float32)


def halves(value):
    high = value.astype(BF16)
    return high, (value - high.astype(F32)).astype(BF16)


def np_halves(value):
    high = value.astype(BF16)
    return high, (value - high.astype(np.float32)).astype(BF16)


def row_order(count):
    return np.arange(count).reshape(count // 4, 4).T.reshape(-1)


def lane_table(count):
    table = np.zeros((LANES, LANES), np.float32)
    table[:count, :count] = hartley_table(count)
    high, low = np_halves(table)
    top = np.concatenate([high, low], axis=1)
    return np.concatenate([top, np.concatenate([high, np.zeros_like(low)], axis=1)], axis=0)


def row_table(table):
    high, low = np_halves(table)
    top = np.concatenate([high, high], axis=1)
    return np.concatenate([top, np.concatenate([low, np.zeros_like(low)], axis=1)], axis=0)


def frequencies(count):
    index = jnp.arange(count, dtype=jnp.int32)
    return jnp.where(index <= count // 2, index, index - count).astype(F32)


def screened_kernel(count):
    freq = frequencies(count)
    square = freq * freq
    scale = (2.0 * math.pi / CELL) ** 2
    wide = jnp.pad(square, (0, LANES - count))
    g_two = scale * (
        square.reshape(count // 2, 1, 2, 1) + square[None, :, None, None] + wide[None, None, None, :]
    )
    positive = g_two > 0
    safe = jnp.where(positive, g_two, 1.0)
    value = 4.0 * math.pi / safe * -jnp.expm1(-safe / (4.0 * OMEGA * OMEGA))
    value = jnp.where(positive, value, math.pi / (OMEGA * OMEGA))
    return (value / float(count**3)).reshape(count // 2, count, 2 * LANES)


def to_rows(parts):
    first, second, third = parts
    lane = lax.broadcasted_iota(jnp.int32, first.shape, 1)
    row1 = jnp.where(lane < 32, pltpu.roll(first, 32, 1), pltpu.roll(second, 32, 1))
    row2 = jnp.where(lane < 64, pltpu.roll(second, 64, 1), pltpu.roll(third, 64, 1))
    row3 = pltpu.roll(third, 96, 1)
    return jnp.concatenate([first, row1, row2, row3], axis=0)


def from_rows(plane):
    step = plane.shape[0] // 4
    row0, row1, row2, row3 = (plane[k * step : (k + 1) * step] for k in range(4))
    lane = lax.broadcasted_iota(jnp.int32, row0.shape, 1)
    first = jnp.where(lane < 96, row0, pltpu.roll(row1, 96, 1))
    second = jnp.where(lane < 64, pltpu.roll(row1, 96, 1), pltpu.roll(row2, 64, 1))
    third = jnp.where(lane < 32, pltpu.roll(row2, 64, 1), pltpu.roll(row3, 32, 1))
    return first, second, third


def dot(a, b):
    return jnp.dot(a, b, preferred_element_type=F32)


def along_lanes(value, table):
    out = dot(jnp.concatenate(halves(value), axis=1), table)
    return out[:, :LANES] + out[:, LANES:]


def along_rows(table, value):
    out = dot(table, jnp.concatenate(halves(value), axis=0))
    half = out.shape[0] // 2
    return out[:half] + out[half:]


def pair_kernel(
    count, fresh, partner, orbital, *refs
):
    acc_in = None if fresh else refs[0]
    lanes, rows_in, rows_mid, rows_out, coulomb, acc, owner, field = refs[-8:]
    third = count // 4

    def density(x):
        parts = []
        for r in range(3):
            place = pl.ds(r * third, third)
            parts.append(orbital[0, x, place, :] * partner[0, x, place, :])
        return to_rows(parts)

    def forward(step, carry):
        base = 2 * GROUP * step
        pairs = [
            jnp.concatenate([density(base + 2 * g), density(base + 2 * g + 1)], axis=0) for g in range(GROUP)
        ]
        pairs = [along_lanes(both, lanes[...]) for both in pairs]
        pairs = [jnp.concatenate([both[:count], both[count:]], axis=1) for both in pairs]
        pairs = [along_rows(rows_in[...], both) for both in pairs]
        start = pl.multiple_of(base * count, 2 * count)
        for g, both in enumerate(pairs):
            field[pl.ds(start + 2 * g * count, count), :] = both[:, :LANES]
            field[pl.ds(start + (2 * g + 1) * count, count), :] = both[:, LANES:]
        return carry

    lax.fori_loop(0, count // 2 // GROUP, forward, 0)

    def middle(step, carry):
        base = 2 * GROUP * step
        pairs = [
            jnp.concatenate(
                [field[pl.ds(base + 2 * g + k, count, stride=count), :] for k in range(2)], axis=1
            )
            for g in range(GROUP)
        ]
        pairs = [along_rows(rows_mid[...], both) for both in pairs]
        pairs = [both * coulomb[GROUP * step + g] for g, both in enumerate(pairs)]
        pairs = [along_rows(rows_mid[...], both) for both in pairs]
        for g, both in enumerate(pairs):
            for k in range(2):
                field[pl.ds(base + 2 * g + k, count, stride=count), :] = both[:, k * LANES : (k + 1) * LANES]
        return carry

    lax.fori_loop(0, count // 2 // GROUP, middle, 0)

    first = pl.program_id(0) == 0

    def backward(step, carry):
        base = 2 * GROUP * step
        start = pl.multiple_of(base * count, 2 * count)
        pairs = [
            jnp.concatenate([field[pl.ds(start + (2 * g + k) * count, count), :] for k in range(2)], axis=1)
            for g in range(GROUP)
        ]
        pairs = [along_rows(rows_out[...], both) for both in pairs]
        pairs = [jnp.concatenate([both[:, :LANES], both[:, LANES:]], axis=0) for both in pairs]
        pairs = [along_lanes(both, lanes[...]) for both in pairs]
        for g, both in enumerate(pairs):
            for k in range(2):
                x = base + 2 * g + k
                for r, part in enumerate(from_rows(both[k * count : (k + 1) * count])):
                    place = pl.ds(r * third, third)
                    near = partner[0, x, place, :] * part
                    acc[0, x, place, :] = near if fresh else acc_in[0, x, place, :] + near
                    term = orbital[0, x, place, :] * part
                    owner[0, x, place, :] = jnp.where(first, 0.0, owner[0, x, place, :]) + term
        return carry

    lax.fori_loop(0, count // 2 // GROUP, backward, 0)


def pair_solve(partner, orbitals, acc, tables):
    number, count, rows, _ = orbitals.shape
    block = (1, count, rows, LANES)
    one = pl.BlockSpec(block, lambda i: (0, 0, 0, 0), pipeline_mode=pl.Buffered(1))
    each = pl.BlockSpec(block, lambda i: (i, 0, 0, 0))
    whole = lambda a: pl.BlockSpec(a.shape, lambda i: (0,) * a.ndim, pipeline_mode=pl.Buffered(1))
    fresh = acc is None
    start = () if fresh else (acc,)
    return pl.pallas_call(
        functools.partial(pair_kernel, count, fresh),
        grid=(number,),
        in_specs=[one, each] + [each] * len(start) + [whole(t) for t in tables],
        out_specs=[each, pl.BlockSpec(block, lambda i: (0, 0, 0, 0))],
        out_shape=[jax.ShapeDtypeStruct(orbitals.shape, F32), jax.ShapeDtypeStruct(partner.shape, F32)],
        scratch_shapes=[pltpu.VMEM((count * count, LANES), F32)],
        input_output_aliases={} if fresh else {2: 0},
        cost_estimate=pl.CostEstimate(
            flops=number * 36 * count**3 * LANES, bytes_accessed=16 * number * count * rows * LANES, transcendentals=0
        ),
        compiler_params=pltpu.CompilerParams(vmem_limit_bytes=60 * 1024 * 1024),
    )(partner, orbitals, *start, *tables)


def make_tables(count):
    table = hartley_table(count)
    order = row_order(count)
    return (
        jnp.asarray(lane_table(count)),
        jnp.asarray(row_table(table[:, order])),
        jnp.asarray(row_table(table)),
        jnp.asarray(row_table(table[order, :])),
        screened_kernel(count),
    )


def piece_row(tile, rows):
    return tile % 3 * (rows // 3) + tile // 3


def pack_kernel(planes, rows, flat, packed):
    for tile in range(rows):
        row = piece_row(tile, rows)
        packed[0, pl.ds(row, planes, stride=rows), :] = flat[0, :, tile * LANES : (tile + 1) * LANES]


def pack(fields):
    number, planes, flat = fields.shape
    rows = flat // LANES
    packed = pl.pallas_call(
        functools.partial(pack_kernel, planes, rows),
        grid=(number,),
        in_specs=[pl.BlockSpec((1, planes, flat), lambda i: (i, 0, 0))],
        out_specs=pl.BlockSpec((1, planes * rows, LANES), lambda i: (i, 0, 0)),
        out_shape=jax.ShapeDtypeStruct((number, planes * rows, LANES), F32),
    )(fields)
    return packed.reshape(number, planes, rows, LANES)


def unpack_kernel(planes, rows, packed, extra, flat):
    more = jnp.where(pl.program_id(0) < PAIR, 1.0, 0.0)
    for tile in range(rows):
        place = pl.ds(piece_row(tile, rows), planes, stride=rows)
        value = packed[0, place, :] + more * extra[0, place, :]
        flat[0, :, tile * LANES : (tile + 1) * LANES] = -ALPHA * value


def unpack(fields, extra):
    number, planes, rows, _ = fields.shape
    block = (1, planes * rows, LANES)
    return pl.pallas_call(
        functools.partial(unpack_kernel, planes, rows),
        grid=(number,),
        in_specs=[
            pl.BlockSpec(block, lambda i: (i, 0, 0)),
            pl.BlockSpec(block, lambda i: (jnp.minimum(i, PAIR - 1), 0, 0)),
        ],
        out_specs=pl.BlockSpec((1, planes, rows * LANES), lambda i: (i, 0, 0)),
        out_shape=jax.ShapeDtypeStruct((number, planes, rows * LANES), F32),
    )(fields.reshape(number, planes * rows, LANES), extra.reshape(PAIR, planes * rows, LANES))


def swap(value, axis, flip):
    size = lax.axis_size(axis)
    return lax.ppermute(value, axis, [(i, i ^ flip) for i in range(size)])


def shift(value, step, low, high):
    return lax.ppermute(value, "z", [(z, z + step) for z in range(low, high + 1)])


def gather_line(slab):
    length = lax.axis_size("z")
    down, up = [slab], [slab]
    for step in range(1, length):
        down.append(shift(down[-1], 1, step - 1, length - 2))
        up.append(shift(up[-1], -1, 1, length - step))
    every = jnp.concatenate(down[:0:-1] + up, axis=0)
    size = slab.shape[0]
    start = (length - 1 - lax.axis_index("z")) * size
    return lax.dynamic_slice_in_dim(every, start, length * size, axis=0)


def scatter_line(field):
    length = lax.axis_size("z")
    size = field.shape[0] // length
    place = lax.axis_index("z")

    def block(offset):
        start = jnp.clip(place + offset, 0, length - 1) * size
        return lax.dynamic_slice_in_dim(field, start, size, axis=0)

    down = up = 0.0
    for step in range(length - 1, 0, -1):
        down = shift(block(step) + down, 1, 0, length - 1 - step)
        up = shift(block(-step) + up, -1, step, length - 1)
    return block(0) + down + up


def whole_orbitals(packed):
    n_local, planes, rows, _ = packed.shape
    zs, core = lax.axis_size("z"), lax.axis_index("core")
    mine = lax.all_to_all(packed, "z", split_axis=0, concat_axis=1, tiled=True)
    mine = mine.reshape(n_local // zs, zs, 1, planes, rows, LANES)
    other = swap(mine, "core", 1)
    whole = jnp.where(
        core == 0, jnp.concatenate([mine, other], axis=2), jnp.concatenate([other, mine], axis=2)
    )
    return whole.reshape(n_local // zs, zs * 2 * planes, rows, LANES)


def spread_sums(sums, planes):
    own, count, rows, _ = sums.shape
    zs, core = lax.axis_size("z"), lax.axis_index("core")
    sums = sums.reshape(own, zs, 2, planes, rows, LANES)
    keep = lax.dynamic_index_in_dim(sums, core, 2, keepdims=False)
    give = lax.dynamic_index_in_dim(sums, 1 - core, 2, keepdims=False)
    total = (keep + swap(give, "core", 1)).reshape(own, zs * planes, rows, LANES)
    return lax.all_to_all(total, "z", split_axis=1, concat_axis=0, tiled=True)


def local(orbitals):
    n_local, planes, flat = orbitals.shape
    zs, bands = lax.axis_size("z"), lax.axis_size("band")
    count = planes * zs * 2
    tables = make_tables(count)
    packed = pack(orbitals)
    tail = packed.shape[2:]
    slab = lax.all_to_all(packed[0:PAIR], "core", split_axis=0, concat_axis=1, tiled=True)[0]
    if bands == ROUNDS:
        own = gather_line(slab)
        side, far = swap(own, "band", 1), swap(own, "band", 2)
        cross = jnp.concatenate(
            [swap(side[: count // 2], "band", 2), swap(far[count // 2 :], "band", 1)], axis=0
        )
        partners = [own, side, far, cross]
    else:
        every = lax.all_gather(slab, ("band", "z"), axis=0, tiled=True)
        partners = list(every.reshape((bands, count) + tail)[:ROUNDS])
    whole = whole_orbitals(packed)
    sums = None
    terms = []
    for partner in partners:
        sums, term = pair_solve(partner[None], whole, sums, tables)
        terms.append(term[0])
    if bands == ROUNDS:
        owner = terms[0] + swap(terms[1], "band", 1) + swap(terms[2], "band", 2) + swap(terms[3], "band", 3)
        owner = scatter_line(owner)
    else:
        owner = jnp.concatenate(terms + [jnp.zeros_like(terms[0])] * (bands - ROUNDS), axis=0)
        owner = lax.psum_scatter(owner, ("band", "z"), scatter_dimension=0, tiled=True)
    owner = lax.all_to_all(owner[None], "core", split_axis=1, concat_axis=0, tiled=True)
    return unpack(spread_sums(sums, planes), owner)


def solution(mesh):
    bands, planes = mesh.devices.shape
    inner = Mesh(mesh.devices.reshape(bands, planes // 2, 2), ("band", "z", "core"))
    placed = P("band", ("z", "core"), None)
    return jax.shard_map(local, mesh=inner, in_specs=(placed,), out_specs=placed, check_vma=False)
```

time: 1370 us -> 830 us (0.61)
  Pallas kernels: 531 us -> 172 us
  waiting for transfers between devices: 620 us -> 486 us
  blocking collectives: 92 us -> 5.53 us
  starting transfers between devices: 4.99 us -> 64.5 us
  local copies, waits for them, and re-layouts: 82.4 us -> 63.5 us
    ppermute x0 -> x21, waiting for transfers between devices: none -> 486 us  [the longest x12 260 us: shift(): lax.ppermute(value, 'z', [(z, z + step) for z in range(low, high + 1)])]
    pallas_call x4 -> x6, Pallas kernels: 531 us -> 172 us  [the longest x4 158 us: pair_solve(): pl.pallas_call(functools.partial(pair_kernel, count, fresh), grid=(number...]
    unnamed x6 -> x0, waiting for transfers between devices: 317 us -> none
    all_gather x2 -> x0, waiting for transfers between devices: 154 us -> none  [the longest x1 154 us: local(): partners = lax.all_gather(mine, ('band', 'z'), axis=0, tiled=False)]
    all_to_all x1 -> x3, waiting for transfers between devices: 149 us -> 0.01 us  [the longest x1 0.01 us: local(): lax.all_to_all(owner[None], 'core', split_axis=1, concat_axis=0, tiled=True)]
    all_to_all x2 -> x0, blocking collectives: 85.6 us -> none  [the longest x1 80.9 us: local(): split = lax.all_to_all(packed, 'z', split_axis=0, concat_axis=1, tiled=True)]
    ppermute x0 -> x21, starting transfers between devices: none -> 44.2 us  [the longest x12 29.8 us: shift(): lax.ppermute(value, 'z', [(z, z + step) for z in range(low, high + 1)])]
    add x0 -> x6, other arithmetic: none -> 18.2 us  [the longest x1 5.71 us: local(): terms[0] + swap(terms[1], 'band', 1) + swap(terms[2], 'band', 2)]
  transfers between devices with their start and end apart: 5 -> 24, of which waited for: 4 -> 14; matrix products, arithmetic and copies ran while one was open for 5% -> 9% of each run, Pallas kernels for 0% -> 0%
where the time goes in v2:
time: 830 us; the launch traced here: 827 us
  waiting for transfers between devices  486 us (59%)
  Pallas kernels  172 us (21%)
  starting transfers between devices  64.5 us (8%)
  local copies, waits for them, and re-layouts  63.5 us (8%)
  other arithmetic  36.1 us (4%)
    ppermute x12, waiting for transfers between devices, shift(): lax.ppermute(value, 'z', [(z, z + step) for z in range(low, high + 1)])  260 us
    ppermute x9, waiting for transfers between devices, swap(): return lax.ppermute(value, axis, [(i, i ^ flip) for i in range(size)])  226 us
    pallas_call x4, Pallas kernels, pair_solve(): pl.pallas_call(functools.partial(pair_kernel, count, fresh), grid=(number...  158 us
    ppermute x12, starting transfers between devices, shift(): lax.ppermute(value, 'z', [(z, z + step) for z in range(low, high + 1)])  29.8 us
  transfers between devices with their start and end apart: 24, of which 14 were waited for; matrix products, arithmetic and copies ran while one was open for 9% of the time, Pallas kernels for 0%

profile of v2, /device:TPU:17, one launch (start us, length us, event | category | flops | bytes accessed | tf_op | source)
XLA Modules:
  0.0 827.4 jit_solution(15735707126907345947)
XLA Ops:
  0.0 6.2 copy.21.flat
  6.2 6.7 shard_map.55
  14.2 5.5 all_to_all.48
  19.7 3.2 collective-permute-start
  22.9 4.7 all-to-all-start.1
  27.6 2.2 collective-permute-start.3
  29.8 13.0 %collective-permute-done = f32[24,72,128]{2,1,0:T(8,128)} collective-permute-done((f32[24,72,128]{2,1,0:T(8,128)}, f32[24,72,128]{2,1,0:T(8,128)}, u32[]{:S(2)}, u32[]{:S(2)}) %collective-permute-start) | collective-permute-done | bytes 884768 | tf_op jit(solution)/shard_map/ppermute | solution.py:272
  42.8 3.2 collective-permute-start.1
  46.0 76.2 %collective-permute-done.3 = f32[24,72,128]{2,1,0:T(8,128)S(1)} collective-permute-done((f32[24,72,128]{2,1,0:T(8,128)}, f32[24,72,128]{2,1,0:T(8,128)S(1)}, u32[]{:S(2)}, u32[]{:S(2)}) %collective-permute-start.3) | collective-permute-done | bytes 884768 | tf_op jit(solution)/shard_map/ppermute | solution.py:272
  123.2 4.9 collective-permute-start.4
  128.1 9.6 %collective-permute-done.1 = f32[24,72,128]{2,1,0:T(8,128)} collective-permute-done((f32[24,72,128]{2,1,0:T(8,128)}, f32[24,72,128]{2,1,0:T(8,128)}, u32[]{:S(2)}, u32[]{:S(2)}) %collective-permute-start.1) | collective-permute-done | bytes 884768 | tf_op jit(solution)/shard_map/ppermute | solution.py:272
  137.6 2.2 collective-permute-start.2
  139.8 4.8 collective-permute-done.4
  144.7 1.6 collective-permute-start.5
  146.2 11.0 %collective-permute-done.2 = f32[24,72,128]{2,1,0:T(8,128)} collective-permute-done((f32[24,72,128]{2,1,0:T(8,128)}, f32[24,72,128]{2,1,0:T(8,128)}, u32[]{:S(2)}, u32[]{:S(2)}) %collective-permute-start.2) | collective-permute-done | bytes 884768 | tf_op jit(solution)/shard_map/ppermute | solution.py:272
  158.5 1.2 constant_dynamic-update-slice_fusion.5
  164.7 2.2 constant_dynamic-slice_fusion.2
  168.5 1.2 collective-permute-start.8
  169.7 2.1 collective-permute-start.10
  171.9 71.6 %collective-permute-done.6 = f32[96,72,128]{2,1,0:T(8,128)} collective-permute-done((f32[96,72,128]{2,1,0:T(8,128)}, f32[96,72,128]{2,1,0:T(8,128)}, u32[]{:S(2)}, u32[]{:S(2)}) %collective-permute-start.6) | collective-permute-done | bytes 3538976 | tf_op jit(solution)/shard_map/ppermute | solution.py:268
  243.4 2.9 slice.17
  246.3 1.2 collective-permute-start.7
  247.6 2.8 slice.18
  251.9 6.6 add.142
  258.5 7.2 add.143
  265.7 7.3 fusion.refs_4_.refs_5_
  273.1 4.0 fusion.7.partner
  277.0 7.0 collective-permute-done.7
  284.0 3.8 collective-permute-done.9
  287.7 4.0 maximum_bitcast_fusion.partner
  291.8 3.6 maximum_select_fusion
  295.4 3.4 copy.22
  298.8 38.7 %shard_map.56 = (f32[2,96,72,128]{3,2,1,0:T(8,128)}, f32[1,96,72,128]{3,2,1,0:T(8,128)}) custom-call(f32[1,96,72,128]{3,2,1,0:T(8,128)} %fusion.7.partner, f32[2,96,72,128]{3,2,1,0:T(8,128)} %bitcast.50, bf16[256,256]{1,0:T(8,128)(2,1)} %constant.74.clone.refs_0_.refs_1_, bf16[192,192]{1,0:T(8,128)(2,1)} %constant.75.clone.refs_1_.refs_2_, ...), custom_call_target="tpu_custom_call" | custom-call | flops 8153726976 | bytes 28311552 | tf_op jit(solution)/shard_map/pallas_call | solution.py:193
  337.5 39.6 %shard_map.57 = (f32[2,96,72,128]{3,2,1,0:T(8,128)}, f32[1,96,72,128]{3,2,1,0:T(8,128)}) custom-call(f32[1,96,72,128]{3,2,1,0:T(8,128)} %bitcast.11.partner, f32[2,96,72,128]{3,2,1,0:T(8,128)} %bitcast.51, f32[2,96,72,128]{3,2,1,0:T(8,128)} %get-tuple-element.13.refs_0_, ...), custom_call_target="tpu_custom_call", output_to_operand_aliasing={{0}: (2, {})} | custom-call | flops 8153726976 | bytes 28311552 | tf_op jit(solution)/shard_map/pallas_call | solution.py:193
  377.1 39.8 %shard_map.58 = (f32[2,96,72,128]{3,2,1,0:T(8,128)}, f32[1,96,72,128]{3,2,1,0:T(8,128)}) custom-call(f32[1,96,72,128]{3,2,1,0:T(8,128)} %bitcast.10.partner, f32[2,96,72,128]{3,2,1,0:T(8,128)} %bitcast.52, f32[2,96,72,128]{3,2,1,0:T(8,128)} %get-tuple-element.14.refs_0_, ...), custom_call_target="tpu_custom_call", output_to_operand_aliasing={{0}: (2, {})} | custom-call | flops 8153726976 | bytes 28311552 | tf_op jit(solution)/shard_map/pallas_call | solution.py:193
  417.0 39.6 %shard_map.59 = (f32[2,96,72,128]{3,2,1,0:T(8,128)}, f32[1,96,72,128]{3,2,1,0:T(8,128)}) custom-call(f32[1,96,72,128]{3,2,1,0:T(8,128)} %maximum_bitcast_fusion.partner, f32[2,96,72,128]{3,2,1,0:T(8,128)} %bitcast.53, f32[2,96,72,128]{3,2,1,0:T(8,128)} %get-tuple-element.15.refs_0_, ...), custom_call_target="tpu_custom_call", output_to_operand_aliasing={{0}: (2, {})} | custom-call | flops 8153726976 | bytes 28311552 | tf_op jit(solution)/shard_map/pallas_call | solution.py:193
  457.7 1.2 collective-permute-start.13
  459.2 4.1 dynamic-slice_bitcast_fusion
  463.3 4.8 collective-permute-start.11
  468.1 63.8 %collective-permute-done.14 = f32[96,72,128]{2,1,0:T(8,128)S(1)} collective-permute-done((f32[96,72,128]{2,1,0:T(8,128)}, f32[96,72,128]{2,1,0:T(8,128)S(1)}, u32[]{:S(2)}, u32[]{:S(2)}) %collective-permute-start.14) | collective-permute-done | bytes 3538976 | tf_op jit(solution)/shard_map/ppermute | solution.py:268
  531.9 80.2 %collective-permute-done.13 = f32[96,72,128]{2,1,0:T(8,128)} collective-permute-done((f32[96,72,128]{2,1,0:T(8,128)}, f32[96,72,128]{2,1,0:T(8,128)}, u32[]{:S(2)}, u32[]{:S(2)}) %collective-permute-start.13) | collective-permute-done | bytes 3538976 | tf_op jit(solution)/shard_map/ppermute | solution.py:268
  612.1 5.7 fusion.2
  618.8 1.6 collective-permute-start.15
  620.4 3.4 bitcast_add_fusion
  623.8 2.1 copy.25
  625.9 7.8 all-to-all-start.2
  633.7 2.2 dynamic-slice_add_fusion.2
  635.9 1.3 collective-permute-start.16
  637.2 92.0 %collective-permute-done.16 = f32[24,72,128]{2,1,0:T(8,128)} collective-permute-done((f32[24,72,128]{2,1,0:T(8,128)}, f32[24,72,128]{2,1,0:T(8,128)}, u32[]{:S(2)}, u32[]{:S(2)}) %collective-permute-start.16) | collective-permute-done | bytes 884768 | tf_op jit(solution)/shard_map/ppermute | solution.py:272
  729.2 2.5 dynamic-slice_add_fusion.3
  731.7 1.3 collective-permute-start.18
  733.0 20.5 %collective-permute-done.18 = f32[24,72,128]{2,1,0:T(8,128)} collective-permute-done((f32[24,72,128]{2,1,0:T(8,128)}, f32[24,72,128]{2,1,0:T(8,128)}, u32[]{:S(2)}, u32[]{:S(2)}) %collective-permute-start.18) | collective-permute-done | bytes 884768 | tf_op jit(solution)/shard_map/ppermute | solution.py:272
  753.5 2.2 dynamic-slice_add_fusion
  755.7 1.9 collective-permute-start.19
  757.6 4.3 collective-permute-start.17
  761.9 14.7 %collective-permute-done.19 = f32[24,72,128]{2,1,0:T(8,128)} collective-permute-done((f32[24,72,128]{2,1,0:T(8,128)}, f32[24,72,128]{2,1,0:T(8,128)}, u32[]{:S(2)}, u32[]{:S(2)}) %collective-permute-start.19) | collective-permute-done | bytes 884768 | tf_op jit(solution)/shard_map/ppermute | solution.py:272
  776.6 2.2 dynamic-slice_add_fusion.1
  778.8 2.2 collective-permute-start.20
  781.0 17.8 %collective-permute-done.20 = f32[24,72,128]{2,1,0:T(8,128)} collective-permute-done((f32[24,72,128]{2,1,0:T(8,128)}, f32[24,72,128]{2,1,0:T(8,128)}, u32[]{:S(2)}, u32[]{:S(2)}) %collective-permute-start.20) | collective-permute-done | bytes 884768 | tf_op jit(solution)/shard_map/ppermute | solution.py:272
  798.8 2.5 add_bitcast_fusion
  801.2 7.8 all-to-all-start.3
  809.1 4.1 copy.27
  814.1 7.1 shard_map.60
  821.2 6.2 copy.29
  (37 shorter events, 14.9 us)
Async XLA Ops:
  19.7 23.1 %collective-permute-start = (f32[24,72,128]{2,1,0:T(8,128)}, f32[24,72,128]{2,1,0:T(8,128)}, u32[]{:S(2)}, u32[]{:S(2)}) collective-permute-start(f32[24,72,128]{2,1,0:T(8,128)} %bitcast.1), channel_id=1, source_target_pairs={{0,2},{2,4},{4,6},{1,3},{3,5},{5,7},{8,10},{10,12},{12,14},{9,11},... | collective-permute-start | bytes 2654216 | tf_op jit(solution)/shard_map/ppermute | solution.py:272
  22.9 146.8 %all-to-all-start.1 = ((f32[8,12,72,128]{3,2,1,0:T(8,128)}), f32[8,12,72,128]{3,2,1,0:T(8,128)S(1)}, u32[]{:S(2)}, u32[]{:S(2)}) async-start(f32[8,12,72,128]{3,2,1,0:T(8,128)} %bitcast.45), calls=%async_computation.1 | async-start | bytes 7077888 | tf_op jit(solution)/shard_map/all_to_all | solution.py:306
  27.6 94.6 %collective-permute-start.3 = (f32[24,72,128]{2,1,0:T(8,128)}, f32[24,72,128]{2,1,0:T(8,128)S(1)}, u32[]{:S(2)}, u32[]{:S(2)}) collective-permute-start(f32[24,72,128]{2,1,0:T(8,128)} %bitcast.1), channel_id=1, source_target_pairs={{2,0},{4,2},{6,4},{3,1},{5,3},{7,5},{10,8},{12,10},{14,12},{11,9},... | collective-permute-start | bytes 2654216 | tf_op jit(solution)/shard_map/ppermute | solution.py:272
  42.8 94.8 %collective-permute-start.1 = (f32[24,72,128]{2,1,0:T(8,128)}, f32[24,72,128]{2,1,0:T(8,128)}, u32[]{:S(2)}, u32[]{:S(2)}) collective-permute-start(f32[24,72,128]{2,1,0:T(8,128)} %collective-permute-done), channel_id=1, source_target_pairs={{2,4},{4,6},{3,5},{5,7},{10,12},{12,14},{11,13},{13,15},{18,20},{2... | collective-permute-start | bytes 2654216 | tf_op jit(solution)/shard_map/ppermute | solution.py:272
  122.2 0.9 copy-start.3
  123.2 21.5 %collective-permute-start.4 = (f32[24,72,128]{2,1,0:T(8,128)S(1)}, f32[24,72,128]{2,1,0:T(8,128)}, u32[]{:S(2)}, u32[]{:S(2)}) collective-permute-start(f32[24,72,128]{2,1,0:T(8,128)S(1)} %collective-permute-done.3), channel_id=1, source_target_pairs={{2,0},{4,2},{3,1},{5,3},{10,8},{12,10},{11,9},{13,11},{18,16},{20,... | collective-permute-start | bytes 2654216 | tf_op jit(solution)/shard_map/ppermute | solution.py:272
  137.6 19.6 %collective-permute-start.2 = (f32[24,72,128]{2,1,0:T(8,128)}, f32[24,72,128]{2,1,0:T(8,128)}, u32[]{:S(2)}, u32[]{:S(2)}) collective-permute-start(f32[24,72,128]{2,1,0:T(8,128)} %collective-permute-done.1), channel_id=1, source_target_pairs={{4,6},{5,7},{12,14},{13,15},{20,22},{21,23},{28,30},{29,31}} | collective-permute-start | bytes 2654216 | tf_op jit(solution)/shard_map/ppermute | solution.py:272
  144.7 18.8 %collective-permute-start.5 = (f32[24,72,128]{2,1,0:T(8,128)}, f32[24,72,128]{2,1,0:T(8,128)}, u32[]{:S(2)}, u32[]{:S(2)}) collective-permute-start(f32[24,72,128]{2,1,0:T(8,128)} %collective-permute-done.4), channel_id=1, source_target_pairs={{2,0},{3,1},{10,8},{11,9},{18,16},{19,17},{26,24},{27,25}} | collective-permute-start | bytes 2654216 | tf_op jit(solution)/shard_map/ppermute | solution.py:272
  146.2 15.9 %copy-start.4 = (f32[24,72,128]{2,1,0:T(8,128)S(1)}, f32[24,72,128]{2,1,0:T(8,128)}, u32[]{:S(2)}) copy-start(f32[24,72,128]{2,1,0:T(8,128)} %copy-done.3) | copy-start | bytes 2654212
  164.7 3.8 copy-start
  166.9 76.5 %collective-permute-start.6 = (f32[96,72,128]{2,1,0:T(8,128)}, f32[96,72,128]{2,1,0:T(8,128)}, u32[]{:S(2)}, u32[]{:S(2)}) collective-permute-start(f32[96,72,128]{2,1,0:T(8,128)} %constant_dynamic-slice_fusion.2), channel_id=1, source_target_pairs={{0,8},{8,0},{16,24},{24,16},{1,9},{9,1},{17,25},{25,17},{2,10},{10... | collective-permute-start | bytes 10616840 | tf_op jit(solution)/shard_map/ppermute | solution.py:268
  168.5 79.1 %collective-permute-start.8 = (f32[96,72,128]{2,1,0:T(8,128)}, f32[96,72,128]{2,1,0:T(8,128)}, u32[]{:S(2)}, u32[]{:S(2)}) collective-permute-start(f32[96,72,128]{2,1,0:T(8,128)} %constant_dynamic-slice_fusion.2), channel_id=1, source_target_pairs={{0,16},{8,24},{16,0},{24,8},{1,17},{9,25},{17,1},{25,9},{2,18},{10... | collective-permute-start | bytes 10616840 | tf_op jit(solution)/shard_map/ppermute | solution.py:268
  169.7 122.0 %collective-permute-start.10 = (f32[2,4,1,12,72,128]{5,4,3,0,1,2:T(8,128)S(1)}, f32[2,4,1,12,72,128]{5,4,3,0,1,2:T(8,128)}, u32[]{:S(2)}, u32[]{:S(2)}) collective-permute-start(f32[2,4,1,12,72,128]{5,4,3,0,1,2:T(8,128)S(1)} %bitcast.46), channel_id=1, source_target_pairs={{0,1},{1,0},{2,3},{3,2},{4,5},{5,4},{6,7},{7,6},{8,9},{9,8},{10,11... | collective-permute-start | bytes 10616840 | tf_op jit(solution)/shard_map/ppermute | solution.py:268
  246.3 37.7 %collective-permute-start.7 = (f32[48,72,128]{2,1,0:T(8,128)}, f32[48,72,128]{2,1,0:T(8,128)}, u32[]{:S(2)}, u32[]{:S(2)}) collective-permute-start(f32[48,72,128]{2,1,0:T(8,128)} %slice.17), channel_id=1, source_target_pairs={{0,16},{8,24},{16,0},{24,8},{1,17},{9,25},{17,1},{25,9},{2,18},{10... | collective-permute-start | bytes 5308424 | tf_op jit(solution)/shard_map/ppermute | solution.py:268
  250.4 37.4 %collective-permute-start.9 = (f32[48,72,128]{2,1,0:T(8,128)}, f32[48,72,128]{2,1,0:T(8,128)}, u32[]{:S(2)}, u32[]{:S(2)}) collective-permute-start(f32[48,72,128]{2,1,0:T(8,128)} %slice.18), channel_id=1, source_target_pairs={{0,8},{8,0},{16,24},{24,16},{1,9},{9,1},{17,25},{25,17},{2,10},{10... | collective-permute-start | bytes 5308424 | tf_op jit(solution)/shard_map/ppermute | solution.py:268
  456.6 75.3 %collective-permute-start.14 = (f32[96,72,128]{2,1,0:T(8,128)}, f32[96,72,128]{2,1,0:T(8,128)S(1)}, u32[]{:S(2)}, u32[]{:S(2)}) collective-permute-start(f32[96,72,128]{2,1,0:T(8,128)} %bitcast.60), channel_id=1, source_target_pairs={{0,24},{8,16},{16,8},{24,0},{1,25},{9,17},{17,9},{25,1},{2,26},{10... | collective-permute-start | bytes 10616840 | tf_op jit(solution)/shard_map/ppermute | solution.py:268
  457.7 154.3 %collective-permute-start.13 = (f32[96,72,128]{2,1,0:T(8,128)}, f32[96,72,128]{2,1,0:T(8,128)}, u32[]{:S(2)}, u32[]{:S(2)}) collective-permute-start(f32[96,72,128]{2,1,0:T(8,128)} %bitcast.59), channel_id=1, source_target_pairs={{0,16},{8,24},{16,0},{24,8},{1,17},{9,25},{17,1},{25,9},{2,18},{10... | collective-permute-start | bytes 10616840 | tf_op jit(solution)/shard_map/ppermute | solution.py:268
  459.0 153.1 %collective-permute-start.12 = (f32[96,72,128]{2,1,0:T(8,128)}, f32[96,72,128]{2,1,0:T(8,128)}, u32[]{:S(2)}, u32[]{:S(2)}) collective-permute-start(f32[96,72,128]{2,1,0:T(8,128)} %bitcast.58), channel_id=1, source_target_pairs={{0,8},{8,0},{16,24},{24,16},{1,9},{9,1},{17,25},{25,17},{2,10},{10... | collective-permute-start | bytes 10616840 | tf_op jit(solution)/shard_map/ppermute | solution.py:268
  463.3 157.1 %collective-permute-start.11 = (f32[2,4,12,72,128]{4,3,2,1,0:T(8,128)}, f32[2,4,12,72,128]{4,3,2,1,0:T(8,128)}, u32[]{:S(2)}, u32[]{:S(2)}) collective-permute-start(f32[2,4,12,72,128]{4,3,2,1,0:T(8,128)} %dynamic-slice_bitcast_fusion), channel_id=1, source_target_pairs={{0,1},{1,0},{2,3},{3,2},{4,5},{5,4},{6,7},{7,6},{8,9},{9,8},{10,11... | collective-permute-start | bytes 10616840 | tf_op jit(solution)/shard_map/ppermute | solution.py:268
  531.9 80.2 %copy-start.2 = (f32[96,72,128]{2,1,0:T(8,128)}, f32[96,72,128]{2,1,0:T(8,128)S(1)}, u32[]{:S(2)}) copy-start(f32[96,72,128]{2,1,0:T(8,128)S(1)} %collective-permute-done.14) | copy-start | bytes 10616836
  618.8 14.9 %collective-permute-start.15 = (f32[24,72,128]{2,1,0:T(8,128)}, f32[24,72,128]{2,1,0:T(8,128)}, u32[]{:S(2)}, u32[]{:S(2)}) collective-permute-start(f32[24,72,128]{2,1,0:T(8,128)} %constant_dynamic-slice_fusion.1), channel_id=1, source_target_pairs={{0,2},{1,3},{8,10},{9,11},{16,18},{17,19},{24,26},{25,27}} | collective-permute-start | bytes 2654216 | tf_op jit(solution)/shard_map/ppermute | solution.py:272
  625.9 175.4 %all-to-all-start.2 = ((f32[2,48,72,128]{3,2,0,1:T(8,128)}), f32[2,48,72,128]{3,2,0,1:T(8,128)}, u32[]{:S(2)}, u32[]{:S(2)}) async-start(f32[2,48,72,128]{3,2,0,1:T(8,128)} %copy.25), calls=%async_computation.2 | async-start | bytes 7077888 | tf_op jit(solution)/shard_map/all_to_all | solution.py:322
  635.9 93.3 %collective-permute-start.16 = (f32[24,72,128]{2,1,0:T(8,128)}, f32[24,72,128]{2,1,0:T(8,128)}, u32[]{:S(2)}, u32[]{:S(2)}) collective-permute-start(f32[24,72,128]{2,1,0:T(8,128)} %dynamic-slice_add_fusion.2), channel_id=1, source_target_pairs={{0,2},{2,4},{1,3},{3,5},{8,10},{10,12},{9,11},{11,13},{16,18},{18,... | collective-permute-start | bytes 2654216 | tf_op jit(solution)/shard_map/ppermute | solution.py:272
  731.7 21.8 %collective-permute-start.18 = (f32[24,72,128]{2,1,0:T(8,128)}, f32[24,72,128]{2,1,0:T(8,128)}, u32[]{:S(2)}, u32[]{:S(2)}) collective-permute-start(f32[24,72,128]{2,1,0:T(8,128)} %get-tuple-element.22), channel_id=1, source_target_pairs={{6,4},{7,5},{14,12},{15,13},{22,20},{23,21},{30,28},{31,29}} | collective-permute-start | bytes 2654216 | tf_op jit(solution)/shard_map/ppermute | solution.py:272
  755.7 20.9 %collective-permute-start.19 = (f32[24,72,128]{2,1,0:T(8,128)}, f32[24,72,128]{2,1,0:T(8,128)}, u32[]{:S(2)}, u32[]{:S(2)}) collective-permute-start(f32[24,72,128]{2,1,0:T(8,128)} %dynamic-slice_add_fusion), channel_id=1, source_target_pairs={{4,2},{6,4},{5,3},{7,5},{12,10},{14,12},{13,11},{15,13},{20,18},{2... | collective-permute-start | bytes 2654216 | tf_op jit(solution)/shard_map/ppermute | solution.py:272
  757.6 23.4 %collective-permute-start.17 = (f32[24,72,128]{2,1,0:T(8,128)}, f32[24,72,128]{2,1,0:T(8,128)}, u32[]{:S(2)}, u32[]{:S(2)}) collective-permute-start(f32[24,72,128]{2,1,0:T(8,128)} %get-tuple-element.21), channel_id=1, source_target_pairs={{0,2},{2,4},{4,6},{1,3},{3,5},{5,7},{8,10},{10,12},{12,14},{9,11},... | collective-permute-start | bytes 2654216 | tf_op jit(solution)/shard_map/ppermute | solution.py:272
  778.8 20.0 %collective-permute-start.20 = (f32[24,72,128]{2,1,0:T(8,128)}, f32[24,72,128]{2,1,0:T(8,128)}, u32[]{:S(2)}, u32[]{:S(2)}) collective-permute-start(f32[24,72,128]{2,1,0:T(8,128)} %dynamic-slice_add_fusion.1), channel_id=1, source_target_pairs={{2,0},{4,2},{6,4},{3,1},{5,3},{7,5},{10,8},{12,10},{14,12},{11,9},... | collective-permute-start | bytes 2654216 | tf_op jit(solution)/shard_map/ppermute | solution.py:272
  801.2 11.9 %all-to-all-start.3 = ((f32[1,24,72,128]{3,2,0,1:T(8,128)}), f32[1,24,72,128]{3,2,0,1:T(8,128)S(1)}, u32[]{:S(2)}, u32[]{:S(2)}) async-start(f32[1,24,72,128]{3,2,0,1:T(8,128)} %add_bitcast_fusion), calls=%async_computation.3 | async-start | bytes 1769472 | tf_op jit(solution)/shard_map/all_to_all | solution.py:355
  813.2 0.9 copy-start.1

commit v3 on v1

v3 whole, which is shorter than its diff:
```python
import functools
import math

import jax
import jax.numpy as jnp
import numpy as np
from jax import lax
from jax.experimental import pallas as pl
from jax.experimental.pallas import tpu as pltpu
from jax.sharding import Mesh, PartitionSpec as P

PAIR = 2
ROUNDS = 4
OMEGA = 0.106
CELL = 41.05
ALPHA = 0.25
LANES = 128
F32 = jnp.float32
BF16 = jnp.bfloat16
MIDDLE = 12
PIECES = 5
COST_BYTES = 1 << 20


def hartley_table(count):
    index = np.arange(count)
    angle = (index[:, None] * index[None, :] % count).astype(np.float64) * (2.0 * math.pi / count)
    return (np.cos(angle) + np.sin(angle)).astype(np.float32)


def halves(value):
    high = value.astype(BF16)
    return high, (value - high.astype(F32)).astype(BF16)


def np_halves(value):
    high = value.astype(BF16)
    return high, (value - high.astype(np.float32)).astype(BF16)


def row_order(count):
    return np.arange(count).reshape(count // 4, 4).T.reshape(-1)


def lane_table(count):
    table = np.zeros((LANES, LANES), np.float32)
    table[:count, :count] = hartley_table(count)
    high, low = np_halves(table)
    top = np.concatenate([high, low], axis=1)
    return np.concatenate([top, np.concatenate([high, np.zeros_like(low)], axis=1)], axis=0)


def row_table(table):
    high, low = np_halves(table)
    top = np.concatenate([high, high], axis=1)
    return np.concatenate([top, np.concatenate([low, np.zeros_like(low)], axis=1)], axis=0)


def screened_kernel(count):
    shape = (count // 2, count, 2 * LANES)

    def squared(axis, place):
        index = place(lax.broadcasted_iota(jnp.int32, shape, axis))
        freq = jnp.where(index <= count // 2, index, index - count).astype(F32)
        return freq * freq

    second = 2 * lax.broadcasted_iota(jnp.int32, shape, 0)
    second = second + (lax.broadcasted_iota(jnp.int32, shape, 2) >= LANES).astype(jnp.int32)
    scale = (2.0 * math.pi / CELL) ** 2
    g_two = scale * (squared(0, lambda i: second) + squared(1, lambda i: i) + squared(2, lambda i: i % LANES))
    positive = g_two > 0
    safe = jnp.where(positive, g_two, 1.0)
    value = 4.0 * math.pi / safe * -jnp.expm1(-safe / (4.0 * OMEGA * OMEGA))
    value = jnp.where(positive, value, math.pi / (OMEGA * OMEGA))
    return value / float(count**3)


def to_rows(parts):
    first, second, third = parts
    lane = lax.broadcasted_iota(jnp.int32, first.shape, 1)
    row1 = jnp.where(lane < 32, pltpu.roll(first, 32, 1), pltpu.roll(second, 32, 1))
    row2 = jnp.where(lane < 64, pltpu.roll(second, 64, 1), pltpu.roll(third, 64, 1))
    row3 = pltpu.roll(third, 96, 1)
    return jnp.concatenate([first, row1, row2, row3], axis=0)


def from_rows(plane):
    step = plane.shape[0] // 4
    row0, row1, row2, row3 = (plane[k * step : (k + 1) * step] for k in range(4))
    lane = lax.broadcasted_iota(jnp.int32, row0.shape, 1)
    first = jnp.where(lane < 96, row0, pltpu.roll(row1, 96, 1))
    second = jnp.where(lane < 64, pltpu.roll(row1, 96, 1), pltpu.roll(row2, 64, 1))
    third = jnp.where(lane < 32, pltpu.roll(row2, 64, 1), pltpu.roll(row3, 32, 1))
    return first, second, third


def dot(a, b):
    return jnp.dot(a, b, preferred_element_type=F32)


def along_lanes(value, table):
    out = dot(jnp.concatenate(halves(value), axis=1), table)
    return out[:, :LANES] + out[:, LANES:]


def along_rows(table, value):
    out = dot(table, jnp.concatenate(halves(value), axis=0))
    half = out.shape[0] // 2
    return out[:half] + out[half:]


def pair_kernel(count, sizes, layout, *refs):
    split_in, sums_in, sums_split, terms_in, split_out = layout
    zs, planes = sizes
    slab = 2 * planes
    third = count // 4
    refs = list(refs)
    place = refs.pop(0)
    partner_hbm = [refs.pop(0) for _ in range(PIECES if split_in else 1)]
    mine_hbm, other_hbm = refs.pop(0), refs.pop(0)
    sums_hbm = refs.pop(0) if sums_in else None
    terms_hbm = refs.pop(0) if terms_in else None
    tables_hbm, coulomb_hbm = refs.pop(0), refs.pop(0)
    sums_out = [refs.pop(0) for _ in range(2 if sums_split else 1)]
    terms_out = [refs.pop(0) for _ in range(PIECES if split_out else 1)]
    partner, orbital, sums, terms, field, tables, coulomb, sem, sem_c = refs
    lanes = tables.at[: 2 * LANES]
    rows_in, rows_mid, rows_out = (
        tables.at[pl.ds(2 * LANES + 2 * count * k, 2 * count), : 2 * count] for k in range(3)
    )
    z, core = place[0], place[1]

    def part(ref, index, size=slab):
        return ref.at[pl.ds(pl.multiple_of(index * size, size), size)]

    def pieces(refs_):
        spots = [(z, None), (z - 1, z >= 1), (z + 1, z < zs - 1), (z ^ 2, None), (3 - z, (z == 0) | (z == 3))]
        return [(ref, spot, there) for ref, (spot, there) in zip(refs_, spots)]

    def start(source, target, semaphore, there=None):
        def go():
            pltpu.make_async_copy(source, target, semaphore).start()

        if there is None:
            go()
        else:
            pl.when(there)(go)

    def wait(like_source, like_target, semaphore):
        pltpu.make_async_copy(like_source, like_target, semaphore).wait()

    start(tables_hbm, tables, sem_c.at[1])
    if split_in:
        for ref, spot, there in pieces(partner_hbm):
            start(ref, part(partner, spot), sem.at[0, spot], there)
    else:
        for s in range(zs):
            start(part(partner_hbm[0], s), part(partner, s), sem.at[0, s])
    for s in range(zs):
        start(mine_hbm.at[s], part(orbital, 2 * s + core, planes), sem.at[1, s])
        start(other_hbm.at[s], part(orbital, 2 * s + 1 - core, planes), sem.at[2, s])
    start(coulomb_hbm, coulomb, sem_c.at[0])
    for s in range(zs):
        if sums_in:
            start(part(sums_hbm, s), part(sums, s), sem.at[3, s])
        if terms_in:
            start(part(terms_hbm, s), part(terms, s), sem.at[4, s])

    def density(x):
        parts = []
        for r in range(3):
            rows = pl.ds(r * third, third)
            parts.append(orbital[x, rows, :] * partner[x, rows, :])
        return to_rows(parts)

    group = planes

    def forward(step, carry):
        wait(part(partner, step), part(partner, step), sem.at[0, step])
        wait(part(orbital, 2 * step, planes), part(orbital, 2 * step, planes), sem.at[1, step])
        wait(part(orbital, 2 * step, planes), part(orbital, 2 * step, planes), sem.at[2, step])
        base = 2 * group * step
        pairs = [jnp.concatenate([density(base + 2 * g), density(base + 2 * g + 1)], axis=0) for g in range(group)]
        pairs = [along_lanes(both, lanes[...]) for both in pairs]
        pairs = [jnp.concatenate([both[:count], both[count:]], axis=1) for both in pairs]
        pairs = [along_rows(rows_in[...], both) for both in pairs]
        begin = pl.multiple_of(base * count, 2 * count)
        for g, both in enumerate(pairs):
            field[pl.ds(begin + 2 * g * count, count), :] = both[:, :LANES]
            field[pl.ds(begin + (2 * g + 1) * count, count), :] = both[:, LANES:]
        return carry

    wait(tables_hbm, tables, sem_c.at[1])
    lax.fori_loop(0, zs, forward, 0)
    wait(coulomb_hbm, coulomb, sem_c.at[0])

    def middle(step, carry):
        base = 2 * MIDDLE * step
        pairs = [
            jnp.concatenate(
                [field[pl.ds(base + 2 * g + k, count, stride=count), :] for k in range(2)], axis=1
            )
            for g in range(MIDDLE)
        ]
        pairs = [along_rows(rows_mid[...], both) for both in pairs]
        pairs = [both * coulomb[MIDDLE * step + g] for g, both in enumerate(pairs)]
        pairs = [along_rows(rows_mid[...], both) for both in pairs]
        for g, both in enumerate(pairs):
            for k in range(2):
                field[pl.ds(base + 2 * g + k, count, stride=count), :] = both[:, k * LANES : (k + 1) * LANES]
        return carry

    lax.fori_loop(0, count // 2 // MIDDLE, middle, 0)

    def backward(step, carry):
        if sums_in:
            wait(part(sums_hbm, step), part(sums, step), sem.at[3, step])
        if terms_in:
            wait(part(terms_hbm, step), part(terms, step), sem.at[4, step])
        base = 2 * group * step
        begin = pl.multiple_of(base * count, 2 * count)
        pairs = [
            jnp.concatenate([field[pl.ds(begin + (2 * g + k) * count, count), :] for k in range(2)], axis=1)
            for g in range(group)
        ]
        pairs = [along_rows(rows_out[...], both) for both in pairs]
        pairs = [jnp.concatenate([both[:, :LANES], both[:, LANES:]], axis=0) for both in pairs]
        pairs = [along_lanes(both, lanes[...]) for both in pairs]
        for g, both in enumerate(pairs):
            for k in range(2):
                x = base + 2 * g + k
                for r, value in enumerate(from_rows(both[k * count : (k + 1) * count])):
                    rows = pl.ds(r * third, third)
                    near = partner[x, rows, :] * value
                    sums[x, rows, :] = sums[x, rows, :] + near if sums_in else near
                    far = orbital[x, rows, :] * value
                    terms[x, rows, :] = terms[x, rows, :] + far if terms_in else far
        if sums_split:
            start(part(sums, 2 * step + core, planes), sums_out[0].at[step], sem.at[5, step])
            start(part(sums, 2 * step + 1 - core, planes), sums_out[1].at[step], sem.at[6, step])
        else:
            start(part(sums, step), part(sums_out[0], step), sem.at[5, step])
        if split_out:
            for ref, spot, there in pieces(terms_out):
                start(part(terms, step), ref, sem.at[7, step], (spot == step) if there is None else (spot == step) & there)
        else:
            start(part(terms, step), part(terms_out[0], step), sem.at[7, step])
        return carry

    lax.fori_loop(0, zs, backward, 0)
    for s in range(zs):
        if sums_split:
            for k in range(2):
                wait(part(sums, s, planes), sums_out[k].at[s], sem.at[5 + k, s])
        else:
            wait(part(sums, s), part(sums_out[0], s), sem.at[5, s])
        target = terms_out[0] if split_out else part(terms_out[0], s)
        wait(part(terms, s), target, sem.at[7, s])


def pair_solve(place, partner, mine, other, sums, terms, tables, last_partner, last_orbital):
    zs, planes, rows, _ = mine.shape
    count = zs * 2 * planes
    split_in = len(partner) > 1
    layout = (split_in, sums is not None, last_partner, terms is not None, last_orbital and split_in)
    field = jax.ShapeDtypeStruct((count, rows, LANES), F32)
    kinds = [jax.ShapeDtypeStruct(mine.shape, F32)] * 2 if last_partner else [field]
    pieces = [jax.ShapeDtypeStruct(p.shape, F32) for p in partner] if layout[4] else [field]
    more = [a for a in (sums, terms) if a is not None]
    anywhere = pl.BlockSpec(memory_space=pltpu.HBM)
    block = (count, rows, LANES)
    out = pl.pallas_call(
        functools.partial(pair_kernel, count, (zs, planes), layout),
        in_specs=[pl.BlockSpec(memory_space=pltpu.SMEM)]
        + [anywhere] * (len(partner) + 4 + len(more)),
        out_specs=[anywhere] * (len(kinds) + len(pieces)),
        out_shape=kinds + pieces,
        scratch_shapes=[pltpu.VMEM(block, F32)] * 4
        + [
            pltpu.VMEM((count * count, LANES), F32),
            pltpu.VMEM(tables[0].shape, BF16),
            pltpu.VMEM(tables[1].shape, F32),
            pltpu.SemaphoreType.DMA((8, zs)),
            pltpu.SemaphoreType.DMA((2,)),
        ],
        cost_estimate=pl.CostEstimate(
            flops=12 * count**4, bytes_accessed=COST_BYTES, transcendentals=0
        ),
        compiler_params=pltpu.CompilerParams(vmem_limit_bytes=48 * 1024 * 1024),
    )(place, *partner, mine, other, *more, *tables)
    sums = out[:2] if last_partner else out[0]
    terms = out[len(kinds) :] if layout[4] else out[-1]
    return sums, terms


def make_tables(count):
    table = hartley_table(count)
    order = row_order(count)
    rows = [row_table(t) for t in (table[:, order], table, table[order, :])]
    rows = [np.pad(t, ((0, 0), (0, 2 * LANES - t.shape[1]))) for t in rows]
    return jnp.asarray(np.concatenate([lane_table(count)] + rows, axis=0)), screened_kernel(count)


def piece_row(tile, rows):
    return tile % 3 * (rows // 3) + tile // 3


def pack_kernel(sets, planes, rows, flat, *packed):
    size = flat.shape[1] // sets
    plane = pl.program_id(0)
    for tile in range(rows):
        row = plane * rows + piece_row(tile, rows)
        for k in range(sets):
            value = flat[0, k * size : (k + 1) * size, tile * LANES : (tile + 1) * LANES]
            packed[k][pl.ds(row, size, stride=planes * rows), :] = value


def pack(fields, sets):
    planes, number, flat = fields.shape
    rows, size = flat // LANES, number // sets
    out = (size * planes * rows, LANES)
    packed = pl.pallas_call(
        functools.partial(pack_kernel, sets, planes, rows),
        grid=(planes,),
        in_specs=[pl.BlockSpec((1, number, flat), lambda i: (i, 0, 0))],
        out_specs=[pl.BlockSpec(out, lambda i: (0, 0))] * sets,
        out_shape=[jax.ShapeDtypeStruct(out, F32)] * sets,
        compiler_params=pltpu.CompilerParams(vmem_limit_bytes=32 * 1024 * 1024),
    )(fields)
    return [p.reshape(size, planes, rows, LANES) for p in packed]


def unpack_kernel(sets, planes, rows, *refs):
    packed, extra, flat = refs[:sets], refs[sets], refs[-1]
    size = flat.shape[1] // sets
    plane = pl.program_id(0)
    for tile in range(rows):
        row = plane * rows + piece_row(tile, rows)
        more = extra[pl.ds(row, PAIR, stride=planes * rows), :]
        for k in range(sets):
            value = packed[k][pl.ds(row, size, stride=planes * rows), :]
            if k == 0:
                value = jnp.concatenate([value[:PAIR] + more, value[PAIR:]], axis=0)
            flat[0, k * size : (k + 1) * size, tile * LANES : (tile + 1) * LANES] = -ALPHA * value


def unpack(fields, extra):
    sets = len(fields)
    size, planes, rows, _ = fields[0].shape
    whole = lambda n: pl.BlockSpec((n * planes * rows, LANES), lambda i: (0, 0), pipeline_mode=pl.Buffered(1))
    return pl.pallas_call(
        functools.partial(unpack_kernel, sets, planes, rows),
        grid=(planes,),
        in_specs=[whole(size)] * sets + [whole(PAIR)],
        out_specs=pl.BlockSpec((1, sets * size, rows * LANES), lambda i: (i, 0, 0)),
        out_shape=jax.ShapeDtypeStruct((planes, sets * size, rows * LANES), F32),
        compiler_params=pltpu.CompilerParams(vmem_limit_bytes=32 * 1024 * 1024),
    )(*(f.reshape(size * planes * rows, LANES) for f in fields), extra.reshape(PAIR * planes * rows, LANES))


def swap(value, axis, flip):
    size = lax.axis_size(axis)
    return lax.ppermute(value, axis, [(i, i ^ flip) for i in range(size)])


def across(value, flip, chips):
    zs = lax.axis_size("z")
    pairs = [(b * zs + z, (b ^ flip) * zs + z) for b in range(lax.axis_size("band")) for z in chips]
    return lax.ppermute(value, ("band", "z"), pairs)


def along(value, pairs):
    return lax.ppermute(value, "z", pairs)


RIGHT = [(0, 1), (1, 2), (2, 3)]
LEFT = [(1, 0), (2, 1), (3, 2)]
THERE = ((0, 1, 2, 3), (1, 2, 3), (0, 1, 2), (0, 1, 2, 3), (0, 3))
EVEN = (True, False, False, True, False)


def gather_line(slab):
    before, after = along(slab, RIGHT), along(slab, LEFT)
    two = along(before, RIGHT[1:]) + along(after, LEFT[:2])
    three = along(two, [(2, 3), (1, 0)])
    return [slab, before, after, two, three]


def scatter_line(terms):
    slab, before, after, two, three = terms
    two = two + along(three, [(0, 1), (3, 2)])
    after = after + along(two, RIGHT[:2])
    before = before + along(two, LEFT[1:])
    return slab + along(after, RIGHT) + along(before, LEFT)


def spread(own):
    side, far, cross = [], [], []

    def send(out, piece, flip, chips, earlier):
        if len(earlier) > 1:
            piece, earlier[-2] = lax.optimization_barrier((piece, earlier[-2]))
        out.append(across(piece, flip, chips))

    for piece, chips in zip(own, THERE):
        send(side, piece, 1, chips, side)
        send(far, piece, 2, chips, far)
    cross = [
        across(s, 2, chips) if even else across(f, 1, chips) for s, f, chips, even in zip(side, far, THERE, EVEN)
    ]
    return [own, side, far, cross]


def collect(own, side, far, cross):
    out = [None] * PIECES
    for k in (4, 3, 2, 1, 0):
        handed = across(cross[k], 2 if EVEN[k] else 1, THERE[k])
        s, f = (side[k] + handed, far[k]) if EVEN[k] else (side[k], far[k] + handed)
        out[k] = own[k] + across(s, 1, THERE[k]) + across(f, 2, THERE[k])
    return out


def local(orbitals):
    n_local, planes, flat = orbitals.shape
    zs, bands, core = lax.axis_size("z"), lax.axis_size("band"), lax.axis_index("core")
    count = planes * zs * 2
    place = jnp.stack([lax.axis_index("z"), core]).astype(jnp.int32)
    tables = make_tables(count)
    sets = pack(orbitals.swapaxes(0, 1), n_local // zs)
    tail = sets[0].shape[2:]
    slab = lax.all_to_all(sets[0][:PAIR], "core", split_axis=0, concat_axis=1, tiled=True)[0]
    square = bands == ROUNDS == 4 and zs == 4
    if square:
        own = gather_line(slab)
        partners = spread(own)
        partners[:3] = lax.optimization_barrier(partners[:3])
        orders = [(0, 1, 2, 3), (3, 1, 2, 0)]
        ready = own[3]
    else:
        every = lax.all_gather(slab, ("band", "z"), axis=0, tiled=True).reshape((bands, count) + tail)
        partners = [[every[k]] for k in range(ROUNDS)]
        orders = [range(ROUNDS)] * len(sets)
        ready = slab
    mine = []
    for fields in sets:
        fields, ready = lax.optimization_barrier((fields, ready))
        ready = lax.all_to_all(fields, "z", split_axis=0, concat_axis=0, tiled=True)
        mine.append(ready)
    other = [swap(m, "core", 1) for m in mine]
    terms = [None] * ROUNDS
    spread_sums = []
    for k, order in zip(range(len(sets)), orders):
        sums = None
        for turn in order:
            sums, terms[turn] = pair_solve(
                place, partners[turn], mine[k], other[k], sums, terms[turn], tables, turn == order[-1], k == len(sets) - 1
            )
        keep, give = sums
        spread_sums.append(lax.all_to_all(keep + swap(give, "core", 1), "z", split_axis=0, concat_axis=0, tiled=True))
    if square:
        owner = scatter_line(collect(*terms))
    else:
        owner = jnp.concatenate([t[None] for t in terms] + [jnp.zeros((bands - ROUNDS, count) + tail, F32)], axis=0)
        owner = owner.reshape((bands * count,) + tail)
        owner = lax.psum_scatter(owner, ("band", "z"), scatter_dimension=0, tiled=True)
    owner = lax.all_to_all(owner[None], "core", split_axis=1, concat_axis=0, tiled=True)
    return unpack(spread_sums, owner).swapaxes(0, 1)


def solution(mesh):
    bands, planes = mesh.devices.shape
    inner = Mesh(mesh.devices.reshape(bands, planes // 2, 2), ("band", "z", "core"))
    placed = P("band", ("z", "core"), None)
    return jax.shard_map(local, mesh=inner, in_specs=(placed,), out_specs=placed, check_vma=False)
```

time: 1370 us -> 544 us (0.40)
  waiting for transfers between devices: 620 us -> 193 us
  Pallas kernels: 531 us -> 165 us
  starting transfers between devices: 4.99 us -> 128 us
  blocking collectives: 92 us -> 14.5 us
  local copies, waits for them, and re-layouts: 82.4 us -> 12.8 us
    pallas_call x4 -> x10, Pallas kernels: 531 us -> 165 us  [the longest x8 155 us: pair_solve(): pl.pallas_call(functools.partial(pair_kernel, count, (zs, planes), layout...]
    unnamed x6 -> x0, waiting for transfers between devices: 317 us -> none
    ppermute x0 -> x44, waiting for transfers between devices: none -> 162 us  [the longest x10 85.7 us: along(): return lax.ppermute(value, 'z', pairs)]
    all_gather x2 -> x0, waiting for transfers between devices: 154 us -> none  [the longest x1 154 us: local(): partners = lax.all_gather(mine, ('band', 'z'), axis=0, tiled=False)]
    all_to_all x1 -> x4, waiting for transfers between devices: 149 us -> 30.9 us  [the longest x2 30.9 us: local(): ready = lax.all_to_all(fields, 'z', split_axis=0, concat_axis=0, tiled=True)]
    ppermute x0 -> x44, starting transfers between devices: none -> 83.2 us  [the longest x30 54.1 us: across(): return lax.ppermute(value, ('band', 'z'), pairs)]
    all_to_all x3 -> x2, blocking collectives: 92 us -> 14.5 us  [the longest x1 9.79 us: local(): lax.all_to_all(owner[None], 'core', split_axis=1, concat_axis=0, tiled=True)]
    all_to_all x1 -> x4, starting transfers between devices: 4.69 us -> 44.8 us  [the longest x2 30.9 us: local(): lax.all_to_all(keep + swap(give, 'core', 1), 'z', split_axis=0, concat_ax...]
  transfers between devices with their start and end apart: 5 -> 48, of which waited for: 4 -> 16; matrix products, arithmetic and copies ran while one was open for 5% -> 4% of each run, Pallas kernels for 0% -> 29%
where the time goes in v3:
time: 544 us; the launch traced here: 537 us
  waiting for transfers between devices  193 us (35%)
  Pallas kernels  165 us (30%)
  starting transfers between devices  128 us (24%)
  other arithmetic  21.8 us (4%)
  blocking collectives  14.5 us (3%)
  local copies, waits for them, and re-layouts  12.8 us (2%)
    pallas_call x8, Pallas kernels, pair_solve(): pl.pallas_call(functools.partial(pair_kernel, count, (zs, planes), layout...  155 us
    ppermute x10, waiting for transfers between devices, along(): return lax.ppermute(value, 'z', pairs)  85.7 us
    ppermute x30, waiting for transfers between devices, across(): return lax.ppermute(value, ('band', 'z'), pairs)  76.3 us
    ppermute x30, starting transfers between devices, across(): return lax.ppermute(value, ('band', 'z'), pairs)  54.1 us
    all_to_all x2, starting transfers between devices, local(): lax.all_to_all(keep + swap(give, 'core', 1), 'z', split_axis=0, concat_ax...  30.9 us
    all_to_all x2, waiting for transfers between devices, local(): ready = lax.all_to_all(fields, 'z', split_axis=0, concat_axis=0, tiled=True)  30.9 us
    ppermute x10, starting transfers between devices, along(): return lax.ppermute(value, 'z', pairs)  21.1 us
    all_to_all x2, starting transfers between devices, local(): ready = lax.all_to_all(fields, 'z', split_axis=0, concat_axis=0, tiled=True)  13.9 us
  transfers between devices with their start and end apart: 48, of which 16 were waited for; matrix products, arithmetic and copies ran while one was open for 4% of the time, Pallas kernels for 29%

profile of v3, /device:TPU:17, one launch (start us, length us, event | category | flops | bytes accessed | tf_op | source)
XLA Modules:
  0.0 536.6 jit_solution(262642495749737897)
XLA Ops:
  0.0 2.0 copy-done.3
  2.0 2.4 shard_map.28
  4.5 4.7 all_to_all.38
  9.2 3.2 collective-permute-start.3
  12.4 2.1 collective-permute-start
  14.5 17.5 %collective-permute-done.3.refs_2_ = f32[24,72,128]{2,1,0:T(8,128)S(1)} collective-permute-done((f32[24,72,128]{2,1,0:T(8,128)S(1)}, f32[24,72,128]{2,1,0:T(8,128)S(1)}, u32[]{:S(2)}, u32[]{:S(2)}) %collective-permute-start.3) | collective-permute-done | bytes 884768 | tf_op jit(solution)/shard_map/ppermute | solution.py:373
  32.0 3.2 collective-permute-start.4
  35.2 2.2 collective-permute-start.5
  37.4 16.4 %collective-permute-done.4 = f32[24,72,128]{2,1,0:T(8,128)S(1)} collective-permute-done((f32[24,72,128]{2,1,0:T(8,128)S(1)}, f32[24,72,128]{2,1,0:T(8,128)S(1)}, u32[]{:S(2)}, u32[]{:S(2)}) %collective-permute-start.4) | collective-permute-done | bytes 884768 | tf_op jit(solution)/shard_map/ppermute | solution.py:373
  54.9 6.4 %all-to-all-start.1 = ((f32[4,12,72,128]{3,2,1,0:T(8,128)}), f32[4,12,72,128]{3,2,1,0:T(8,128)}, u32[]{:S(2)}, u32[]{:S(2)}) async-start(f32[4,12,72,128]{3,2,1,0:T(8,128)} %bitcast.22), calls=%async_computation.1 | async-start | bytes 3538944 | tf_op jit(solution)/shard_map/all_to_all | solution.py:447
  63.8 2.1 collective-permute-start.6
  65.9 2.2 collective-permute-start.12
  68.1 30.9 %all-to-all-done.1.refs_6_ = f32[4,12,72,128]{3,2,1,0:T(8,128)} async-done(((f32[4,12,72,128]{3,2,1,0:T(8,128)}), f32[4,12,72,128]{3,2,1,0:T(8,128)}, u32[]{:S(2)}, u32[]{:S(2)}) %all-to-all-start.1) | async-done | bytes 1769504 | tf_op jit(solution)/shard_map/all_to_all | solution.py:447
  99.0 7.5 %all-to-all-start.3 = ((f32[4,12,72,128]{3,2,1,0:T(8,128)}), f32[4,12,72,128]{3,2,1,0:T(8,128)}, u32[]{:S(2)}, u32[]{:S(2)}) async-start(f32[4,12,72,128]{3,2,1,0:T(8,128)} %bitcast.25), calls=%async_computation.3 | async-start | bytes 3538944 | tf_op jit(solution)/shard_map/all_to_all | solution.py:447
  106.5 3.1 collective-permute-start.10
  109.6 1.5 collective-permute-start.8
  111.2 3.1 collective-permute-start.18
  115.6 2.6 collective-permute-start.17
  118.2 9.9 %collective-permute-done.10.refs_3_ = f32[24,72,128]{2,1,0:T(8,128)} collective-permute-done((f32[24,72,128]{2,1,0:T(8,128)}, f32[24,72,128]{2,1,0:T(8,128)}, u32[]{:S(2)}, u32[]{:S(2)}) %collective-permute-start.10) | collective-permute-done | bytes 884768 | tf_op jit(solution)/shard_map/ppermute | solution.py:369
  129.3 23.3 %collective-permute-done.8.refs_5_ = f32[24,72,128]{2,1,0:T(8,128)S(1)} collective-permute-done((f32[24,72,128]{2,1,0:T(8,128)S(1)}, f32[24,72,128]{2,1,0:T(8,128)S(1)}, u32[]{:S(2)}, u32[]{:S(2)}) %collective-permute-start.8) | collective-permute-done | bytes 884768 | tf_op jit(solution)/shard_map/ppermute | solution.py:373
  154.8 1.6 collective-permute-start.15
  159.0 3.1 collective-permute-start.7
  162.1 9.3 %collective-permute-done.20.refs_4_ = f32[24,72,128]{2,1,0:T(8,128)S(1)} collective-permute-done((f32[24,72,128]{2,1,0:T(8,128)S(1)}, f32[24,72,128]{2,1,0:T(8,128)S(1)}, u32[]{:S(2)}, u32[]{:S(2)}) %collective-permute-start.20) | collective-permute-done | bytes 884768 | tf_op jit(solution)/shard_map/ppermute | solution.py:369
  172.4 3.1 collective-permute-start.11
  177.8 1.6 collective-permute-start.16
  179.4 3.8 collective-permute-start.22
  183.2 4.8 fusion.refs_9_.refs_10_.refs_11_
  190.4 18.8 %shard_map.29 = (f32[96,72,128]{2,1,0:T(8,128)}, f32[96,72,128]{2,1,0:T(8,128)}) custom-call(s32[2]{0:T(128)S(1)} %pad_add_fusion.refs_0_, f32[24,72,128]{2,1,0:T(8,128)S(1)} %bitcast.19, f32[24,72,128]{2,1,0:T(8,128)S(1)} %collective-permute-done.3.refs_2_, f32[24,72,128]{2,1,0:T(8,128)S(1)} %copy-done.6, f32[24,72,128]{2,1,0:T(8,128)S(1)} %add.145.refs_4_, ...), custom_call_target="tpu_custom_call" | custom-call | flops 1019215872 | bytes 1048576 | tf_op jit(solution)/shard_map/pallas_call | solution.py:272
  209.2 19.0 %shard_map.30 = (f32[96,72,128]{2,1,0:T(8,128)}, f32[96,72,128]{2,1,0:T(8,128)}) custom-call(s32[2]{0:T(128)S(1)} %pad_add_fusion.refs_0_, f32[24,72,128]{2,1,0:T(8,128)} %collective-permute-done.1.refs_1_, f32[24,72,128]{2,1,0:T(8,128)} %collective-permute-done.12.refs_2_, f32[24,72,128]{2,1,0:T(8,128)S(1)} %copy-done.10, ...), custom_call_target="tpu_custom_call" | custom-call | flops 1019215872 | bytes 1048576 | tf_op jit(solution)/shard_map/pallas_call | solution.py:272
  228.3 18.9 %shard_map.31 = (f32[96,72,128]{2,1,0:T(8,128)}, f32[96,72,128]{2,1,0:T(8,128)}) custom-call(s32[2]{0:T(128)S(1)} %pad_add_fusion.refs_0_, f32[24,72,128]{2,1,0:T(8,128)} %collective-permute-done.9.refs_1_, f32[24,72,128]{2,1,0:T(8,128)} %collective-permute-done.6.refs_2_, f32[24,72,128]{2,1,0:T(8,128)} %collective-permute-done.10.refs_3_, ...), custom_call_target="tpu_custom_call" | custom-call | flops 1019215872 | bytes 1048576 | tf_op jit(solution)/shard_map/pallas_call | solution.py:272
  247.3 19.1 %shard_map.32 = (f32[4,12,72,128]{3,2,1,0:T(8,128)}, f32[4,12,72,128]{3,2,1,0:T(8,128)}, f32[96,72,128]{2,1,0:T(8,128)}) custom-call(s32[2]{0:T(128)S(1)} %pad_add_fusion.refs_0_, f32[24,72,128]{2,1,0:T(8,128)S(1)} %copy-done.14, f32[24,72,128]{2,1,0:T(8,128)} %collective-permute-done.7.refs_2_, f32[24,72,128]{2,1,0:T(8,128)} %collective-permute-done.11.refs_3_, ...), custom_call_target="tpu_custom_call" | custom-call | flops 1019215872 | bytes 1048576 | tf_op jit(solution)/shard_map/pallas_call | solution.py:272
  266.4 19.7 %shard_map.33 = (f32[96,72,128]{2,1,0:T(8,128)}, f32[24,72,128]{2,1,0:T(8,128)}, f32[24,72,128]{2,1,0:T(8,128)S(1)}, f32[24,72,128]{2,1,0:T(8,128)}, f32[24,72,128]{2,1,0:T(8,128)S(1)}, /*index=5*/f32[24,72,128]{2,1,0:T(8,128)}) custom-call(s32[2]{0:T(128)S(1)} %pad_add_fusion.refs_0_, f32[24,72,128]{2,1,0:T(8,128)S(1)} %copy-done.14, ...), custom_call_target="tpu_custom_call" | custom-call | flops 1019215872 | bytes 1048576 | tf_op jit(solution)/shard_map/pallas_call | solution.py:272
  288.0 1.6 collective-permute-start.34
  289.6 1.5 add.150
  291.1 22.8 %all-to-all-start.2 = ((f32[4,12,72,128]{3,2,1,0:T(8,128)}), f32[4,12,72,128]{3,2,1,0:T(8,128)S(1)}, u32[]{:S(2)}, u32[]{:S(2)}) async-start(f32[4,12,72,128]{3,2,1,0:T(8,128)} %add.150), calls=%async_computation.2 | async-start | bytes 3538944 | tf_op jit(solution)/shard_map/all_to_all | solution.py:459
  313.9 19.5 %shard_map.34 = (f32[96,72,128]{2,1,0:T(8,128)}, f32[24,72,128]{2,1,0:T(8,128)S(1)}, f32[24,72,128]{2,1,0:T(8,128)}, f32[24,72,128]{2,1,0:T(8,128)S(1)}, f32[24,...) custom-call(s32[2]{0:T(128)S(1)} %pad_add_fusion.refs_0_, f32[24,72,128]{2,1,0:T(8,128)} %collective-permute-done.1.refs_1_, ...), custom_call_target="tpu_custom_call" | custom-call | flops 1019215872 | bytes 1048576 | tf_op jit(solution)/shard_map/pallas_call | solution.py:272
  336.2 19.6 %shard_map.35 = (f32[96,72,128]{2,1,0:T(8,128)}, f32[24,72,128]{2,1,0:T(8,128)S(1)}, f32[24,72,128]{2,1,0:T(8,128)S(1)}, f32[24,72,128]{2,1,0:T(8,128)S(1)}, f32...) custom-call(s32[2]{0:T(128)S(1)} %pad_add_fusion.refs_0_, f32[24,72,128]{2,1,0:T(8,128)} %collective-permute-done.9.refs_1_, ...), custom_call_target="tpu_custom_call" | custom-call | flops 1019215872 | bytes 1048576 | tf_op jit(solution)/shard_map/pallas_call | solution.py:272
  355.8 2.8 add.162
  358.6 1.6 collective-permute-start.35
  360.3 20.4 %shard_map.36 = (f32[4,12,72,128]{3,2,1,0:T(8,128)}, f32[4,12,72,128]{3,2,1,0:T(8,128)}, f32[24,72,128]{2,1,0:T(8,128)S(1)}, f32[24,72,128]{2,1,0:T(8,128)S(1)},...) custom-call(s32[2]{0:T(128)S(1)} %pad_add_fusion.refs_0_, ...), custom_call_target="tpu_custom_call" | custom-call | flops 1019215872 | bytes 1048576 | tf_op jit(solution)/shard_map/pallas_call | solution.py:272
  380.7 1.6 collective-permute-start.23
  383.6 3.1 collective-permute-start.40
  391.0 12.5 %collective-permute-done.32 = f32[24,72,128]{2,1,0:T(8,128)S(1)} collective-permute-done((f32[24,72,128]{2,1,0:T(8,128)S(1)}, f32[24,72,128]{2,1,0:T(8,128)S(1)}, u32[]{:S(2)}, u32[]{:S(2)}) %collective-permute-start.32) | collective-permute-done | bytes 884768 | tf_op jit(solution)/shard_map/ppermute | solution.py:369
  403.6 3.1 collective-permute-start.28
  406.7 2.8 collective-permute-start.39
  409.5 15.8 %collective-permute-done.31 = f32[24,72,128]{2,1,0:T(8,128)S(1)} collective-permute-done((f32[24,72,128]{2,1,0:T(8,128)S(1)}, f32[24,72,128]{2,1,0:T(8,128)S(1)}, u32[]{:S(2)}, u32[]{:S(2)}) %collective-permute-start.31) | collective-permute-done | bytes 884768 | tf_op jit(solution)/shard_map/ppermute | solution.py:369
  426.6 3.1 collective-permute-start.41
  430.9 2.2 collective-permute-start.42
  434.5 8.2 %all-to-all-start.4 = ((f32[4,12,72,128]{3,2,1,0:T(8,128)}), f32[4,12,72,128]{3,2,1,0:T(8,128)}, u32[]{:S(2)}, u32[]{:S(2)}) async-start(f32[4,12,72,128]{3,2,1,0:T(8,128)} %add.151), calls=%async_computation.4 | async-start | bytes 3538944 | tf_op jit(solution)/shard_map/all_to_all | solution.py:459
  442.7 1.7 collective-permute-done.28
  444.4 3.1 collective-permute-start.27
  447.5 1.6 add.156
  449.1 14.2 %collective-permute-done.39 = f32[24,72,128]{2,1,0:T(8,128)} collective-permute-done((f32[24,72,128]{2,1,0:T(8,128)}, f32[24,72,128]{2,1,0:T(8,128)}, u32[]{:S(2)}, u32[]{:S(2)}) %collective-permute-start.39) | collective-permute-done | bytes 884768 | tf_op jit(solution)/shard_map/ppermute | solution.py:369
  463.3 2.1 collective-permute-start.29
  470.6 2.1 add_add_fusion
  472.7 9.5 %collective-permute-done.27 = f32[24,72,128]{2,1,0:T(8,128)S(1)} collective-permute-done((f32[24,72,128]{2,1,0:T(8,128)}, f32[24,72,128]{2,1,0:T(8,128)S(1)}, u32[]{:S(2)}, u32[]{:S(2)}) %collective-permute-start.27) | collective-permute-done | bytes 884768 | tf_op jit(solution)/shard_map/ppermute | solution.py:369
  482.2 2.3 collective-permute-start.43
  484.5 13.5 %collective-permute-done.37 = f32[24,72,128]{2,1,0:T(8,128)S(1)} collective-permute-done((f32[24,72,128]{2,1,0:T(8,128)}, f32[24,72,128]{2,1,0:T(8,128)S(1)}, u32[]{:S(2)}, u32[]{:S(2)}) %collective-permute-start.37) | collective-permute-done | bytes 884768 | tf_op jit(solution)/shard_map/ppermute | solution.py:373
  498.1 1.9 collective-permute-start.38
  500.1 3.3 collective-permute-done.26
  503.4 3.3 collective-permute-done.43
  506.6 10.8 %collective-permute-done.38 = f32[24,72,128]{2,1,0:T(8,128)S(1)} collective-permute-done((f32[24,72,128]{2,1,0:T(8,128)S(1)}, f32[24,72,128]{2,1,0:T(8,128)S(1)}, u32[]{:S(2)}, u32[]{:S(2)}) %collective-permute-start.38) | collective-permute-done | bytes 884768 | tf_op jit(solution)/shard_map/ppermute | solution.py:373
  518.6 9.8 %all_to_all.39 = f32[1,24,72,128]{3,2,0,1:T(8,128)S(1)} all-to-all(f32[1,24,72,128]{3,2,0,1:T(8,128)} %add_bitcast_fusion), channel_id=1, replica_groups=mesh['band'=4,'z'=4,'core'=2] {'core'}, dimensions={1} | all-to-all | bytes 1769472 | tf_op jit(solution)/shard_map/all_to_all | solution.py:466
  528.4 7.8 %shard_map.37 = f32[12,8,9216]{2,1,0:T(8,128)} custom-call(f32[3456,128]{1,0:T(8,128)S(1)} %bitcast.21, f32[3456,128]{1,0:T(8,128)} %bitcast.8.refs_1_, f32[1728,128]{1,0:T(8,128)S(1)} %bitcast.24), custom_call_target="tpu_custom_call" | custom-call | tf_op jit(solution)/shard_map/pallas_call | solution.py:351
  (133 shorter events, 37.1 us)
Async XLA Ops:
  4.4 50.4 %copy-start.17 = (f32[3456,128]{1,0:T(8,128)}, f32[3456,128]{1,0:T(8,128)S(1)}, u32[]{:S(2)}) copy-start(f32[3456,128]{1,0:T(8,128)S(1)} %get-tuple-element.104) | copy-start | bytes 5308420
  4.4 50.5 %copy-start.2 = (f32[3456,128]{1,0:T(8,128)}, f32[3456,128]{1,0:T(8,128)S(1)}, u32[]{:S(2)}) copy-start(f32[3456,128]{1,0:T(8,128)S(1)} %get-tuple-element.70) | copy-start | bytes 5308420
  9.2 22.7 %collective-permute-start.3 = (f32[24,72,128]{2,1,0:T(8,128)S(1)}, f32[24,72,128]{2,1,0:T(8,128)S(1)}, u32[]{:S(2)}, u32[]{:S(2)}) collective-permute-start(f32[24,72,128]{2,1,0:T(8,128)S(1)} %bitcast.15), channel_id=1, source_target_pairs={{0,2},{2,4},{4,6},{1,3},{3,5},{5,7},{8,10},{10,12},{12,14},{9,11},... | collective-permute-start | bytes 2654216 | tf_op jit(solution)/shard_map/ppermute | solution.py:373
  12.4 22.7 %collective-permute-start = (f32[24,72,128]{2,1,0:T(8,128)S(1)}, f32[24,72,128]{2,1,0:T(8,128)S(1)}, u32[]{:S(2)}, u32[]{:S(2)}) collective-permute-start(f32[24,72,128]{2,1,0:T(8,128)S(1)} %bitcast.16), channel_id=1, source_target_pairs={{2,0},{4,2},{6,4},{3,1},{5,3},{7,5},{10,8},{12,10},{14,12},{11,9},... | collective-permute-start | bytes 2654216 | tf_op jit(solution)/shard_map/ppermute | solution.py:373
  32.0 156.1 %copy-start.4 = (f32[24,72,128]{2,1,0:T(8,128)}, f32[24,72,128]{2,1,0:T(8,128)S(1)}, u32[]{:S(2)}) copy-start(f32[24,72,128]{2,1,0:T(8,128)S(1)} %collective-permute-done.3.refs_2_) | copy-start | bytes 2654212
  32.0 21.8 %collective-permute-start.4 = (f32[24,72,128]{2,1,0:T(8,128)S(1)}, f32[24,72,128]{2,1,0:T(8,128)S(1)}, u32[]{:S(2)}, u32[]{:S(2)}) collective-permute-start(f32[24,72,128]{2,1,0:T(8,128)S(1)} %collective-permute-done.3.refs_2_), channel_id=1, source_target_pairs={{2,4},{4,6},{3,5},{5,7},{10,12},{12,14},{11,13},{13,15},{18,20},{2... | collective-permute-start | bytes 2654216 | tf_op jit(solution)/shard_map/ppermute | solution.py:373
  35.2 19.6 %collective-permute-start.5 = (f32[24,72,128]{2,1,0:T(8,128)S(1)}, f32[24,72,128]{2,1,0:T(8,128)S(1)}, u32[]{:S(2)}, u32[]{:S(2)}) collective-permute-start(f32[24,72,128]{2,1,0:T(8,128)S(1)} %collective-permute-done.refs_3_), channel_id=1, source_target_pairs={{2,0},{4,2},{3,1},{5,3},{10,8},{12,10},{11,9},{13,11},{18,16},{20,... | collective-permute-start | bytes 2654216 | tf_op jit(solution)/shard_map/ppermute | solution.py:373
  54.9 133.2 %copy-start.1 = (f32[24,72,128]{2,1,0:T(8,128)}, f32[24,72,128]{2,1,0:T(8,128)S(1)}, u32[]{:S(2)}) copy-start(f32[24,72,128]{2,1,0:T(8,128)S(1)} %add.145.refs_4_) | copy-start | bytes 2654212
  54.9 44.1 %all-to-all-start.1 = ((f32[4,12,72,128]{3,2,1,0:T(8,128)}), f32[4,12,72,128]{3,2,1,0:T(8,128)}, u32[]{:S(2)}, u32[]{:S(2)}) async-start(f32[4,12,72,128]{3,2,1,0:T(8,128)} %bitcast.22), calls=%async_computation.1 | async-start | bytes 3538944 | tf_op jit(solution)/shard_map/all_to_all | solution.py:447
  61.3 126.7 %copy-start = (bf16[832,256]{1,0:T(8,128)(2,1)S(1)}, bf16[832,256]{1,0:T(8,128)(2,1)}, u32[]{:S(2)}) copy-start(bf16[832,256]{1,0:T(8,128)(2,1)} %constant.52.clone.refs_8_.refs_9_.refs_10_) | copy-start | bytes 1277956
  61.3 45.1 %collective-permute-start.9 = (f32[24,72,128]{2,1,0:T(8,128)S(1)}, f32[24,72,128]{2,1,0:T(8,128)}, u32[]{:S(2)}, u32[]{:S(2)}) collective-permute-start(f32[24,72,128]{2,1,0:T(8,128)S(1)} %bitcast.17), channel_id=1, source_target_pairs={{0,16},{2,18},{4,20},{6,22},{8,24},{10,26},{12,28},{14,30},{16,0},... | collective-permute-start | bytes 2654216 | tf_op jit(solution)/shard_map/ppermute | solution.py:369
  62.6 48.6 %collective-permute-start.1 = (f32[24,72,128]{2,1,0:T(8,128)S(1)}, f32[24,72,128]{2,1,0:T(8,128)}, u32[]{:S(2)}, u32[]{:S(2)}) collective-permute-start(f32[24,72,128]{2,1,0:T(8,128)S(1)} %bitcast.18), channel_id=1, source_target_pairs={{0,8},{2,10},{4,12},{6,14},{8,0},{10,2},{12,4},{14,6},{16,24},{18,... | collective-permute-start | bytes 2654216 | tf_op jit(solution)/shard_map/ppermute | solution.py:369
  63.8 50.5 %collective-permute-start.6 = (f32[24,72,128]{2,1,0:T(8,128)S(1)}, f32[24,72,128]{2,1,0:T(8,128)}, u32[]{:S(2)}, u32[]{:S(2)}) collective-permute-start(f32[24,72,128]{2,1,0:T(8,128)S(1)} %collective-permute-done.3.refs_2_), channel_id=1, source_target_pairs={{2,18},{4,20},{6,22},{10,26},{12,28},{14,30},{18,2},{20,4},{22,6},... | collective-permute-start | bytes 2654216 | tf_op jit(solution)/shard_map/ppermute | solution.py:369
  65.9 49.7 %collective-permute-start.12 = (f32[24,72,128]{2,1,0:T(8,128)S(1)}, f32[24,72,128]{2,1,0:T(8,128)}, u32[]{:S(2)}, u32[]{:S(2)}) collective-permute-start(f32[24,72,128]{2,1,0:T(8,128)S(1)} %collective-permute-done.3.refs_2_), channel_id=1, source_target_pairs={{2,10},{4,12},{6,14},{10,2},{12,4},{14,6},{18,26},{20,28},{22,30},... | collective-permute-start | bytes 2654216 | tf_op jit(solution)/shard_map/ppermute | solution.py:369
  99.0 80.4 %all-to-all-start.3 = ((f32[4,12,72,128]{3,2,1,0:T(8,128)}), f32[4,12,72,128]{3,2,1,0:T(8,128)}, u32[]{:S(2)}, u32[]{:S(2)}) async-start(f32[4,12,72,128]{3,2,1,0:T(8,128)} %bitcast.25), calls=%async_computation.3 | async-start | bytes 3538944 | tf_op jit(solution)/shard_map/all_to_all | solution.py:447
  106.5 21.6 %collective-permute-start.10 = (f32[24,72,128]{2,1,0:T(8,128)}, f32[24,72,128]{2,1,0:T(8,128)}, u32[]{:S(2)}, u32[]{:S(2)}) collective-permute-start(f32[24,72,128]{2,1,0:T(8,128)} %copy-done.5), channel_id=1, source_target_pairs={{0,16},{2,18},{4,20},{8,24},{10,26},{12,28},{16,0},{18,2},{20,4},{... | collective-permute-start | bytes 2654216 | tf_op jit(solution)/shard_map/ppermute | solution.py:369
  109.6 43.0 %collective-permute-start.8 = (f32[24,72,128]{2,1,0:T(8,128)S(1)}, f32[24,72,128]{2,1,0:T(8,128)S(1)}, u32[]{:S(2)}, u32[]{:S(2)}) collective-permute-start(f32[24,72,128]{2,1,0:T(8,128)S(1)} %add.145.refs_4_), channel_id=1, source_target_pairs={{4,6},{2,0},{5,7},{3,1},{12,14},{10,8},{13,15},{11,9},{20,22},{18,... | collective-permute-start | bytes 2654216 | tf_op jit(solution)/shard_map/ppermute | solution.py:373
  111.2 42.7 %collective-permute-start.18 = (f32[24,72,128]{2,1,0:T(8,128)}, f32[24,72,128]{2,1,0:T(8,128)S(1)}, u32[]{:S(2)}, u32[]{:S(2)}) collective-permute-start(f32[24,72,128]{2,1,0:T(8,128)} %copy-done.5), channel_id=1, source_target_pairs={{0,8},{2,10},{4,12},{8,0},{10,2},{12,4},{16,24},{18,26},{20,28},{2... | collective-permute-start | bytes 2654216 | tf_op jit(solution)/shard_map/ppermute | solution.py:369
  114.3 42.1 %collective-permute-start.2 = (f32[24,72,128]{2,1,0:T(8,128)}, f32[24,72,128]{2,1,0:T(8,128)S(1)}, u32[]{:S(2)}, u32[]{:S(2)}) collective-permute-start(f32[24,72,128]{2,1,0:T(8,128)} %collective-permute-done.1.refs_1_), channel_id=1, source_target_pairs={{0,16},{2,18},{4,20},{6,22},{8,24},{10,26},{12,28},{14,30},{16,0},... | collective-permute-start | bytes 2654216 | tf_op jit(solution)/shard_map/ppermute | solution.py:369
  115.6 63.8 %collective-permute-start.17 = (f32[4,12,72,128]{3,2,1,0:T(8,128)}, f32[4,12,72,128]{3,2,1,0:T(8,128)}, u32[]{:S(2)}, u32[]{:S(2)}) collective-permute-start(f32[4,12,72,128]{3,2,1,0:T(8,128)} %all-to-all-done.1.refs_6_), channel_id=1, source_target_pairs={{0,1},{1,0},{2,3},{3,2},{4,5},{5,4},{6,7},{7,6},{8,9},{9,8},{10,11... | collective-permute-start | bytes 5308424 | tf_op jit(solution)/shard_map/ppermute | solution.py:363
  128.1 30.9 %collective-permute-start.13 = (f32[24,72,128]{2,1,0:T(8,128)S(1)}, f32[24,72,128]{2,1,0:T(8,128)}, u32[]{:S(2)}, u32[]{:S(2)}) collective-permute-start(f32[24,72,128]{2,1,0:T(8,128)S(1)} %add.145.refs_4_), channel_id=1, source_target_pairs={{0,8},{2,10},{4,12},{6,14},{8,0},{10,2},{12,4},{14,6},{16,24},{18,... | collective-permute-start | bytes 2654216 | tf_op jit(solution)/shard_map/ppermute | solution.py:369
  152.6 18.9 %collective-permute-start.20 = (f32[24,72,128]{2,1,0:T(8,128)S(1)}, f32[24,72,128]{2,1,0:T(8,128)S(1)}, u32[]{:S(2)}, u32[]{:S(2)}) collective-permute-start(f32[24,72,128]{2,1,0:T(8,128)S(1)} %add.145.refs_4_), channel_id=1, source_target_pairs={{0,16},{2,18},{4,20},{6,22},{8,24},{10,26},{12,28},{14,30},{16,0},... | collective-permute-start | bytes 2654216 | tf_op jit(solution)/shard_map/ppermute | solution.py:369
  154.8 20.7 %collective-permute-start.15 = (f32[24,72,128]{2,1,0:T(8,128)S(1)}, f32[24,72,128]{2,1,0:T(8,128)}, u32[]{:S(2)}, u32[]{:S(2)}) collective-permute-start(f32[24,72,128]{2,1,0:T(8,128)S(1)} %collective-permute-done.8.refs_5_), channel_id=1, source_target_pairs={{0,16},{6,22},{8,24},{14,30},{16,0},{22,6},{24,8},{30,14},{1,17},{... | collective-permute-start | bytes 2654216 | tf_op jit(solution)/shard_map/ppermute | solution.py:369
  157.3 19.5 %collective-permute-start.19 = (f32[24,72,128]{2,1,0:T(8,128)S(1)}, f32[24,72,128]{2,1,0:T(8,128)S(1)}, u32[]{:S(2)}, u32[]{:S(2)}) collective-permute-start(f32[24,72,128]{2,1,0:T(8,128)S(1)} %collective-permute-done.8.refs_5_), channel_id=1, source_target_pairs={{0,8},{6,14},{8,0},{14,6},{16,24},{22,30},{24,16},{30,22},{1,9},{7... | collective-permute-start | bytes 2654216 | tf_op jit(solution)/shard_map/ppermute | solution.py:369
  159.0 88.2 %collective-permute-start.7 = (f32[24,72,128]{2,1,0:T(8,128)}, f32[24,72,128]{2,1,0:T(8,128)}, u32[]{:S(2)}, u32[]{:S(2)}) collective-permute-start(f32[24,72,128]{2,1,0:T(8,128)} %collective-permute-done.6.refs_2_), channel_id=1, source_target_pairs={{2,10},{4,12},{6,14},{10,2},{12,4},{14,6},{18,26},{20,28},{22,30},... | collective-permute-start | bytes 2654216 | tf_op jit(solution)/shard_map/ppermute | solution.py:369
  172.4 74.9 %collective-permute-start.11 = (f32[24,72,128]{2,1,0:T(8,128)}, f32[24,72,128]{2,1,0:T(8,128)}, u32[]{:S(2)}, u32[]{:S(2)}) collective-permute-start(f32[24,72,128]{2,1,0:T(8,128)} %collective-permute-done.10.refs_3_), channel_id=1, source_target_pairs={{0,8},{2,10},{4,12},{8,0},{10,2},{12,4},{16,24},{18,26},{20,28},{2... | collective-permute-start | bytes 2654216 | tf_op jit(solution)/shard_map/ppermute | solution.py:369
  175.5 71.7 %collective-permute-start.14 = (f32[24,72,128]{2,1,0:T(8,128)}, f32[24,72,128]{2,1,0:T(8,128)}, u32[]{:S(2)}, u32[]{:S(2)}) collective-permute-start(f32[24,72,128]{2,1,0:T(8,128)} %collective-permute-done.13.refs_4_), channel_id=1, source_target_pairs={{0,16},{2,18},{4,20},{6,22},{8,24},{10,26},{12,28},{14,30},{16,0},... | collective-permute-start | bytes 2654216 | tf_op jit(solution)/shard_map/ppermute | solution.py:369
  177.8 69.5 %collective-permute-start.16 = (f32[24,72,128]{2,1,0:T(8,128)}, f32[24,72,128]{2,1,0:T(8,128)}, u32[]{:S(2)}, u32[]{:S(2)}) collective-permute-start(f32[24,72,128]{2,1,0:T(8,128)} %collective-permute-done.15.refs_5_), channel_id=1, source_target_pairs={{0,8},{6,14},{8,0},{14,6},{16,24},{22,30},{24,16},{30,22},{1,9},{7... | collective-permute-start | bytes 2654216 | tf_op jit(solution)/shard_map/ppermute | solution.py:369
  179.4 87.0 %collective-permute-start.22 = (f32[4,12,72,128]{3,2,1,0:T(8,128)}, f32[4,12,72,128]{3,2,1,0:T(8,128)}, u32[]{:S(2)}, u32[]{:S(2)}) collective-permute-start(f32[4,12,72,128]{3,2,1,0:T(8,128)} %all-to-all-done.3.refs_6_), channel_id=1, source_target_pairs={{0,1},{1,0},{2,3},{3,2},{4,5},{5,4},{6,7},{7,6},{8,9},{9,8},{10,11... | collective-permute-start | bytes 5308424 | tf_op jit(solution)/shard_map/ppermute | solution.py:363
  228.3 19.0 %copy-start.14 = (f32[24,72,128]{2,1,0:T(8,128)S(1)}, f32[24,72,128]{2,1,0:T(8,128)}, u32[]{:S(2)}) copy-start(f32[24,72,128]{2,1,0:T(8,128)} %copy-done.13) | copy-start | bytes 2654212
  266.3 23.3 %collective-permute-start.21 = (f32[4,12,72,128]{3,2,1,0:T(8,128)}, f32[4,12,72,128]{3,2,1,0:T(8,128)S(1)}, u32[]{:S(2)}, u32[]{:S(2)}) collective-permute-start(f32[4,12,72,128]{3,2,1,0:T(8,128)} %get-tuple-element.103), channel_id=1, source_target_pairs={{0,1},{1,0},{2,3},{3,2},{4,5},{5,4},{6,7},{7,6},{8,9},{9,8},{10,11... | collective-permute-start | bytes 5308424 | tf_op jit(solution)/shard_map/ppermute | solution.py:363
  266.4 23.2 %copy-start.33 = (f32[4,12,72,128]{3,2,1,0:T(8,128)S(1)}, f32[4,12,72,128]{3,2,1,0:T(8,128)}, u32[]{:S(2)}) copy-start(f32[4,12,72,128]{3,2,1,0:T(8,128)} %get-tuple-element.102) | copy-start | bytes 5308420
  288.0 67.8 %collective-permute-start.34 = (f32[24,72,128]{2,1,0:T(8,128)}, f32[24,72,128]{2,1,0:T(8,128)}, u32[]{:S(2)}, u32[]{:S(2)}) collective-permute-start(f32[24,72,128]{2,1,0:T(8,128)} %get-tuple-element.130), channel_id=1, source_target_pairs={{0,8},{6,14},{8,0},{14,6},{16,24},{22,30},{24,16},{30,22},{1,9},{7... | collective-permute-start | bytes 2654216 | tf_op jit(solution)/shard_map/ppermute | solution.py:369
  291.1 143.4 %all-to-all-start.2 = ((f32[4,12,72,128]{3,2,1,0:T(8,128)}), f32[4,12,72,128]{3,2,1,0:T(8,128)S(1)}, u32[]{:S(2)}, u32[]{:S(2)}) async-start(f32[4,12,72,128]{3,2,1,0:T(8,128)} %add.150), calls=%async_computation.2 | async-start | bytes 3538944 | tf_op jit(solution)/shard_map/all_to_all | solution.py:459
  313.9 22.0 %copy-start.31 = (f32[24,72,128]{2,1,0:T(8,128)S(1)}, f32[24,72,128]{2,1,0:T(8,128)}, u32[]{:S(2)}) copy-start(f32[24,72,128]{2,1,0:T(8,128)} %copy-done.30) | copy-start | bytes 2654212
  335.2 52.8 %collective-permute-start.33 = (f32[24,72,128]{2,1,0:T(8,128)S(1)}, f32[24,72,128]{2,1,0:T(8,128)S(1)}, u32[]{:S(2)}, u32[]{:S(2)}) collective-permute-start(f32[24,72,128]{2,1,0:T(8,128)S(1)} %get-tuple-element.128), channel_id=1, source_target_pairs={{0,8},{6,14},{8,0},{14,6},{16,24},{22,30},{24,16},{30,22},{1,9},{7... | collective-permute-start | bytes 2654216 | tf_op jit(solution)/shard_map/ppermute | solution.py:369
  335.9 47.7 %collective-permute-start.30 = (f32[24,72,128]{2,1,0:T(8,128)S(1)}, f32[24,72,128]{2,1,0:T(8,128)}, u32[]{:S(2)}, u32[]{:S(2)}) collective-permute-start(f32[24,72,128]{2,1,0:T(8,128)S(1)} %copy-done.31), channel_id=1, source_target_pairs={{0,16},{2,18},{4,20},{6,22},{8,24},{10,26},{12,28},{14,30},{16,0},... | collective-permute-start | bytes 2654216 | tf_op jit(solution)/shard_map/ppermute | solution.py:369
  358.6 29.6 %collective-permute-start.35 = (f32[24,72,128]{2,1,0:T(8,128)}, f32[24,72,128]{2,1,0:T(8,128)}, u32[]{:S(2)}, u32[]{:S(2)}) collective-permute-start(f32[24,72,128]{2,1,0:T(8,128)} %add.162), channel_id=1, source_target_pairs={{0,16},{6,22},{8,24},{14,30},{16,0},{22,6},{24,8},{30,14},{1,17},{... | collective-permute-start | bytes 2654216 | tf_op jit(solution)/shard_map/ppermute | solution.py:369
  360.3 23.3 %copy-start.29 = (f32[24,72,128]{2,1,0:T(8,128)S(1)}, f32[24,72,128]{2,1,0:T(8,128)}, u32[]{:S(2)}) copy-start(f32[24,72,128]{2,1,0:T(8,128)} %copy-done.28) | copy-start | bytes 2654212
  380.7 50.2 %copy-start.21 = (f32[24,72,128]{2,1,0:T(8,128)}, f32[24,72,128]{2,1,0:T(8,128)S(1)}, u32[]{:S(2)}) copy-start(f32[24,72,128]{2,1,0:T(8,128)S(1)} %get-tuple-element.115) | copy-start | bytes 2654212
  380.7 50.2 %copy-start.23 = (f32[24,72,128]{2,1,0:T(8,128)}, f32[24,72,128]{2,1,0:T(8,128)S(1)}, u32[]{:S(2)}) copy-start(f32[24,72,128]{2,1,0:T(8,128)S(1)} %get-tuple-element.119) | copy-start | bytes 2654212
  380.7 50.2 %copy-start.25 = (f32[24,72,128]{2,1,0:T(8,128)}, f32[24,72,128]{2,1,0:T(8,128)S(1)}, u32[]{:S(2)}) copy-start(f32[24,72,128]{2,1,0:T(8,128)S(1)} %get-tuple-element.131) | copy-start | bytes 2654212
  380.7 50.2 %collective-permute-start.23 = (f32[4,12,72,128]{3,2,1,0:T(8,128)}, f32[4,12,72,128]{3,2,1,0:T(8,128)S(1)}, u32[]{:S(2)}, u32[]{:S(2)}) collective-permute-start(f32[4,12,72,128]{3,2,1,0:T(8,128)} %get-tuple-element.114), channel_id=1, source_target_pairs={{0,1},{1,0},{2,3},{3,2},{4,5},{5,4},{6,7},{7,6},{8,9},{9,8},{10,11... | collective-permute-start | bytes 5308424 | tf_op jit(solution)/shard_map/ppermute | solution.py:363
  382.3 21.2 %collective-permute-start.32 = (f32[24,72,128]{2,1,0:T(8,128)S(1)}, f32[24,72,128]{2,1,0:T(8,128)S(1)}, u32[]{:S(2)}, u32[]{:S(2)}) collective-permute-start(f32[24,72,128]{2,1,0:T(8,128)S(1)} %get-tuple-element.126), channel_id=1, source_target_pairs={{0,16},{2,18},{4,20},{6,22},{8,24},{10,26},{12,28},{14,30},{16,0},... | collective-permute-start | bytes 2654216 | tf_op jit(solution)/shard_map/ppermute | solution.py:369
  383.6 23.1 %collective-permute-start.40 = (f32[24,72,128]{2,1,0:T(8,128)S(1)}, f32[24,72,128]{2,1,0:T(8,128)S(1)}, u32[]{:S(2)}, u32[]{:S(2)}) collective-permute-start(f32[24,72,128]{2,1,0:T(8,128)S(1)} %copy-done.29), channel_id=1, source_target_pairs={{2,10},{4,12},{6,14},{10,2},{12,4},{14,6},{18,26},{20,28},{22,30},... | collective-permute-start | bytes 2654216 | tf_op jit(solution)/shard_map/ppermute | solution.py:369
  388.0 37.3 %collective-permute-start.31 = (f32[24,72,128]{2,1,0:T(8,128)S(1)}, f32[24,72,128]{2,1,0:T(8,128)S(1)}, u32[]{:S(2)}, u32[]{:S(2)}) collective-permute-start(f32[24,72,128]{2,1,0:T(8,128)S(1)} %add.158), channel_id=1, source_target_pairs={{0,8},{2,10},{4,12},{6,14},{8,0},{10,2},{12,4},{14,6},{16,24},{18,... | collective-permute-start | bytes 2654216 | tf_op jit(solution)/shard_map/ppermute | solution.py:369
  388.3 44.8 %copy-start.32 = (f32[4,12,72,128]{3,2,1,0:T(8,128)S(1)}, f32[4,12,72,128]{3,2,1,0:T(8,128)}, u32[]{:S(2)}) copy-start(f32[4,12,72,128]{3,2,1,0:T(8,128)} %get-tuple-element.113) | copy-start | bytes 5308420
  389.7 36.8 %collective-permute-start.36 = (f32[24,72,128]{2,1,0:T(8,128)S(1)}, f32[24,72,128]{2,1,0:T(8,128)S(1)}, u32[]{:S(2)}, u32[]{:S(2)}) collective-permute-start(f32[24,72,128]{2,1,0:T(8,128)S(1)} %add_add_fusion.1), channel_id=1, source_target_pairs={{0,2},{6,4},{1,3},{7,5},{8,10},{14,12},{9,11},{15,13},{16,18},{22,... | collective-permute-start | bytes 2654216 | tf_op jit(solution)/shard_map/ppermute | solution.py:373
  403.6 40.8 %collective-permute-start.28 = (f32[24,72,128]{2,1,0:T(8,128)}, f32[24,72,128]{2,1,0:T(8,128)}, u32[]{:S(2)}, u32[]{:S(2)}) collective-permute-start(f32[24,72,128]{2,1,0:T(8,128)} %get-tuple-element.122), channel_id=1, source_target_pairs={{0,8},{2,10},{4,12},{8,0},{10,2},{12,4},{16,24},{18,26},{20,28},{2... | collective-permute-start | bytes 2654216 | tf_op jit(solution)/shard_map/ppermute | solution.py:369
  406.7 56.7 %collective-permute-start.39 = (f32[24,72,128]{2,1,0:T(8,128)}, f32[24,72,128]{2,1,0:T(8,128)}, u32[]{:S(2)}, u32[]{:S(2)}) collective-permute-start(f32[24,72,128]{2,1,0:T(8,128)} %get-tuple-element.132), channel_id=1, source_target_pairs={{2,10},{4,12},{6,14},{10,2},{12,4},{14,6},{18,26},{20,28},{22,30},... | collective-permute-start | bytes 2654216 | tf_op jit(solution)/shard_map/ppermute | solution.py:369
  425.3 40.2 %collective-permute-start.24 = (f32[24,72,128]{2,1,0:T(8,128)}, f32[24,72,128]{2,1,0:T(8,128)}, u32[]{:S(2)}, u32[]{:S(2)}) collective-permute-start(f32[24,72,128]{2,1,0:T(8,128)} %get-tuple-element.117), channel_id=1, source_target_pairs={{0,16},{2,18},{4,20},{6,22},{8,24},{10,26},{12,28},{14,30},{16,0},... | collective-permute-start | bytes 2654216 | tf_op jit(solution)/shard_map/ppermute | solution.py:369
  426.6 41.5 %collective-permute-start.41 = (f32[24,72,128]{2,1,0:T(8,128)}, f32[24,72,128]{2,1,0:T(8,128)}, u32[]{:S(2)}, u32[]{:S(2)}) collective-permute-start(f32[24,72,128]{2,1,0:T(8,128)} %add.168), channel_id=1, source_target_pairs={{2,18},{4,20},{6,22},{10,26},{12,28},{14,30},{18,2},{20,4},{22,6},... | collective-permute-start | bytes 2654216 | tf_op jit(solution)/shard_map/ppermute | solution.py:369
  430.9 38.5 %collective-permute-start.42 = (f32[24,72,128]{2,1,0:T(8,128)}, f32[24,72,128]{2,1,0:T(8,128)}, u32[]{:S(2)}, u32[]{:S(2)}) collective-permute-start(f32[24,72,128]{2,1,0:T(8,128)} %add_add_fusion.2), channel_id=1, source_target_pairs={{4,2},{6,4},{5,3},{7,5},{12,10},{14,12},{13,11},{15,13},{20,18},{2... | collective-permute-start | bytes 2654216 | tf_op jit(solution)/shard_map/ppermute | solution.py:373
  433.1 33.7 %copy-start.19 = (f32[24,72,128]{2,1,0:T(8,128)S(1)}, f32[24,72,128]{2,1,0:T(8,128)}, u32[]{:S(2)}) copy-start(f32[24,72,128]{2,1,0:T(8,128)} %copy-done.18) | copy-start | bytes 2654212
  434.5 84.1 %all-to-all-start.4 = ((f32[4,12,72,128]{3,2,1,0:T(8,128)}), f32[4,12,72,128]{3,2,1,0:T(8,128)}, u32[]{:S(2)}, u32[]{:S(2)}) async-start(f32[4,12,72,128]{3,2,1,0:T(8,128)} %add.151), calls=%async_computation.4 | async-start | bytes 3538944 | tf_op jit(solution)/shard_map/all_to_all | solution.py:459
  444.4 37.8 %collective-permute-start.27 = (f32[24,72,128]{2,1,0:T(8,128)}, f32[24,72,128]{2,1,0:T(8,128)S(1)}, u32[]{:S(2)}, u32[]{:S(2)}) collective-permute-start(f32[24,72,128]{2,1,0:T(8,128)} %copy-done.27), channel_id=1, source_target_pairs={{0,8},{2,10},{4,12},{8,0},{10,2},{12,4},{16,24},{18,26},{20,28},{2... | collective-permute-start | bytes 2654216 | tf_op jit(solution)/shard_map/ppermute | solution.py:369
  447.5 50.5 %copy-start.24 = (f32[24,72,128]{2,1,0:T(8,128)S(1)}, f32[24,72,128]{2,1,0:T(8,128)}, u32[]{:S(2)}) copy-start(f32[24,72,128]{2,1,0:T(8,128)} %copy-done.23) | copy-start | bytes 2654212
  463.3 21.1 %collective-permute-start.29 = (f32[24,72,128]{2,1,0:T(8,128)S(1)}, f32[24,72,128]{2,1,0:T(8,128)S(1)}, u32[]{:S(2)}, u32[]{:S(2)}) collective-permute-start(f32[24,72,128]{2,1,0:T(8,128)S(1)} %add.156), channel_id=1, source_target_pairs={{0,16},{2,18},{4,20},{8,24},{10,26},{12,28},{16,0},{18,2},{20,4},{... | collective-permute-start | bytes 2654216 | tf_op jit(solution)/shard_map/ppermute | solution.py:369
  465.5 32.5 %collective-permute-start.37 = (f32[24,72,128]{2,1,0:T(8,128)}, f32[24,72,128]{2,1,0:T(8,128)S(1)}, u32[]{:S(2)}, u32[]{:S(2)}) collective-permute-start(f32[24,72,128]{2,1,0:T(8,128)} %add_add_fusion.2), channel_id=1, source_target_pairs={{0,2},{2,4},{1,3},{3,5},{8,10},{10,12},{9,11},{11,13},{16,18},{18,... | collective-permute-start | bytes 2654216 | tf_op jit(solution)/shard_map/ppermute | solution.py:373
  468.1 49.4 %copy-start.22 = (f32[24,72,128]{2,1,0:T(8,128)S(1)}, f32[24,72,128]{2,1,0:T(8,128)}, u32[]{:S(2)}) copy-start(f32[24,72,128]{2,1,0:T(8,128)} %copy-done.21) | copy-start | bytes 2654212
  468.1 35.3 %collective-permute-start.26 = (f32[24,72,128]{2,1,0:T(8,128)}, f32[24,72,128]{2,1,0:T(8,128)S(1)}, u32[]{:S(2)}, u32[]{:S(2)}) collective-permute-start(f32[24,72,128]{2,1,0:T(8,128)} %copy-done.26), channel_id=1, source_target_pairs={{0,16},{2,18},{4,20},{6,22},{8,24},{10,26},{12,28},{14,30},{16,0},... | collective-permute-start | bytes 2654216 | tf_op jit(solution)/shard_map/ppermute | solution.py:369
  469.4 34.0 %collective-permute-start.25 = (f32[24,72,128]{2,1,0:T(8,128)S(1)}, f32[24,72,128]{2,1,0:T(8,128)S(1)}, u32[]{:S(2)}, u32[]{:S(2)}) collective-permute-start(f32[24,72,128]{2,1,0:T(8,128)S(1)} %add.152), channel_id=1, source_target_pairs={{0,8},{2,10},{4,12},{6,14},{8,0},{10,2},{12,4},{14,6},{16,24},{18,... | collective-permute-start | bytes 2654216 | tf_op jit(solution)/shard_map/ppermute | solution.py:369
  482.2 24.4 %collective-permute-start.43 = (f32[24,72,128]{2,1,0:T(8,128)S(1)}, f32[24,72,128]{2,1,0:T(8,128)S(1)}, u32[]{:S(2)}, u32[]{:S(2)}) collective-permute-start(f32[24,72,128]{2,1,0:T(8,128)S(1)} %add_add_fusion), channel_id=1, source_target_pairs={{2,0},{4,2},{6,4},{3,1},{5,3},{7,5},{10,8},{12,10},{14,12},{11,9},... | collective-permute-start | bytes 2654216 | tf_op jit(solution)/shard_map/ppermute | solution.py:373
  498.1 19.3 %collective-permute-start.38 = (f32[24,72,128]{2,1,0:T(8,128)S(1)}, f32[24,72,128]{2,1,0:T(8,128)S(1)}, u32[]{:S(2)}, u32[]{:S(2)}) collective-permute-start(f32[24,72,128]{2,1,0:T(8,128)S(1)} %add_add_fusion.3), channel_id=1, source_target_pairs={{0,2},{2,4},{4,6},{1,3},{3,5},{5,7},{8,10},{10,12},{12,14},{9,11},... | collective-permute-start | bytes 2654216 | tf_op jit(solution)/shard_map/ppermute | solution.py:373
  (18 other events, 96.9 us)

commit v4 on v3

--- a/solution.py
+++ b/solution.py
@@ -18,8 +18,7 @@
 F32 = jnp.float32
 BF16 = jnp.bfloat16
 MIDDLE = 12
-PIECES = 5
-COST_BYTES = 1 << 20
+PIECES = 4
 
 
 def hartley_table(count):
@@ -134,8 +133,8 @@
         return ref.at[pl.ds(pl.multiple_of(index * size, size), size)]
 
     def pieces(refs_):
-        spots = [(z, None), (z - 1, z >= 1), (z + 1, z < zs - 1), (z ^ 2, None), (3 - z, (z == 0) | (z == 3))]
-        return [(ref, spot, there) for ref, (spot, there) in zip(refs_, spots)]
+        near = jnp.where(z == 0, 1, z - 1)
+        return list(zip(refs_, [z, near, z ^ 2, 6 - z - near - (z ^ 2)]))
 
     def start(source, target, semaphore, there=None):
         def go():
@@ -151,8 +150,8 @@
 
     start(tables_hbm, tables, sem_c.at[1])
     if split_in:
-        for ref, spot, there in pieces(partner_hbm):
-            start(ref, part(partner, spot), sem.at[0, spot], there)
+        for ref, spot in pieces(partner_hbm):
+            start(ref, part(partner, spot), sem.at[0, spot])
     else:
         for s in range(zs):
             start(part(partner_hbm[0], s), part(partner, s), sem.at[0, s])
@@ -241,8 +240,8 @@
         else:
             start(part(sums, step), part(sums_out[0], step), sem.at[5, step])
         if split_out:
-            for ref, spot, there in pieces(terms_out):
-                start(part(terms, step), ref, sem.at[7, step], (spot == step) if there is None else (spot == step) & there)
+            for ref, spot in pieces(terms_out):
+                start(part(terms, step), ref, sem.at[7, step], spot == step)
         else:
             start(part(terms, step), part(terms_out[0], step), sem.at[7, step])
         return carry
@@ -267,7 +266,7 @@
     kinds = [jax.ShapeDtypeStruct(mine.shape, F32)] * 2 if last_partner else [field]
     pieces = [jax.ShapeDtypeStruct(p.shape, F32) for p in partner] if layout[4] else [field]
     more = [a for a in (sums, terms) if a is not None]
-    anywhere = pl.BlockSpec(memory_space=pltpu.HBM)
+    anywhere = pl.BlockSpec(memory_space=pl.ANY)
     block = (count, rows, LANES)
     out = pl.pallas_call(
         functools.partial(pair_kernel, count, (zs, planes), layout),
@@ -284,9 +283,9 @@
             pltpu.SemaphoreType.DMA((2,)),
         ],
         cost_estimate=pl.CostEstimate(
-            flops=12 * count**4, bytes_accessed=COST_BYTES, transcendentals=0
+            flops=12 * count**4, bytes_accessed=20 * count * rows * LANES, transcendentals=0
         ),
-        compiler_params=pltpu.CompilerParams(vmem_limit_bytes=48 * 1024 * 1024),
+        compiler_params=pltpu.CompilerParams(vmem_limit_bytes=60 * 1024 * 1024),
     )(place, *partner, mine, other, *more, *tables)
     sums = out[:2] if last_partner else out[0]
     terms = out[len(kinds) :] if layout[4] else out[-1]
@@ -363,61 +362,54 @@
     return lax.ppermute(value, axis, [(i, i ^ flip) for i in range(size)])
 
 
-def across(value, flip, chips):
-    zs = lax.axis_size("z")
-    pairs = [(b * zs + z, (b ^ flip) * zs + z) for b in range(lax.axis_size("band")) for z in chips]
-    return lax.ppermute(value, ("band", "z"), pairs)
-
-
 def along(value, pairs):
     return lax.ppermute(value, "z", pairs)
 
 
+def tie(values, done):
+    return lax.optimization_barrier((values, done))[0]
+
+
 RIGHT = [(0, 1), (1, 2), (2, 3)]
 LEFT = [(1, 0), (2, 1), (3, 2)]
-THERE = ((0, 1, 2, 3), (1, 2, 3), (0, 1, 2), (0, 1, 2, 3), (0, 3))
-EVEN = (True, False, False, True, False)
-
-
-def gather_line(slab):
+
+
+def spread(slab, first):
+    z = lax.axis_index("z")
+    side, far = [], []
+
+    def both(piece):
+        side.append(swap(piece, "band", 1))
+        far.append(swap(piece, "band", 2))
+
     before, after = along(slab, RIGHT), along(slab, LEFT)
+    both(slab)
+    before, after = tie((before, after), (side[-1], far[-1], first))
+    near = jnp.where(z == 0, after, before)
     two = along(before, RIGHT[1:]) + along(after, LEFT[:2])
-    three = along(two, [(2, 3), (1, 0)])
-    return [slab, before, after, two, three]
-
-
-def scatter_line(terms):
-    slab, before, after, two, three = terms
-    two = two + along(three, [(0, 1), (3, 2)])
-    after = after + along(two, RIGHT[:2])
-    before = before + along(two, LEFT[1:])
-    return slab + along(after, RIGHT) + along(before, LEFT)
-
-
-def spread(own):
-    side, far, cross = [], [], []
-
-    def send(out, piece, flip, chips, earlier):
-        if len(earlier) > 1:
-            piece, earlier[-2] = lax.optimization_barrier((piece, earlier[-2]))
-        out.append(across(piece, flip, chips))
-
-    for piece, chips in zip(own, THERE):
-        send(side, piece, 1, chips, side)
-        send(far, piece, 2, chips, far)
-    cross = [
-        across(s, 2, chips) if even else across(f, 1, chips) for s, f, chips, even in zip(side, far, THERE, EVEN)
-    ]
-    return [own, side, far, cross]
-
-
-def collect(own, side, far, cross):
-    out = [None] * PIECES
-    for k in (4, 3, 2, 1, 0):
-        handed = across(cross[k], 2 if EVEN[k] else 1, THERE[k])
-        s, f = (side[k] + handed, far[k]) if EVEN[k] else (side[k], far[k] + handed)
-        out[k] = own[k] + across(s, 1, THERE[k]) + across(f, 2, THERE[k])
-    return out
+    both(near)
+    two = tie(two, (side[-1], far[-1]))
+    both(two)
+    rest = jnp.where((z == 0) | (z == 3), along(two, [(2, 3), (1, 0)]), after)
+    rest = tie(rest, (side[-1], far[-1]))
+    both(rest)
+    cross = [swap(tie(piece, rest), "band", flip) for piece, flip in zip((side[0], far[1], side[2], far[3]), (2, 1, 2, 1))]
+    return [[slab, near, two, rest], side, far, cross]
+
+
+def hand_over(cross):
+    first = [swap(cross[2], "band", 2), swap(cross[3], "band", 1)]
+    later = [swap(tie(cross[0], first), "band", 2), swap(tie(cross[1], first), "band", 1)]
+    return [later[0], later[1], first[0], first[1]]
+
+
+def scatter_line(slab, near, two, rest, near_in, slab_in):
+    z = lax.axis_index("z")
+    two = tie(two + along(rest, [(0, 1), (3, 2)]), near_in)
+    near = near + near_in[0] + near_in[1]
+    after, before = along(two, RIGHT[:2]), along(two, LEFT[1:])
+    after, before = tie((jnp.where(z == 0, near, rest + after), near + before), slab_in)
+    return slab + slab_in[0] + slab_in[1] + along(after, RIGHT) + along(before, LEFT)
 
 
 def local(orbitals):
@@ -428,43 +420,77 @@
     tables = make_tables(count)
     sets = pack(orbitals.swapaxes(0, 1), n_local // zs)
     tail = sets[0].shape[2:]
-    slab = lax.all_to_all(sets[0][:PAIR], "core", split_axis=0, concat_axis=1, tiled=True)[0]
-    square = bands == ROUNDS == 4 and zs == 4
+    keep = lax.dynamic_index_in_dim(sets[0], core, 0, keepdims=False)
+    come = swap(lax.dynamic_index_in_dim(sets[0], 1 - core, 0, keepdims=False), "core", 1)
+    slab = jnp.concatenate([jnp.where(core == 0, keep, come), jnp.where(core == 0, come, keep)], axis=0)
+    square = bands == ROUNDS == 4 and zs == 4 and len(sets) == 2
     if square:
-        own = gather_line(slab)
-        partners = spread(own)
-        partners[:3] = lax.optimization_barrier(partners[:3])
-        orders = [(0, 1, 2, 3), (3, 1, 2, 0)]
-        ready = own[3]
-    else:
-        every = lax.all_gather(slab, ("band", "z"), axis=0, tiled=True).reshape((bands, count) + tail)
-        partners = [[every[k]] for k in range(ROUNDS)]
-        orders = [range(ROUNDS)] * len(sets)
-        ready = slab
-    mine = []
-    for fields in sets:
-        fields, ready = lax.optimization_barrier((fields, ready))
-        ready = lax.all_to_all(fields, "z", split_axis=0, concat_axis=0, tiled=True)
-        mine.append(ready)
-    other = [swap(m, "core", 1) for m in mine]
+        return square_local(place, tables, sets, slab)
+    every = lax.all_gather(slab, ("band", "z"), axis=0, tiled=True).reshape((bands, count) + tail)
     terms = [None] * ROUNDS
-    spread_sums = []
-    for k, order in zip(range(len(sets)), orders):
+    sums_out = []
+    for k, fields in enumerate(sets):
+        mine = lax.all_to_all(fields, "z", split_axis=0, concat_axis=0, tiled=True)
+        other = swap(mine, "core", 1)
         sums = None
-        for turn in order:
+        for turn in range(ROUNDS):
             sums, terms[turn] = pair_solve(
-                place, partners[turn], mine[k], other[k], sums, terms[turn], tables, turn == order[-1], k == len(sets) - 1
+                place, [every[turn]], mine, other, sums, terms[turn], tables, turn == ROUNDS - 1, k == len(sets) - 1
             )
-        keep, give = sums
-        spread_sums.append(lax.all_to_all(keep + swap(give, "core", 1), "z", split_axis=0, concat_axis=0, tiled=True))
-    if square:
-        owner = scatter_line(collect(*terms))
-    else:
-        owner = jnp.concatenate([t[None] for t in terms] + [jnp.zeros((bands - ROUNDS, count) + tail, F32)], axis=0)
-        owner = owner.reshape((bands * count,) + tail)
-        owner = lax.psum_scatter(owner, ("band", "z"), scatter_dimension=0, tiled=True)
-    owner = lax.all_to_all(owner[None], "core", split_axis=1, concat_axis=0, tiled=True)
-    return unpack(spread_sums, owner).swapaxes(0, 1)
+        sums_out.append(sums)
+    owner = jnp.concatenate([t[None] for t in terms] + [jnp.zeros((bands - ROUNDS, count) + tail, F32)], axis=0)
+    owner = owner.reshape((bands * count,) + tail)
+    owner = lax.psum_scatter(owner, ("band", "z"), scatter_dimension=0, tiled=True)
+    return finish([send_back(core_sum(*sums)) for sums in sums_out], owner)
+
+
+def core_sum(keep, give):
+    return keep + swap(give, "core", 1)
+
+
+def send_back(total):
+    return lax.all_to_all(total, "z", split_axis=0, concat_axis=0, tiled=True)
+
+
+def finish(sums, owner):
+    core, planes = lax.axis_index("core"), owner.shape[0] // 2
+    keep = lax.dynamic_slice_in_dim(owner, core * planes, planes)
+    come = swap(lax.dynamic_slice_in_dim(owner, (1 - core) * planes, planes), "core", 1)
+    owner = jnp.stack([jnp.where(core == 0, keep, come), jnp.where(core == 0, come, keep)])
+    return unpack(sums, owner).swapaxes(0, 1)
+
+
+def square_local(place, tables, sets, slab):
+    first = lax.all_to_all(sets[0], "z", split_axis=0, concat_axis=0, tiled=True)
+    partners = spread(slab, first)
+    mine, other = [first], [swap(first, "core", 1)]
+
+    def pair(k, turn, sums, term=None, after=None, last=False):
+        partner = partners[turn] if after is None else tie(partners[turn], after)
+        return pair_solve(place, partner, mine[k], other[k], sums, term, tables, last, k == 1)
+
+    terms = [None] * ROUNDS
+    sums, terms[0] = pair(0, 0, None, after=partners[1][:3] + partners[2][:3])
+    mine.append(lax.all_to_all(tie(sets[1], terms[0]), "z", split_axis=0, concat_axis=0, tiled=True))
+    other.append(swap(mine[1], "core", 1))
+    sums, terms[1] = pair(0, 1, sums)
+    sums, terms[2] = pair(0, 2, sums)
+    sums, terms[3] = pair(0, 3, sums, last=True)
+    back = [send_back(core_sum(*sums))]
+    sums, cross = pair(1, 3, None, terms[3])
+    handed = hand_over(cross)
+    sums, side = pair(1, 1, sums, terms[1])
+    sums, far = pair(1, 2, sums, terms[2], after=handed[2:])
+    side = [side[0] + handed[0], side[1], side[2] + handed[2], side[3]]
+    far = [far[0], far[1] + handed[1], far[2], far[3] + handed[3]]
+    sent = swap(side[3], "band", 1)
+    sums, own = pair(1, 0, sums, terms[0], after=[sent] + handed[:2], last=True)
+    total = core_sum(*sums)
+    back.append(send_back(total))
+    arrived = [(swap(side[k], "band", 1), swap(far[k], "band", 2)) for k in range(PIECES - 1)]
+    rest = own[3] + sent + swap(far[3], "band", 2)
+    two = tie(own[2] + arrived[2][0] + arrived[2][1], total)
+    return finish(back, scatter_line(own[0], own[1], two, rest, arrived[1], arrived[0]))
 
 
 def solution(mesh):

time: 544 us -> 505 us (0.928)
  starting transfers between devices: 128 us -> 79.1 us
  blocking collectives: 14.5 us -> 0 us
  Pallas kernels: 165 us -> 178 us
  other arithmetic: 21.8 us -> 31.5 us
  waiting for transfers between devices: 193 us -> 199 us
    ppermute x30 -> x0, waiting for transfers between devices: 76.3 us -> none  [across(): return lax.ppermute(value, ('band', 'z'), pairs)]
    ppermute x4 -> x30, waiting for transfers between devices: 0.01 us -> 54.9 us  [swap(): return lax.ppermute(value, axis, [(i, i ^ flip) for i in range(size)])]
    ppermute x30 -> x0, starting transfers between devices: 54.1 us -> none  [across(): return lax.ppermute(value, ('band', 'z'), pairs)]
    ppermute x10, waiting for transfers between devices: 85.7 us -> 109 us  [along(): return lax.ppermute(value, 'z', pairs)]
    ppermute x4 -> x30, starting transfers between devices: 8.08 us -> 31.6 us  [swap(): return lax.ppermute(value, axis, [(i, i ^ flip) for i in range(size)])]
    all_to_all x4, starting transfers between devices: 44.8 us -> 23.7 us  [the longest x2 13.7 us: send_back(): return lax.all_to_all(total, 'z', split_axis=0, concat_axis=0, tiled=True)]
    all_to_all x2 -> x0, blocking collectives: 14.5 us -> none  [the longest x1 9.79 us: local(): lax.all_to_all(owner[None], 'core', split_axis=1, concat_axis=0, tiled=True)]
    pallas_call x8, Pallas kernels: 155 us -> 167 us  [pair_solve(): pl.pallas_call(functools.partial(pair_kernel, count, (zs, planes), layout...]
  transfers between devices with their start and end apart: 48 -> 44, of which waited for: 16 -> 21; matrix products, arithmetic and copies ran while one was open for 4% -> 7% of each run, Pallas kernels for 29% -> 25%
where the time goes in v4:
time: 505 us; the launch traced here: 498 us
  waiting for transfers between devices  199 us (39%)
  Pallas kernels  178 us (35%)
  starting transfers between devices  79.1 us (16%)
  other arithmetic  31.5 us (6%)
  local copies, waits for them, and re-layouts  9.45 us (2%)
    pallas_call x8, Pallas kernels, pair_solve(): pl.pallas_call(functools.partial(pair_kernel, count, (zs, planes), layout...  167 us
    ppermute x10, waiting for transfers between devices, along(): return lax.ppermute(value, 'z', pairs)  109 us
    ppermute x30, waiting for transfers between devices, swap(): return lax.ppermute(value, axis, [(i, i ^ flip) for i in range(size)])  54.9 us
    all_to_all x1, waiting for transfers between devices, square_local(): lax.all_to_all(tie(sets[1], terms[0]), 'z', split_axis=0, concat_axis=0,...  35 us
    ppermute x30, starting transfers between devices, swap(): return lax.ppermute(value, axis, [(i, i ^ flip) for i in range(size)])  31.6 us
    ppermute x10, starting transfers between devices, along(): return lax.ppermute(value, 'z', pairs)  23.8 us
    all_to_all x2, starting transfers between devices, send_back(): return lax.all_to_all(total, 'z', split_axis=0, concat_axis=0, tiled=True)  13.7 us
  transfers between devices with their start and end apart: 44, of which 21 were waited for; matrix products, arithmetic and copies ran while one was open for 7% of the time, Pallas kernels for 25%

profile of v4, /device:TPU:17, one launch (start us, length us, event | category | flops | bytes accessed | tf_op | source)
XLA Modules:
  0.0 498.0 jit_solution(3060950699850580714)
XLA Ops:
  0.0 2.0 copy-done
  2.0 4.2 shard_map.28
  6.2 4.6 all-to-all-start
  11.9 1.3 collective-permute-start
  13.2 1.4 collective-permute-done
  17.1 3.1 collective-permute-start.2
  20.2 2.2 collective-permute-start.3
  22.4 1.3 collective-permute-start.4
  23.7 13.2 %collective-permute-done.1.refs_1_ = f32[24,72,128]{2,1,0:T(8,128)} collective-permute-done((f32[24,72,128]{2,1,0:T(8,128)S(1)}, f32[24,72,128]{2,1,0:T(8,128)}, u32[]{:S(2)}, u32[]{:S(2)}) %collective-permute-start.1) | collective-permute-done | bytes 884768 | tf_op jit(solution)/shard_map/ppermute | solution.py:362
  36.9 31.3 %collective-permute-done.2 = f32[24,72,128]{2,1,0:T(8,128)} collective-permute-done((f32[24,72,128]{2,1,0:T(8,128)S(1)}, f32[24,72,128]{2,1,0:T(8,128)}, u32[]{:S(2)}, u32[]{:S(2)}) %collective-permute-start.2) | collective-permute-done | bytes 884768 | tf_op jit(solution)/shard_map/ppermute | solution.py:366
  68.2 1.9 collective-permute-start.5
  70.1 3.5 collective-permute-start.6
  77.5 3.1 collective-permute-start.17
  80.5 9.1 %collective-permute-done.5 = f32[24,72,128]{2,1,0:T(8,128)S(1)} collective-permute-done((f32[24,72,128]{2,1,0:T(8,128)}, f32[24,72,128]{2,1,0:T(8,128)S(1)}, u32[]{:S(2)}, u32[]{:S(2)}) %collective-permute-start.5) | collective-permute-done | bytes 884768 | tf_op jit(solution)/shard_map/ppermute | solution.py:366
  91.6 2.0 collective-permute-done.7.refs_2_
  95.5 2.2 collective-permute-start.9
  99.3 4.8 fusion.refs_8_.refs_9_.refs_10_
  104.7 8.0 %collective-permute-done.9 = f32[24,72,128]{2,1,0:T(8,128)} collective-permute-done((f32[24,72,128]{2,1,0:T(8,128)}, f32[24,72,128]{2,1,0:T(8,128)}, u32[]{:S(2)}, u32[]{:S(2)}) %collective-permute-start.9) | collective-permute-done | bytes 884768 | tf_op jit(solution)/shard_map/ppermute | solution.py:366
  112.7 2.2 broadcast_select_fusion.1.refs_4_
  116.9 19.6 %shard_map.29 = (f32[96,72,128]{2,1,0:T(8,128)}, f32[96,72,128]{2,1,0:T(8,128)}) custom-call(s32[2]{0:T(128)} %pad_add_fusion.refs_0_, f32[24,72,128]{2,1,0:T(8,128)} %copy-done.6, f32[24,72,128]{2,1,0:T(8,128)} %copy-done.7, f32[24,72,128]{2,1,0:T(8,128)} %add.152.refs_3_, f32[24,72,128]{2,1,0:T(8,128)} %broadcast_select_fusion.1.refs_4_, ...), custom_call_target="tpu_custom_call" | custom-call | flops 1019215872 | bytes 17694720 | tf_op jit(solution)/shard_map/pallas_call | solution.py:271
  136.5 5.4 %all-to-all-start.2 = ((f32[4,12,72,128]{3,2,1,0:T(8,128)}), f32[4,12,72,128]{3,2,1,0:T(8,128)S(1)}, u32[]{:S(2)}, u32[]{:S(2)}) async-start(f32[4,12,72,128]{3,2,1,0:T(8,128)} %bitcast.7), calls=%async_computation.2 | async-start | bytes 3538944 | tf_op jit(solution)/shard_map/all_to_all | solution.py:474
  141.9 1.3 collective-permute-start.15
  143.2 1.3 collective-permute-start.18
  144.6 35.0 %all-to-all-done.2.refs_5_ = f32[4,12,72,128]{3,2,1,0:T(8,128)S(1)} async-done(((f32[4,12,72,128]{3,2,1,0:T(8,128)}), f32[4,12,72,128]{3,2,1,0:T(8,128)S(1)}, u32[]{:S(2)}, u32[]{:S(2)}) %all-to-all-start.2) | async-done | bytes 1769504 | tf_op jit(solution)/shard_map/all_to_all | solution.py:474
  179.6 1.5 collective-permute-start.20
  182.3 1.3 collective-permute-start.13
  184.0 20.5 %shard_map.30 = (f32[96,72,128]{2,1,0:T(8,128)}, f32[96,72,128]{2,1,0:T(8,128)}) custom-call(s32[2]{0:T(128)} %pad_add_fusion.refs_0_, f32[24,72,128]{2,1,0:T(8,128)} %collective-permute-done.1.refs_1_, f32[24,72,128]{2,1,0:T(8,128)} %copy-done.12, f32[24,72,128]{2,1,0:T(8,128)} %collective-permute-done.10.refs_3_, ...), custom_call_target="tpu_custom_call" | custom-call | flops 1019215872 | bytes 17694720 | tf_op jit(solution)/shard_map/pallas_call | solution.py:271
  204.5 20.5 %shard_map.31 = (f32[96,72,128]{2,1,0:T(8,128)}, f32[96,72,128]{2,1,0:T(8,128)}) custom-call(s32[2]{0:T(128)} %pad_add_fusion.refs_0_, f32[24,72,128]{2,1,0:T(8,128)} %copy-done.10, f32[24,72,128]{2,1,0:T(8,128)} %copy-done.11, f32[24,72,128]{2,1,0:T(8,128)} %collective-permute-done.11.refs_3_, f32[24,72,128]{2,1,0:T(8,128)} %collective-permute-done.15.refs_4_, ...), custom_call_target="tpu_custom_call" | custom-call | flops 1019215872 | bytes 17694720 | tf_op jit(solution)/shard_map/pallas_call | solution.py:271
  225.0 20.5 %shard_map.32 = (f32[4,12,72,128]{3,2,1,0:T(8,128)}, f32[4,12,72,128]{3,2,1,0:T(8,128)}, f32[96,72,128]{2,1,0:T(8,128)}) custom-call(s32[2]{0:T(128)} %pad_add_fusion.refs_0_, f32[24,72,128]{2,1,0:T(8,128)} %collective-permute-done.12.refs_1_, f32[24,72,128]{2,1,0:T(8,128)} %collective-permute-done.13.refs_2_, ...), custom_call_target="tpu_custom_call" | custom-call | flops 1019215872 | bytes 17694720 | tf_op jit(solution)/shard_map/pallas_call | solution.py:271
  246.8 20.6 %shard_map.33 = (f32[96,72,128]{2,1,0:T(8,128)}, f32[24,72,128]{2,1,0:T(8,128)}, f32[24,72,128]{2,1,0:T(8,128)}, f32[24,72,128]{2,1,0:T(8,128)}, f32[24,72,128]{2,1,0:T(8,128)}) custom-call(s32[2]{0:T(128)} %pad_add_fusion.refs_0_, f32[24,72,128]{2,1,0:T(8,128)} %collective-permute-done.12.refs_1_, f32[24,72,128]{2,1,0:T(8,128)} %collective-permute-done.13.refs_2_, ...), custom_call_target="tpu_custom_call" | custom-call | flops 1019215872 | bytes 17694720 | tf_op jit(solution)/shard_map/pallas_call | solution.py:271
  267.4 1.3 collective-permute-start.22
  268.7 1.3 collective-permute-start.23
  270.0 1.7 collective-permute-start.19
  271.7 21.8 %shard_map.34 = (f32[96,72,128]{2,1,0:T(8,128)}, f32[24,72,128]{2,1,0:T(8,128)}, f32[24,72,128]{2,1,0:T(8,128)}, f32[24,72,128]{2,1,0:T(8,128)}, f32[24,72,128]{2,1,0:T(8,128)}) custom-call(s32[2]{0:T(128)} %pad_add_fusion.refs_0_, f32[24,72,128]{2,1,0:T(8,128)} %collective-permute-done.1.refs_1_, f32[24,72,128]{2,1,0:T(8,128)} %copy-done.12, ...), custom_call_target="tpu_custom_call" | custom-call | flops 1019215872 | bytes 17694720 | tf_op jit(solution)/shard_map/pallas_call | solution.py:271
  294.0 1.3 collective-permute-start.25
  295.3 21.8 %shard_map.35 = (f32[96,72,128]{2,1,0:T(8,128)}, f32[24,72,128]{2,1,0:T(8,128)}, f32[24,72,128]{2,1,0:T(8,128)}, f32[24,72,128]{2,1,0:T(8,128)}, f32[24,72,128]{2,1,0:T(8,128)}) custom-call(s32[2]{0:T(128)} %pad_add_fusion.refs_0_, f32[24,72,128]{2,1,0:T(8,128)} %copy-done.10, f32[24,72,128]{2,1,0:T(8,128)} %copy-done.11, ...), custom_call_target="tpu_custom_call" | custom-call | flops 1019215872 | bytes 17694720 | tf_op jit(solution)/shard_map/pallas_call | solution.py:271
  317.2 2.5 add.166
  320.9 1.4 add.157
  322.2 6.8 %all-to-all-start.1 = ((f32[4,12,72,128]{3,2,1,0:T(8,128)}), f32[4,12,72,128]{3,2,1,0:T(8,128)S(1)}, u32[]{:S(2)}, u32[]{:S(2)}) async-start(f32[4,12,72,128]{3,2,1,0:T(8,128)} %add.157), calls=%async_computation.1 | async-start | bytes 3538944 | tf_op jit(solution)/shard_map/all_to_all | solution.py:452
  329.1 5.0 %collective-permute-done.25 = f32[24,72,128]{2,1,0:T(8,128)} collective-permute-done((f32[24,72,128]{2,1,0:T(8,128)}, f32[24,72,128]{2,1,0:T(8,128)}, u32[]{:S(2)}, u32[]{:S(2)}) %collective-permute-start.25) | collective-permute-done | bytes 884768 | tf_op jit(solution)/shard_map/ppermute | solution.py:362
  334.1 21.9 %shard_map.36 = (f32[4,12,72,128]{3,2,1,0:T(8,128)}, f32[4,12,72,128]{3,2,1,0:T(8,128)}, f32[24,72,128]{2,1,0:T(8,128)}, f32[24,72,128]{2,1,0:T(8,128)}, f32[24,72,128]{2,1,0:T(8,128)}, /*index=5*/f32[24,72,128]{2,1,0:T(8,128)}) custom-call(s32[2]{0:T(128)} %pad_add_fusion.refs_0_, f32[24,72,128]{2,1,0:T(8,128)} %copy-done.6, f32[24,72,128]{2,1,0:T(8,128)} %copy-done.7, ...), custom_call_target="tpu_custom_call" | custom-call | flops 1019215872 | bytes 17694720 | tf_op jit(solution)/shard_map/pallas_call | solution.py:271
  357.5 1.3 collective-permute-start.29
  358.8 2.0 add_add_fusion.2
  360.8 1.3 collective-permute-start.34
  363.4 15.0 %collective-permute-done.33 = f32[24,72,128]{2,1,0:T(8,128)S(1)} collective-permute-done((f32[24,72,128]{2,1,0:T(8,128)}, f32[24,72,128]{2,1,0:T(8,128)S(1)}, u32[]{:S(2)}, u32[]{:S(2)}) %collective-permute-start.33) | collective-permute-done | bytes 884768 | tf_op jit(solution)/shard_map/ppermute | solution.py:362
  378.7 1.4 add.158
  380.1 2.8 collective-permute-done.34
  383.9 13.2 %collective-permute-done.29 = f32[24,72,128]{2,1,0:T(8,128)S(1)} collective-permute-done((f32[24,72,128]{2,1,0:T(8,128)}, f32[24,72,128]{2,1,0:T(8,128)S(1)}, u32[]{:S(2)}, u32[]{:S(2)}) %collective-permute-start.29) | collective-permute-done | bytes 884768 | tf_op jit(solution)/shard_map/ppermute | solution.py:362
  397.2 1.5 collective-permute-done.30
  398.7 2.1 collective-permute-start.36
  400.8 1.3 collective-permute-start.35
  402.4 2.2 add.159
  404.7 6.9 %all-to-all-start.3 = ((f32[4,12,72,128]{3,2,1,0:T(8,128)}), f32[4,12,72,128]{3,2,1,0:T(8,128)S(1)}, u32[]{:S(2)}, u32[]{:S(2)}) async-start(f32[4,12,72,128]{3,2,1,0:T(8,128)} %add.158), calls=%async_computation.3 | async-start | bytes 3538944 | tf_op jit(solution)/shard_map/all_to_all | solution.py:452
  411.6 8.6 %collective-permute-done.36 = f32[24,72,128]{2,1,0:T(8,128)} collective-permute-done((f32[24,72,128]{2,1,0:T(8,128)}, f32[24,72,128]{2,1,0:T(8,128)}, u32[]{:S(2)}, u32[]{:S(2)}) %collective-permute-start.36) | collective-permute-done | bytes 884768 | tf_op jit(solution)/shard_map/ppermute | solution.py:366
  420.3 1.8 collective-permute-done.35
  422.1 4.0 fusion.9
  426.1 3.2 collective-permute-start.38
  429.3 3.0 collective-permute-start.37
  432.3 42.9 %collective-permute-done.38 = f32[24,72,128]{2,1,0:T(8,128)} collective-permute-done((f32[24,72,128]{2,1,0:T(8,128)}, f32[24,72,128]{2,1,0:T(8,128)}, u32[]{:S(2)}, u32[]{:S(2)}) %collective-permute-start.38) | collective-permute-done | bytes 884768 | tf_op jit(solution)/shard_map/ppermute | solution.py:366
  475.2 3.8 collective-permute-done.37
  479.0 2.4 add_add_fusion
  483.2 2.9 collective-permute-start.39
  486.1 1.8 collective-permute-done.39
  491.3 6.3 %shard_map.37 = f32[12,8,9216]{2,1,0:T(8,128)} custom-call(f32[3456,128]{1,0:T(8,128)S(1)} %bitcast.18, f32[3456,128]{1,0:T(8,128)S(1)} %bitcast.19, f32[1728,128]{1,0:T(8,128)S(1)} %bitcast.21), custom_call_target="tpu_custom_call" | custom-call | tf_op jit(solution)/shard_map/pallas_call | solution.py:350
  (109 shorter events, 29.7 us)
Async XLA Ops:
  0.0 2.0 copy-start
  6.2 62.0 %all-to-all-start = ((f32[4,12,72,128]{3,2,1,0:T(8,128)}), f32[4,12,72,128]{3,2,1,0:T(8,128)S(1)}, u32[]{:S(2)}, u32[]{:S(2)}) async-start(f32[4,12,72,128]{3,2,1,0:T(8,128)} %bitcast.3), calls=%async_computation | async-start | bytes 3538944 | tf_op jit(solution)/shard_map/all_to_all | solution.py:464
  11.9 2.7 collective-permute-start
  15.8 61.6 %copy-start.6 = (f32[24,72,128]{2,1,0:T(8,128)}, f32[24,72,128]{2,1,0:T(8,128)S(1)}, u32[]{:S(2)}) copy-start(f32[24,72,128]{2,1,0:T(8,128)S(1)} %pad_maximum_fusion.refs_1_) | copy-start | bytes 2654212
  15.8 21.0 %collective-permute-start.1 = (f32[24,72,128]{2,1,0:T(8,128)S(1)}, f32[24,72,128]{2,1,0:T(8,128)}, u32[]{:S(2)}, u32[]{:S(2)}) collective-permute-start(f32[24,72,128]{2,1,0:T(8,128)S(1)} %pad_maximum_fusion.refs_1_), channel_id=1, source_target_pairs={{0,8},{8,0},{16,24},{24,16},{1,9},{9,1},{17,25},{25,17},{2,10},{10... | collective-permute-start | bytes 2654216 | tf_op jit(solution)/shard_map/ppermute | solution.py:362
  17.1 51.1 %collective-permute-start.2 = (f32[24,72,128]{2,1,0:T(8,128)S(1)}, f32[24,72,128]{2,1,0:T(8,128)}, u32[]{:S(2)}, u32[]{:S(2)}) collective-permute-start(f32[24,72,128]{2,1,0:T(8,128)S(1)} %pad_maximum_fusion.refs_1_), channel_id=1, source_target_pairs={{0,2},{2,4},{4,6},{1,3},{3,5},{5,7},{8,10},{10,12},{12,14},{9,11},... | collective-permute-start | bytes 2654216 | tf_op jit(solution)/shard_map/ppermute | solution.py:366
  20.2 48.0 %collective-permute-start.3 = (f32[24,72,128]{2,1,0:T(8,128)S(1)}, f32[24,72,128]{2,1,0:T(8,128)}, u32[]{:S(2)}, u32[]{:S(2)}) collective-permute-start(f32[24,72,128]{2,1,0:T(8,128)S(1)} %pad_maximum_fusion.refs_1_), channel_id=1, source_target_pairs={{2,0},{4,2},{6,4},{3,1},{5,3},{7,5},{10,8},{12,10},{14,12},{11,9},... | collective-permute-start | bytes 2654216 | tf_op jit(solution)/shard_map/ppermute | solution.py:366
  22.4 45.8 %collective-permute-start.4 = (f32[24,72,128]{2,1,0:T(8,128)S(1)}, f32[24,72,128]{2,1,0:T(8,128)S(1)}, u32[]{:S(2)}, u32[]{:S(2)}) collective-permute-start(f32[24,72,128]{2,1,0:T(8,128)S(1)} %pad_maximum_fusion.refs_1_), channel_id=1, source_target_pairs={{0,16},{8,24},{16,0},{24,8},{1,17},{9,25},{17,1},{25,9},{2,18},{10... | collective-permute-start | bytes 2654216 | tf_op jit(solution)/shard_map/ppermute | solution.py:362
  68.2 9.3 %copy-start.10 = (f32[24,72,128]{2,1,0:T(8,128)}, f32[24,72,128]{2,1,0:T(8,128)S(1)}, u32[]{:S(2)}) copy-start(f32[24,72,128]{2,1,0:T(8,128)S(1)} %collective-permute-done.4.refs_1_) | copy-start | bytes 2654212
  68.2 36.0 %copy-start.2 = (f32[4,12,72,128]{3,2,1,0:T(8,128)}, f32[4,12,72,128]{3,2,1,0:T(8,128)S(1)}, u32[]{:S(2)}) copy-start(f32[4,12,72,128]{3,2,1,0:T(8,128)S(1)} %all-to-all-done.refs_5_) | copy-start | bytes 5308420
  68.2 21.4 %collective-permute-start.5 = (f32[24,72,128]{2,1,0:T(8,128)}, f32[24,72,128]{2,1,0:T(8,128)S(1)}, u32[]{:S(2)}, u32[]{:S(2)}) collective-permute-start(f32[24,72,128]{2,1,0:T(8,128)} %collective-permute-done.2), channel_id=1, source_target_pairs={{2,4},{4,6},{3,5},{5,7},{10,12},{12,14},{11,13},{13,15},{18,20},{2... | collective-permute-start | bytes 2654216 | tf_op jit(solution)/shard_map/ppermute | solution.py:366
  70.1 20.5 %collective-permute-start.6 = (f32[24,72,128]{2,1,0:T(8,128)}, f32[24,72,128]{2,1,0:T(8,128)S(1)}, u32[]{:S(2)}, u32[]{:S(2)}) collective-permute-start(f32[24,72,128]{2,1,0:T(8,128)} %collective-permute-done.3), channel_id=1, source_target_pairs={{2,0},{4,2},{3,1},{5,3},{10,8},{12,10},{11,9},{13,11},{18,16},{20,... | collective-permute-start | bytes 2654216 | tf_op jit(solution)/shard_map/ppermute | solution.py:366
  74.9 2.6 copy-start.7
  74.9 18.8 %collective-permute-start.7 = (f32[24,72,128]{2,1,0:T(8,128)S(1)}, f32[24,72,128]{2,1,0:T(8,128)S(1)}, u32[]{:S(2)}, u32[]{:S(2)}) collective-permute-start(f32[24,72,128]{2,1,0:T(8,128)S(1)} %broadcast_select_fusion.refs_2_), channel_id=1, source_target_pairs={{0,8},{8,0},{16,24},{24,16},{1,9},{9,1},{17,25},{25,17},{2,10},{10... | collective-permute-start | bytes 2654216 | tf_op jit(solution)/shard_map/ppermute | solution.py:362
  76.2 18.4 %collective-permute-start.8 = (f32[24,72,128]{2,1,0:T(8,128)S(1)}, f32[24,72,128]{2,1,0:T(8,128)S(1)}, u32[]{:S(2)}, u32[]{:S(2)}) collective-permute-start(f32[24,72,128]{2,1,0:T(8,128)S(1)} %broadcast_select_fusion.refs_2_), channel_id=1, source_target_pairs={{0,16},{8,24},{16,0},{24,8},{1,17},{9,25},{17,1},{25,9},{2,18},{10... | collective-permute-start | bytes 2654216 | tf_op jit(solution)/shard_map/ppermute | solution.py:362
  77.5 38.2 %collective-permute-start.17 = (f32[4,12,72,128]{3,2,1,0:T(8,128)S(1)}, f32[4,12,72,128]{3,2,1,0:T(8,128)S(1)}, u32[]{:S(2)}, u32[]{:S(2)}) collective-permute-start(f32[4,12,72,128]{3,2,1,0:T(8,128)S(1)} %all-to-all-done.refs_5_), channel_id=1, source_target_pairs={{0,1},{1,0},{2,3},{3,2},{4,5},{5,4},{6,7},{7,6},{8,9},{9,8},{10,11... | collective-permute-start | bytes 5308424 | tf_op jit(solution)/shard_map/ppermute | solution.py:362
  93.7 4.1 copy-start.12
  95.5 17.2 %collective-permute-start.9 = (f32[24,72,128]{2,1,0:T(8,128)}, f32[24,72,128]{2,1,0:T(8,128)}, u32[]{:S(2)}, u32[]{:S(2)}) collective-permute-start(f32[24,72,128]{2,1,0:T(8,128)} %add.152.refs_3_), channel_id=1, source_target_pairs={{4,6},{2,0},{5,7},{3,1},{12,14},{10,8},{13,15},{11,9},{20,22},{18,... | collective-permute-start | bytes 2654216 | tf_op jit(solution)/shard_map/ppermute | solution.py:366
  97.8 17.8 %collective-permute-start.10 = (f32[24,72,128]{2,1,0:T(8,128)}, f32[24,72,128]{2,1,0:T(8,128)}, u32[]{:S(2)}, u32[]{:S(2)}) collective-permute-start(f32[24,72,128]{2,1,0:T(8,128)} %add.152.refs_3_), channel_id=1, source_target_pairs={{0,8},{8,0},{16,24},{24,16},{1,9},{9,1},{17,25},{25,17},{2,10},{10... | collective-permute-start | bytes 2654216 | tf_op jit(solution)/shard_map/ppermute | solution.py:362
  98.1 17.6 %collective-permute-start.11 = (f32[24,72,128]{2,1,0:T(8,128)}, f32[24,72,128]{2,1,0:T(8,128)}, u32[]{:S(2)}, u32[]{:S(2)}) collective-permute-start(f32[24,72,128]{2,1,0:T(8,128)} %add.152.refs_3_), channel_id=1, source_target_pairs={{0,16},{8,24},{16,0},{24,8},{1,17},{9,25},{17,1},{25,9},{2,18},{10... | collective-permute-start | bytes 2654216 | tf_op jit(solution)/shard_map/ppermute | solution.py:362
  136.5 43.1 %all-to-all-start.2 = ((f32[4,12,72,128]{3,2,1,0:T(8,128)}), f32[4,12,72,128]{3,2,1,0:T(8,128)S(1)}, u32[]{:S(2)}, u32[]{:S(2)}) async-start(f32[4,12,72,128]{3,2,1,0:T(8,128)} %bitcast.7), calls=%async_computation.2 | async-start | bytes 3538944 | tf_op jit(solution)/shard_map/all_to_all | solution.py:474
  141.9 41.7 %collective-permute-start.15 = (f32[24,72,128]{2,1,0:T(8,128)}, f32[24,72,128]{2,1,0:T(8,128)}, u32[]{:S(2)}, u32[]{:S(2)}) collective-permute-start(f32[24,72,128]{2,1,0:T(8,128)} %broadcast_select_fusion.1.refs_4_), channel_id=1, source_target_pairs={{0,16},{8,24},{16,0},{24,8},{1,17},{9,25},{17,1},{25,9},{2,18},{10... | collective-permute-start | bytes 2654216 | tf_op jit(solution)/shard_map/ppermute | solution.py:362
  143.2 40.6 %collective-permute-start.18 = (f32[24,72,128]{2,1,0:T(8,128)}, f32[24,72,128]{2,1,0:T(8,128)}, u32[]{:S(2)}, u32[]{:S(2)}) collective-permute-start(f32[24,72,128]{2,1,0:T(8,128)} %broadcast_select_fusion.1.refs_4_), channel_id=1, source_target_pairs={{0,8},{8,0},{16,24},{24,16},{1,9},{9,1},{17,25},{25,17},{2,10},{10... | collective-permute-start | bytes 2654216 | tf_op jit(solution)/shard_map/ppermute | solution.py:362
  179.6 24.9 %copy-start.3 = (f32[4,12,72,128]{3,2,1,0:T(8,128)}, f32[4,12,72,128]{3,2,1,0:T(8,128)S(1)}, u32[]{:S(2)}) copy-start(f32[4,12,72,128]{3,2,1,0:T(8,128)S(1)} %all-to-all-done.2.refs_5_) | copy-start | bytes 5308420
  179.6 65.9 %collective-permute-start.20 = (f32[4,12,72,128]{3,2,1,0:T(8,128)S(1)}, f32[4,12,72,128]{3,2,1,0:T(8,128)S(1)}, u32[]{:S(2)}, u32[]{:S(2)}) collective-permute-start(f32[4,12,72,128]{3,2,1,0:T(8,128)S(1)} %all-to-all-done.2.refs_5_), channel_id=1, source_target_pairs={{0,1},{1,0},{2,3},{3,2},{4,5},{5,4},{6,7},{7,6},{8,9},{9,8},{10,11... | collective-permute-start | bytes 5308424 | tf_op jit(solution)/shard_map/ppermute | solution.py:362
  181.1 43.9 %collective-permute-start.12 = (f32[24,72,128]{2,1,0:T(8,128)}, f32[24,72,128]{2,1,0:T(8,128)}, u32[]{:S(2)}, u32[]{:S(2)}) collective-permute-start(f32[24,72,128]{2,1,0:T(8,128)} %collective-permute-done.1.refs_1_), channel_id=1, source_target_pairs={{0,16},{8,24},{16,0},{24,8},{1,17},{9,25},{17,1},{25,9},{2,18},{10... | collective-permute-start | bytes 2654216 | tf_op jit(solution)/shard_map/ppermute | solution.py:362
  182.3 42.6 %collective-permute-start.13 = (f32[24,72,128]{2,1,0:T(8,128)}, f32[24,72,128]{2,1,0:T(8,128)}, u32[]{:S(2)}, u32[]{:S(2)}) collective-permute-start(f32[24,72,128]{2,1,0:T(8,128)} %copy-done.11), channel_id=1, source_target_pairs={{0,8},{8,0},{16,24},{24,16},{1,9},{9,1},{17,25},{25,17},{2,10},{10... | collective-permute-start | bytes 2654216 | tf_op jit(solution)/shard_map/ppermute | solution.py:362
  183.6 41.3 %collective-permute-start.14 = (f32[24,72,128]{2,1,0:T(8,128)}, f32[24,72,128]{2,1,0:T(8,128)}, u32[]{:S(2)}, u32[]{:S(2)}) collective-permute-start(f32[24,72,128]{2,1,0:T(8,128)} %collective-permute-done.10.refs_3_), channel_id=1, source_target_pairs={{0,16},{8,24},{16,0},{24,8},{1,17},{9,25},{17,1},{25,9},{2,18},{10... | collective-permute-start | bytes 2654216 | tf_op jit(solution)/shard_map/ppermute | solution.py:362
  183.8 41.1 %collective-permute-start.16 = (f32[24,72,128]{2,1,0:T(8,128)}, f32[24,72,128]{2,1,0:T(8,128)}, u32[]{:S(2)}, u32[]{:S(2)}) collective-permute-start(f32[24,72,128]{2,1,0:T(8,128)} %collective-permute-done.15.refs_4_), channel_id=1, source_target_pairs={{0,8},{8,0},{16,24},{24,16},{1,9},{9,1},{17,25},{25,17},{2,10},{10... | collective-permute-start | bytes 2654216 | tf_op jit(solution)/shard_map/ppermute | solution.py:362
  245.5 1.3 copy-start.5
  267.4 26.3 %collective-permute-start.22 = (f32[24,72,128]{2,1,0:T(8,128)}, f32[24,72,128]{2,1,0:T(8,128)S(1)}, u32[]{:S(2)}, u32[]{:S(2)}) collective-permute-start(f32[24,72,128]{2,1,0:T(8,128)} %get-tuple-element.90), channel_id=1, source_target_pairs={{0,16},{8,24},{16,0},{24,8},{1,17},{9,25},{17,1},{25,9},{2,18},{10... | collective-permute-start | bytes 2654216 | tf_op jit(solution)/shard_map/ppermute | solution.py:362
  268.7 25.0 %collective-permute-start.23 = (f32[24,72,128]{2,1,0:T(8,128)}, f32[24,72,128]{2,1,0:T(8,128)S(1)}, u32[]{:S(2)}, u32[]{:S(2)}) collective-permute-start(f32[24,72,128]{2,1,0:T(8,128)} %get-tuple-element.91), channel_id=1, source_target_pairs={{0,8},{8,0},{16,24},{24,16},{1,9},{9,1},{17,25},{25,17},{2,10},{10... | collective-permute-start | bytes 2654216 | tf_op jit(solution)/shard_map/ppermute | solution.py:362
  270.0 50.8 %collective-permute-start.19 = (f32[4,12,72,128]{3,2,1,0:T(8,128)}, f32[4,12,72,128]{3,2,1,0:T(8,128)S(1)}, u32[]{:S(2)}, u32[]{:S(2)}) collective-permute-start(f32[4,12,72,128]{3,2,1,0:T(8,128)} %get-tuple-element.81), channel_id=1, source_target_pairs={{0,1},{1,0},{2,3},{3,2},{4,5},{5,4},{6,7},{7,6},{8,9},{9,8},{10,11... | collective-permute-start | bytes 5308424 | tf_op jit(solution)/shard_map/ppermute | solution.py:362
  293.5 35.6 %collective-permute-start.21 = (f32[24,72,128]{2,1,0:T(8,128)}, f32[24,72,128]{2,1,0:T(8,128)}, u32[]{:S(2)}, u32[]{:S(2)}) collective-permute-start(f32[24,72,128]{2,1,0:T(8,128)} %get-tuple-element.88), channel_id=1, source_target_pairs={{0,8},{8,0},{16,24},{24,16},{1,9},{9,1},{17,25},{25,17},{2,10},{10... | collective-permute-start | bytes 2654216 | tf_op jit(solution)/shard_map/ppermute | solution.py:362
  293.7 1.6 copy-start.19
  293.7 1.6 copy-start.23
  293.7 35.3 %collective-permute-start.24 = (f32[24,72,128]{2,1,0:T(8,128)}, f32[24,72,128]{2,1,0:T(8,128)}, u32[]{:S(2)}, u32[]{:S(2)}) collective-permute-start(f32[24,72,128]{2,1,0:T(8,128)} %get-tuple-element.92), channel_id=1, source_target_pairs={{0,16},{8,24},{16,0},{24,8},{1,17},{9,25},{17,1},{25,9},{2,18},{10... | collective-permute-start | bytes 2654216 | tf_op jit(solution)/shard_map/ppermute | solution.py:362
  294.0 40.1 %collective-permute-start.25 = (f32[24,72,128]{2,1,0:T(8,128)}, f32[24,72,128]{2,1,0:T(8,128)}, u32[]{:S(2)}, u32[]{:S(2)}) collective-permute-start(f32[24,72,128]{2,1,0:T(8,128)} %get-tuple-element.94), channel_id=1, source_target_pairs={{0,8},{8,0},{16,24},{24,16},{1,9},{9,1},{17,25},{25,17},{2,10},{10... | collective-permute-start | bytes 2654216 | tf_op jit(solution)/shard_map/ppermute | solution.py:362
  295.3 25.5 %copy-start.13 = (f32[4,12,72,128]{3,2,1,0:T(8,128)S(1)}, f32[4,12,72,128]{3,2,1,0:T(8,128)}, u32[]{:S(2)}) copy-start(f32[4,12,72,128]{3,2,1,0:T(8,128)} %get-tuple-element.80) | copy-start | bytes 5308420
  319.6 39.2 %collective-permute-start.31 = (f32[24,72,128]{2,1,0:T(8,128)}, f32[24,72,128]{2,1,0:T(8,128)}, u32[]{:S(2)}, u32[]{:S(2)}) collective-permute-start(f32[24,72,128]{2,1,0:T(8,128)} %add.166), channel_id=1, source_target_pairs={{0,16},{8,24},{16,0},{24,8},{1,17},{9,25},{17,1},{25,9},{2,18},{10... | collective-permute-start | bytes 2654216 | tf_op jit(solution)/shard_map/ppermute | solution.py:362
  322.2 82.5 %all-to-all-start.1 = ((f32[4,12,72,128]{3,2,1,0:T(8,128)}), f32[4,12,72,128]{3,2,1,0:T(8,128)S(1)}, u32[]{:S(2)}, u32[]{:S(2)}) async-start(f32[4,12,72,128]{3,2,1,0:T(8,128)} %add.157), calls=%async_computation.1 | async-start | bytes 3538944 | tf_op jit(solution)/shard_map/all_to_all | solution.py:452
  334.1 23.0 %copy-start.20 = (f32[24,72,128]{2,1,0:T(8,128)S(1)}, f32[24,72,128]{2,1,0:T(8,128)}, u32[]{:S(2)}) copy-start(f32[24,72,128]{2,1,0:T(8,128)} %copy-done.19) | copy-start | bytes 2654212
  334.1 23.0 %copy-start.21 = (f32[24,72,128]{2,1,0:T(8,128)S(1)}, f32[24,72,128]{2,1,0:T(8,128)}, u32[]{:S(2)}) copy-start(f32[24,72,128]{2,1,0:T(8,128)} %get-tuple-element.117) | copy-start | bytes 2654212
  356.0 6.0 %copy-start.22 = (f32[24,72,128]{2,1,0:T(8,128)S(1)}, f32[24,72,128]{2,1,0:T(8,128)}, u32[]{:S(2)}) copy-start(f32[24,72,128]{2,1,0:T(8,128)} %get-tuple-element.113) | copy-start | bytes 2654212
  356.0 22.5 %copy-start.15 = (f32[24,72,128]{2,1,0:T(8,128)S(1)}, f32[24,72,128]{2,1,0:T(8,128)}, u32[]{:S(2)}) copy-start(f32[24,72,128]{2,1,0:T(8,128)} %get-tuple-element.116) | copy-start | bytes 2654212
  356.1 22.7 %collective-permute-start.26 = (f32[4,12,72,128]{3,2,1,0:T(8,128)}, f32[4,12,72,128]{3,2,1,0:T(8,128)S(1)}, u32[]{:S(2)}, u32[]{:S(2)}) collective-permute-start(f32[4,12,72,128]{3,2,1,0:T(8,128)} %get-tuple-element.107), channel_id=1, source_target_pairs={{0,1},{1,0},{2,3},{3,2},{4,5},{5,4},{6,7},{7,6},{8,9},{9,8},{10,11... | collective-permute-start | bytes 5308424 | tf_op jit(solution)/shard_map/ppermute | solution.py:362
  356.9 21.4 %collective-permute-start.33 = (f32[24,72,128]{2,1,0:T(8,128)}, f32[24,72,128]{2,1,0:T(8,128)S(1)}, u32[]{:S(2)}, u32[]{:S(2)}) collective-permute-start(f32[24,72,128]{2,1,0:T(8,128)} %get-tuple-element.118), channel_id=1, source_target_pairs={{0,16},{8,24},{16,0},{24,8},{1,17},{9,25},{17,1},{25,9},{2,18},{10... | collective-permute-start | bytes 2654216 | tf_op jit(solution)/shard_map/ppermute | solution.py:362
  357.2 21.3 %collective-permute-start.32 = (f32[24,72,128]{2,1,0:T(8,128)S(1)}, f32[24,72,128]{2,1,0:T(8,128)S(1)}, u32[]{:S(2)}, u32[]{:S(2)}) collective-permute-start(f32[24,72,128]{2,1,0:T(8,128)S(1)} %add.168), channel_id=1, source_target_pairs={{0,8},{8,0},{16,24},{24,16},{1,9},{9,1},{17,25},{25,17},{2,10},{10... | collective-permute-start | bytes 2654216 | tf_op jit(solution)/shard_map/ppermute | solution.py:362
  357.5 39.7 %collective-permute-start.29 = (f32[24,72,128]{2,1,0:T(8,128)}, f32[24,72,128]{2,1,0:T(8,128)S(1)}, u32[]{:S(2)}, u32[]{:S(2)}) collective-permute-start(f32[24,72,128]{2,1,0:T(8,128)} %get-tuple-element.112), channel_id=1, source_target_pairs={{0,8},{8,0},{16,24},{24,16},{1,9},{9,1},{17,25},{25,17},{2,10},{10... | collective-permute-start | bytes 2654216 | tf_op jit(solution)/shard_map/ppermute | solution.py:362
  358.8 20.0 %copy-start.14 = (f32[4,12,72,128]{3,2,1,0:T(8,128)S(1)}, f32[4,12,72,128]{3,2,1,0:T(8,128)}, u32[]{:S(2)}) copy-start(f32[4,12,72,128]{3,2,1,0:T(8,128)} %get-tuple-element.106) | copy-start | bytes 5308420
  360.7 19.4 %copy-start.8 = (f32[24,72,128]{2,1,0:T(8,128)}, f32[24,72,128]{2,1,0:T(8,128)S(1)}, u32[]{:S(2)}) copy-start(f32[24,72,128]{2,1,0:T(8,128)S(1)} %add_add_fusion.2) | copy-start | bytes 2654212
  360.8 22.1 %collective-permute-start.34 = (f32[24,72,128]{2,1,0:T(8,128)S(1)}, f32[24,72,128]{2,1,0:T(8,128)S(1)}, u32[]{:S(2)}, u32[]{:S(2)}) collective-permute-start(f32[24,72,128]{2,1,0:T(8,128)S(1)} %add_add_fusion.2), channel_id=1, source_target_pairs={{0,2},{6,4},{1,3},{7,5},{8,10},{14,12},{9,11},{15,13},{16,18},{22,... | collective-permute-start | bytes 2654216 | tf_op jit(solution)/shard_map/ppermute | solution.py:366
  378.3 20.3 %collective-permute-start.30 = (f32[24,72,128]{2,1,0:T(8,128)S(1)}, f32[24,72,128]{2,1,0:T(8,128)S(1)}, u32[]{:S(2)}, u32[]{:S(2)}) collective-permute-start(f32[24,72,128]{2,1,0:T(8,128)S(1)} %add.163), channel_id=1, source_target_pairs={{0,16},{8,24},{16,0},{24,8},{1,17},{9,25},{17,1},{25,9},{2,18},{10... | collective-permute-start | bytes 2654216 | tf_op jit(solution)/shard_map/ppermute | solution.py:362
  378.7 23.7 %copy-start.18 = (f32[24,72,128]{2,1,0:T(8,128)S(1)}, f32[24,72,128]{2,1,0:T(8,128)}, u32[]{:S(2)}) copy-start(f32[24,72,128]{2,1,0:T(8,128)} %get-tuple-element.109) | copy-start | bytes 2654212
  397.2 7.4 %copy-start.16 = (f32[24,72,128]{2,1,0:T(8,128)}, f32[24,72,128]{2,1,0:T(8,128)S(1)}, u32[]{:S(2)}) copy-start(f32[24,72,128]{2,1,0:T(8,128)S(1)} %collective-permute-done.29) | copy-start | bytes 2654212
  398.7 5.9 %copy-start.17 = (f32[24,72,128]{2,1,0:T(8,128)}, f32[24,72,128]{2,1,0:T(8,128)S(1)}, u32[]{:S(2)}) copy-start(f32[24,72,128]{2,1,0:T(8,128)S(1)} %collective-permute-done.30) | copy-start | bytes 2654212
  398.7 21.6 %collective-permute-start.36 = (f32[24,72,128]{2,1,0:T(8,128)}, f32[24,72,128]{2,1,0:T(8,128)}, u32[]{:S(2)}, u32[]{:S(2)}) collective-permute-start(f32[24,72,128]{2,1,0:T(8,128)} %add.171), channel_id=1, source_target_pairs={{4,2},{6,4},{5,3},{7,5},{12,10},{14,12},{13,11},{15,13},{20,18},{2... | collective-permute-start | bytes 2654216 | tf_op jit(solution)/shard_map/ppermute | solution.py:366
  400.8 21.3 %collective-permute-start.35 = (f32[24,72,128]{2,1,0:T(8,128)}, f32[24,72,128]{2,1,0:T(8,128)}, u32[]{:S(2)}, u32[]{:S(2)}) collective-permute-start(f32[24,72,128]{2,1,0:T(8,128)} %add.171), channel_id=1, source_target_pairs={{0,2},{2,4},{1,3},{3,5},{8,10},{10,12},{9,11},{11,13},{16,18},{18,... | collective-permute-start | bytes 2654216 | tf_op jit(solution)/shard_map/ppermute | solution.py:366
  402.1 24.0 %collective-permute-start.28 = (f32[24,72,128]{2,1,0:T(8,128)}, f32[24,72,128]{2,1,0:T(8,128)}, u32[]{:S(2)}, u32[]{:S(2)}) collective-permute-start(f32[24,72,128]{2,1,0:T(8,128)} %get-tuple-element.110), channel_id=1, source_target_pairs={{0,16},{8,24},{16,0},{24,8},{1,17},{9,25},{17,1},{25,9},{2,18},{10... | collective-permute-start | bytes 2654216 | tf_op jit(solution)/shard_map/ppermute | solution.py:362
  404.6 21.5 %collective-permute-start.27 = (f32[24,72,128]{2,1,0:T(8,128)}, f32[24,72,128]{2,1,0:T(8,128)}, u32[]{:S(2)}, u32[]{:S(2)}) collective-permute-start(f32[24,72,128]{2,1,0:T(8,128)} %add.159), channel_id=1, source_target_pairs={{0,8},{8,0},{16,24},{24,16},{1,9},{9,1},{17,25},{25,17},{2,10},{10... | collective-permute-start | bytes 2654216 | tf_op jit(solution)/shard_map/ppermute | solution.py:362
  404.7 85.4 %all-to-all-start.3 = ((f32[4,12,72,128]{3,2,1,0:T(8,128)}), f32[4,12,72,128]{3,2,1,0:T(8,128)S(1)}, u32[]{:S(2)}, u32[]{:S(2)}) async-start(f32[4,12,72,128]{3,2,1,0:T(8,128)} %add.158), calls=%async_computation.3 | async-start | bytes 3538944 | tf_op jit(solution)/shard_map/all_to_all | solution.py:452
  426.1 49.1 %collective-permute-start.38 = (f32[24,72,128]{2,1,0:T(8,128)}, f32[24,72,128]{2,1,0:T(8,128)}, u32[]{:S(2)}, u32[]{:S(2)}) collective-permute-start(f32[24,72,128]{2,1,0:T(8,128)} %get-tuple-element.122), channel_id=1, source_target_pairs={{2,0},{4,2},{6,4},{3,1},{5,3},{7,5},{10,8},{12,10},{14,12},{11,9},... | collective-permute-start | bytes 2654216 | tf_op jit(solution)/shard_map/ppermute | solution.py:366
  429.3 49.8 %collective-permute-start.37 = (f32[24,72,128]{2,1,0:T(8,128)}, f32[24,72,128]{2,1,0:T(8,128)}, u32[]{:S(2)}, u32[]{:S(2)}) collective-permute-start(f32[24,72,128]{2,1,0:T(8,128)} %get-tuple-element.121), channel_id=1, source_target_pairs={{0,2},{2,4},{4,6},{1,3},{3,5},{5,7},{8,10},{10,12},{12,14},{9,11},... | collective-permute-start | bytes 2654216 | tf_op jit(solution)/shard_map/ppermute | solution.py:366
  483.2 4.7 collective-permute-start.39
  (4 other events, 4.2 us)

commit v5 on v4

--- a/solution.py
+++ b/solution.py
@@ -18,6 +18,7 @@
 F32 = jnp.float32
 BF16 = jnp.bfloat16
 MIDDLE = 12
+GAP = 8
 PIECES = 4
 
 
@@ -112,7 +113,7 @@
     split_in, sums_in, sums_split, terms_in, split_out = layout
     zs, planes = sizes
     slab = 2 * planes
-    third = count // 4
+    third, pitch = count // 4, count + GAP
     refs = list(refs)
     place = refs.pop(0)
     partner_hbm = [refs.pop(0) for _ in range(PIECES if split_in else 1)]
@@ -149,21 +150,18 @@
         pltpu.make_async_copy(like_source, like_target, semaphore).wait()
 
     start(tables_hbm, tables, sem_c.at[1])
-    if split_in:
-        for ref, spot in pieces(partner_hbm):
-            start(ref, part(partner, spot), sem.at[0, spot])
-    else:
-        for s in range(zs):
+
+    def load(s):
+        if split_in:
+            for ref, spot in pieces(partner_hbm):
+                start(ref, part(partner, s), sem.at[0, s], spot == s)
+        else:
             start(part(partner_hbm[0], s), part(partner, s), sem.at[0, s])
-    for s in range(zs):
         start(mine_hbm.at[s], part(orbital, 2 * s + core, planes), sem.at[1, s])
         start(other_hbm.at[s], part(orbital, 2 * s + 1 - core, planes), sem.at[2, s])
-    start(coulomb_hbm, coulomb, sem_c.at[0])
-    for s in range(zs):
-        if sums_in:
-            start(part(sums_hbm, s), part(sums, s), sem.at[3, s])
-        if terms_in:
-            start(part(terms_hbm, s), part(terms, s), sem.at[4, s])
+
+    load(0)
+    load(1)
 
     def density(x):
         parts = []
@@ -178,26 +176,33 @@
         wait(part(partner, step), part(partner, step), sem.at[0, step])
         wait(part(orbital, 2 * step, planes), part(orbital, 2 * step, planes), sem.at[1, step])
         wait(part(orbital, 2 * step, planes), part(orbital, 2 * step, planes), sem.at[2, step])
+        pl.when(step + 2 < zs)(lambda: load(step + 2))
+        pl.when(step == zs - 2)(lambda: start(coulomb_hbm, coulomb, sem_c.at[0]))
         base = 2 * group * step
         pairs = [jnp.concatenate([density(base + 2 * g), density(base + 2 * g + 1)], axis=0) for g in range(group)]
         pairs = [along_lanes(both, lanes[...]) for both in pairs]
         pairs = [jnp.concatenate([both[:count], both[count:]], axis=1) for both in pairs]
         pairs = [along_rows(rows_in[...], both) for both in pairs]
-        begin = pl.multiple_of(base * count, 2 * count)
+        begin = pl.multiple_of(base * pitch, 2 * pitch)
         for g, both in enumerate(pairs):
-            field[pl.ds(begin + 2 * g * count, count), :] = both[:, :LANES]
-            field[pl.ds(begin + (2 * g + 1) * count, count), :] = both[:, LANES:]
+            field[pl.ds(begin + 2 * g * pitch, count), :] = both[:, :LANES]
+            field[pl.ds(begin + (2 * g + 1) * pitch, count), :] = both[:, LANES:]
         return carry
 
     wait(tables_hbm, tables, sem_c.at[1])
     lax.fori_loop(0, zs, forward, 0)
+    for s in range(zs):
+        if sums_in:
+            start(part(sums_hbm, s), part(sums, s), sem.at[3, s])
+        if terms_in:
+            start(part(terms_hbm, s), part(terms, s), sem.at[4, s])
     wait(coulomb_hbm, coulomb, sem_c.at[0])
 
     def middle(step, carry):
         base = 2 * MIDDLE * step
         pairs = [
             jnp.concatenate(
-                [field[pl.ds(base + 2 * g + k, count, stride=count), :] for k in range(2)], axis=1
+                [field[pl.ds(base + 2 * g + k, count, stride=pitch), :] for k in range(2)], axis=1
             )
             for g in range(MIDDLE)
         ]
@@ -206,7 +211,7 @@
         pairs = [along_rows(rows_mid[...], both) for both in pairs]
         for g, both in enumerate(pairs):
             for k in range(2):
-                field[pl.ds(base + 2 * g + k, count, stride=count), :] = both[:, k * LANES : (k + 1) * LANES]
+                field[pl.ds(base + 2 * g + k, count, stride=pitch), :] = both[:, k * LANES : (k + 1) * LANES]
         return carry
 
     lax.fori_loop(0, count // 2 // MIDDLE, middle, 0)
@@ -217,9 +222,9 @@
         if terms_in:
             wait(part(terms_hbm, step), part(terms, step), sem.at[4, step])
         base = 2 * group * step
-        begin = pl.multiple_of(base * count, 2 * count)
+        begin = pl.multiple_of(base * pitch, 2 * pitch)
         pairs = [
-            jnp.concatenate([field[pl.ds(begin + (2 * g + k) * count, count), :] for k in range(2)], axis=1)
+            jnp.concatenate([field[pl.ds(begin + (2 * g + k) * pitch, count), :] for k in range(2)], axis=1)
             for g in range(group)
         ]
         pairs = [along_rows(rows_out[...], both) for both in pairs]
@@ -276,7 +281,7 @@
         out_shape=kinds + pieces,
         scratch_shapes=[pltpu.VMEM(block, F32)] * 4
         + [
-            pltpu.VMEM((count * count, LANES), F32),
+            pltpu.VMEM((count * (count + GAP), LANES), F32),
             pltpu.VMEM(tables[0].shape, BF16),
             pltpu.VMEM(tables[1].shape, F32),
             pltpu.SemaphoreType.DMA((8, zs)),
@@ -471,10 +476,11 @@
 
     terms = [None] * ROUNDS
     sums, terms[0] = pair(0, 0, None, after=partners[1][:3] + partners[2][:3])
-    mine.append(lax.all_to_all(tie(sets[1], terms[0]), "z", split_axis=0, concat_axis=0, tiled=True))
-    other.append(swap(mine[1], "core", 1))
+    second = lax.all_to_all(tie(sets[1], terms[0]), "z", split_axis=0, concat_axis=0, tiled=True)
     sums, terms[1] = pair(0, 1, sums)
     sums, terms[2] = pair(0, 2, sums)
+    mine.append(tie(second, terms[2]))
+    other.append(swap(mine[1], "core", 1))
     sums, terms[3] = pair(0, 3, sums, last=True)
     back = [send_back(core_sum(*sums))]
     sums, cross = pair(1, 3, None, terms[3])

time: 505 us -> 484 us (0.958); the launches traced: 498 us -> 483 us
  Pallas kernels: 178 us -> 132 us
  waiting for transfers between devices: 199 us -> 225 us
    ppermute x30, waiting for transfers between devices: 54.9 us -> 117 us  [swap(): return lax.ppermute(value, axis, [(i, i ^ flip) for i in range(size)])]
    pallas_call x8, Pallas kernels: 167 us -> 122 us  [pair_solve(): pl.pallas_call(functools.partial(pair_kernel, count, (zs, planes), layout...]
    all_to_all x1, waiting for transfers between devices: 35 us -> 0.01 us  [square_local(): lax.all_to_all(tie(sets[1], terms[0]), 'z', split_axis=0, concat_axis=0,...]
    ppermute x30, starting transfers between devices: 31.6 us -> 39 us  [swap(): return lax.ppermute(value, axis, [(i, i ^ flip) for i in range(size)])]
  transfers between devices with their start and end apart: 44 -> 44, of which waited for: 21 -> 27; matrix products, arithmetic and copies ran while one was open for 7% -> 7% of each run, Pallas kernels for 25% -> 19%
where the time goes in v5:
time: 484 us; the launch traced here: 483 us
  waiting for transfers between devices  225 us (46%)
  Pallas kernels  132 us (27%)
  starting transfers between devices  82.6 us (17%)
  other arithmetic  32.5 us (7%)
  local copies, waits for them, and re-layouts  10.4 us (2%)
    pallas_call x8, Pallas kernels, pair_solve(): pl.pallas_call(functools.partial(pair_kernel, count, (zs, planes), layout...  122 us
    ppermute x30, waiting for transfers between devices, swap(): return lax.ppermute(value, axis, [(i, i ^ flip) for i in range(size)])  117 us
    ppermute x10, waiting for transfers between devices, along(): return lax.ppermute(value, 'z', pairs)  108 us
    ppermute x30, starting transfers between devices, swap(): return lax.ppermute(value, axis, [(i, i ^ flip) for i in range(size)])  39 us
    ppermute x10, starting transfers between devices, along(): return lax.ppermute(value, 'z', pairs)  23.8 us
    all_to_all x2, starting transfers between devices, send_back(): return lax.all_to_all(total, 'z', split_axis=0, concat_axis=0, tiled=True)  10.2 us
  transfers between devices with their start and end apart: 44, of which 27 were waited for; matrix products, arithmetic and copies ran while one was open for 7% of the time, Pallas kernels for 19%

profile of v5, /device:TPU:17, one launch (start us, length us, event | category | flops | bytes accessed | tf_op | source)
XLA Modules:
  0.0 482.8 jit_solution(14440387671599888488)
XLA Ops:
  0.0 2.0 copy-done
  2.0 4.3 shard_map.28
  6.3 4.6 all-to-all-start
  12.0 1.3 collective-permute-start
  13.3 1.4 collective-permute-done
  15.9 1.3 collective-permute-start.1
  17.2 3.1 collective-permute-start.2
  20.2 2.2 collective-permute-start.3
  22.4 1.3 collective-permute-start.4
  23.7 13.2 %collective-permute-done.1.refs_1_ = f32[24,72,128]{2,1,0:T(8,128)} collective-permute-done((f32[24,72,128]{2,1,0:T(8,128)S(1)}, f32[24,72,128]{2,1,0:T(8,128)}, u32[]{:S(2)}, u32[]{:S(2)}) %collective-permute-start.1) | collective-permute-done | bytes 884768 | tf_op jit(solution)/shard_map/ppermute | solution.py:367
  36.9 31.3 %collective-permute-done.2 = f32[24,72,128]{2,1,0:T(8,128)} collective-permute-done((f32[24,72,128]{2,1,0:T(8,128)S(1)}, f32[24,72,128]{2,1,0:T(8,128)}, u32[]{:S(2)}, u32[]{:S(2)}) %collective-permute-start.2) | collective-permute-done | bytes 884768 | tf_op jit(solution)/shard_map/ppermute | solution.py:371
  68.2 1.9 collective-permute-start.5
  70.2 3.5 collective-permute-start.6
  73.6 1.3 broadcast_select_fusion.refs_2_
  77.5 3.1 collective-permute-start.17
  80.6 9.2 %collective-permute-done.5 = f32[24,72,128]{2,1,0:T(8,128)S(1)} collective-permute-done((f32[24,72,128]{2,1,0:T(8,128)}, f32[24,72,128]{2,1,0:T(8,128)S(1)}, u32[]{:S(2)}, u32[]{:S(2)}) %collective-permute-start.5) | collective-permute-done | bytes 884768 | tf_op jit(solution)/shard_map/ppermute | solution.py:371
  91.7 2.1 collective-permute-done.7.refs_2_
  94.8 2.2 collective-permute-start.9
  99.4 4.8 fusion.refs_8_.refs_9_.refs_10_
  104.9 7.1 %collective-permute-done.9 = f32[24,72,128]{2,1,0:T(8,128)} collective-permute-done((f32[24,72,128]{2,1,0:T(8,128)}, f32[24,72,128]{2,1,0:T(8,128)}, u32[]{:S(2)}, u32[]{:S(2)}) %collective-permute-start.9) | collective-permute-done | bytes 884768 | tf_op jit(solution)/shard_map/ppermute | solution.py:371
  111.9 2.2 broadcast_select_fusion.1.refs_4_
  114.8 1.3 collective-permute-done.11.refs_3_
  117.3 15.3 %shard_map.29 = (f32[96,72,128]{2,1,0:T(8,128)}, f32[96,72,128]{2,1,0:T(8,128)}) custom-call(s32[2]{0:T(128)} %pad_add_fusion.refs_0_, f32[24,72,128]{2,1,0:T(8,128)} %copy-done.6, f32[24,72,128]{2,1,0:T(8,128)} %copy-done.7, f32[24,72,128]{2,1,0:T(8,128)} %add.152.refs_3_, f32[24,72,128]{2,1,0:T(8,128)} %broadcast_select_fusion.1.refs_4_, ...), custom_call_target="tpu_custom_call" | custom-call | flops 1019215872 | bytes 17694720 | tf_op jit(solution)/shard_map/pallas_call | solution.py:276
  132.7 4.9 %all-to-all-start.2 = ((f32[4,12,72,128]{3,2,1,0:T(8,128)}), f32[4,12,72,128]{3,2,1,0:T(8,128)S(1)}, u32[]{:S(2)}, u32[]{:S(2)}) async-start(f32[4,12,72,128]{3,2,1,0:T(8,128)} %bitcast.7), calls=%async_computation.2 | async-start | bytes 3538944 | tf_op jit(solution)/shard_map/all_to_all | solution.py:479
  140.0 14.7 %collective-permute-done.18.refs_4_ = f32[24,72,128]{2,1,0:T(8,128)S(1)} collective-permute-done((f32[24,72,128]{2,1,0:T(8,128)S(1)}, f32[24,72,128]{2,1,0:T(8,128)S(1)}, u32[]{:S(2)}, u32[]{:S(2)}) %collective-permute-start.18) | collective-permute-done | bytes 884768 | tf_op jit(solution)/shard_map/ppermute | solution.py:367
  155.7 15.2 %shard_map.30 = (f32[96,72,128]{2,1,0:T(8,128)}, f32[96,72,128]{2,1,0:T(8,128)}) custom-call(s32[2]{0:T(128)} %pad_add_fusion.refs_0_, f32[24,72,128]{2,1,0:T(8,128)} %collective-permute-done.1.refs_1_, f32[24,72,128]{2,1,0:T(8,128)} %copy-done.11, f32[24,72,128]{2,1,0:T(8,128)} %collective-permute-done.10.refs_3_, f32[24,72,128]{2,1,0:T(8,128)} %copy-done.13, ...), custom_call_target="tpu_custom_call" | custom-call | flops 1019215872 | bytes 17694720 | tf_op jit(solution)/shard_map/pallas_call | solution.py:276
  171.7 15.2 %shard_map.31 = (f32[96,72,128]{2,1,0:T(8,128)}, f32[96,72,128]{2,1,0:T(8,128)}) custom-call(s32[2]{0:T(128)} %pad_add_fusion.refs_0_, f32[24,72,128]{2,1,0:T(8,128)} %copy-done.10, f32[24,72,128]{2,1,0:T(8,128)} %collective-permute-done.8.refs_2_, f32[24,72,128]{2,1,0:T(8,128)} %collective-permute-done.11.refs_3_, f32[24,72,128]{2,1,0:T(8,128)} %copy-done.12, ...), custom_call_target="tpu_custom_call" | custom-call | flops 1019215872 | bytes 17694720 | tf_op jit(solution)/shard_map/pallas_call | solution.py:276
  186.9 5.0 %collective-permute-start.20 = (f32[4,12,72,128]{3,2,1,0:T(8,128)S(1)}, f32[4,12,72,128]{3,2,1,0:T(8,128)S(1)}, u32[]{:S(2)}, u32[]{:S(2)}) collective-permute-start(f32[4,12,72,128]{3,2,1,0:T(8,128)S(1)} %all-to-all-done.2.refs_5_), channel_id=1, source_target_pairs={{0,1},{1,0},{2,3},{3,2},{4,5},{5,4},{6,7},{7,6},{8,9},{9,8},{10,11... | collective-permute-start | bytes 5308424 | tf_op jit(solution)/shard_map/ppermute | solution.py:367
  194.8 18.6 %collective-permute-done.12.refs_1_ = f32[24,72,128]{2,1,0:T(8,128)} collective-permute-done((f32[24,72,128]{2,1,0:T(8,128)}, f32[24,72,128]{2,1,0:T(8,128)}, u32[]{:S(2)}, u32[]{:S(2)}) %collective-permute-start.12) | collective-permute-done | bytes 884768 | tf_op jit(solution)/shard_map/ppermute | solution.py:367
  214.4 18.0 %collective-permute-done.14.refs_3_ = f32[24,72,128]{2,1,0:T(8,128)} collective-permute-done((f32[24,72,128]{2,1,0:T(8,128)}, f32[24,72,128]{2,1,0:T(8,128)}, u32[]{:S(2)}, u32[]{:S(2)}) %collective-permute-start.14) | collective-permute-done | bytes 884768 | tf_op jit(solution)/shard_map/ppermute | solution.py:367
  233.3 15.2 %shard_map.32 = (f32[4,12,72,128]{3,2,1,0:T(8,128)}, f32[4,12,72,128]{3,2,1,0:T(8,128)}, f32[96,72,128]{2,1,0:T(8,128)}) custom-call(s32[2]{0:T(128)} %pad_add_fusion.refs_0_, f32[24,72,128]{2,1,0:T(8,128)} %collective-permute-done.12.refs_1_, f32[24,72,128]{2,1,0:T(8,128)} %collective-permute-done.13.refs_2_, ...), custom_call_target="tpu_custom_call" | custom-call | flops 1019215872 | bytes 17694720 | tf_op jit(solution)/shard_map/pallas_call | solution.py:276
  249.8 15.1 %shard_map.33 = (f32[96,72,128]{2,1,0:T(8,128)}, f32[24,72,128]{2,1,0:T(8,128)}, f32[24,72,128]{2,1,0:T(8,128)}, f32[24,72,128]{2,1,0:T(8,128)}, f32[24,72,128]{2,1,0:T(8,128)}) custom-call(s32[2]{0:T(128)} %pad_add_fusion.refs_0_, f32[24,72,128]{2,1,0:T(8,128)} %collective-permute-done.12.refs_1_, f32[24,72,128]{2,1,0:T(8,128)} %collective-permute-done.13.refs_2_, ...), custom_call_target="tpu_custom_call" | custom-call | flops 1019215872 | bytes 17694720 | tf_op jit(solution)/shard_map/pallas_call | solution.py:276
  266.6 1.6 collective-permute-start.19
  268.2 15.2 %shard_map.34 = (f32[96,72,128]{2,1,0:T(8,128)}, f32[24,72,128]{2,1,0:T(8,128)}, f32[24,72,128]{2,1,0:T(8,128)}, f32[24,72,128]{2,1,0:T(8,128)}, f32[24,72,128]{2,1,0:T(8,128)}) custom-call(s32[2]{0:T(128)} %pad_add_fusion.refs_0_, f32[24,72,128]{2,1,0:T(8,128)} %collective-permute-done.1.refs_1_, f32[24,72,128]{2,1,0:T(8,128)} %copy-done.11, ...), custom_call_target="tpu_custom_call" | custom-call | flops 1019215872 | bytes 17694720 | tf_op jit(solution)/shard_map/pallas_call | solution.py:276
  283.7 1.5 collective-permute-done.22
  287.6 15.3 %shard_map.35 = (f32[96,72,128]{2,1,0:T(8,128)}, f32[24,72,128]{2,1,0:T(8,128)}, f32[24,72,128]{2,1,0:T(8,128)}, f32[24,72,128]{2,1,0:T(8,128)}, f32[24,72,128]{2,1,0:T(8,128)}) custom-call(s32[2]{0:T(128)} %pad_add_fusion.refs_0_, f32[24,72,128]{2,1,0:T(8,128)} %copy-done.10, f32[24,72,128]{2,1,0:T(8,128)} %collective-permute-done.8.refs_2_, ...), custom_call_target="tpu_custom_call" | custom-call | flops 1019215872 | bytes 17694720 | tf_op jit(solution)/shard_map/pallas_call | solution.py:276
  302.9 2.4 add.166
  305.8 1.4 add.157
  307.2 4.5 all-to-all-start.1
  311.7 12.8 %collective-permute-done.25 = f32[24,72,128]{2,1,0:T(8,128)} collective-permute-done((f32[24,72,128]{2,1,0:T(8,128)}, f32[24,72,128]{2,1,0:T(8,128)}, u32[]{:S(2)}, u32[]{:S(2)}) %collective-permute-start.25) | collective-permute-done | bytes 884768 | tf_op jit(solution)/shard_map/ppermute | solution.py:367
  324.5 15.4 %shard_map.36 = (f32[4,12,72,128]{3,2,1,0:T(8,128)}, f32[4,12,72,128]{3,2,1,0:T(8,128)}, f32[24,72,128]{2,1,0:T(8,128)}, f32[24,72,128]{2,1,0:T(8,128)}, f32[24,72,128]{2,1,0:T(8,128)}, /*index=5*/f32[24,72,128]{2,1,0:T(8,128)}) custom-call(s32[2]{0:T(128)} %pad_add_fusion.refs_0_, f32[24,72,128]{2,1,0:T(8,128)} %copy-done.6, f32[24,72,128]{2,1,0:T(8,128)} %copy-done.7, ...), custom_call_target="tpu_custom_call" | custom-call | flops 1019215872 | bytes 17694720 | tf_op jit(solution)/shard_map/pallas_call | solution.py:276
  343.9 2.0 add_add_fusion.2
  345.9 1.3 collective-permute-start.34
  347.2 1.3 add.163
  348.5 14.1 %collective-permute-done.33 = f32[24,72,128]{2,1,0:T(8,128)S(1)} collective-permute-done((f32[24,72,128]{2,1,0:T(8,128)}, f32[24,72,128]{2,1,0:T(8,128)S(1)}, u32[]{:S(2)}, u32[]{:S(2)}) %collective-permute-start.33) | collective-permute-done | bytes 884768 | tf_op jit(solution)/shard_map/ppermute | solution.py:367
  363.9 1.4 add.158
  365.2 2.8 collective-permute-done.34
  369.1 13.2 %collective-permute-done.29 = f32[24,72,128]{2,1,0:T(8,128)S(1)} collective-permute-done((f32[24,72,128]{2,1,0:T(8,128)}, f32[24,72,128]{2,1,0:T(8,128)S(1)}, u32[]{:S(2)}, u32[]{:S(2)}) %collective-permute-start.29) | collective-permute-done | bytes 884768 | tf_op jit(solution)/shard_map/ppermute | solution.py:367
  382.9 2.2 collective-permute-start.36
  385.0 1.3 collective-permute-start.35
  387.5 2.2 add.159
  391.1 5.7 %all-to-all-start.3 = ((f32[4,12,72,128]{3,2,1,0:T(8,128)}), f32[4,12,72,128]{3,2,1,0:T(8,128)S(1)}, u32[]{:S(2)}, u32[]{:S(2)}) async-start(f32[4,12,72,128]{3,2,1,0:T(8,128)} %add.158), calls=%async_computation.3 | async-start | bytes 3538944 | tf_op jit(solution)/shard_map/all_to_all | solution.py:457
  396.7 7.7 %collective-permute-done.36 = f32[24,72,128]{2,1,0:T(8,128)} collective-permute-done((f32[24,72,128]{2,1,0:T(8,128)}, f32[24,72,128]{2,1,0:T(8,128)}, u32[]{:S(2)}, u32[]{:S(2)}) %collective-permute-start.36) | collective-permute-done | bytes 884768 | tf_op jit(solution)/shard_map/ppermute | solution.py:371
  404.5 1.9 collective-permute-done.35
  406.4 4.0 fusion.9
  410.4 2.3 collective-permute-start.38
  412.7 3.9 collective-permute-start.37
  416.6 42.9 %collective-permute-done.38 = f32[24,72,128]{2,1,0:T(8,128)} collective-permute-done((f32[24,72,128]{2,1,0:T(8,128)}, f32[24,72,128]{2,1,0:T(8,128)}, u32[]{:S(2)}, u32[]{:S(2)}) %collective-permute-start.38) | collective-permute-done | bytes 884768 | tf_op jit(solution)/shard_map/ppermute | solution.py:371
  459.4 3.8 collective-permute-done.37
  463.3 3.4 add_add_fusion
  466.6 1.8 constant_dynamic-slice_fusion
  468.5 2.9 collective-permute-start.39
  471.4 1.8 collective-permute-done.39
  476.5 6.3 %shard_map.37 = f32[12,8,9216]{2,1,0:T(8,128)} custom-call(f32[3456,128]{1,0:T(8,128)S(1)} %bitcast.18, f32[3456,128]{1,0:T(8,128)S(1)} %bitcast.19, f32[1728,128]{1,0:T(8,128)S(1)} %bitcast.21), custom_call_target="tpu_custom_call" | custom-call | tf_op jit(solution)/shard_map/pallas_call | solution.py:355
  (111 shorter events, 40.5 us)
Async XLA Ops:
  0.0 2.0 copy-start
  6.3 62.0 %all-to-all-start = ((f32[4,12,72,128]{3,2,1,0:T(8,128)}), f32[4,12,72,128]{3,2,1,0:T(8,128)S(1)}, u32[]{:S(2)}, u32[]{:S(2)}) async-start(f32[4,12,72,128]{3,2,1,0:T(8,128)} %bitcast.3), calls=%async_computation | async-start | bytes 3538944 | tf_op jit(solution)/shard_map/all_to_all | solution.py:469
  12.0 2.7 collective-permute-start
  15.9 61.6 %copy-start.6 = (f32[24,72,128]{2,1,0:T(8,128)}, f32[24,72,128]{2,1,0:T(8,128)S(1)}, u32[]{:S(2)}) copy-start(f32[24,72,128]{2,1,0:T(8,128)S(1)} %pad_maximum_fusion.refs_1_) | copy-start | bytes 2654212
  15.9 21.0 %collective-permute-start.1 = (f32[24,72,128]{2,1,0:T(8,128)S(1)}, f32[24,72,128]{2,1,0:T(8,128)}, u32[]{:S(2)}, u32[]{:S(2)}) collective-permute-start(f32[24,72,128]{2,1,0:T(8,128)S(1)} %pad_maximum_fusion.refs_1_), channel_id=1, source_target_pairs={{0,8},{8,0},{16,24},{24,16},{1,9},{9,1},{17,25},{25,17},{2,10},{10... | collective-permute-start | bytes 2654216 | tf_op jit(solution)/shard_map/ppermute | solution.py:367
  17.2 51.1 %collective-permute-start.2 = (f32[24,72,128]{2,1,0:T(8,128)S(1)}, f32[24,72,128]{2,1,0:T(8,128)}, u32[]{:S(2)}, u32[]{:S(2)}) collective-permute-start(f32[24,72,128]{2,1,0:T(8,128)S(1)} %pad_maximum_fusion.refs_1_), channel_id=1, source_target_pairs={{0,2},{2,4},{4,6},{1,3},{3,5},{5,7},{8,10},{10,12},{12,14},{9,11},... | collective-permute-start | bytes 2654216 | tf_op jit(solution)/shard_map/ppermute | solution.py:371
  20.2 48.0 %collective-permute-start.3 = (f32[24,72,128]{2,1,0:T(8,128)S(1)}, f32[24,72,128]{2,1,0:T(8,128)}, u32[]{:S(2)}, u32[]{:S(2)}) collective-permute-start(f32[24,72,128]{2,1,0:T(8,128)S(1)} %pad_maximum_fusion.refs_1_), channel_id=1, source_target_pairs={{2,0},{4,2},{6,4},{3,1},{5,3},{7,5},{10,8},{12,10},{14,12},{11,9},... | collective-permute-start | bytes 2654216 | tf_op jit(solution)/shard_map/ppermute | solution.py:371
  22.4 45.8 %collective-permute-start.4 = (f32[24,72,128]{2,1,0:T(8,128)S(1)}, f32[24,72,128]{2,1,0:T(8,128)S(1)}, u32[]{:S(2)}, u32[]{:S(2)}) collective-permute-start(f32[24,72,128]{2,1,0:T(8,128)S(1)} %pad_maximum_fusion.refs_1_), channel_id=1, source_target_pairs={{0,16},{8,24},{16,0},{24,8},{1,17},{9,25},{17,1},{25,9},{2,18},{10... | collective-permute-start | bytes 2654216 | tf_op jit(solution)/shard_map/ppermute | solution.py:367
  68.2 9.3 %copy-start.10 = (f32[24,72,128]{2,1,0:T(8,128)}, f32[24,72,128]{2,1,0:T(8,128)S(1)}, u32[]{:S(2)}) copy-start(f32[24,72,128]{2,1,0:T(8,128)S(1)} %collective-permute-done.4.refs_1_) | copy-start | bytes 2654212
  68.2 36.0 %copy-start.2 = (f32[4,12,72,128]{3,2,1,0:T(8,128)}, f32[4,12,72,128]{3,2,1,0:T(8,128)S(1)}, u32[]{:S(2)}) copy-start(f32[4,12,72,128]{3,2,1,0:T(8,128)S(1)} %all-to-all-done.refs_5_) | copy-start | bytes 5308420
  68.2 21.5 %collective-permute-start.5 = (f32[24,72,128]{2,1,0:T(8,128)}, f32[24,72,128]{2,1,0:T(8,128)S(1)}, u32[]{:S(2)}, u32[]{:S(2)}) collective-permute-start(f32[24,72,128]{2,1,0:T(8,128)} %collective-permute-done.2), channel_id=1, source_target_pairs={{2,4},{4,6},{3,5},{5,7},{10,12},{12,14},{11,13},{13,15},{18,20},{2... | collective-permute-start | bytes 2654216 | tf_op jit(solution)/shard_map/ppermute | solution.py:371
  70.2 20.5 %collective-permute-start.6 = (f32[24,72,128]{2,1,0:T(8,128)}, f32[24,72,128]{2,1,0:T(8,128)S(1)}, u32[]{:S(2)}, u32[]{:S(2)}) collective-permute-start(f32[24,72,128]{2,1,0:T(8,128)} %collective-permute-done.3), channel_id=1, source_target_pairs={{2,0},{4,2},{3,1},{5,3},{10,8},{12,10},{11,9},{13,11},{18,16},{20,... | collective-permute-start | bytes 2654216 | tf_op jit(solution)/shard_map/ppermute | solution.py:371
  74.9 2.6 copy-start.7
  74.9 18.9 %collective-permute-start.7 = (f32[24,72,128]{2,1,0:T(8,128)S(1)}, f32[24,72,128]{2,1,0:T(8,128)S(1)}, u32[]{:S(2)}, u32[]{:S(2)}) collective-permute-start(f32[24,72,128]{2,1,0:T(8,128)S(1)} %broadcast_select_fusion.refs_2_), channel_id=1, source_target_pairs={{0,8},{8,0},{16,24},{24,16},{1,9},{9,1},{17,25},{25,17},{2,10},{10... | collective-permute-start | bytes 2654216 | tf_op jit(solution)/shard_map/ppermute | solution.py:367
  76.2 18.5 %collective-permute-start.8 = (f32[24,72,128]{2,1,0:T(8,128)S(1)}, f32[24,72,128]{2,1,0:T(8,128)}, u32[]{:S(2)}, u32[]{:S(2)}) collective-permute-start(f32[24,72,128]{2,1,0:T(8,128)S(1)} %broadcast_select_fusion.refs_2_), channel_id=1, source_target_pairs={{0,16},{8,24},{16,0},{24,8},{1,17},{9,25},{17,1},{25,9},{2,18},{10... | collective-permute-start | bytes 2654216 | tf_op jit(solution)/shard_map/ppermute | solution.py:367
  77.5 38.6 %collective-permute-start.17 = (f32[4,12,72,128]{3,2,1,0:T(8,128)S(1)}, f32[4,12,72,128]{3,2,1,0:T(8,128)S(1)}, u32[]{:S(2)}, u32[]{:S(2)}) collective-permute-start(f32[4,12,72,128]{3,2,1,0:T(8,128)S(1)} %all-to-all-done.refs_5_), channel_id=1, source_target_pairs={{0,1},{1,0},{2,3},{3,2},{4,5},{5,4},{6,7},{7,6},{8,9},{9,8},{10,11... | collective-permute-start | bytes 5308424 | tf_op jit(solution)/shard_map/ppermute | solution.py:367
  94.8 17.2 %collective-permute-start.9 = (f32[24,72,128]{2,1,0:T(8,128)}, f32[24,72,128]{2,1,0:T(8,128)}, u32[]{:S(2)}, u32[]{:S(2)}) collective-permute-start(f32[24,72,128]{2,1,0:T(8,128)} %add.152.refs_3_), channel_id=1, source_target_pairs={{4,6},{2,0},{5,7},{3,1},{12,14},{10,8},{13,15},{11,9},{20,22},{18,... | collective-permute-start | bytes 2654216 | tf_op jit(solution)/shard_map/ppermute | solution.py:371
  97.0 17.8 %collective-permute-start.10 = (f32[24,72,128]{2,1,0:T(8,128)}, f32[24,72,128]{2,1,0:T(8,128)}, u32[]{:S(2)}, u32[]{:S(2)}) collective-permute-start(f32[24,72,128]{2,1,0:T(8,128)} %add.152.refs_3_), channel_id=1, source_target_pairs={{0,8},{8,0},{16,24},{24,16},{1,9},{9,1},{17,25},{25,17},{2,10},{10... | collective-permute-start | bytes 2654216 | tf_op jit(solution)/shard_map/ppermute | solution.py:367
  98.2 17.9 %collective-permute-start.11 = (f32[24,72,128]{2,1,0:T(8,128)}, f32[24,72,128]{2,1,0:T(8,128)}, u32[]{:S(2)}, u32[]{:S(2)}) collective-permute-start(f32[24,72,128]{2,1,0:T(8,128)} %add.152.refs_3_), channel_id=1, source_target_pairs={{0,16},{8,24},{16,0},{24,8},{1,17},{9,25},{17,1},{25,9},{2,18},{10... | collective-permute-start | bytes 2654216 | tf_op jit(solution)/shard_map/ppermute | solution.py:367
  117.3 20.3 %copy-start.8 = (f32[24,72,128]{2,1,0:T(8,128)S(1)}, f32[24,72,128]{2,1,0:T(8,128)}, u32[]{:S(2)}) copy-start(f32[24,72,128]{2,1,0:T(8,128)} %broadcast_select_fusion.1.refs_4_) | copy-start | bytes 2654212
  132.7 54.2 %all-to-all-start.2 = ((f32[4,12,72,128]{3,2,1,0:T(8,128)}), f32[4,12,72,128]{3,2,1,0:T(8,128)S(1)}, u32[]{:S(2)}, u32[]{:S(2)}) async-start(f32[4,12,72,128]{3,2,1,0:T(8,128)} %bitcast.7), calls=%async_computation.2 | async-start | bytes 3538944 | tf_op jit(solution)/shard_map/all_to_all | solution.py:479
  137.6 17.2 %collective-permute-start.18 = (f32[24,72,128]{2,1,0:T(8,128)S(1)}, f32[24,72,128]{2,1,0:T(8,128)S(1)}, u32[]{:S(2)}, u32[]{:S(2)}) collective-permute-start(f32[24,72,128]{2,1,0:T(8,128)S(1)} %copy-done.8), channel_id=1, source_target_pairs={{0,8},{8,0},{16,24},{24,16},{1,9},{9,1},{17,25},{25,17},{2,10},{10... | collective-permute-start | bytes 2654216 | tf_op jit(solution)/shard_map/ppermute | solution.py:367
  138.8 32.0 %collective-permute-start.15 = (f32[24,72,128]{2,1,0:T(8,128)S(1)}, f32[24,72,128]{2,1,0:T(8,128)S(1)}, u32[]{:S(2)}, u32[]{:S(2)}) collective-permute-start(f32[24,72,128]{2,1,0:T(8,128)S(1)} %copy-done.8), channel_id=1, source_target_pairs={{0,16},{8,24},{16,0},{24,8},{1,17},{9,25},{17,1},{25,9},{2,18},{10... | collective-permute-start | bytes 2654216 | tf_op jit(solution)/shard_map/ppermute | solution.py:367
  186.9 61.6 %copy-start.3 = (f32[4,12,72,128]{3,2,1,0:T(8,128)}, f32[4,12,72,128]{3,2,1,0:T(8,128)S(1)}, u32[]{:S(2)}) copy-start(f32[4,12,72,128]{3,2,1,0:T(8,128)S(1)} %all-to-all-done.2.refs_5_) | copy-start | bytes 5308420
  186.9 61.6 %collective-permute-start.20 = (f32[4,12,72,128]{3,2,1,0:T(8,128)S(1)}, f32[4,12,72,128]{3,2,1,0:T(8,128)S(1)}, u32[]{:S(2)}, u32[]{:S(2)}) collective-permute-start(f32[4,12,72,128]{3,2,1,0:T(8,128)S(1)} %all-to-all-done.2.refs_5_), channel_id=1, source_target_pairs={{0,1},{1,0},{2,3},{3,2},{4,5},{5,4},{6,7},{7,6},{8,9},{9,8},{10,11... | collective-permute-start | bytes 5308424 | tf_op jit(solution)/shard_map/ppermute | solution.py:367
  191.9 21.5 %collective-permute-start.12 = (f32[24,72,128]{2,1,0:T(8,128)}, f32[24,72,128]{2,1,0:T(8,128)}, u32[]{:S(2)}, u32[]{:S(2)}) collective-permute-start(f32[24,72,128]{2,1,0:T(8,128)} %collective-permute-done.1.refs_1_), channel_id=1, source_target_pairs={{0,16},{8,24},{16,0},{24,8},{1,17},{9,25},{17,1},{25,9},{2,18},{10... | collective-permute-start | bytes 2654216 | tf_op jit(solution)/shard_map/ppermute | solution.py:367
  193.1 21.2 %collective-permute-start.13 = (f32[24,72,128]{2,1,0:T(8,128)}, f32[24,72,128]{2,1,0:T(8,128)}, u32[]{:S(2)}, u32[]{:S(2)}) collective-permute-start(f32[24,72,128]{2,1,0:T(8,128)} %collective-permute-done.8.refs_2_), channel_id=1, source_target_pairs={{0,8},{8,0},{16,24},{24,16},{1,9},{9,1},{17,25},{25,17},{2,10},{10... | collective-permute-start | bytes 2654216 | tf_op jit(solution)/shard_map/ppermute | solution.py:367
  194.4 38.0 %collective-permute-start.14 = (f32[24,72,128]{2,1,0:T(8,128)}, f32[24,72,128]{2,1,0:T(8,128)}, u32[]{:S(2)}, u32[]{:S(2)}) collective-permute-start(f32[24,72,128]{2,1,0:T(8,128)} %collective-permute-done.10.refs_3_), channel_id=1, source_target_pairs={{0,16},{8,24},{16,0},{24,8},{1,17},{9,25},{17,1},{25,9},{2,18},{10... | collective-permute-start | bytes 2654216 | tf_op jit(solution)/shard_map/ppermute | solution.py:367
  194.6 38.7 %collective-permute-start.16 = (f32[24,72,128]{2,1,0:T(8,128)}, f32[24,72,128]{2,1,0:T(8,128)}, u32[]{:S(2)}, u32[]{:S(2)}) collective-permute-start(f32[24,72,128]{2,1,0:T(8,128)} %copy-done.12), channel_id=1, source_target_pairs={{0,8},{8,0},{16,24},{24,16},{1,9},{9,1},{17,25},{25,17},{2,10},{10... | collective-permute-start | bytes 2654216 | tf_op jit(solution)/shard_map/ppermute | solution.py:367
  248.6 1.3 copy-start.5
  264.9 20.2 %collective-permute-start.22 = (f32[24,72,128]{2,1,0:T(8,128)}, f32[24,72,128]{2,1,0:T(8,128)S(1)}, u32[]{:S(2)}, u32[]{:S(2)}) collective-permute-start(f32[24,72,128]{2,1,0:T(8,128)} %get-tuple-element.93), channel_id=1, source_target_pairs={{0,16},{8,24},{16,0},{24,8},{1,17},{9,25},{17,1},{25,9},{2,18},{10... | collective-permute-start | bytes 2654216 | tf_op jit(solution)/shard_map/ppermute | solution.py:367
  265.3 20.0 %collective-permute-start.23 = (f32[24,72,128]{2,1,0:T(8,128)}, f32[24,72,128]{2,1,0:T(8,128)S(1)}, u32[]{:S(2)}, u32[]{:S(2)}) collective-permute-start(f32[24,72,128]{2,1,0:T(8,128)} %get-tuple-element.94), channel_id=1, source_target_pairs={{0,8},{8,0},{16,24},{24,16},{1,9},{9,1},{17,25},{25,17},{2,10},{10... | collective-permute-start | bytes 2654216 | tf_op jit(solution)/shard_map/ppermute | solution.py:367
  266.6 39.2 %collective-permute-start.19 = (f32[4,12,72,128]{3,2,1,0:T(8,128)}, f32[4,12,72,128]{3,2,1,0:T(8,128)S(1)}, u32[]{:S(2)}, u32[]{:S(2)}) collective-permute-start(f32[4,12,72,128]{3,2,1,0:T(8,128)} %get-tuple-element.82), channel_id=1, source_target_pairs={{0,1},{1,0},{2,3},{3,2},{4,5},{5,4},{6,7},{7,6},{8,9},{9,8},{10,11... | collective-permute-start | bytes 5308424 | tf_op jit(solution)/shard_map/ppermute | solution.py:367
  283.4 28.3 %collective-permute-start.21 = (f32[24,72,128]{2,1,0:T(8,128)}, f32[24,72,128]{2,1,0:T(8,128)}, u32[]{:S(2)}, u32[]{:S(2)}) collective-permute-start(f32[24,72,128]{2,1,0:T(8,128)} %get-tuple-element.91), channel_id=1, source_target_pairs={{0,8},{8,0},{16,24},{24,16},{1,9},{9,1},{17,25},{25,17},{2,10},{10... | collective-permute-start | bytes 2654216 | tf_op jit(solution)/shard_map/ppermute | solution.py:367
  285.2 2.4 copy-start.20
  285.3 2.2 copy-start.24
  285.4 26.3 %collective-permute-start.24 = (f32[24,72,128]{2,1,0:T(8,128)}, f32[24,72,128]{2,1,0:T(8,128)}, u32[]{:S(2)}, u32[]{:S(2)}) collective-permute-start(f32[24,72,128]{2,1,0:T(8,128)} %get-tuple-element.95), channel_id=1, source_target_pairs={{0,16},{8,24},{16,0},{24,8},{1,17},{9,25},{17,1},{25,9},{2,18},{10... | collective-permute-start | bytes 2654216 | tf_op jit(solution)/shard_map/ppermute | solution.py:367
  286.4 38.1 %collective-permute-start.25 = (f32[24,72,128]{2,1,0:T(8,128)}, f32[24,72,128]{2,1,0:T(8,128)}, u32[]{:S(2)}, u32[]{:S(2)}) collective-permute-start(f32[24,72,128]{2,1,0:T(8,128)} %get-tuple-element.97), channel_id=1, source_target_pairs={{0,8},{8,0},{16,24},{24,16},{1,9},{9,1},{17,25},{25,17},{2,10},{10... | collective-permute-start | bytes 2654216 | tf_op jit(solution)/shard_map/ppermute | solution.py:367
  287.6 18.2 %copy-start.14 = (f32[4,12,72,128]{3,2,1,0:T(8,128)S(1)}, f32[4,12,72,128]{3,2,1,0:T(8,128)}, u32[]{:S(2)}) copy-start(f32[4,12,72,128]{3,2,1,0:T(8,128)} %get-tuple-element.81) | copy-start | bytes 5308420
  305.3 38.6 %collective-permute-start.31 = (f32[24,72,128]{2,1,0:T(8,128)}, f32[24,72,128]{2,1,0:T(8,128)}, u32[]{:S(2)}, u32[]{:S(2)}) collective-permute-start(f32[24,72,128]{2,1,0:T(8,128)} %add.166), channel_id=1, source_target_pairs={{0,16},{8,24},{16,0},{24,8},{1,17},{9,25},{17,1},{25,9},{2,18},{10... | collective-permute-start | bytes 2654216 | tf_op jit(solution)/shard_map/ppermute | solution.py:367
  307.2 83.9 %all-to-all-start.1 = ((f32[4,12,72,128]{3,2,1,0:T(8,128)}), f32[4,12,72,128]{3,2,1,0:T(8,128)S(1)}, u32[]{:S(2)}, u32[]{:S(2)}) async-start(f32[4,12,72,128]{3,2,1,0:T(8,128)} %add.157), calls=%async_computation.1 | async-start | bytes 3538944 | tf_op jit(solution)/shard_map/all_to_all | solution.py:457
  324.5 17.8 %copy-start.21 = (f32[24,72,128]{2,1,0:T(8,128)S(1)}, f32[24,72,128]{2,1,0:T(8,128)}, u32[]{:S(2)}) copy-start(f32[24,72,128]{2,1,0:T(8,128)} %copy-done.20) | copy-start | bytes 2654212
  324.5 17.8 %copy-start.22 = (f32[24,72,128]{2,1,0:T(8,128)S(1)}, f32[24,72,128]{2,1,0:T(8,128)}, u32[]{:S(2)}) copy-start(f32[24,72,128]{2,1,0:T(8,128)} %get-tuple-element.119) | copy-start | bytes 2654212
  339.9 7.3 %copy-start.23 = (f32[24,72,128]{2,1,0:T(8,128)S(1)}, f32[24,72,128]{2,1,0:T(8,128)}, u32[]{:S(2)}) copy-start(f32[24,72,128]{2,1,0:T(8,128)} %get-tuple-element.115) | copy-start | bytes 2654212
  339.9 23.8 %copy-start.16 = (f32[24,72,128]{2,1,0:T(8,128)S(1)}, f32[24,72,128]{2,1,0:T(8,128)}, u32[]{:S(2)}) copy-start(f32[24,72,128]{2,1,0:T(8,128)} %get-tuple-element.118) | copy-start | bytes 2654212
  339.9 24.0 %collective-permute-start.26 = (f32[4,12,72,128]{3,2,1,0:T(8,128)}, f32[4,12,72,128]{3,2,1,0:T(8,128)S(1)}, u32[]{:S(2)}, u32[]{:S(2)}) collective-permute-start(f32[4,12,72,128]{3,2,1,0:T(8,128)} %get-tuple-element.109), channel_id=1, source_target_pairs={{0,1},{1,0},{2,3},{3,2},{4,5},{5,4},{6,7},{7,6},{8,9},{9,8},{10,11... | collective-permute-start | bytes 5308424 | tf_op jit(solution)/shard_map/ppermute | solution.py:367
  341.1 21.4 %collective-permute-start.33 = (f32[24,72,128]{2,1,0:T(8,128)}, f32[24,72,128]{2,1,0:T(8,128)S(1)}, u32[]{:S(2)}, u32[]{:S(2)}) collective-permute-start(f32[24,72,128]{2,1,0:T(8,128)} %get-tuple-element.120), channel_id=1, source_target_pairs={{0,16},{8,24},{16,0},{24,8},{1,17},{9,25},{17,1},{25,9},{2,18},{10... | collective-permute-start | bytes 2654216 | tf_op jit(solution)/shard_map/ppermute | solution.py:367
  342.4 21.3 %collective-permute-start.32 = (f32[24,72,128]{2,1,0:T(8,128)S(1)}, f32[24,72,128]{2,1,0:T(8,128)S(1)}, u32[]{:S(2)}, u32[]{:S(2)}) collective-permute-start(f32[24,72,128]{2,1,0:T(8,128)S(1)} %add.168), channel_id=1, source_target_pairs={{0,8},{8,0},{16,24},{24,16},{1,9},{9,1},{17,25},{25,17},{2,10},{10... | collective-permute-start | bytes 2654216 | tf_op jit(solution)/shard_map/ppermute | solution.py:367
  343.6 38.6 %collective-permute-start.29 = (f32[24,72,128]{2,1,0:T(8,128)}, f32[24,72,128]{2,1,0:T(8,128)S(1)}, u32[]{:S(2)}, u32[]{:S(2)}) collective-permute-start(f32[24,72,128]{2,1,0:T(8,128)} %get-tuple-element.114), channel_id=1, source_target_pairs={{0,8},{8,0},{16,24},{24,16},{1,9},{9,1},{17,25},{25,17},{2,10},{10... | collective-permute-start | bytes 2654216 | tf_op jit(solution)/shard_map/ppermute | solution.py:367
  343.9 19.9 %copy-start.15 = (f32[4,12,72,128]{3,2,1,0:T(8,128)S(1)}, f32[4,12,72,128]{3,2,1,0:T(8,128)}, u32[]{:S(2)}) copy-start(f32[4,12,72,128]{3,2,1,0:T(8,128)} %get-tuple-element.108) | copy-start | bytes 5308420
  345.9 43.9 %copy-start.9 = (f32[24,72,128]{2,1,0:T(8,128)}, f32[24,72,128]{2,1,0:T(8,128)S(1)}, u32[]{:S(2)}) copy-start(f32[24,72,128]{2,1,0:T(8,128)S(1)} %add_add_fusion.2) | copy-start | bytes 2654212
  345.9 22.2 %collective-permute-start.34 = (f32[24,72,128]{2,1,0:T(8,128)S(1)}, f32[24,72,128]{2,1,0:T(8,128)S(1)}, u32[]{:S(2)}, u32[]{:S(2)}) collective-permute-start(f32[24,72,128]{2,1,0:T(8,128)S(1)} %add_add_fusion.2), channel_id=1, source_target_pairs={{0,2},{6,4},{1,3},{7,5},{8,10},{14,12},{9,11},{15,13},{16,18},{22,... | collective-permute-start | bytes 2654216 | tf_op jit(solution)/shard_map/ppermute | solution.py:371
  362.5 20.3 %collective-permute-start.30 = (f32[24,72,128]{2,1,0:T(8,128)S(1)}, f32[24,72,128]{2,1,0:T(8,128)S(1)}, u32[]{:S(2)}, u32[]{:S(2)}) collective-permute-start(f32[24,72,128]{2,1,0:T(8,128)S(1)} %add.163), channel_id=1, source_target_pairs={{0,16},{8,24},{16,0},{24,8},{1,17},{9,25},{17,1},{25,9},{2,18},{10... | collective-permute-start | bytes 2654216 | tf_op jit(solution)/shard_map/ppermute | solution.py:367
  363.8 23.7 %copy-start.19 = (f32[24,72,128]{2,1,0:T(8,128)S(1)}, f32[24,72,128]{2,1,0:T(8,128)}, u32[]{:S(2)}) copy-start(f32[24,72,128]{2,1,0:T(8,128)} %get-tuple-element.111) | copy-start | bytes 2654212
  382.3 7.5 %copy-start.17 = (f32[24,72,128]{2,1,0:T(8,128)}, f32[24,72,128]{2,1,0:T(8,128)S(1)}, u32[]{:S(2)}) copy-start(f32[24,72,128]{2,1,0:T(8,128)S(1)} %collective-permute-done.29) | copy-start | bytes 2654212
  382.9 6.9 %copy-start.18 = (f32[24,72,128]{2,1,0:T(8,128)}, f32[24,72,128]{2,1,0:T(8,128)S(1)}, u32[]{:S(2)}) copy-start(f32[24,72,128]{2,1,0:T(8,128)S(1)} %collective-permute-done.30) | copy-start | bytes 2654212
  382.9 21.6 %collective-permute-start.36 = (f32[24,72,128]{2,1,0:T(8,128)}, f32[24,72,128]{2,1,0:T(8,128)}, u32[]{:S(2)}, u32[]{:S(2)}) collective-permute-start(f32[24,72,128]{2,1,0:T(8,128)} %add.171), channel_id=1, source_target_pairs={{4,2},{6,4},{5,3},{7,5},{12,10},{14,12},{13,11},{15,13},{20,18},{2... | collective-permute-start | bytes 2654216 | tf_op jit(solution)/shard_map/ppermute | solution.py:371
  385.0 21.3 %collective-permute-start.35 = (f32[24,72,128]{2,1,0:T(8,128)}, f32[24,72,128]{2,1,0:T(8,128)}, u32[]{:S(2)}, u32[]{:S(2)}) collective-permute-start(f32[24,72,128]{2,1,0:T(8,128)} %add.171), channel_id=1, source_target_pairs={{0,2},{2,4},{1,3},{3,5},{8,10},{10,12},{9,11},{11,13},{16,18},{18,... | collective-permute-start | bytes 2654216 | tf_op jit(solution)/shard_map/ppermute | solution.py:371
  386.3 24.0 %collective-permute-start.28 = (f32[24,72,128]{2,1,0:T(8,128)}, f32[24,72,128]{2,1,0:T(8,128)}, u32[]{:S(2)}, u32[]{:S(2)}) collective-permute-start(f32[24,72,128]{2,1,0:T(8,128)} %get-tuple-element.112), channel_id=1, source_target_pairs={{0,16},{8,24},{16,0},{24,8},{1,17},{9,25},{17,1},{25,9},{2,18},{10... | collective-permute-start | bytes 2654216 | tf_op jit(solution)/shard_map/ppermute | solution.py:367
  389.8 20.6 %collective-permute-start.27 = (f32[24,72,128]{2,1,0:T(8,128)}, f32[24,72,128]{2,1,0:T(8,128)}, u32[]{:S(2)}, u32[]{:S(2)}) collective-permute-start(f32[24,72,128]{2,1,0:T(8,128)} %add.159), channel_id=1, source_target_pairs={{0,8},{8,0},{16,24},{24,16},{1,9},{9,1},{17,25},{25,17},{2,10},{10... | collective-permute-start | bytes 2654216 | tf_op jit(solution)/shard_map/ppermute | solution.py:367
  391.1 84.3 %all-to-all-start.3 = ((f32[4,12,72,128]{3,2,1,0:T(8,128)}), f32[4,12,72,128]{3,2,1,0:T(8,128)S(1)}, u32[]{:S(2)}, u32[]{:S(2)}) async-start(f32[4,12,72,128]{3,2,1,0:T(8,128)} %add.158), calls=%async_computation.3 | async-start | bytes 3538944 | tf_op jit(solution)/shard_map/all_to_all | solution.py:457
  410.4 49.1 %collective-permute-start.38 = (f32[24,72,128]{2,1,0:T(8,128)}, f32[24,72,128]{2,1,0:T(8,128)}, u32[]{:S(2)}, u32[]{:S(2)}) collective-permute-start(f32[24,72,128]{2,1,0:T(8,128)} %get-tuple-element.124), channel_id=1, source_target_pairs={{2,0},{4,2},{6,4},{3,1},{5,3},{7,5},{10,8},{12,10},{14,12},{11,9},... | collective-permute-start | bytes 2654216 | tf_op jit(solution)/shard_map/ppermute | solution.py:371
  412.7 50.6 %collective-permute-start.37 = (f32[24,72,128]{2,1,0:T(8,128)}, f32[24,72,128]{2,1,0:T(8,128)}, u32[]{:S(2)}, u32[]{:S(2)}) collective-permute-start(f32[24,72,128]{2,1,0:T(8,128)} %get-tuple-element.123), channel_id=1, source_target_pairs={{0,2},{2,4},{4,6},{1,3},{3,5},{5,7},{8,10},{10,12},{12,14},{9,11},... | collective-permute-start | bytes 2654216 | tf_op jit(solution)/shard_map/ppermute | solution.py:371
  468.5 4.7 collective-permute-start.39
  (5 other events, 5.1 us)

commit v6 on v5

--- a/solution.py
+++ b/solution.py
@@ -288,7 +288,7 @@
             pltpu.SemaphoreType.DMA((2,)),
         ],
         cost_estimate=pl.CostEstimate(
-            flops=12 * count**4, bytes_accessed=20 * count * rows * LANES, transcendentals=0
+            flops=200 * count**4, bytes_accessed=20 * count * rows * LANES, transcendentals=0
         ),
         compiler_params=pltpu.CompilerParams(vmem_limit_bytes=60 * 1024 * 1024),
     )(place, *partner, mine, other, *more, *tables)
@@ -389,7 +389,8 @@
 
     before, after = along(slab, RIGHT), along(slab, LEFT)
     both(slab)
-    before, after = tie((before, after), (side[-1], far[-1], first))
+    cross = [swap(side[0], "band", 2)]
+    before, after = tie((before, after), (side[-1], far[-1], first, cross))
     near = jnp.where(z == 0, after, before)
     two = along(before, RIGHT[1:]) + along(after, LEFT[:2])
     both(near)
@@ -398,23 +399,10 @@
     rest = jnp.where((z == 0) | (z == 3), along(two, [(2, 3), (1, 0)]), after)
     rest = tie(rest, (side[-1], far[-1]))
     both(rest)
-    cross = [swap(tie(piece, rest), "band", flip) for piece, flip in zip((side[0], far[1], side[2], far[3]), (2, 1, 2, 1))]
+    done = (side[3], far[3])
+    cross += [swap(tie(far[1], done), "band", 1), swap(tie(side[2], done), "band", 2)]
+    cross.append(swap(tie(far[3], cross[1]), "band", 1))
     return [[slab, near, two, rest], side, far, cross]
-
-
-def hand_over(cross):
-    first = [swap(cross[2], "band", 2), swap(cross[3], "band", 1)]
-    later = [swap(tie(cross[0], first), "band", 2), swap(tie(cross[1], first), "band", 1)]
-    return [later[0], later[1], first[0], first[1]]
-
-
-def scatter_line(slab, near, two, rest, near_in, slab_in):
-    z = lax.axis_index("z")
-    two = tie(two + along(rest, [(0, 1), (3, 2)]), near_in)
-    near = near + near_in[0] + near_in[1]
-    after, before = along(two, RIGHT[:2]), along(two, LEFT[1:])
-    after, before = tie((jnp.where(z == 0, near, rest + after), near + before), slab_in)
-    return slab + slab_in[0] + slab_in[1] + along(after, RIGHT) + along(before, LEFT)
 
 
 def local(orbitals):
@@ -475,28 +463,41 @@
         return pair_solve(place, partner, mine[k], other[k], sums, term, tables, last, k == 1)
 
     terms = [None] * ROUNDS
-    sums, terms[0] = pair(0, 0, None, after=partners[1][:3] + partners[2][:3])
-    second = lax.all_to_all(tie(sets[1], terms[0]), "z", split_axis=0, concat_axis=0, tiled=True)
+    sums, terms[0] = pair(0, 0, None)
+    second = lax.all_to_all(tie(sets[1], partners[0][3]), "z", split_axis=0, concat_axis=0, tiled=True)
     sums, terms[1] = pair(0, 1, sums)
-    sums, terms[2] = pair(0, 2, sums)
-    mine.append(tie(second, terms[2]))
+    sums, terms[2] = pair(0, 2, sums, after=partners[3][:3])
+    sums, terms[3] = pair(0, 3, sums, last=True)
+    mine.append(tie(second, terms[3]))
     other.append(swap(mine[1], "core", 1))
-    sums, terms[3] = pair(0, 3, sums, last=True)
     back = [send_back(core_sum(*sums))]
+    z = lax.axis_index("z")
+    x_swap = lambda value, done: swap(tie(value, done), "band", 1)
+    y_swap = lambda value, done: swap(tie(value, done), "band", 2)
     sums, cross = pair(1, 3, None, terms[3])
-    handed = hand_over(cross)
+    handed3, handed2 = swap(cross[3], "band", 1), swap(cross[2], "band", 2)
     sums, side = pair(1, 1, sums, terms[1])
-    sums, far = pair(1, 2, sums, terms[2], after=handed[2:])
-    side = [side[0] + handed[0], side[1], side[2] + handed[2], side[3]]
-    far = [far[0], far[1] + handed[1], far[2], far[3] + handed[3]]
-    sent = swap(side[3], "band", 1)
-    sums, own = pair(1, 0, sums, terms[0], after=[sent] + handed[:2], last=True)
+    done = (handed3, handed2)
+    side3, handed0 = x_swap(side[3], done), y_swap(cross[0], done)
+    sums, far = pair(1, 2, sums, terms[2], after=done)
+    done = (side3, handed0)
+    side2, far3 = x_swap(side[2] + handed2, done), y_swap(far[3] + handed3, done)
+    sums, own = pair(1, 0, sums, terms[0], after=done, last=True)
     total = core_sum(*sums)
     back.append(send_back(total))
-    arrived = [(swap(side[k], "band", 1), swap(far[k], "band", 2)) for k in range(PIECES - 1)]
-    rest = own[3] + sent + swap(far[3], "band", 2)
-    two = tie(own[2] + arrived[2][0] + arrived[2][1], total)
-    return finish(back, scatter_line(own[0], own[1], two, rest, arrived[1], arrived[0]))
+    done = (side2, far3)
+    handed1, far2 = x_swap(cross[1], done), y_swap(far[2], done)
+    rest = along(own[3] + side3 + far3, [(0, 1), (3, 2)])
+    done = (handed1, far2)
+    side1, far1 = x_swap(side[1], done), y_swap(far[1] + handed1, done)
+    two = tie(own[2] + side2 + far2 + rest, total)
+    after, before = along(two, RIGHT[:2]), along(two, LEFT[1:])
+    done = (side1, far1)
+    side0, far0 = x_swap(side[0] + handed0, done), y_swap(far[0], done)
+    near = own[1] + side1 + far1
+    after = jnp.where(z == 0, near, own[3] + side3 + far3 + after)
+    after, before = along(after, RIGHT), along(near + before, LEFT)
+    return finish(back, own[0] + side0 + far0 + after + before)
 
 
 def solution(mesh):

time: 484 us -> 440 us (0.909)
  waiting for transfers between devices: 225 us -> 181 us
    ppermute x30, waiting for transfers between devices: 117 us -> 36.3 us  [swap(): return lax.ppermute(value, axis, [(i, i ^ flip) for i in range(size)])]
    ppermute x10, waiting for transfers between devices: 108 us -> 144 us  [along(): return lax.ppermute(value, 'z', pairs)]
    add x9 -> x7, other arithmetic: 16.5 us -> 15 us  [the longest x1 2.47 us: square_local(): side0, far0 = (x_swap(side[0] + handed0, done), y_swap(far[0], done))]
  transfers between devices with their start and end apart: 44 -> 44, of which waited for: 27 -> 20; matrix products, arithmetic and copies ran while one was open for 7% -> 8% of each run, Pallas kernels for 19% -> 28%
where the time goes in v6:
time: 440 us; the launch traced here: 437 us
  waiting for transfers between devices  181 us (41%)
  Pallas kernels  132 us (30%)
  starting transfers between devices  79 us (18%)
  other arithmetic  34.6 us (8%)
  local copies, waits for them, and re-layouts  9.82 us (2%)
    ppermute x10, waiting for transfers between devices, along(): return lax.ppermute(value, 'z', pairs)  144 us
    pallas_call x8, Pallas kernels, pair_solve(): pl.pallas_call(functools.partial(pair_kernel, count, (zs, planes), layout...  122 us
    ppermute x30, waiting for transfers between devices, swap(): return lax.ppermute(value, axis, [(i, i ^ flip) for i in range(size)])  36.3 us
    ppermute x30, starting transfers between devices, swap(): return lax.ppermute(value, axis, [(i, i ^ flip) for i in range(size)])  34.5 us
    ppermute x10, starting transfers between devices, along(): return lax.ppermute(value, 'z', pairs)  25.6 us
  transfers between devices with their start and end apart: 44, of which 20 were waited for; matrix products, arithmetic and copies ran while one was open for 8% of the time, Pallas kernels for 28%

profile of v6, /device:TPU:17, one launch (start us, length us, event | category | flops | bytes accessed | tf_op | source)
XLA Modules:
  0.0 436.8 jit_solution(14564440165669749278)
XLA Ops:
  0.0 2.0 copy-done
  2.0 4.3 shard_map.28
  6.3 4.6 %all-to-all-start = ((f32[4,12,72,128]{3,2,1,0:T(8,128)}), f32[4,12,72,128]{3,2,1,0:T(8,128)S(1)}, u32[]{:S(2)}, u32[]{:S(2)}) async-start(f32[4,12,72,128]{3,2,1,0:T(8,128)} %bitcast.3), calls=%async_computation | async-start | bytes 3538944 | tf_op jit(solution)/shard_map/all_to_all | solution.py:457
  12.0 1.3 collective-permute-start
  13.3 1.4 collective-permute-done
  15.9 1.3 collective-permute-start.1
  17.1 3.1 collective-permute-start.3
  20.2 2.2 collective-permute-start.4
  22.4 1.3 collective-permute-start.5
  23.7 13.2 %collective-permute-done.1.refs_1_ = f32[24,72,128]{2,1,0:T(8,128)} collective-permute-done((f32[24,72,128]{2,1,0:T(8,128)S(1)}, f32[24,72,128]{2,1,0:T(8,128)}, u32[]{:S(2)}, u32[]{:S(2)}) %collective-permute-start.1) | collective-permute-done | bytes 884768 | tf_op jit(solution)/shard_map/ppermute | solution.py:367
  36.9 1.2 collective-permute-start.2
  38.1 30.1 %collective-permute-done.3 = f32[24,72,128]{2,1,0:T(8,128)} collective-permute-done((f32[24,72,128]{2,1,0:T(8,128)S(1)}, f32[24,72,128]{2,1,0:T(8,128)}, u32[]{:S(2)}, u32[]{:S(2)}) %collective-permute-start.3) | collective-permute-done | bytes 884768 | tf_op jit(solution)/shard_map/ppermute | solution.py:371
  68.2 1.9 collective-permute-start.7
  70.2 3.5 collective-permute-start.8
  73.6 1.3 broadcast_select_fusion.1.refs_2_
  74.9 1.3 collective-permute-start.6
  76.2 1.2 collective-permute-start.9
  77.5 3.1 collective-permute-start.18
  80.5 9.1 %collective-permute-done.7 = f32[24,72,128]{2,1,0:T(8,128)S(1)} collective-permute-done((f32[24,72,128]{2,1,0:T(8,128)}, f32[24,72,128]{2,1,0:T(8,128)S(1)}, u32[]{:S(2)}, u32[]{:S(2)}) %collective-permute-start.7) | collective-permute-done | bytes 884768 | tf_op jit(solution)/shard_map/ppermute | solution.py:371
  91.4 2.3 collective-permute-done.6.refs_2_
  94.7 2.2 collective-permute-start.10
  99.3 4.8 %fusion.refs_8_.refs_9_.refs_10_ = f32[48,96,256]{2,1,0:T(8,128)} fusion(s32[256]{0:T(256)S(1)} %get-tuple-element.141, s32[256]{0:T(256)S(1)} %get-tuple-element.142, s32[96]{0:T(128)S(1)} %iota_add_fusion, s32[256]{0:T(256)S(1)} %get-tuple-element.140, s32[48]{0:T(128)S(1)} %iota_multiply_fusion, pred[96]{0:T(512)(128)(4,1)S(1)} %iota_compare_fusion, ...), kind=kLoop, calls=%fused_computation.4 | loop fusion | flops 31850496 | bytes 4722592 | tf_op jit(solution)/shard_map/div | solution.py:75
  104.8 7.1 %collective-permute-done.10 = f32[24,72,128]{2,1,0:T(8,128)} collective-permute-done((f32[24,72,128]{2,1,0:T(8,128)}, f32[24,72,128]{2,1,0:T(8,128)}, u32[]{:S(2)}, u32[]{:S(2)}) %collective-permute-start.10) | collective-permute-done | bytes 884768 | tf_op jit(solution)/shard_map/ppermute | solution.py:371
  112.0 2.7 collective-permute-done.11.refs_3_
  115.9 1.5 collective-permute-start.14
  117.4 5.9 %all-to-all-start.2 = ((f32[4,12,72,128]{3,2,1,0:T(8,128)}), f32[4,12,72,128]{3,2,1,0:T(8,128)}, u32[]{:S(2)}, u32[]{:S(2)}) async-start(f32[4,12,72,128]{3,2,1,0:T(8,128)} %bitcast.7), calls=%async_computation.2 | async-start | bytes 3538944 | tf_op jit(solution)/shard_map/all_to_all | solution.py:467
  123.3 15.3 %shard_map.29 = (f32[96,72,128]{2,1,0:T(8,128)}, f32[96,72,128]{2,1,0:T(8,128)}) custom-call(s32[2]{0:T(128)} %pad_add_fusion.refs_0_, f32[24,72,128]{2,1,0:T(8,128)} %copy-done.8, f32[24,72,128]{2,1,0:T(8,128)} %copy-done.9, f32[24,72,128]{2,1,0:T(8,128)} %add.154.refs_3_, f32[24,72,128]{2,1,0:T(8,128)} %copy-done.10, f32[4,12,72,128]{3,2,1,0:T(8,128)} %copy-done.4, ...), custom_call_target="tpu_custom_call" | custom-call | flops 16986931200 | bytes 17694720 | tf_op jit(solution)/shard_map/pallas_call | solution.py:276
  139.2 15.2 %shard_map.30 = (f32[96,72,128]{2,1,0:T(8,128)}, f32[96,72,128]{2,1,0:T(8,128)}) custom-call(s32[2]{0:T(128)} %pad_add_fusion.refs_0_, f32[24,72,128]{2,1,0:T(8,128)} %collective-permute-done.1.refs_1_, f32[24,72,128]{2,1,0:T(8,128)} %copy-done.19, f32[24,72,128]{2,1,0:T(8,128)} %collective-permute-done.11.refs_3_, ...), custom_call_target="tpu_custom_call" | custom-call | flops 16986931200 | bytes 17694720 | tf_op jit(solution)/shard_map/pallas_call | solution.py:276
  155.7 15.2 %shard_map.31 = (f32[96,72,128]{2,1,0:T(8,128)}, f32[96,72,128]{2,1,0:T(8,128)}) custom-call(s32[2]{0:T(128)} %pad_add_fusion.refs_0_, f32[24,72,128]{2,1,0:T(8,128)} %collective-permute-done.5.refs_1_, f32[24,72,128]{2,1,0:T(8,128)} %copy-done.17, f32[24,72,128]{2,1,0:T(8,128)} %collective-permute-done.12.refs_3_, ...), custom_call_target="tpu_custom_call" | custom-call | flops 16986931200 | bytes 17694720 | tf_op jit(solution)/shard_map/pallas_call | solution.py:276
  170.9 2.6 collective-permute-done.17.refs_4_
  174.5 15.2 %shard_map.32 = (f32[4,12,72,128]{3,2,1,0:T(8,128)}, f32[4,12,72,128]{3,2,1,0:T(8,128)}, f32[96,72,128]{2,1,0:T(8,128)}) custom-call(s32[2]{0:T(128)} %pad_add_fusion.refs_0_, f32[24,72,128]{2,1,0:T(8,128)} %collective-permute-done.2.refs_1_, f32[24,72,128]{2,1,0:T(8,128)} %copy-done.20, f32[24,72,128]{2,1,0:T(8,128)} %copy-done.21, ...), custom_call_target="tpu_custom_call" | custom-call | flops 16986931200 | bytes 17694720 | tf_op jit(solution)/shard_map/pallas_call | solution.py:276
  189.7 6.3 %collective-permute-start.20 = (f32[4,12,72,128]{3,2,1,0:T(8,128)}, f32[4,12,72,128]{3,2,1,0:T(8,128)S(1)}, u32[]{:S(2)}, u32[]{:S(2)}) collective-permute-start(f32[4,12,72,128]{3,2,1,0:T(8,128)} %all-to-all-done.2.refs_5_), channel_id=1, source_target_pairs={{0,1},{1,0},{2,3},{3,2},{4,5},{5,4},{6,7},{7,6},{8,9},{9,8},{10,11... | collective-permute-start | bytes 5308424 | tf_op jit(solution)/shard_map/ppermute | solution.py:367
  196.1 3.5 collective-permute-done.20.refs_6_
  199.6 1.2 copy-done.16
  200.8 15.1 %shard_map.33 = (f32[96,72,128]{2,1,0:T(8,128)}, f32[24,72,128]{2,1,0:T(8,128)}, f32[24,72,128]{2,1,0:T(8,128)}, f32[24,72,128]{2,1,0:T(8,128)}, f32[24,72,128]{2,1,0:T(8,128)}) custom-call(s32[2]{0:T(128)} %pad_add_fusion.refs_0_, f32[24,72,128]{2,1,0:T(8,128)} %collective-permute-done.2.refs_1_, f32[24,72,128]{2,1,0:T(8,128)} %copy-done.20, ...), custom_call_target="tpu_custom_call" | custom-call | flops 16986931200 | bytes 17694720 | tf_op jit(solution)/shard_map/pallas_call | solution.py:276
  216.5 15.2 %shard_map.34 = (f32[96,72,128]{2,1,0:T(8,128)}, f32[24,72,128]{2,1,0:T(8,128)}, f32[24,72,128]{2,1,0:T(8,128)}, f32[24,72,128]{2,1,0:T(8,128)}, f32[24,72,128]{2,1,0:T(8,128)}) custom-call(s32[2]{0:T(128)} %pad_add_fusion.refs_0_, f32[24,72,128]{2,1,0:T(8,128)} %collective-permute-done.1.refs_1_, f32[24,72,128]{2,1,0:T(8,128)} %copy-done.19, ...), custom_call_target="tpu_custom_call" | custom-call | flops 16986931200 | bytes 17694720 | tf_op jit(solution)/shard_map/pallas_call | solution.py:276
  231.7 5.4 %collective-permute-done.21 = f32[24,72,128]{2,1,0:T(8,128)S(1)} collective-permute-done((f32[24,72,128]{2,1,0:T(8,128)}, f32[24,72,128]{2,1,0:T(8,128)S(1)}, u32[]{:S(2)}, u32[]{:S(2)}) %collective-permute-start.21) | collective-permute-done | bytes 884768 | tf_op jit(solution)/shard_map/ppermute | solution.py:367
  239.2 15.2 %shard_map.35 = (f32[96,72,128]{2,1,0:T(8,128)}, f32[24,72,128]{2,1,0:T(8,128)}, f32[24,72,128]{2,1,0:T(8,128)}, f32[24,72,128]{2,1,0:T(8,128)}, f32[24,72,128]{2,1,0:T(8,128)}) custom-call(s32[2]{0:T(128)} %pad_add_fusion.refs_0_, f32[24,72,128]{2,1,0:T(8,128)} %collective-permute-done.5.refs_1_, f32[24,72,128]{2,1,0:T(8,128)} %copy-done.17, ...), custom_call_target="tpu_custom_call" | custom-call | flops 16986931200 | bytes 17694720 | tf_op jit(solution)/shard_map/pallas_call | solution.py:276
  254.4 2.5 add.163
  256.8 2.4 add.162
  259.3 1.3 collective-permute-start.27
  261.2 15.4 %shard_map.36 = (f32[4,12,72,128]{3,2,1,0:T(8,128)}, f32[4,12,72,128]{3,2,1,0:T(8,128)}, f32[24,72,128]{2,1,0:T(8,128)}, f32[24,72,128]{2,1,0:T(8,128)}, f32[24,72,128]{2,1,0:T(8,128)}, /*index=5*/f32[24,72,128]{2,1,0:T(8,128)}) custom-call(s32[2]{0:T(128)} %pad_add_fusion.refs_0_, f32[24,72,128]{2,1,0:T(8,128)} %copy-done.8, f32[24,72,128]{2,1,0:T(8,128)} %copy-done.9, ...), custom_call_target="tpu_custom_call" | custom-call | flops 16986931200 | bytes 17694720 | tf_op jit(solution)/shard_map/pallas_call | solution.py:276
  276.5 2.4 collective-permute-start.25
  278.9 1.4 add.159
  280.3 4.6 %all-to-all-start.1 = ((f32[4,12,72,128]{3,2,1,0:T(8,128)}), f32[4,12,72,128]{3,2,1,0:T(8,128)S(1)}, u32[]{:S(2)}, u32[]{:S(2)}) async-start(f32[4,12,72,128]{3,2,1,0:T(8,128)} %add.159), calls=%async_computation.1 | async-start | bytes 3538944 | tf_op jit(solution)/shard_map/all_to_all | solution.py:445
  285.0 1.9 add_add_fusion.2
  286.9 1.3 collective-permute-start.34
  289.5 2.9 add.160
  292.4 41.9 %collective-permute-done.34 = f32[24,72,128]{2,1,0:T(8,128)S(1)} collective-permute-done((f32[24,72,128]{2,1,0:T(8,128)S(1)}, f32[24,72,128]{2,1,0:T(8,128)S(1)}, u32[]{:S(2)}, u32[]{:S(2)}) %collective-permute-start.34) | collective-permute-done | bytes 884768 | tf_op jit(solution)/shard_map/ppermute | solution.py:371
  334.4 2.3 add_add_fusion.1
  336.7 1.3 collective-permute-start.35
  340.2 4.0 collective-permute-start.37
  344.2 3.7 all-to-all-start.3
  347.9 2.5 add.161
  350.3 8.5 %collective-permute-done.35 = f32[24,72,128]{2,1,0:T(8,128)} collective-permute-done((f32[24,72,128]{2,1,0:T(8,128)}, f32[24,72,128]{2,1,0:T(8,128)}, u32[]{:S(2)}, u32[]{:S(2)}) %collective-permute-start.35) | collective-permute-done | bytes 884768 | tf_op jit(solution)/shard_map/ppermute | solution.py:371
  359.3 2.5 collective-permute-done.37
  361.8 4.0 add_select_fusion
  365.9 4.3 collective-permute-start.38
  370.2 1.9 collective-permute-start.36
  373.9 44.5 %collective-permute-done.38 = f32[24,72,128]{2,1,0:T(8,128)} collective-permute-done((f32[24,72,128]{2,1,0:T(8,128)}, f32[24,72,128]{2,1,0:T(8,128)}, u32[]{:S(2)}, u32[]{:S(2)}) %collective-permute-start.38) | collective-permute-done | bytes 884768 | tf_op jit(solution)/shard_map/ppermute | solution.py:371
  418.4 2.4 add_add_fusion
  422.5 2.9 collective-permute-start.39
  425.4 1.8 collective-permute-done.39
  430.5 6.3 %shard_map.37 = f32[12,8,9216]{2,1,0:T(8,128)} custom-call(f32[3456,128]{1,0:T(8,128)S(1)} %bitcast.18, f32[3456,128]{1,0:T(8,128)S(1)} %bitcast.19, f32[1728,128]{1,0:T(8,128)S(1)} %bitcast.21), custom_call_target="tpu_custom_call" | custom-call | tf_op jit(solution)/shard_map/pallas_call | solution.py:355
  (106 shorter events, 26.4 us)
Async XLA Ops:
  0.0 2.0 copy-start
  6.3 62.0 %all-to-all-start = ((f32[4,12,72,128]{3,2,1,0:T(8,128)}), f32[4,12,72,128]{3,2,1,0:T(8,128)S(1)}, u32[]{:S(2)}, u32[]{:S(2)}) async-start(f32[4,12,72,128]{3,2,1,0:T(8,128)} %bitcast.3), calls=%async_computation | async-start | bytes 3538944 | tf_op jit(solution)/shard_map/all_to_all | solution.py:457
  12.0 2.7 collective-permute-start
  15.8 88.3 %copy-start.8 = (f32[24,72,128]{2,1,0:T(8,128)}, f32[24,72,128]{2,1,0:T(8,128)S(1)}, u32[]{:S(2)}) copy-start(f32[24,72,128]{2,1,0:T(8,128)S(1)} %pad_maximum_fusion.refs_1_) | copy-start | bytes 2654212
  15.9 21.0 %collective-permute-start.1 = (f32[24,72,128]{2,1,0:T(8,128)S(1)}, f32[24,72,128]{2,1,0:T(8,128)}, u32[]{:S(2)}, u32[]{:S(2)}) collective-permute-start(f32[24,72,128]{2,1,0:T(8,128)S(1)} %pad_maximum_fusion.refs_1_), channel_id=1, source_target_pairs={{0,8},{8,0},{16,24},{24,16},{1,9},{9,1},{17,25},{25,17},{2,10},{10... | collective-permute-start | bytes 2654216 | tf_op jit(solution)/shard_map/ppermute | solution.py:367
  17.1 51.1 %collective-permute-start.3 = (f32[24,72,128]{2,1,0:T(8,128)S(1)}, f32[24,72,128]{2,1,0:T(8,128)}, u32[]{:S(2)}, u32[]{:S(2)}) collective-permute-start(f32[24,72,128]{2,1,0:T(8,128)S(1)} %pad_maximum_fusion.refs_1_), channel_id=1, source_target_pairs={{0,2},{2,4},{4,6},{1,3},{3,5},{5,7},{8,10},{10,12},{12,14},{9,11},... | collective-permute-start | bytes 2654216 | tf_op jit(solution)/shard_map/ppermute | solution.py:371
  20.2 48.0 %collective-permute-start.4 = (f32[24,72,128]{2,1,0:T(8,128)S(1)}, f32[24,72,128]{2,1,0:T(8,128)S(1)}, u32[]{:S(2)}, u32[]{:S(2)}) collective-permute-start(f32[24,72,128]{2,1,0:T(8,128)S(1)} %pad_maximum_fusion.refs_1_), channel_id=1, source_target_pairs={{2,0},{4,2},{6,4},{3,1},{5,3},{7,5},{10,8},{12,10},{14,12},{11,9},... | collective-permute-start | bytes 2654216 | tf_op jit(solution)/shard_map/ppermute | solution.py:371
  22.4 45.8 %collective-permute-start.5 = (f32[24,72,128]{2,1,0:T(8,128)S(1)}, f32[24,72,128]{2,1,0:T(8,128)}, u32[]{:S(2)}, u32[]{:S(2)}) collective-permute-start(f32[24,72,128]{2,1,0:T(8,128)S(1)} %pad_maximum_fusion.refs_1_), channel_id=1, source_target_pairs={{0,16},{8,24},{16,0},{24,8},{1,17},{9,25},{17,1},{25,9},{2,18},{10... | collective-permute-start | bytes 2654216 | tf_op jit(solution)/shard_map/ppermute | solution.py:367
  36.9 31.3 %collective-permute-start.2 = (f32[24,72,128]{2,1,0:T(8,128)}, f32[24,72,128]{2,1,0:T(8,128)}, u32[]{:S(2)}, u32[]{:S(2)}) collective-permute-start(f32[24,72,128]{2,1,0:T(8,128)} %collective-permute-done.1.refs_1_), channel_id=1, source_target_pairs={{0,16},{8,24},{16,0},{24,8},{1,17},{9,25},{17,1},{25,9},{2,18},{10... | collective-permute-start | bytes 2654216 | tf_op jit(solution)/shard_map/ppermute | solution.py:367
  68.2 35.9 %copy-start.4 = (f32[4,12,72,128]{3,2,1,0:T(8,128)}, f32[4,12,72,128]{3,2,1,0:T(8,128)S(1)}, u32[]{:S(2)}) copy-start(f32[4,12,72,128]{3,2,1,0:T(8,128)S(1)} %all-to-all-done.refs_5_) | copy-start | bytes 5308420
  68.2 21.4 %collective-permute-start.7 = (f32[24,72,128]{2,1,0:T(8,128)}, f32[24,72,128]{2,1,0:T(8,128)S(1)}, u32[]{:S(2)}, u32[]{:S(2)}) collective-permute-start(f32[24,72,128]{2,1,0:T(8,128)} %collective-permute-done.3), channel_id=1, source_target_pairs={{2,4},{4,6},{3,5},{5,7},{10,12},{12,14},{11,13},{13,15},{18,20},{2... | collective-permute-start | bytes 2654216 | tf_op jit(solution)/shard_map/ppermute | solution.py:371
  70.2 20.2 %collective-permute-start.8 = (f32[24,72,128]{2,1,0:T(8,128)S(1)}, f32[24,72,128]{2,1,0:T(8,128)S(1)}, u32[]{:S(2)}, u32[]{:S(2)}) collective-permute-start(f32[24,72,128]{2,1,0:T(8,128)S(1)} %collective-permute-done.4), channel_id=1, source_target_pairs={{2,0},{4,2},{3,1},{5,3},{10,8},{12,10},{11,9},{13,11},{18,16},{20,... | collective-permute-start | bytes 2654216 | tf_op jit(solution)/shard_map/ppermute | solution.py:371
  74.9 15.5 %copy-start.9 = (f32[24,72,128]{2,1,0:T(8,128)}, f32[24,72,128]{2,1,0:T(8,128)S(1)}, u32[]{:S(2)}) copy-start(f32[24,72,128]{2,1,0:T(8,128)S(1)} %broadcast_select_fusion.1.refs_2_) | copy-start | bytes 2654212
  74.9 18.8 %collective-permute-start.6 = (f32[24,72,128]{2,1,0:T(8,128)S(1)}, f32[24,72,128]{2,1,0:T(8,128)S(1)}, u32[]{:S(2)}, u32[]{:S(2)}) collective-permute-start(f32[24,72,128]{2,1,0:T(8,128)S(1)} %broadcast_select_fusion.1.refs_2_), channel_id=1, source_target_pairs={{0,16},{8,24},{16,0},{24,8},{1,17},{9,25},{17,1},{25,9},{2,18},{10... | collective-permute-start | bytes 2654216 | tf_op jit(solution)/shard_map/ppermute | solution.py:367
  76.2 18.4 %collective-permute-start.9 = (f32[24,72,128]{2,1,0:T(8,128)S(1)}, f32[24,72,128]{2,1,0:T(8,128)S(1)}, u32[]{:S(2)}, u32[]{:S(2)}) collective-permute-start(f32[24,72,128]{2,1,0:T(8,128)S(1)} %broadcast_select_fusion.1.refs_2_), channel_id=1, source_target_pairs={{0,8},{8,0},{16,24},{24,16},{1,9},{9,1},{17,25},{25,17},{2,10},{10... | collective-permute-start | bytes 2654216 | tf_op jit(solution)/shard_map/ppermute | solution.py:367
  77.5 45.8 %collective-permute-start.18 = (f32[4,12,72,128]{3,2,1,0:T(8,128)S(1)}, f32[4,12,72,128]{3,2,1,0:T(8,128)}, u32[]{:S(2)}, u32[]{:S(2)}) collective-permute-start(f32[4,12,72,128]{3,2,1,0:T(8,128)S(1)} %all-to-all-done.refs_5_), channel_id=1, source_target_pairs={{0,1},{1,0},{2,3},{3,2},{4,5},{5,4},{6,7},{7,6},{8,9},{9,8},{10,11... | collective-permute-start | bytes 5308424 | tf_op jit(solution)/shard_map/ppermute | solution.py:367
  93.7 1.0 copy-start.17
  94.7 2.2 copy-start.19
  94.7 17.2 %collective-permute-start.10 = (f32[24,72,128]{2,1,0:T(8,128)}, f32[24,72,128]{2,1,0:T(8,128)}, u32[]{:S(2)}, u32[]{:S(2)}) collective-permute-start(f32[24,72,128]{2,1,0:T(8,128)} %add.154.refs_3_), channel_id=1, source_target_pairs={{4,6},{2,0},{5,7},{3,1},{12,14},{10,8},{13,15},{11,9},{20,22},{18,... | collective-permute-start | bytes 2654216 | tf_op jit(solution)/shard_map/ppermute | solution.py:371
  96.9 17.8 %collective-permute-start.11 = (f32[24,72,128]{2,1,0:T(8,128)}, f32[24,72,128]{2,1,0:T(8,128)}, u32[]{:S(2)}, u32[]{:S(2)}) collective-permute-start(f32[24,72,128]{2,1,0:T(8,128)} %add.154.refs_3_), channel_id=1, source_target_pairs={{0,8},{8,0},{16,24},{24,16},{1,9},{9,1},{17,25},{25,17},{2,10},{10... | collective-permute-start | bytes 2654216 | tf_op jit(solution)/shard_map/ppermute | solution.py:367
  98.1 17.6 %collective-permute-start.12 = (f32[24,72,128]{2,1,0:T(8,128)}, f32[24,72,128]{2,1,0:T(8,128)}, u32[]{:S(2)}, u32[]{:S(2)}) collective-permute-start(f32[24,72,128]{2,1,0:T(8,128)} %add.154.refs_3_), channel_id=1, source_target_pairs={{0,16},{8,24},{16,0},{24,8},{1,17},{9,25},{17,1},{25,9},{2,18},{10... | collective-permute-start | bytes 2654216 | tf_op jit(solution)/shard_map/ppermute | solution.py:367
  111.9 11.3 %copy-start.10 = (f32[24,72,128]{2,1,0:T(8,128)}, f32[24,72,128]{2,1,0:T(8,128)S(1)}, u32[]{:S(2)}) copy-start(f32[24,72,128]{2,1,0:T(8,128)S(1)} %broadcast_select_fusion.refs_4_) | copy-start | bytes 2654212
  115.6 23.0 %collective-permute-start.13 = (f32[24,72,128]{2,1,0:T(8,128)S(1)}, f32[24,72,128]{2,1,0:T(8,128)}, u32[]{:S(2)}, u32[]{:S(2)}) collective-permute-start(f32[24,72,128]{2,1,0:T(8,128)S(1)} %broadcast_select_fusion.refs_4_), channel_id=1, source_target_pairs={{0,8},{8,0},{16,24},{24,16},{1,9},{9,1},{17,25},{25,17},{2,10},{10... | collective-permute-start | bytes 2654216 | tf_op jit(solution)/shard_map/ppermute | solution.py:367
  115.9 22.7 %collective-permute-start.14 = (f32[24,72,128]{2,1,0:T(8,128)S(1)}, f32[24,72,128]{2,1,0:T(8,128)}, u32[]{:S(2)}, u32[]{:S(2)}) collective-permute-start(f32[24,72,128]{2,1,0:T(8,128)S(1)} %broadcast_select_fusion.refs_4_), channel_id=1, source_target_pairs={{0,16},{8,24},{16,0},{24,8},{1,17},{9,25},{17,1},{25,9},{2,18},{10... | collective-permute-start | bytes 2654216 | tf_op jit(solution)/shard_map/ppermute | solution.py:367
  117.4 72.3 %all-to-all-start.2 = ((f32[4,12,72,128]{3,2,1,0:T(8,128)}), f32[4,12,72,128]{3,2,1,0:T(8,128)}, u32[]{:S(2)}, u32[]{:S(2)}) async-start(f32[4,12,72,128]{3,2,1,0:T(8,128)} %bitcast.7), calls=%async_computation.2 | async-start | bytes 3538944 | tf_op jit(solution)/shard_map/all_to_all | solution.py:467
  123.3 15.4 %copy-start.18 = (f32[24,72,128]{2,1,0:T(8,128)S(1)}, f32[24,72,128]{2,1,0:T(8,128)}, u32[]{:S(2)}) copy-start(f32[24,72,128]{2,1,0:T(8,128)} %copy-done.17) | copy-start | bytes 2654212
  138.7 16.8 %collective-permute-start.15 = (f32[24,72,128]{2,1,0:T(8,128)S(1)}, f32[24,72,128]{2,1,0:T(8,128)S(1)}, u32[]{:S(2)}, u32[]{:S(2)}) collective-permute-start(f32[24,72,128]{2,1,0:T(8,128)S(1)} %copy-done.18), channel_id=1, source_target_pairs={{0,8},{8,0},{16,24},{24,16},{1,9},{9,1},{17,25},{25,17},{2,10},{10... | collective-permute-start | bytes 2654216 | tf_op jit(solution)/shard_map/ppermute | solution.py:367
  139.0 16.7 %collective-permute-start.16 = (f32[24,72,128]{2,1,0:T(8,128)}, f32[24,72,128]{2,1,0:T(8,128)S(1)}, u32[]{:S(2)}, u32[]{:S(2)}) collective-permute-start(f32[24,72,128]{2,1,0:T(8,128)} %collective-permute-done.11.refs_3_), channel_id=1, source_target_pairs={{0,16},{8,24},{16,0},{24,8},{1,17},{9,25},{17,1},{25,9},{2,18},{10... | collective-permute-start | bytes 2654216 | tf_op jit(solution)/shard_map/ppermute | solution.py:367
  155.4 15.4 %copy-start.20 = (f32[24,72,128]{2,1,0:T(8,128)}, f32[24,72,128]{2,1,0:T(8,128)S(1)}, u32[]{:S(2)}) copy-start(f32[24,72,128]{2,1,0:T(8,128)S(1)} %collective-permute-done.15.refs_2_) | copy-start | bytes 2654212
  155.4 18.1 %collective-permute-start.17 = (f32[24,72,128]{2,1,0:T(8,128)}, f32[24,72,128]{2,1,0:T(8,128)S(1)}, u32[]{:S(2)}, u32[]{:S(2)}) collective-permute-start(f32[24,72,128]{2,1,0:T(8,128)} %collective-permute-done.14.refs_4_), channel_id=1, source_target_pairs={{0,8},{8,0},{16,24},{24,16},{1,9},{9,1},{17,25},{25,17},{2,10},{10... | collective-permute-start | bytes 2654216 | tf_op jit(solution)/shard_map/ppermute | solution.py:367
  155.7 15.2 %copy-start.21 = (f32[24,72,128]{2,1,0:T(8,128)}, f32[24,72,128]{2,1,0:T(8,128)S(1)}, u32[]{:S(2)}) copy-start(f32[24,72,128]{2,1,0:T(8,128)S(1)} %collective-permute-done.16.refs_3_) | copy-start | bytes 2654212
  189.7 9.8 %collective-permute-start.20 = (f32[4,12,72,128]{3,2,1,0:T(8,128)}, f32[4,12,72,128]{3,2,1,0:T(8,128)S(1)}, u32[]{:S(2)}, u32[]{:S(2)}) collective-permute-start(f32[4,12,72,128]{3,2,1,0:T(8,128)} %all-to-all-done.2.refs_5_), channel_id=1, source_target_pairs={{0,1},{1,0},{2,3},{3,2},{4,5},{5,4},{6,7},{7,6},{8,9},{9,8},{10,11... | collective-permute-start | bytes 5308424 | tf_op jit(solution)/shard_map/ppermute | solution.py:367
  196.0 82.9 %collective-permute-start.19 = (f32[4,12,72,128]{3,2,1,0:T(8,128)}, f32[4,12,72,128]{3,2,1,0:T(8,128)S(1)}, u32[]{:S(2)}, u32[]{:S(2)}) collective-permute-start(f32[4,12,72,128]{3,2,1,0:T(8,128)} %get-tuple-element.85), channel_id=1, source_target_pairs={{0,1},{1,0},{2,3},{3,2},{4,5},{5,4},{6,7},{7,6},{8,9},{9,8},{10,11... | collective-permute-start | bytes 5308424 | tf_op jit(solution)/shard_map/ppermute | solution.py:367
  199.5 1.2 copy-start.16
  215.9 21.1 %collective-permute-start.21 = (f32[24,72,128]{2,1,0:T(8,128)}, f32[24,72,128]{2,1,0:T(8,128)S(1)}, u32[]{:S(2)}, u32[]{:S(2)}) collective-permute-start(f32[24,72,128]{2,1,0:T(8,128)} %get-tuple-element.93), channel_id=1, source_target_pairs={{0,8},{8,0},{16,24},{24,16},{1,9},{9,1},{17,25},{25,17},{2,10},{10... | collective-permute-start | bytes 2654216 | tf_op jit(solution)/shard_map/ppermute | solution.py:367
  216.2 20.8 %collective-permute-start.22 = (f32[24,72,128]{2,1,0:T(8,128)}, f32[24,72,128]{2,1,0:T(8,128)S(1)}, u32[]{:S(2)}, u32[]{:S(2)}) collective-permute-start(f32[24,72,128]{2,1,0:T(8,128)} %get-tuple-element.94), channel_id=1, source_target_pairs={{0,16},{8,24},{16,0},{24,8},{1,17},{9,25},{17,1},{25,9},{2,18},{10... | collective-permute-start | bytes 2654216 | tf_op jit(solution)/shard_map/ppermute | solution.py:367
  237.1 1.0 copy-start.13
  238.0 21.2 %collective-permute-start.23 = (f32[24,72,128]{2,1,0:T(8,128)}, f32[24,72,128]{2,1,0:T(8,128)S(1)}, u32[]{:S(2)}, u32[]{:S(2)}) collective-permute-start(f32[24,72,128]{2,1,0:T(8,128)} %get-tuple-element.95), channel_id=1, source_target_pairs={{0,8},{8,0},{16,24},{24,16},{1,9},{9,1},{17,25},{25,17},{2,10},{10... | collective-permute-start | bytes 2654216 | tf_op jit(solution)/shard_map/ppermute | solution.py:367
  238.9 20.3 %collective-permute-start.24 = (f32[24,72,128]{2,1,0:T(8,128)}, f32[24,72,128]{2,1,0:T(8,128)S(1)}, u32[]{:S(2)}, u32[]{:S(2)}) collective-permute-start(f32[24,72,128]{2,1,0:T(8,128)} %get-tuple-element.97), channel_id=1, source_target_pairs={{0,16},{8,24},{16,0},{24,8},{1,17},{9,25},{17,1},{25,9},{2,18},{10... | collective-permute-start | bytes 2654216 | tf_op jit(solution)/shard_map/ppermute | solution.py:367
  259.3 1.9 copy-start.7
  259.3 1.9 copy-start.11
  259.3 25.7 %collective-permute-start.27 = (f32[24,72,128]{2,1,0:T(8,128)}, f32[24,72,128]{2,1,0:T(8,128)}, u32[]{:S(2)}, u32[]{:S(2)}) collective-permute-start(f32[24,72,128]{2,1,0:T(8,128)} %add.163), channel_id=1, source_target_pairs={{0,16},{8,24},{16,0},{24,8},{1,17},{9,25},{17,1},{25,9},{2,18},{10... | collective-permute-start | bytes 2654216 | tf_op jit(solution)/shard_map/ppermute | solution.py:367
  260.6 27.6 %collective-permute-start.26 = (f32[24,72,128]{2,1,0:T(8,128)}, f32[24,72,128]{2,1,0:T(8,128)}, u32[]{:S(2)}, u32[]{:S(2)}) collective-permute-start(f32[24,72,128]{2,1,0:T(8,128)} %add.162), channel_id=1, source_target_pairs={{0,8},{8,0},{16,24},{24,16},{1,9},{9,1},{17,25},{25,17},{2,10},{10... | collective-permute-start | bytes 2654216 | tf_op jit(solution)/shard_map/ppermute | solution.py:367
  261.2 17.8 %copy-start.5 = (f32[4,12,72,128]{3,2,1,0:T(8,128)S(1)}, f32[4,12,72,128]{3,2,1,0:T(8,128)}, u32[]{:S(2)}) copy-start(f32[4,12,72,128]{3,2,1,0:T(8,128)} %get-tuple-element.84) | copy-start | bytes 5308420
  276.5 13.0 %collective-permute-start.25 = (f32[4,12,72,128]{3,2,1,0:T(8,128)}, f32[4,12,72,128]{3,2,1,0:T(8,128)}, u32[]{:S(2)}, u32[]{:S(2)}) collective-permute-start(f32[4,12,72,128]{3,2,1,0:T(8,128)} %get-tuple-element.111), channel_id=1, source_target_pairs={{0,1},{1,0},{2,3},{3,2},{4,5},{5,4},{6,7},{7,6},{8,9},{9,8},{10,11... | collective-permute-start | bytes 5308424 | tf_op jit(solution)/shard_map/ppermute | solution.py:367
  280.3 9.2 %copy-start.6 = (f32[4,12,72,128]{3,2,1,0:T(8,128)S(1)}, f32[4,12,72,128]{3,2,1,0:T(8,128)}, u32[]{:S(2)}) copy-start(f32[4,12,72,128]{3,2,1,0:T(8,128)} %get-tuple-element.110) | copy-start | bytes 5308420
  280.3 63.9 %all-to-all-start.1 = ((f32[4,12,72,128]{3,2,1,0:T(8,128)}), f32[4,12,72,128]{3,2,1,0:T(8,128)S(1)}, u32[]{:S(2)}, u32[]{:S(2)}) async-start(f32[4,12,72,128]{3,2,1,0:T(8,128)} %add.159), calls=%async_computation.1 | async-start | bytes 3538944 | tf_op jit(solution)/shard_map/all_to_all | solution.py:445
  285.0 49.4 %copy-start.15 = (f32[24,72,128]{2,1,0:T(8,128)S(1)}, f32[24,72,128]{2,1,0:T(8,128)}, u32[]{:S(2)}) copy-start(f32[24,72,128]{2,1,0:T(8,128)} %get-tuple-element.131) | copy-start | bytes 2654212
  286.9 49.8 %copy-start.2 = (f32[24,72,128]{2,1,0:T(8,128)}, f32[24,72,128]{2,1,0:T(8,128)S(1)}, u32[]{:S(2)}) copy-start(f32[24,72,128]{2,1,0:T(8,128)S(1)} %add_add_fusion.2) | copy-start | bytes 2654212
  286.9 47.5 %collective-permute-start.34 = (f32[24,72,128]{2,1,0:T(8,128)S(1)}, f32[24,72,128]{2,1,0:T(8,128)S(1)}, u32[]{:S(2)}, u32[]{:S(2)}) collective-permute-start(f32[24,72,128]{2,1,0:T(8,128)S(1)} %add_add_fusion.2), channel_id=1, source_target_pairs={{0,2},{6,4},{1,3},{7,5},{8,10},{14,12},{9,11},{15,13},{16,18},{22,... | collective-permute-start | bytes 2654216 | tf_op jit(solution)/shard_map/ppermute | solution.py:371
  288.2 46.1 %collective-permute-start.29 = (f32[24,72,128]{2,1,0:T(8,128)}, f32[24,72,128]{2,1,0:T(8,128)S(1)}, u32[]{:S(2)}, u32[]{:S(2)}) collective-permute-start(f32[24,72,128]{2,1,0:T(8,128)} %get-tuple-element.122), channel_id=1, source_target_pairs={{0,16},{8,24},{16,0},{24,8},{1,17},{9,25},{17,1},{25,9},{2,18},{10... | collective-permute-start | bytes 2654216 | tf_op jit(solution)/shard_map/ppermute | solution.py:367
  288.6 49.4 %collective-permute-start.28 = (f32[24,72,128]{2,1,0:T(8,128)}, f32[24,72,128]{2,1,0:T(8,128)S(1)}, u32[]{:S(2)}, u32[]{:S(2)}) collective-permute-start(f32[24,72,128]{2,1,0:T(8,128)} %get-tuple-element.120), channel_id=1, source_target_pairs={{0,8},{8,0},{16,24},{24,16},{1,9},{9,1},{17,25},{25,17},{2,10},{10... | collective-permute-start | bytes 2654216 | tf_op jit(solution)/shard_map/ppermute | solution.py:367
  289.5 48.5 %copy-start.12 = (f32[24,72,128]{2,1,0:T(8,128)S(1)}, f32[24,72,128]{2,1,0:T(8,128)}, u32[]{:S(2)}) copy-start(f32[24,72,128]{2,1,0:T(8,128)} %get-tuple-element.124) | copy-start | bytes 2654212
  336.7 22.2 %collective-permute-start.35 = (f32[24,72,128]{2,1,0:T(8,128)}, f32[24,72,128]{2,1,0:T(8,128)}, u32[]{:S(2)}, u32[]{:S(2)}) collective-permute-start(f32[24,72,128]{2,1,0:T(8,128)} %add_add_fusion.1), channel_id=1, source_target_pairs={{0,2},{2,4},{1,3},{3,5},{8,10},{10,12},{9,11},{11,13},{16,18},{18,... | collective-permute-start | bytes 2654216 | tf_op jit(solution)/shard_map/ppermute | solution.py:371
  339.0 20.3 %collective-permute-start.31 = (f32[24,72,128]{2,1,0:T(8,128)}, f32[24,72,128]{2,1,0:T(8,128)}, u32[]{:S(2)}, u32[]{:S(2)}) collective-permute-start(f32[24,72,128]{2,1,0:T(8,128)} %add.164), channel_id=1, source_target_pairs={{0,16},{8,24},{16,0},{24,8},{1,17},{9,25},{17,1},{25,9},{2,18},{10... | collective-permute-start | bytes 2654216 | tf_op jit(solution)/shard_map/ppermute | solution.py:367
  339.3 20.0 %collective-permute-start.30 = (f32[24,72,128]{2,1,0:T(8,128)}, f32[24,72,128]{2,1,0:T(8,128)}, u32[]{:S(2)}, u32[]{:S(2)}) collective-permute-start(f32[24,72,128]{2,1,0:T(8,128)} %get-tuple-element.123), channel_id=1, source_target_pairs={{0,8},{8,0},{16,24},{24,16},{1,9},{9,1},{17,25},{25,17},{2,10},{10... | collective-permute-start | bytes 2654216 | tf_op jit(solution)/shard_map/ppermute | solution.py:367
  340.2 21.6 %collective-permute-start.37 = (f32[24,72,128]{2,1,0:T(8,128)}, f32[24,72,128]{2,1,0:T(8,128)}, u32[]{:S(2)}, u32[]{:S(2)}) collective-permute-start(f32[24,72,128]{2,1,0:T(8,128)} %add_add_fusion.1), channel_id=1, source_target_pairs={{4,2},{6,4},{5,3},{7,5},{12,10},{14,12},{13,11},{15,13},{20,18},{2... | collective-permute-start | bytes 2654216 | tf_op jit(solution)/shard_map/ppermute | solution.py:371
  344.2 85.2 %all-to-all-start.3 = ((f32[4,12,72,128]{3,2,1,0:T(8,128)}), f32[4,12,72,128]{3,2,1,0:T(8,128)S(1)}, u32[]{:S(2)}, u32[]{:S(2)}) async-start(f32[4,12,72,128]{3,2,1,0:T(8,128)} %add.160), calls=%async_computation.3 | async-start | bytes 3538944 | tf_op jit(solution)/shard_map/all_to_all | solution.py:445
  365.9 52.5 %collective-permute-start.38 = (f32[24,72,128]{2,1,0:T(8,128)}, f32[24,72,128]{2,1,0:T(8,128)}, u32[]{:S(2)}, u32[]{:S(2)}) collective-permute-start(f32[24,72,128]{2,1,0:T(8,128)} %get-tuple-element.134), channel_id=1, source_target_pairs={{2,0},{4,2},{6,4},{3,1},{5,3},{7,5},{10,8},{12,10},{14,12},{11,9},... | collective-permute-start | bytes 2654216 | tf_op jit(solution)/shard_map/ppermute | solution.py:371
  370.2 48.2 %collective-permute-start.36 = (f32[24,72,128]{2,1,0:T(8,128)}, f32[24,72,128]{2,1,0:T(8,128)}, u32[]{:S(2)}, u32[]{:S(2)}) collective-permute-start(f32[24,72,128]{2,1,0:T(8,128)} %get-tuple-element.133), channel_id=1, source_target_pairs={{0,2},{2,4},{4,6},{1,3},{3,5},{5,7},{8,10},{10,12},{12,14},{9,11},... | collective-permute-start | bytes 2654216 | tf_op jit(solution)/shard_map/ppermute | solution.py:371
  372.1 46.3 %collective-permute-start.33 = (f32[24,72,128]{2,1,0:T(8,128)}, f32[24,72,128]{2,1,0:T(8,128)}, u32[]{:S(2)}, u32[]{:S(2)}) collective-permute-start(f32[24,72,128]{2,1,0:T(8,128)} %get-tuple-element.128), channel_id=1, source_target_pairs={{0,16},{8,24},{16,0},{24,8},{1,17},{9,25},{17,1},{25,9},{2,18},{10... | collective-permute-start | bytes 2654216 | tf_op jit(solution)/shard_map/ppermute | solution.py:367
  373.0 45.4 %collective-permute-start.32 = (f32[24,72,128]{2,1,0:T(8,128)}, f32[24,72,128]{2,1,0:T(8,128)}, u32[]{:S(2)}, u32[]{:S(2)}) collective-permute-start(f32[24,72,128]{2,1,0:T(8,128)} %add.161), channel_id=1, source_target_pairs={{0,8},{8,0},{16,24},{24,16},{1,9},{9,1},{17,25},{25,17},{2,10},{10... | collective-permute-start | bytes 2654216 | tf_op jit(solution)/shard_map/ppermute | solution.py:367
  422.5 4.7 %collective-permute-start.39 = (f32[12,72,128]{2,1,0:T(8,128)}, f32[12,72,128]{2,1,0:T(8,128)}, u32[]{:S(2)}, u32[]{:S(2)}) collective-permute-start(f32[12,72,128]{2,1,0:T(8,128)} %constant_dynamic-slice_fusion), channel_id=1, source_target_pairs={{0,1},{1,0},{2,3},{3,2},{4,5},{5,4},{6,7},{7,6},{8,9},{9,8},{10,11... | collective-permute-start | bytes 1327112 | tf_op jit(solution)/shard_map/ppermute | solution.py:367
  429.4 1.2 copy-start.1
  (3 other events, 2.8 us)

commit v7 on v6

--- a/solution.py
+++ b/solution.py
@@ -482,7 +482,7 @@
     sums, far = pair(1, 2, sums, terms[2], after=done)
     done = (side3, handed0)
     side2, far3 = x_swap(side[2] + handed2, done), y_swap(far[3] + handed3, done)
-    sums, own = pair(1, 0, sums, terms[0], after=done, last=True)
+    sums, own = pair(1, 0, sums, terms[0], after=done + (back[0],), last=True)
     total = core_sum(*sums)
     back.append(send_back(total))
     done = (side2, far3)

time: 440 us -> 415 us (0.943)
  waiting for transfers between devices: 181 us -> 148 us
  starting transfers between devices: 79 us -> 85.6 us
    ppermute x10, waiting for transfers between devices: 144 us -> 100 us  [along(): return lax.ppermute(value, 'z', pairs)]
    ppermute x30, waiting for transfers between devices: 36.3 us -> 47.7 us  [swap(): return lax.ppermute(value, axis, [(i, i ^ flip) for i in range(size)])]
    ppermute x30, starting transfers between devices: 34.5 us -> 40.4 us  [swap(): return lax.ppermute(value, axis, [(i, i ^ flip) for i in range(size)])]
  transfers between devices with their start and end apart: 44 -> 44, of which waited for: 20 -> 20; matrix products, arithmetic and copies ran while one was open for 8% -> 9% of each run, Pallas kernels for 28% -> 30%
where the time goes in v7:
time: 415 us; the launch traced here: 411 us
  waiting for transfers between devices  148 us (36%)
  Pallas kernels  132 us (32%)
  starting transfers between devices  85.6 us (21%)
  other arithmetic  35.1 us (8%)
  local copies, waits for them, and re-layouts  10.1 us (2%)
    pallas_call x8, Pallas kernels, pair_solve(): pl.pallas_call(functools.partial(pair_kernel, count, (zs, planes), layout...  121 us
    ppermute x10, waiting for transfers between devices, along(): return lax.ppermute(value, 'z', pairs)  100 us
    ppermute x30, waiting for transfers between devices, swap(): return lax.ppermute(value, axis, [(i, i ^ flip) for i in range(size)])  47.7 us
    ppermute x30, starting transfers between devices, swap(): return lax.ppermute(value, axis, [(i, i ^ flip) for i in range(size)])  40.4 us
    ppermute x10, starting transfers between devices, along(): return lax.ppermute(value, 'z', pairs)  26 us
    all_to_all x2, starting transfers between devices, send_back(): return lax.all_to_all(total, 'z', split_axis=0, concat_axis=0, tiled=True)  8.79 us
  transfers between devices with their start and end apart: 44, of which 20 were waited for; matrix products, arithmetic and copies ran while one was open for 9% of the time, Pallas kernels for 30%

profile of v7, /device:TPU:17, one launch (start us, length us, event | category | flops | bytes accessed | tf_op | source)
XLA Modules:
  0.0 411.4 jit_solution(15820934860466106429)
XLA Ops:
  0.0 2.0 copy-done
  2.0 4.3 %shard_map.28 = (f32[3456,128]{1,0:T(8,128)}, f32[3456,128]{1,0:T(8,128)}) custom-call(f32[12,8,9216]{2,1,0:T(8,128)S(1)} %bitcast.20), custom_call_target="tpu_custom_call" | custom-call | tf_op jit(solution)/shard_map/pallas_call | solution.py:326
  6.3 4.6 %all-to-all-start = ((f32[4,12,72,128]{3,2,1,0:T(8,128)}), f32[4,12,72,128]{3,2,1,0:T(8,128)S(1)}, u32[]{:S(2)}, u32[]{:S(2)}) async-start(f32[4,12,72,128]{3,2,1,0:T(8,128)} %bitcast.3), calls=%async_computation | async-start | bytes 3538944 | tf_op jit(solution)/shard_map/all_to_all | solution.py:457
  12.0 1.3 collective-permute-start
  13.3 1.4 collective-permute-done
  15.9 1.3 collective-permute-start.1
  17.2 3.1 collective-permute-start.3
  20.3 2.2 collective-permute-start.4
  22.5 1.3 collective-permute-start.5
  23.8 13.2 %collective-permute-done.1.refs_1_ = f32[24,72,128]{2,1,0:T(8,128)} collective-permute-done((f32[24,72,128]{2,1,0:T(8,128)S(1)}, f32[24,72,128]{2,1,0:T(8,128)}, u32[]{:S(2)}, u32[]{:S(2)}) %collective-permute-start.1) | collective-permute-done | bytes 884768 | tf_op jit(solution)/shard_map/ppermute | solution.py:367
  38.2 30.1 %collective-permute-done.3 = f32[24,72,128]{2,1,0:T(8,128)} collective-permute-done((f32[24,72,128]{2,1,0:T(8,128)S(1)}, f32[24,72,128]{2,1,0:T(8,128)}, u32[]{:S(2)}, u32[]{:S(2)}) %collective-permute-start.3) | collective-permute-done | bytes 884768 | tf_op jit(solution)/shard_map/ppermute | solution.py:371
  68.3 1.9 collective-permute-start.7
  70.2 3.5 collective-permute-start.8
  73.7 1.3 broadcast_select_fusion.1.refs_2_
  75.0 1.3 collective-permute-start.6
  77.5 3.1 collective-permute-start.18
  80.6 9.1 %collective-permute-done.7 = f32[24,72,128]{2,1,0:T(8,128)S(1)} collective-permute-done((f32[24,72,128]{2,1,0:T(8,128)}, f32[24,72,128]{2,1,0:T(8,128)S(1)}, u32[]{:S(2)}, u32[]{:S(2)}) %collective-permute-start.7) | collective-permute-done | bytes 884768 | tf_op jit(solution)/shard_map/ppermute | solution.py:371
  91.4 2.3 collective-permute-done.6.refs_2_
  94.7 2.2 collective-permute-start.10
  99.4 4.8 %fusion.refs_8_.refs_9_.refs_10_ = f32[48,96,256]{2,1,0:T(8,128)} fusion(s32[256]{0:T(256)S(1)} %get-tuple-element.141, s32[256]{0:T(256)S(1)} %get-tuple-element.142, s32[96]{0:T(128)S(1)} %iota_add_fusion, s32[256]{0:T(256)S(1)} %get-tuple-element.140, s32[48]{0:T(128)S(1)} %iota_multiply_fusion, pred[96]{0:T(512)(128)(4,1)S(1)} %iota_compare_fusion, ...), kind=kLoop, calls=%fused_computation.4 | loop fusion | flops 31850496 | bytes 4722592 | tf_op jit(solution)/shard_map/div | solution.py:75
  104.8 7.0 %collective-permute-done.10 = f32[24,72,128]{2,1,0:T(8,128)} collective-permute-done((f32[24,72,128]{2,1,0:T(8,128)}, f32[24,72,128]{2,1,0:T(8,128)}, u32[]{:S(2)}, u32[]{:S(2)}) %collective-permute-start.10) | collective-permute-done | bytes 884768 | tf_op jit(solution)/shard_map/ppermute | solution.py:371
  112.0 2.8 collective-permute-done.11.refs_3_
  116.0 1.5 collective-permute-start.14
  117.5 5.8 %all-to-all-start.2 = ((f32[4,12,72,128]{3,2,1,0:T(8,128)}), f32[4,12,72,128]{3,2,1,0:T(8,128)}, u32[]{:S(2)}, u32[]{:S(2)}) async-start(f32[4,12,72,128]{3,2,1,0:T(8,128)} %bitcast.7), calls=%async_computation.2 | async-start | bytes 3538944 | tf_op jit(solution)/shard_map/all_to_all | solution.py:467
  123.3 15.3 %shard_map.29 = (f32[96,72,128]{2,1,0:T(8,128)}, f32[96,72,128]{2,1,0:T(8,128)}) custom-call(s32[2]{0:T(128)} %pad_add_fusion.refs_0_, f32[24,72,128]{2,1,0:T(8,128)} %copy-done.6, f32[24,72,128]{2,1,0:T(8,128)} %copy-done.7, f32[24,72,128]{2,1,0:T(8,128)} %add.154.refs_3_, f32[24,72,128]{2,1,0:T(8,128)} %copy-done.8, f32[4,12,72,128]{3,2,1,0:T(8,128)} %copy-done.4, ...), custom_call_target="tpu_custom_call" | custom-call | flops 16986931200 | bytes 17694720 | tf_op jit(solution)/shard_map/pallas_call | solution.py:276
  139.2 15.2 %shard_map.30 = (f32[96,72,128]{2,1,0:T(8,128)}, f32[96,72,128]{2,1,0:T(8,128)}) custom-call(s32[2]{0:T(128)} %pad_add_fusion.refs_0_, f32[24,72,128]{2,1,0:T(8,128)} %collective-permute-done.1.refs_1_, f32[24,72,128]{2,1,0:T(8,128)} %copy-done.14, f32[24,72,128]{2,1,0:T(8,128)} %collective-permute-done.11.refs_3_, ...), custom_call_target="tpu_custom_call" | custom-call | flops 16986931200 | bytes 17694720 | tf_op jit(solution)/shard_map/pallas_call | solution.py:276
  155.7 15.1 %shard_map.31 = (f32[96,72,128]{2,1,0:T(8,128)}, f32[96,72,128]{2,1,0:T(8,128)}) custom-call(s32[2]{0:T(128)} %pad_add_fusion.refs_0_, f32[24,72,128]{2,1,0:T(8,128)} %collective-permute-done.5.refs_1_, f32[24,72,128]{2,1,0:T(8,128)} %copy-done.12, f32[24,72,128]{2,1,0:T(8,128)} %collective-permute-done.12.refs_3_, ...), custom_call_target="tpu_custom_call" | custom-call | flops 16986931200 | bytes 17694720 | tf_op jit(solution)/shard_map/pallas_call | solution.py:276
  170.9 2.6 collective-permute-done.17.refs_4_
  174.5 15.2 %shard_map.32 = (f32[4,12,72,128]{3,2,1,0:T(8,128)}, f32[4,12,72,128]{3,2,1,0:T(8,128)}, f32[96,72,128]{2,1,0:T(8,128)}) custom-call(s32[2]{0:T(128)} %pad_add_fusion.refs_0_, f32[24,72,128]{2,1,0:T(8,128)} %collective-permute-done.2.refs_1_, f32[24,72,128]{2,1,0:T(8,128)} %copy-done.15, f32[24,72,128]{2,1,0:T(8,128)} %copy-done.16, ...), custom_call_target="tpu_custom_call" | custom-call | flops 16986931200 | bytes 17694720 | tf_op jit(solution)/shard_map/pallas_call | solution.py:276
  189.6 6.3 %collective-permute-start.19 = (f32[4,12,72,128]{3,2,1,0:T(8,128)}, f32[4,12,72,128]{3,2,1,0:T(8,128)S(1)}, u32[]{:S(2)}, u32[]{:S(2)}) collective-permute-start(f32[4,12,72,128]{3,2,1,0:T(8,128)} %get-tuple-element.85), channel_id=1, source_target_pairs={{0,1},{1,0},{2,3},{3,2},{4,5},{5,4},{6,7},{7,6},{8,9},{9,8},{10,11... | collective-permute-start | bytes 5308424 | tf_op jit(solution)/shard_map/ppermute | solution.py:367
  196.0 3.4 collective-permute-done.19
  199.5 2.9 add.159
  202.4 4.5 %all-to-all-start.1 = ((f32[4,12,72,128]{3,2,1,0:T(8,128)}), f32[4,12,72,128]{3,2,1,0:T(8,128)S(1)}, u32[]{:S(2)}, u32[]{:S(2)}) async-start(f32[4,12,72,128]{3,2,1,0:T(8,128)} %add.159), calls=%async_computation.1 | async-start | bytes 3538944 | tf_op jit(solution)/shard_map/all_to_all | solution.py:445
  206.9 1.3 copy-done.11
  208.2 15.1 %shard_map.33 = (f32[96,72,128]{2,1,0:T(8,128)}, f32[24,72,128]{2,1,0:T(8,128)}, f32[24,72,128]{2,1,0:T(8,128)}, f32[24,72,128]{2,1,0:T(8,128)}, f32[24,72,128]{2,1,0:T(8,128)}) custom-call(s32[2]{0:T(128)} %pad_add_fusion.refs_0_, f32[24,72,128]{2,1,0:T(8,128)} %collective-permute-done.2.refs_1_, f32[24,72,128]{2,1,0:T(8,128)} %copy-done.15, ...), custom_call_target="tpu_custom_call" | custom-call | flops 16986931200 | bytes 17694720 | tf_op jit(solution)/shard_map/pallas_call | solution.py:276
  223.9 15.1 %shard_map.34 = (f32[96,72,128]{2,1,0:T(8,128)}, f32[24,72,128]{2,1,0:T(8,128)}, f32[24,72,128]{2,1,0:T(8,128)}, f32[24,72,128]{2,1,0:T(8,128)}, f32[24,72,128]{2,1,0:T(8,128)}) custom-call(s32[2]{0:T(128)} %pad_add_fusion.refs_0_, f32[24,72,128]{2,1,0:T(8,128)} %collective-permute-done.1.refs_1_, f32[24,72,128]{2,1,0:T(8,128)} %copy-done.14, ...), custom_call_target="tpu_custom_call" | custom-call | flops 16986931200 | bytes 17694720 | tf_op jit(solution)/shard_map/pallas_call | solution.py:276
  239.0 4.8 %collective-permute-done.21 = f32[24,72,128]{2,1,0:T(8,128)S(1)} collective-permute-done((f32[24,72,128]{2,1,0:T(8,128)}, f32[24,72,128]{2,1,0:T(8,128)S(1)}, u32[]{:S(2)}, u32[]{:S(2)}) %collective-permute-start.21) | collective-permute-done | bytes 884768 | tf_op jit(solution)/shard_map/ppermute | solution.py:367
  246.1 15.1 %shard_map.35 = (f32[96,72,128]{2,1,0:T(8,128)}, f32[24,72,128]{2,1,0:T(8,128)}, f32[24,72,128]{2,1,0:T(8,128)}, f32[24,72,128]{2,1,0:T(8,128)}, f32[24,72,128]{2,1,0:T(8,128)}) custom-call(s32[2]{0:T(128)} %pad_add_fusion.refs_0_, f32[24,72,128]{2,1,0:T(8,128)} %collective-permute-done.5.refs_1_, f32[24,72,128]{2,1,0:T(8,128)} %copy-done.12, ...), custom_call_target="tpu_custom_call" | custom-call | flops 16986931200 | bytes 17694720 | tf_op jit(solution)/shard_map/pallas_call | solution.py:276
  261.3 2.2 add.163
  263.5 2.4 add.162
  265.9 1.2 collective-permute-start.27
  267.5 15.2 %shard_map.36 = (f32[4,12,72,128]{3,2,1,0:T(8,128)}, f32[4,12,72,128]{3,2,1,0:T(8,128)}, f32[24,72,128]{2,1,0:T(8,128)}, f32[24,72,128]{2,1,0:T(8,128)}, f32[24,72,128]{2,1,0:T(8,128)}, /*index=5*/f32[24,72,128]{2,1,0:T(8,128)}) custom-call(s32[2]{0:T(128)} %pad_add_fusion.refs_0_, f32[24,72,128]{2,1,0:T(8,128)} %copy-done.6, f32[24,72,128]{2,1,0:T(8,128)} %copy-done.7, ...), custom_call_target="tpu_custom_call" | custom-call | flops 16986931200 | bytes 17694720 | tf_op jit(solution)/shard_map/pallas_call | solution.py:276
  282.7 3.3 collective-permute-start.25
  287.4 1.4 add_add_fusion.2
  289.8 1.5 collective-permute-start.34
  291.4 12.4 %collective-permute-done.28 = f32[24,72,128]{2,1,0:T(8,128)S(1)} collective-permute-done((f32[24,72,128]{2,1,0:T(8,128)}, f32[24,72,128]{2,1,0:T(8,128)S(1)}, u32[]{:S(2)}, u32[]{:S(2)}) %collective-permute-start.28) | collective-permute-done | bytes 884768 | tf_op jit(solution)/shard_map/ppermute | solution.py:367
  303.8 2.2 add.164
  307.2 2.1 collective-permute-start.30
  309.6 2.4 add_add_fusion.1
  312.0 1.4 add.160
  313.4 1.3 collective-permute-start.35
  314.7 4.0 collective-permute-start.37
  318.7 4.3 %all-to-all-start.3 = ((f32[4,12,72,128]{3,2,1,0:T(8,128)}), f32[4,12,72,128]{3,2,1,0:T(8,128)S(1)}, u32[]{:S(2)}, u32[]{:S(2)}) async-start(f32[4,12,72,128]{3,2,1,0:T(8,128)} %add.160), calls=%async_computation.3 | async-start | bytes 3538944 | tf_op jit(solution)/shard_map/all_to_all | solution.py:445
  322.9 2.4 add.161
  326.9 5.7 %collective-permute-done.35 = f32[24,72,128]{2,1,0:T(8,128)} collective-permute-done((f32[24,72,128]{2,1,0:T(8,128)}, f32[24,72,128]{2,1,0:T(8,128)}, u32[]{:S(2)}, u32[]{:S(2)}) %collective-permute-start.35) | collective-permute-done | bytes 884768 | tf_op jit(solution)/shard_map/ppermute | solution.py:371
  332.6 1.3 collective-permute-done.37
  333.9 4.0 add_select_fusion
  337.9 4.3 %collective-permute-start.38 = (f32[24,72,128]{2,1,0:T(8,128)}, f32[24,72,128]{2,1,0:T(8,128)}, u32[]{:S(2)}, u32[]{:S(2)}) collective-permute-start(f32[24,72,128]{2,1,0:T(8,128)} %get-tuple-element.134), channel_id=1, source_target_pairs={{2,0},{4,2},{6,4},{3,1},{5,3},{7,5},{10,8},{12,10},{14,12},{11,9},... | collective-permute-start | bytes 2654216 | tf_op jit(solution)/shard_map/ppermute | solution.py:371
  342.2 1.9 collective-permute-start.36
  344.2 46.2 %collective-permute-done.38 = f32[24,72,128]{2,1,0:T(8,128)} collective-permute-done((f32[24,72,128]{2,1,0:T(8,128)}, f32[24,72,128]{2,1,0:T(8,128)}, u32[]{:S(2)}, u32[]{:S(2)}) %collective-permute-start.38) | collective-permute-done | bytes 884768 | tf_op jit(solution)/shard_map/ppermute | solution.py:371
  390.4 2.4 add_add_fusion
  394.6 5.3 %collective-permute-start.39 = (f32[12,72,128]{2,1,0:T(8,128)}, f32[12,72,128]{2,1,0:T(8,128)}, u32[]{:S(2)}, u32[]{:S(2)}) collective-permute-start(f32[12,72,128]{2,1,0:T(8,128)} %constant_dynamic-slice_fusion), channel_id=1, source_target_pairs={{0,1},{1,0},{2,3},{3,2},{4,5},{5,4},{6,7},{7,6},{8,9},{9,8},{10,11... | collective-permute-start | bytes 1327112 | tf_op jit(solution)/shard_map/ppermute | solution.py:367
  399.9 1.8 collective-permute-done.39
  405.1 6.3 %shard_map.37 = f32[12,8,9216]{2,1,0:T(8,128)} custom-call(f32[3456,128]{1,0:T(8,128)S(1)} %bitcast.18, f32[3456,128]{1,0:T(8,128)S(1)} %bitcast.19, f32[1728,128]{1,0:T(8,128)S(1)} %bitcast.21), custom_call_target="tpu_custom_call" | custom-call | tf_op jit(solution)/shard_map/pallas_call | solution.py:355
  (96 shorter events, 28.5 us)
Async XLA Ops:
  0.0 2.0 copy-start
  6.3 62.0 %all-to-all-start = ((f32[4,12,72,128]{3,2,1,0:T(8,128)}), f32[4,12,72,128]{3,2,1,0:T(8,128)S(1)}, u32[]{:S(2)}, u32[]{:S(2)}) async-start(f32[4,12,72,128]{3,2,1,0:T(8,128)} %bitcast.3), calls=%async_computation | async-start | bytes 3538944 | tf_op jit(solution)/shard_map/all_to_all | solution.py:457
  12.0 2.7 collective-permute-start
  15.9 88.3 %copy-start.6 = (f32[24,72,128]{2,1,0:T(8,128)}, f32[24,72,128]{2,1,0:T(8,128)S(1)}, u32[]{:S(2)}) copy-start(f32[24,72,128]{2,1,0:T(8,128)S(1)} %pad_maximum_fusion.refs_1_) | copy-start | bytes 2654212
  15.9 21.0 %collective-permute-start.1 = (f32[24,72,128]{2,1,0:T(8,128)S(1)}, f32[24,72,128]{2,1,0:T(8,128)}, u32[]{:S(2)}, u32[]{:S(2)}) collective-permute-start(f32[24,72,128]{2,1,0:T(8,128)S(1)} %pad_maximum_fusion.refs_1_), channel_id=1, source_target_pairs={{0,8},{8,0},{16,24},{24,16},{1,9},{9,1},{17,25},{25,17},{2,10},{10... | collective-permute-start | bytes 2654216 | tf_op jit(solution)/shard_map/ppermute | solution.py:367
  17.2 51.1 %collective-permute-start.3 = (f32[24,72,128]{2,1,0:T(8,128)S(1)}, f32[24,72,128]{2,1,0:T(8,128)}, u32[]{:S(2)}, u32[]{:S(2)}) collective-permute-start(f32[24,72,128]{2,1,0:T(8,128)S(1)} %pad_maximum_fusion.refs_1_), channel_id=1, source_target_pairs={{0,2},{2,4},{4,6},{1,3},{3,5},{5,7},{8,10},{10,12},{12,14},{9,11},... | collective-permute-start | bytes 2654216 | tf_op jit(solution)/shard_map/ppermute | solution.py:371
  20.3 48.0 %collective-permute-start.4 = (f32[24,72,128]{2,1,0:T(8,128)S(1)}, f32[24,72,128]{2,1,0:T(8,128)S(1)}, u32[]{:S(2)}, u32[]{:S(2)}) collective-permute-start(f32[24,72,128]{2,1,0:T(8,128)S(1)} %pad_maximum_fusion.refs_1_), channel_id=1, source_target_pairs={{2,0},{4,2},{6,4},{3,1},{5,3},{7,5},{10,8},{12,10},{14,12},{11,9},... | collective-permute-start | bytes 2654216 | tf_op jit(solution)/shard_map/ppermute | solution.py:371
  22.5 45.8 %collective-permute-start.5 = (f32[24,72,128]{2,1,0:T(8,128)S(1)}, f32[24,72,128]{2,1,0:T(8,128)}, u32[]{:S(2)}, u32[]{:S(2)}) collective-permute-start(f32[24,72,128]{2,1,0:T(8,128)S(1)} %pad_maximum_fusion.refs_1_), channel_id=1, source_target_pairs={{0,16},{8,24},{16,0},{24,8},{1,17},{9,25},{17,1},{25,9},{2,18},{10... | collective-permute-start | bytes 2654216 | tf_op jit(solution)/shard_map/ppermute | solution.py:367
  36.9 31.3 %collective-permute-start.2 = (f32[24,72,128]{2,1,0:T(8,128)}, f32[24,72,128]{2,1,0:T(8,128)}, u32[]{:S(2)}, u32[]{:S(2)}) collective-permute-start(f32[24,72,128]{2,1,0:T(8,128)} %collective-permute-done.1.refs_1_), channel_id=1, source_target_pairs={{0,16},{8,24},{16,0},{24,8},{1,17},{9,25},{17,1},{25,9},{2,18},{10... | collective-permute-start | bytes 2654216 | tf_op jit(solution)/shard_map/ppermute | solution.py:367
  68.3 35.9 %copy-start.4 = (f32[4,12,72,128]{3,2,1,0:T(8,128)}, f32[4,12,72,128]{3,2,1,0:T(8,128)S(1)}, u32[]{:S(2)}) copy-start(f32[4,12,72,128]{3,2,1,0:T(8,128)S(1)} %all-to-all-done.refs_5_) | copy-start | bytes 5308420
  68.3 21.4 %collective-permute-start.7 = (f32[24,72,128]{2,1,0:T(8,128)}, f32[24,72,128]{2,1,0:T(8,128)S(1)}, u32[]{:S(2)}, u32[]{:S(2)}) collective-permute-start(f32[24,72,128]{2,1,0:T(8,128)} %collective-permute-done.3), channel_id=1, source_target_pairs={{2,4},{4,6},{3,5},{5,7},{10,12},{12,14},{11,13},{13,15},{18,20},{2... | collective-permute-start | bytes 2654216 | tf_op jit(solution)/shard_map/ppermute | solution.py:371
  70.2 20.2 %collective-permute-start.8 = (f32[24,72,128]{2,1,0:T(8,128)S(1)}, f32[24,72,128]{2,1,0:T(8,128)S(1)}, u32[]{:S(2)}, u32[]{:S(2)}) collective-permute-start(f32[24,72,128]{2,1,0:T(8,128)S(1)} %collective-permute-done.4), channel_id=1, source_target_pairs={{2,0},{4,2},{3,1},{5,3},{10,8},{12,10},{11,9},{13,11},{18,16},{20,... | collective-permute-start | bytes 2654216 | tf_op jit(solution)/shard_map/ppermute | solution.py:371
  75.0 15.5 %copy-start.7 = (f32[24,72,128]{2,1,0:T(8,128)}, f32[24,72,128]{2,1,0:T(8,128)S(1)}, u32[]{:S(2)}) copy-start(f32[24,72,128]{2,1,0:T(8,128)S(1)} %broadcast_select_fusion.1.refs_2_) | copy-start | bytes 2654212
  75.0 18.8 %collective-permute-start.6 = (f32[24,72,128]{2,1,0:T(8,128)S(1)}, f32[24,72,128]{2,1,0:T(8,128)S(1)}, u32[]{:S(2)}, u32[]{:S(2)}) collective-permute-start(f32[24,72,128]{2,1,0:T(8,128)S(1)} %broadcast_select_fusion.1.refs_2_), channel_id=1, source_target_pairs={{0,16},{8,24},{16,0},{24,8},{1,17},{9,25},{17,1},{25,9},{2,18},{10... | collective-permute-start | bytes 2654216 | tf_op jit(solution)/shard_map/ppermute | solution.py:367
  76.3 18.4 %collective-permute-start.9 = (f32[24,72,128]{2,1,0:T(8,128)S(1)}, f32[24,72,128]{2,1,0:T(8,128)S(1)}, u32[]{:S(2)}, u32[]{:S(2)}) collective-permute-start(f32[24,72,128]{2,1,0:T(8,128)S(1)} %broadcast_select_fusion.1.refs_2_), channel_id=1, source_target_pairs={{0,8},{8,0},{16,24},{24,16},{1,9},{9,1},{17,25},{25,17},{2,10},{10... | collective-permute-start | bytes 2654216 | tf_op jit(solution)/shard_map/ppermute | solution.py:367
  77.5 45.8 %collective-permute-start.18 = (f32[4,12,72,128]{3,2,1,0:T(8,128)S(1)}, f32[4,12,72,128]{3,2,1,0:T(8,128)}, u32[]{:S(2)}, u32[]{:S(2)}) collective-permute-start(f32[4,12,72,128]{3,2,1,0:T(8,128)S(1)} %all-to-all-done.refs_5_), channel_id=1, source_target_pairs={{0,1},{1,0},{2,3},{3,2},{4,5},{5,4},{6,7},{7,6},{8,9},{9,8},{10,11... | collective-permute-start | bytes 5308424 | tf_op jit(solution)/shard_map/ppermute | solution.py:367
  93.7 1.0 copy-start.12
  94.7 2.2 copy-start.14
  94.7 17.2 %collective-permute-start.10 = (f32[24,72,128]{2,1,0:T(8,128)}, f32[24,72,128]{2,1,0:T(8,128)}, u32[]{:S(2)}, u32[]{:S(2)}) collective-permute-start(f32[24,72,128]{2,1,0:T(8,128)} %add.154.refs_3_), channel_id=1, source_target_pairs={{4,6},{2,0},{5,7},{3,1},{12,14},{10,8},{13,15},{11,9},{20,22},{18,... | collective-permute-start | bytes 2654216 | tf_op jit(solution)/shard_map/ppermute | solution.py:371
  96.9 17.8 %collective-permute-start.11 = (f32[24,72,128]{2,1,0:T(8,128)}, f32[24,72,128]{2,1,0:T(8,128)}, u32[]{:S(2)}, u32[]{:S(2)}) collective-permute-start(f32[24,72,128]{2,1,0:T(8,128)} %add.154.refs_3_), channel_id=1, source_target_pairs={{0,8},{8,0},{16,24},{24,16},{1,9},{9,1},{17,25},{25,17},{2,10},{10... | collective-permute-start | bytes 2654216 | tf_op jit(solution)/shard_map/ppermute | solution.py:367
  98.2 17.6 %collective-permute-start.12 = (f32[24,72,128]{2,1,0:T(8,128)}, f32[24,72,128]{2,1,0:T(8,128)}, u32[]{:S(2)}, u32[]{:S(2)}) collective-permute-start(f32[24,72,128]{2,1,0:T(8,128)} %add.154.refs_3_), channel_id=1, source_target_pairs={{0,16},{8,24},{16,0},{24,8},{1,17},{9,25},{17,1},{25,9},{2,18},{10... | collective-permute-start | bytes 2654216 | tf_op jit(solution)/shard_map/ppermute | solution.py:367
  112.0 11.3 %copy-start.8 = (f32[24,72,128]{2,1,0:T(8,128)}, f32[24,72,128]{2,1,0:T(8,128)S(1)}, u32[]{:S(2)}) copy-start(f32[24,72,128]{2,1,0:T(8,128)S(1)} %broadcast_select_fusion.refs_4_) | copy-start | bytes 2654212
  115.7 22.9 %collective-permute-start.13 = (f32[24,72,128]{2,1,0:T(8,128)S(1)}, f32[24,72,128]{2,1,0:T(8,128)}, u32[]{:S(2)}, u32[]{:S(2)}) collective-permute-start(f32[24,72,128]{2,1,0:T(8,128)S(1)} %broadcast_select_fusion.refs_4_), channel_id=1, source_target_pairs={{0,8},{8,0},{16,24},{24,16},{1,9},{9,1},{17,25},{25,17},{2,10},{10... | collective-permute-start | bytes 2654216 | tf_op jit(solution)/shard_map/ppermute | solution.py:367
  116.0 22.7 %collective-permute-start.14 = (f32[24,72,128]{2,1,0:T(8,128)S(1)}, f32[24,72,128]{2,1,0:T(8,128)}, u32[]{:S(2)}, u32[]{:S(2)}) collective-permute-start(f32[24,72,128]{2,1,0:T(8,128)S(1)} %broadcast_select_fusion.refs_4_), channel_id=1, source_target_pairs={{0,16},{8,24},{16,0},{24,8},{1,17},{9,25},{17,1},{25,9},{2,18},{10... | collective-permute-start | bytes 2654216 | tf_op jit(solution)/shard_map/ppermute | solution.py:367
  117.5 78.5 %all-to-all-start.2 = ((f32[4,12,72,128]{3,2,1,0:T(8,128)}), f32[4,12,72,128]{3,2,1,0:T(8,128)}, u32[]{:S(2)}, u32[]{:S(2)}) async-start(f32[4,12,72,128]{3,2,1,0:T(8,128)} %bitcast.7), calls=%async_computation.2 | async-start | bytes 3538944 | tf_op jit(solution)/shard_map/all_to_all | solution.py:467
  123.3 15.4 %copy-start.13 = (f32[24,72,128]{2,1,0:T(8,128)S(1)}, f32[24,72,128]{2,1,0:T(8,128)}, u32[]{:S(2)}) copy-start(f32[24,72,128]{2,1,0:T(8,128)} %copy-done.12) | copy-start | bytes 2654212
  138.7 16.8 %collective-permute-start.15 = (f32[24,72,128]{2,1,0:T(8,128)S(1)}, f32[24,72,128]{2,1,0:T(8,128)S(1)}, u32[]{:S(2)}, u32[]{:S(2)}) collective-permute-start(f32[24,72,128]{2,1,0:T(8,128)S(1)} %copy-done.13), channel_id=1, source_target_pairs={{0,8},{8,0},{16,24},{24,16},{1,9},{9,1},{17,25},{25,17},{2,10},{10... | collective-permute-start | bytes 2654216 | tf_op jit(solution)/shard_map/ppermute | solution.py:367
  139.0 16.7 %collective-permute-start.16 = (f32[24,72,128]{2,1,0:T(8,128)}, f32[24,72,128]{2,1,0:T(8,128)S(1)}, u32[]{:S(2)}, u32[]{:S(2)}) collective-permute-start(f32[24,72,128]{2,1,0:T(8,128)} %collective-permute-done.11.refs_3_), channel_id=1, source_target_pairs={{0,16},{8,24},{16,0},{24,8},{1,17},{9,25},{17,1},{25,9},{2,18},{10... | collective-permute-start | bytes 2654216 | tf_op jit(solution)/shard_map/ppermute | solution.py:367
  155.4 15.4 %copy-start.15 = (f32[24,72,128]{2,1,0:T(8,128)}, f32[24,72,128]{2,1,0:T(8,128)S(1)}, u32[]{:S(2)}) copy-start(f32[24,72,128]{2,1,0:T(8,128)S(1)} %collective-permute-done.15.refs_2_) | copy-start | bytes 2654212
  155.4 18.1 %collective-permute-start.17 = (f32[24,72,128]{2,1,0:T(8,128)}, f32[24,72,128]{2,1,0:T(8,128)S(1)}, u32[]{:S(2)}, u32[]{:S(2)}) collective-permute-start(f32[24,72,128]{2,1,0:T(8,128)} %collective-permute-done.14.refs_4_), channel_id=1, source_target_pairs={{0,8},{8,0},{16,24},{24,16},{1,9},{9,1},{17,25},{25,17},{2,10},{10... | collective-permute-start | bytes 2654216 | tf_op jit(solution)/shard_map/ppermute | solution.py:367
  155.7 15.2 %copy-start.16 = (f32[24,72,128]{2,1,0:T(8,128)}, f32[24,72,128]{2,1,0:T(8,128)S(1)}, u32[]{:S(2)}) copy-start(f32[24,72,128]{2,1,0:T(8,128)S(1)} %collective-permute-done.16.refs_3_) | copy-start | bytes 2654212
  173.5 0.9 copy-start.17
  189.6 9.8 %collective-permute-start.19 = (f32[4,12,72,128]{3,2,1,0:T(8,128)}, f32[4,12,72,128]{3,2,1,0:T(8,128)S(1)}, u32[]{:S(2)}, u32[]{:S(2)}) collective-permute-start(f32[4,12,72,128]{3,2,1,0:T(8,128)} %get-tuple-element.85), channel_id=1, source_target_pairs={{0,1},{1,0},{2,3},{3,2},{4,5},{5,4},{6,7},{7,6},{8,9},{9,8},{10,11... | collective-permute-start | bytes 5308424 | tf_op jit(solution)/shard_map/ppermute | solution.py:367
  195.9 11.0 %collective-permute-start.20 = (f32[4,12,72,128]{3,2,1,0:T(8,128)}, f32[4,12,72,128]{3,2,1,0:T(8,128)S(1)}, u32[]{:S(2)}, u32[]{:S(2)}) collective-permute-start(f32[4,12,72,128]{3,2,1,0:T(8,128)} %all-to-all-done.2.refs_5_), channel_id=1, source_target_pairs={{0,1},{1,0},{2,3},{3,2},{4,5},{5,4},{6,7},{7,6},{8,9},{9,8},{10,11... | collective-permute-start | bytes 5308424 | tf_op jit(solution)/shard_map/ppermute | solution.py:367
  202.4 65.1 %all-to-all-start.1 = ((f32[4,12,72,128]{3,2,1,0:T(8,128)}), f32[4,12,72,128]{3,2,1,0:T(8,128)S(1)}, u32[]{:S(2)}, u32[]{:S(2)}) async-start(f32[4,12,72,128]{3,2,1,0:T(8,128)} %add.159), calls=%async_computation.1 | async-start | bytes 3538944 | tf_op jit(solution)/shard_map/all_to_all | solution.py:445
  206.9 1.3 copy-start.11
  223.3 20.5 %collective-permute-start.21 = (f32[24,72,128]{2,1,0:T(8,128)}, f32[24,72,128]{2,1,0:T(8,128)S(1)}, u32[]{:S(2)}, u32[]{:S(2)}) collective-permute-start(f32[24,72,128]{2,1,0:T(8,128)} %get-tuple-element.93), channel_id=1, source_target_pairs={{0,8},{8,0},{16,24},{24,16},{1,9},{9,1},{17,25},{25,17},{2,10},{10... | collective-permute-start | bytes 2654216 | tf_op jit(solution)/shard_map/ppermute | solution.py:367
  223.6 20.2 %collective-permute-start.22 = (f32[24,72,128]{2,1,0:T(8,128)}, f32[24,72,128]{2,1,0:T(8,128)S(1)}, u32[]{:S(2)}, u32[]{:S(2)}) collective-permute-start(f32[24,72,128]{2,1,0:T(8,128)} %get-tuple-element.94), channel_id=1, source_target_pairs={{0,16},{8,24},{16,0},{24,8},{1,17},{9,25},{17,1},{25,9},{2,18},{10... | collective-permute-start | bytes 2654216 | tf_op jit(solution)/shard_map/ppermute | solution.py:367
  243.8 0.9 copy-start.9
  244.7 21.2 %collective-permute-start.23 = (f32[24,72,128]{2,1,0:T(8,128)}, f32[24,72,128]{2,1,0:T(8,128)S(1)}, u32[]{:S(2)}, u32[]{:S(2)}) collective-permute-start(f32[24,72,128]{2,1,0:T(8,128)} %get-tuple-element.95), channel_id=1, source_target_pairs={{0,8},{8,0},{16,24},{24,16},{1,9},{9,1},{17,25},{25,17},{2,10},{10... | collective-permute-start | bytes 2654216 | tf_op jit(solution)/shard_map/ppermute | solution.py:367
  245.9 20.0 %collective-permute-start.24 = (f32[24,72,128]{2,1,0:T(8,128)}, f32[24,72,128]{2,1,0:T(8,128)}, u32[]{:S(2)}, u32[]{:S(2)}) collective-permute-start(f32[24,72,128]{2,1,0:T(8,128)} %get-tuple-element.97), channel_id=1, source_target_pairs={{0,16},{8,24},{16,0},{24,8},{1,17},{9,25},{17,1},{25,9},{2,18},{10... | collective-permute-start | bytes 2654216 | tf_op jit(solution)/shard_map/ppermute | solution.py:367
  265.9 20.1 %collective-permute-start.27 = (f32[24,72,128]{2,1,0:T(8,128)}, f32[24,72,128]{2,1,0:T(8,128)S(1)}, u32[]{:S(2)}, u32[]{:S(2)}) collective-permute-start(f32[24,72,128]{2,1,0:T(8,128)} %add.163), channel_id=1, source_target_pairs={{0,16},{8,24},{16,0},{24,8},{1,17},{9,25},{17,1},{25,9},{2,18},{10... | collective-permute-start | bytes 2654216 | tf_op jit(solution)/shard_map/ppermute | solution.py:367
  267.2 18.8 %collective-permute-start.26 = (f32[24,72,128]{2,1,0:T(8,128)}, f32[24,72,128]{2,1,0:T(8,128)}, u32[]{:S(2)}, u32[]{:S(2)}) collective-permute-start(f32[24,72,128]{2,1,0:T(8,128)} %add.162), channel_id=1, source_target_pairs={{0,8},{8,0},{16,24},{24,16},{1,9},{9,1},{17,25},{25,17},{2,10},{10... | collective-permute-start | bytes 2654216 | tf_op jit(solution)/shard_map/ppermute | solution.py:367
  282.7 26.9 %copy-start.10 = (f32[24,72,128]{2,1,0:T(8,128)S(1)}, f32[24,72,128]{2,1,0:T(8,128)}, u32[]{:S(2)}) copy-start(f32[24,72,128]{2,1,0:T(8,128)} %get-tuple-element.131) | copy-start | bytes 2654212
  282.7 29.3 %collective-permute-start.25 = (f32[4,12,72,128]{3,2,1,0:T(8,128)}, f32[4,12,72,128]{3,2,1,0:T(8,128)S(1)}, u32[]{:S(2)}, u32[]{:S(2)}) collective-permute-start(f32[4,12,72,128]{3,2,1,0:T(8,128)} %get-tuple-element.111), channel_id=1, source_target_pairs={{0,1},{1,0},{2,3},{3,2},{4,5},{5,4},{6,7},{7,6},{8,9},{9,8},{10,11... | collective-permute-start | bytes 5308424 | tf_op jit(solution)/shard_map/ppermute | solution.py:367
  286.0 20.0 %collective-permute-start.29 = (f32[24,72,128]{2,1,0:T(8,128)}, f32[24,72,128]{2,1,0:T(8,128)S(1)}, u32[]{:S(2)}, u32[]{:S(2)}) collective-permute-start(f32[24,72,128]{2,1,0:T(8,128)} %get-tuple-element.122), channel_id=1, source_target_pairs={{0,16},{8,24},{16,0},{24,8},{1,17},{9,25},{17,1},{25,9},{2,18},{10... | collective-permute-start | bytes 2654216 | tf_op jit(solution)/shard_map/ppermute | solution.py:367
  286.2 17.5 %collective-permute-start.28 = (f32[24,72,128]{2,1,0:T(8,128)}, f32[24,72,128]{2,1,0:T(8,128)S(1)}, u32[]{:S(2)}, u32[]{:S(2)}) collective-permute-start(f32[24,72,128]{2,1,0:T(8,128)} %get-tuple-element.120), channel_id=1, source_target_pairs={{0,8},{8,0},{16,24},{24,16},{1,9},{9,1},{17,25},{25,17},{2,10},{10... | collective-permute-start | bytes 2654216 | tf_op jit(solution)/shard_map/ppermute | solution.py:367
  287.4 24.6 %copy-start.5 = (f32[4,12,72,128]{3,2,1,0:T(8,128)S(1)}, f32[4,12,72,128]{3,2,1,0:T(8,128)}, u32[]{:S(2)}) copy-start(f32[4,12,72,128]{3,2,1,0:T(8,128)} %get-tuple-element.110) | copy-start | bytes 5308420
  288.9 0.9 copy-start.2
  289.8 19.8 %collective-permute-start.34 = (f32[24,72,128]{2,1,0:T(8,128)S(1)}, f32[24,72,128]{2,1,0:T(8,128)S(1)}, u32[]{:S(2)}, u32[]{:S(2)}) collective-permute-start(f32[24,72,128]{2,1,0:T(8,128)S(1)} %add_add_fusion.2), channel_id=1, source_target_pairs={{0,2},{6,4},{1,3},{7,5},{8,10},{14,12},{9,11},{15,13},{16,18},{22,... | collective-permute-start | bytes 2654216 | tf_op jit(solution)/shard_map/ppermute | solution.py:371
  306.0 19.4 %collective-permute-start.31 = (f32[24,72,128]{2,1,0:T(8,128)}, f32[24,72,128]{2,1,0:T(8,128)}, u32[]{:S(2)}, u32[]{:S(2)}) collective-permute-start(f32[24,72,128]{2,1,0:T(8,128)} %add.164), channel_id=1, source_target_pairs={{0,16},{8,24},{16,0},{24,8},{1,17},{9,25},{17,1},{25,9},{2,18},{10... | collective-permute-start | bytes 2654216 | tf_op jit(solution)/shard_map/ppermute | solution.py:367
  307.2 18.2 %collective-permute-start.30 = (f32[24,72,128]{2,1,0:T(8,128)}, f32[24,72,128]{2,1,0:T(8,128)}, u32[]{:S(2)}, u32[]{:S(2)}) collective-permute-start(f32[24,72,128]{2,1,0:T(8,128)} %get-tuple-element.123), channel_id=1, source_target_pairs={{0,8},{8,0},{16,24},{24,16},{1,9},{9,1},{17,25},{25,17},{2,10},{10... | collective-permute-start | bytes 2654216 | tf_op jit(solution)/shard_map/ppermute | solution.py:367
  313.4 19.2 %collective-permute-start.35 = (f32[24,72,128]{2,1,0:T(8,128)}, f32[24,72,128]{2,1,0:T(8,128)}, u32[]{:S(2)}, u32[]{:S(2)}) collective-permute-start(f32[24,72,128]{2,1,0:T(8,128)} %add_add_fusion.1), channel_id=1, source_target_pairs={{0,2},{2,4},{1,3},{3,5},{8,10},{10,12},{9,11},{11,13},{16,18},{18,... | collective-permute-start | bytes 2654216 | tf_op jit(solution)/shard_map/ppermute | solution.py:371
  314.7 19.2 %collective-permute-start.37 = (f32[24,72,128]{2,1,0:T(8,128)}, f32[24,72,128]{2,1,0:T(8,128)}, u32[]{:S(2)}, u32[]{:S(2)}) collective-permute-start(f32[24,72,128]{2,1,0:T(8,128)} %add_add_fusion.1), channel_id=1, source_target_pairs={{4,2},{6,4},{5,3},{7,5},{12,10},{14,12},{13,11},{15,13},{20,18},{2... | collective-permute-start | bytes 2654216 | tf_op jit(solution)/shard_map/ppermute | solution.py:371
  318.7 85.2 %all-to-all-start.3 = ((f32[4,12,72,128]{3,2,1,0:T(8,128)}), f32[4,12,72,128]{3,2,1,0:T(8,128)S(1)}, u32[]{:S(2)}, u32[]{:S(2)}) async-start(f32[4,12,72,128]{3,2,1,0:T(8,128)} %add.160), calls=%async_computation.3 | async-start | bytes 3538944 | tf_op jit(solution)/shard_map/all_to_all | solution.py:445
  325.4 18.8 %collective-permute-start.33 = (f32[24,72,128]{2,1,0:T(8,128)}, f32[24,72,128]{2,1,0:T(8,128)}, u32[]{:S(2)}, u32[]{:S(2)}) collective-permute-start(f32[24,72,128]{2,1,0:T(8,128)} %get-tuple-element.128), channel_id=1, source_target_pairs={{0,16},{8,24},{16,0},{24,8},{1,17},{9,25},{17,1},{25,9},{2,18},{10... | collective-permute-start | bytes 2654216 | tf_op jit(solution)/shard_map/ppermute | solution.py:367
  326.6 17.5 %collective-permute-start.32 = (f32[24,72,128]{2,1,0:T(8,128)}, f32[24,72,128]{2,1,0:T(8,128)}, u32[]{:S(2)}, u32[]{:S(2)}) collective-permute-start(f32[24,72,128]{2,1,0:T(8,128)} %add.161), channel_id=1, source_target_pairs={{0,8},{8,0},{16,24},{24,16},{1,9},{9,1},{17,25},{25,17},{2,10},{10... | collective-permute-start | bytes 2654216 | tf_op jit(solution)/shard_map/ppermute | solution.py:367
  337.9 52.5 %collective-permute-start.38 = (f32[24,72,128]{2,1,0:T(8,128)}, f32[24,72,128]{2,1,0:T(8,128)}, u32[]{:S(2)}, u32[]{:S(2)}) collective-permute-start(f32[24,72,128]{2,1,0:T(8,128)} %get-tuple-element.134), channel_id=1, source_target_pairs={{2,0},{4,2},{6,4},{3,1},{5,3},{7,5},{10,8},{12,10},{14,12},{11,9},... | collective-permute-start | bytes 2654216 | tf_op jit(solution)/shard_map/ppermute | solution.py:371
  342.2 48.2 %collective-permute-start.36 = (f32[24,72,128]{2,1,0:T(8,128)}, f32[24,72,128]{2,1,0:T(8,128)}, u32[]{:S(2)}, u32[]{:S(2)}) collective-permute-start(f32[24,72,128]{2,1,0:T(8,128)} %get-tuple-element.133), channel_id=1, source_target_pairs={{0,2},{2,4},{4,6},{1,3},{3,5},{5,7},{8,10},{10,12},{12,14},{9,11},... | collective-permute-start | bytes 2654216 | tf_op jit(solution)/shard_map/ppermute | solution.py:371
  392.8 1.0 copy-start.3
  394.6 7.1 %collective-permute-start.39 = (f32[12,72,128]{2,1,0:T(8,128)}, f32[12,72,128]{2,1,0:T(8,128)}, u32[]{:S(2)}, u32[]{:S(2)}) collective-permute-start(f32[12,72,128]{2,1,0:T(8,128)} %constant_dynamic-slice_fusion), channel_id=1, source_target_pairs={{0,1},{1,0},{2,3},{3,2},{4,5},{5,4},{6,7},{7,6},{8,9},{9,8},{10,11... | collective-permute-start | bytes 1327112 | tf_op jit(solution)/shard_map/ppermute | solution.py:367
  403.9 1.2 copy-start.1

commit v8 on v7

--- a/solution.py
+++ b/solution.py
@@ -110,7 +110,7 @@
 
 
 def pair_kernel(count, sizes, layout, *refs):
-    split_in, sums_in, sums_split, terms_in, split_out = layout
+    split_in, sums_in, sums_split, terms_in, split_out, twice = layout
     zs, planes = sizes
     slab = 2 * planes
     third, pitch = count // 4, count + GAP
@@ -129,6 +129,7 @@
         tables.at[pl.ds(2 * LANES + 2 * count * k, 2 * count), : 2 * count] for k in range(3)
     )
     z, core = place[0], place[1]
+    weight = jnp.where((z == 0) | (z == zs - 1), 2.0, 1.0).astype(F32)
 
     def part(ref, index, size=slab):
         return ref.at[pl.ds(pl.multiple_of(index * size, size), size)]
@@ -238,6 +239,7 @@
                     near = partner[x, rows, :] * value
                     sums[x, rows, :] = sums[x, rows, :] + near if sums_in else near
                     far = orbital[x, rows, :] * value
+                    far = far * weight if twice else far
                     terms[x, rows, :] = terms[x, rows, :] + far if terms_in else far
         if sums_split:
             start(part(sums, 2 * step + core, planes), sums_out[0].at[step], sem.at[5, step])
@@ -262,11 +264,11 @@
         wait(part(terms, s), target, sem.at[7, s])
 
 
-def pair_solve(place, partner, mine, other, sums, terms, tables, last_partner, last_orbital):
+def pair_solve(place, partner, mine, other, sums, terms, tables, last_partner, last_orbital, twice=False):
     zs, planes, rows, _ = mine.shape
     count = zs * 2 * planes
     split_in = len(partner) > 1
-    layout = (split_in, sums is not None, last_partner, terms is not None, last_orbital and split_in)
+    layout = (split_in, sums is not None, last_partner, terms is not None, last_orbital and split_in, twice)
     field = jax.ShapeDtypeStruct((count, rows, LANES), F32)
     kinds = [jax.ShapeDtypeStruct(mine.shape, F32)] * 2 if last_partner else [field]
     pieces = [jax.ShapeDtypeStruct(p.shape, F32) for p in partner] if layout[4] else [field]
@@ -310,56 +312,57 @@
 
 
 def pack_kernel(sets, planes, rows, flat, *packed):
-    size = flat.shape[1] // sets
     plane = pl.program_id(0)
     for tile in range(rows):
         row = plane * rows + piece_row(tile, rows)
-        for k in range(sets):
-            value = flat[0, k * size : (k + 1) * size, tile * LANES : (tile + 1) * LANES]
-            packed[k][pl.ds(row, size, stride=planes * rows), :] = value
+        for runs, out in zip(sets, packed):
+            done = 0
+            for first, size in runs:
+                value = flat[0, first : first + size, tile * LANES : (tile + 1) * LANES]
+                out[pl.ds(row + done * planes * rows, size, stride=planes * rows), :] = value
+                done += size
 
 
 def pack(fields, sets):
     planes, number, flat = fields.shape
-    rows, size = flat // LANES, number // sets
+    rows = flat // LANES
+    size = sum(run[1] for run in sets[0])
     out = (size * planes * rows, LANES)
     packed = pl.pallas_call(
         functools.partial(pack_kernel, sets, planes, rows),
         grid=(planes,),
         in_specs=[pl.BlockSpec((1, number, flat), lambda i: (i, 0, 0))],
-        out_specs=[pl.BlockSpec(out, lambda i: (0, 0))] * sets,
-        out_shape=[jax.ShapeDtypeStruct(out, F32)] * sets,
+        out_specs=[pl.BlockSpec(out, lambda i: (0, 0))] * len(sets),
+        out_shape=[jax.ShapeDtypeStruct(out, F32)] * len(sets),
         compiler_params=pltpu.CompilerParams(vmem_limit_bytes=32 * 1024 * 1024),
     )(fields)
     return [p.reshape(size, planes, rows, LANES) for p in packed]
 
 
-def unpack_kernel(sets, planes, rows, *refs):
-    packed, extra, flat = refs[:sets], refs[sets], refs[-1]
-    size = flat.shape[1] // sets
+def unpack_kernel(order, planes, rows, *refs):
+    packed, flat = refs[:-1], refs[-1]
     plane = pl.program_id(0)
     for tile in range(rows):
         row = plane * rows + piece_row(tile, rows)
-        more = extra[pl.ds(row, PAIR, stride=planes * rows), :]
-        for k in range(sets):
-            value = packed[k][pl.ds(row, size, stride=planes * rows), :]
-            if k == 0:
-                value = jnp.concatenate([value[:PAIR] + more, value[PAIR:]], axis=0)
-            flat[0, k * size : (k + 1) * size, tile * LANES : (tile + 1) * LANES] = -ALPHA * value
-
-
-def unpack(fields, extra):
-    sets = len(fields)
-    size, planes, rows, _ = fields[0].shape
-    whole = lambda n: pl.BlockSpec((n * planes * rows, LANES), lambda i: (0, 0), pipeline_mode=pl.Buffered(1))
+        runs = [
+            packed[k][pl.ds(row + first * planes * rows, size, stride=planes * rows), :] for k, first, size in order
+        ]
+        value = runs[0] if len(runs) == 1 else jnp.concatenate(runs, axis=0)
+        flat[0, :, tile * LANES : (tile + 1) * LANES] = -ALPHA * value
+
+
+def unpack(fields, order):
+    planes, rows = fields[0].shape[1:3]
+    number = sum(run[2] for run in order)
+    flats = [f.reshape(f.shape[0] * planes * rows, LANES) for f in fields]
     return pl.pallas_call(
-        functools.partial(unpack_kernel, sets, planes, rows),
+        functools.partial(unpack_kernel, order, planes, rows),
         grid=(planes,),
-        in_specs=[whole(size)] * sets + [whole(PAIR)],
-        out_specs=pl.BlockSpec((1, sets * size, rows * LANES), lambda i: (i, 0, 0)),
-        out_shape=jax.ShapeDtypeStruct((planes, sets * size, rows * LANES), F32),
+        in_specs=[pl.BlockSpec(f.shape, lambda i: (0, 0), pipeline_mode=pl.Buffered(1)) for f in flats],
+        out_specs=pl.BlockSpec((1, number, rows * LANES), lambda i: (i, 0, 0)),
+        out_shape=jax.ShapeDtypeStruct((planes, number, rows * LANES), F32),
         compiler_params=pltpu.CompilerParams(vmem_limit_bytes=32 * 1024 * 1024),
-    )(*(f.reshape(size * planes * rows, LANES) for f in fields), extra.reshape(PAIR * planes * rows, LANES))
+    )(*flats)
 
 
 def swap(value, axis, flip):
@@ -411,12 +414,14 @@
     count = planes * zs * 2
     place = jnp.stack([lax.axis_index("z"), core]).astype(jnp.int32)
     tables = make_tables(count)
-    sets = pack(orbitals.swapaxes(0, 1), n_local // zs)
+    square = bands == ROUNDS == 4 and zs == 4 and n_local == 8
+    runs = [((2, 4),), ((0, 1), (6, 2), (1, 1))] if square else [((k * zs, zs),) for k in range(n_local // zs)]
+    sets = pack(orbitals.swapaxes(0, 1), runs)
     tail = sets[0].shape[2:]
-    keep = lax.dynamic_index_in_dim(sets[0], core, 0, keepdims=False)
-    come = swap(lax.dynamic_index_in_dim(sets[0], 1 - core, 0, keepdims=False), "core", 1)
+    members, step = (sets[1], zs - 1) if square else (sets[0], 1)
+    keep = lax.dynamic_index_in_dim(members, core * step, 0, keepdims=False)
+    come = swap(lax.dynamic_index_in_dim(members, (1 - core) * step, 0, keepdims=False), "core", 1)
     slab = jnp.concatenate([jnp.where(core == 0, keep, come), jnp.where(core == 0, come, keep)], axis=0)
-    square = bands == ROUNDS == 4 and zs == 4 and len(sets) == 2
     if square:
         return square_local(place, tables, sets, slab)
     every = lax.all_gather(slab, ("band", "z"), axis=0, tiled=True).reshape((bands, count) + tail)
@@ -434,7 +439,9 @@
     owner = jnp.concatenate([t[None] for t in terms] + [jnp.zeros((bands - ROUNDS, count) + tail, F32)], axis=0)
     owner = owner.reshape((bands * count,) + tail)
     owner = lax.psum_scatter(owner, ("band", "z"), scatter_dimension=0, tiled=True)
-    return finish([send_back(core_sum(*sums)) for sums in sums_out], owner)
+    back = [send_back(core_sum(*sums)) for sums in sums_out]
+    back[0] = back[0].at[:PAIR].add(jnp.stack(by_member(owner)))
+    return unpack(back, [(k, 0, zs) for k in range(len(back))]).swapaxes(0, 1)
 
 
 def core_sum(keep, give):
@@ -445,12 +452,22 @@
     return lax.all_to_all(total, "z", split_axis=0, concat_axis=0, tiled=True)
 
 
-def finish(sums, owner):
+def by_member(owner):
     core, planes = lax.axis_index("core"), owner.shape[0] // 2
     keep = lax.dynamic_slice_in_dim(owner, core * planes, planes)
     come = swap(lax.dynamic_slice_in_dim(owner, (1 - core) * planes, planes), "core", 1)
-    owner = jnp.stack([jnp.where(core == 0, keep, come), jnp.where(core == 0, come, keep)])
-    return unpack(sums, owner).swapaxes(0, 1)
+    return jnp.where(core == 0, keep, come), jnp.where(core == 0, come, keep)
+
+
+def send_inner(total):
+    z = lax.axis_index("z")
+    block = lambda index: lax.dynamic_index_in_dim(total, jnp.clip(index, 0, 3), 0, keepdims=False)
+    right, left = along(block(z + 1), RIGHT[1:]), along(block(z - 1), LEFT[:2])
+    jump = along(block(jnp.where(z == 1, 3, 0)), [(1, 3), (2, 0)])
+    own = block(z)
+    first = jnp.where(z == 1, own, jnp.where(z == 0, left, jnp.where(z == 2, right, jump)))
+    second = jnp.where(z == 2, own, jnp.where(z == 3, right, jnp.where(z == 1, left, jump)))
+    return first, second
 
 
 def square_local(place, tables, sets, slab):
@@ -460,7 +477,7 @@
 
     def pair(k, turn, sums, term=None, after=None, last=False):
         partner = partners[turn] if after is None else tie(partners[turn], after)
-        return pair_solve(place, partner, mine[k], other[k], sums, term, tables, last, k == 1)
+        return pair_solve(place, partner, mine[k], other[k], sums, term, tables, last, k == 1, k == 1)
 
     terms = [None] * ROUNDS
     sums, terms[0] = pair(0, 0, None)
@@ -484,20 +501,22 @@
     side2, far3 = x_swap(side[2] + handed2, done), y_swap(far[3] + handed3, done)
     sums, own = pair(1, 0, sums, terms[0], after=done + (back[0],), last=True)
     total = core_sum(*sums)
-    back.append(send_back(total))
+    inner = send_inner(total)
     done = (side2, far3)
     handed1, far2 = x_swap(cross[1], done), y_swap(far[2], done)
     rest = along(own[3] + side3 + far3, [(0, 1), (3, 2)])
     done = (handed1, far2)
     side1, far1 = x_swap(side[1], done), y_swap(far[1] + handed1, done)
-    two = tie(own[2] + side2 + far2 + rest, total)
+    two = tie(own[2] + side2 + far2 + rest, inner)
     after, before = along(two, RIGHT[:2]), along(two, LEFT[1:])
     done = (side1, far1)
     side0, far0 = x_swap(side[0] + handed0, done), y_swap(far[0], done)
     near = own[1] + side1 + far1
     after = jnp.where(z == 0, near, own[3] + side3 + far3 + after)
     after, before = along(after, RIGHT), along(near + before, LEFT)
-    return finish(back, own[0] + side0 + far0 + after + before)
+    owner = by_member(own[0] + side0 + far0 + after + before)
+    fields = [back[0], jnp.stack(owner + inner)]
+    return unpack(fields, [(1, 0, 2), (0, 0, 4), (1, 2, 2)]).swapaxes(0, 1)
 
 
 def solution(mesh):

time: 415 us -> 386 us (0.930)
  waiting for transfers between devices: 148 us -> 117 us
  starting transfers between devices: 85.6 us -> 91.2 us
    ppermute x10 -> x13, waiting for transfers between devices: 100 us -> 78 us  [along(): return lax.ppermute(value, 'z', pairs)]
    ppermute x10 -> x13, starting transfers between devices: 26 us -> 40.3 us  [along(): return lax.ppermute(value, 'z', pairs)]
    ppermute x30, waiting for transfers between devices: 47.7 us -> 39 us  [swap(): return lax.ppermute(value, axis, [(i, i ^ flip) for i in range(size)])]
    ppermute x30, starting transfers between devices: 40.4 us -> 36 us  [swap(): return lax.ppermute(value, axis, [(i, i ^ flip) for i in range(size)])]
    all_to_all x2 -> x1, starting transfers between devices: 8.79 us -> 4.54 us  [send_back(): return lax.all_to_all(total, 'z', split_axis=0, concat_axis=0, tiled=True)]
  transfers between devices with their start and end apart: 44 -> 46, of which waited for: 20 -> 23; matrix products, arithmetic and copies ran while one was open for 9% -> 8% of each run, Pallas kernels for 30% -> 32%
where the time goes in v8:
time: 386 us; the launch traced here: 385 us
  Pallas kernels  132 us (34%)
  waiting for transfers between devices  117 us (30%)
  starting transfers between devices  91.2 us (24%)
  other arithmetic  34.2 us (9%)
  local copies, waits for them, and re-layouts  10 us (3%)
    pallas_call x8, Pallas kernels, pair_solve(): pl.pallas_call(functools.partial(pair_kernel, count, (zs, planes), layout...  121 us
    ppermute x13, waiting for transfers between devices, along(): return lax.ppermute(value, 'z', pairs)  78 us
    ppermute x13, starting transfers between devices, along(): return lax.ppermute(value, 'z', pairs)  40.3 us
    ppermute x30, waiting for transfers between devices, swap(): return lax.ppermute(value, axis, [(i, i ^ flip) for i in range(size)])  39 us
    ppermute x30, starting transfers between devices, swap(): return lax.ppermute(value, axis, [(i, i ^ flip) for i in range(size)])  36 us
  transfers between devices with their start and end apart: 46, of which 23 were waited for; matrix products, arithmetic and copies ran while one was open for 8% of the time, Pallas kernels for 32%

profile of v8, /device:TPU:17, one launch (start us, length us, event | category | flops | bytes accessed | tf_op | source)
XLA Modules:
  0.0 385.0 jit_solution(6820301940734744358)
XLA Ops:
  0.0 2.0 copy-done
  2.0 4.7 %shard_map.28 = (f32[3456,128]{1,0:T(8,128)}, f32[3456,128]{1,0:T(8,128)}) custom-call(f32[12,8,9216]{2,1,0:T(8,128)S(1)} %bitcast.30), custom_call_target="tpu_custom_call" | custom-call | tf_op jit(solution)/shard_map/pallas_call | solution.py:331
  6.7 4.6 %all-to-all-start = ((f32[4,12,72,128]{3,2,1,0:T(8,128)}), f32[4,12,72,128]{3,2,1,0:T(8,128)S(1)}, u32[]{:S(2)}, u32[]{:S(2)}) async-start(f32[4,12,72,128]{3,2,1,0:T(8,128)} %bitcast.6), calls=%async_computation | async-start | bytes 3538944 | tf_op jit(solution)/shard_map/all_to_all | solution.py:474
  12.4 1.3 collective-permute-start
  13.7 1.4 collective-permute-done
  17.6 3.1 collective-permute-start.3
  20.7 2.2 collective-permute-start.4
  22.9 1.3 collective-permute-start.5
  24.2 13.2 %collective-permute-done.1.refs_1_ = f32[24,72,128]{2,1,0:T(8,128)} collective-permute-done((f32[24,72,128]{2,1,0:T(8,128)S(1)}, f32[24,72,128]{2,1,0:T(8,128)}, u32[]{:S(2)}, u32[]{:S(2)}) %collective-permute-start.1) | collective-permute-done | bytes 884768 | tf_op jit(solution)/shard_map/ppermute | solution.py:370
  38.6 30.1 %collective-permute-done.3 = f32[24,72,128]{2,1,0:T(8,128)} collective-permute-done((f32[24,72,128]{2,1,0:T(8,128)S(1)}, f32[24,72,128]{2,1,0:T(8,128)}, u32[]{:S(2)}, u32[]{:S(2)}) %collective-permute-start.3) | collective-permute-done | bytes 884768 | tf_op jit(solution)/shard_map/ppermute | solution.py:374
  68.7 1.9 collective-permute-start.7
  70.6 3.5 collective-permute-start.8
  75.4 1.3 collective-permute-start.6
  77.9 3.1 collective-permute-start.18
  81.0 9.1 %collective-permute-done.7 = f32[24,72,128]{2,1,0:T(8,128)S(1)} collective-permute-done((f32[24,72,128]{2,1,0:T(8,128)}, f32[24,72,128]{2,1,0:T(8,128)S(1)}, u32[]{:S(2)}, u32[]{:S(2)}) %collective-permute-start.7) | collective-permute-done | bytes 884768 | tf_op jit(solution)/shard_map/ppermute | solution.py:374
  91.9 2.3 collective-permute-done.6.refs_2_
  95.2 2.2 collective-permute-start.10
  99.8 4.8 %fusion.refs_8_.refs_9_.refs_10_ = f32[48,96,256]{2,1,0:T(8,128)} fusion(s32[256]{0:T(256)S(1)} %get-tuple-element.146, s32[256]{0:T(256)S(1)} %get-tuple-element.147, s32[96]{0:T(128)S(1)} %iota_add_fusion, s32[256]{0:T(256)S(1)} %get-tuple-element.145, s32[48]{0:T(128)S(1)} %iota_multiply_fusion, pred[96]{0:T(512)(128)(4,1)S(1)} %iota_compare_fusion, ...), kind=kLoop, calls=%fused_computation.4 | loop fusion | flops 31850496 | bytes 4722592 | tf_op jit(solution)/shard_map/div | solution.py:75
  105.2 7.1 %collective-permute-done.10 = f32[24,72,128]{2,1,0:T(8,128)} collective-permute-done((f32[24,72,128]{2,1,0:T(8,128)}, f32[24,72,128]{2,1,0:T(8,128)}, u32[]{:S(2)}, u32[]{:S(2)}) %collective-permute-start.10) | collective-permute-done | bytes 884768 | tf_op jit(solution)/shard_map/ppermute | solution.py:374
  112.4 2.8 collective-permute-done.11.refs_3_
  116.4 1.5 collective-permute-start.14
  117.9 5.8 %all-to-all-start.2 = ((f32[4,12,72,128]{3,2,1,0:T(8,128)}), f32[4,12,72,128]{3,2,1,0:T(8,128)}, u32[]{:S(2)}, u32[]{:S(2)}) async-start(f32[4,12,72,128]{3,2,1,0:T(8,128)} %bitcast.3), calls=%async_computation.2 | async-start | bytes 3538944 | tf_op jit(solution)/shard_map/all_to_all | solution.py:484
  123.7 15.3 %shard_map.29 = (f32[96,72,128]{2,1,0:T(8,128)}, f32[96,72,128]{2,1,0:T(8,128)}) custom-call(s32[2]{0:T(128)} %pad_add_fusion.refs_0_, f32[24,72,128]{2,1,0:T(8,128)} %copy-done.6, f32[24,72,128]{2,1,0:T(8,128)} %copy-done.7, f32[24,72,128]{2,1,0:T(8,128)} %add.162.refs_3_, f32[24,72,128]{2,1,0:T(8,128)} %copy-done.8, f32[4,12,72,128]{3,2,1,0:T(8,128)} %copy-done.1, ...), custom_call_target="tpu_custom_call" | custom-call | flops 16986931200 | bytes 17694720 | tf_op jit(solution)/shard_map/pallas_call | solution.py:278
  139.7 15.2 %shard_map.30 = (f32[96,72,128]{2,1,0:T(8,128)}, f32[96,72,128]{2,1,0:T(8,128)}) custom-call(s32[2]{0:T(128)} %pad_add_fusion.refs_0_, f32[24,72,128]{2,1,0:T(8,128)} %collective-permute-done.1.refs_1_, f32[24,72,128]{2,1,0:T(8,128)} %copy-done.18, f32[24,72,128]{2,1,0:T(8,128)} %collective-permute-done.11.refs_3_, ...), custom_call_target="tpu_custom_call" | custom-call | flops 16986931200 | bytes 17694720 | tf_op jit(solution)/shard_map/pallas_call | solution.py:278
  156.1 15.2 %shard_map.31 = (f32[96,72,128]{2,1,0:T(8,128)}, f32[96,72,128]{2,1,0:T(8,128)}) custom-call(s32[2]{0:T(128)} %pad_add_fusion.refs_0_, f32[24,72,128]{2,1,0:T(8,128)} %collective-permute-done.5.refs_1_, f32[24,72,128]{2,1,0:T(8,128)} %copy-done.16, f32[24,72,128]{2,1,0:T(8,128)} %collective-permute-done.12.refs_3_, ...), custom_call_target="tpu_custom_call" | custom-call | flops 16986931200 | bytes 17694720 | tf_op jit(solution)/shard_map/pallas_call | solution.py:278
  171.3 2.6 collective-permute-done.17.refs_4_
  174.9 15.2 %shard_map.32 = (f32[4,12,72,128]{3,2,1,0:T(8,128)}, f32[4,12,72,128]{3,2,1,0:T(8,128)}, f32[96,72,128]{2,1,0:T(8,128)}) custom-call(s32[2]{0:T(128)} %pad_add_fusion.refs_0_, f32[24,72,128]{2,1,0:T(8,128)} %collective-permute-done.2.refs_1_, f32[24,72,128]{2,1,0:T(8,128)} %copy-done.19, f32[24,72,128]{2,1,0:T(8,128)} %copy-done.20, ...), custom_call_target="tpu_custom_call" | custom-call | flops 16986931200 | bytes 17694720 | tf_op jit(solution)/shard_map/pallas_call | solution.py:278
  190.1 6.3 %collective-permute-start.19 = (f32[4,12,72,128]{3,2,1,0:T(8,128)}, f32[4,12,72,128]{3,2,1,0:T(8,128)S(1)}, u32[]{:S(2)}, u32[]{:S(2)}) collective-permute-start(f32[4,12,72,128]{3,2,1,0:T(8,128)} %get-tuple-element.86), channel_id=1, source_target_pairs={{0,1},{1,0},{2,3},{3,2},{4,5},{5,4},{6,7},{7,6},{8,9},{9,8},{10,11... | collective-permute-start | bytes 5308424 | tf_op jit(solution)/shard_map/ppermute | solution.py:370
  196.5 3.4 collective-permute-done.19
  199.9 2.9 add.167
  202.9 4.5 %all-to-all-start.1 = ((f32[4,12,72,128]{3,2,1,0:T(8,128)}), f32[4,12,72,128]{3,2,1,0:T(8,128)S(1)}, u32[]{:S(2)}, u32[]{:S(2)}) async-start(f32[4,12,72,128]{3,2,1,0:T(8,128)} %add.167), calls=%async_computation.1 | async-start | bytes 3538944 | tf_op jit(solution)/shard_map/all_to_all | solution.py:452
  208.7 15.1 %shard_map.33 = (f32[96,72,128]{2,1,0:T(8,128)}, f32[24,72,128]{2,1,0:T(8,128)}, f32[24,72,128]{2,1,0:T(8,128)}, f32[24,72,128]{2,1,0:T(8,128)}, f32[24,72,128]{2,1,0:T(8,128)}) custom-call(s32[2]{0:T(128)} %pad_add_fusion.refs_0_, f32[24,72,128]{2,1,0:T(8,128)} %collective-permute-done.2.refs_1_, f32[24,72,128]{2,1,0:T(8,128)} %copy-done.19, ...), custom_call_target="tpu_custom_call" | custom-call | flops 16986931200 | bytes 17694720 | tf_op jit(solution)/shard_map/pallas_call | solution.py:278
  224.4 15.2 %shard_map.34 = (f32[96,72,128]{2,1,0:T(8,128)}, f32[24,72,128]{2,1,0:T(8,128)}, f32[24,72,128]{2,1,0:T(8,128)}, f32[24,72,128]{2,1,0:T(8,128)}, f32[24,72,128]{2,1,0:T(8,128)}) custom-call(s32[2]{0:T(128)} %pad_add_fusion.refs_0_, f32[24,72,128]{2,1,0:T(8,128)} %collective-permute-done.1.refs_1_, f32[24,72,128]{2,1,0:T(8,128)} %copy-done.18, ...), custom_call_target="tpu_custom_call" | custom-call | flops 16986931200 | bytes 17694720 | tf_op jit(solution)/shard_map/pallas_call | solution.py:278
  239.5 4.8 %collective-permute-done.21 = f32[24,72,128]{2,1,0:T(8,128)S(1)} collective-permute-done((f32[24,72,128]{2,1,0:T(8,128)}, f32[24,72,128]{2,1,0:T(8,128)S(1)}, u32[]{:S(2)}, u32[]{:S(2)}) %collective-permute-start.21) | collective-permute-done | bytes 884768 | tf_op jit(solution)/shard_map/ppermute | solution.py:370
  246.4 15.1 %shard_map.35 = (f32[96,72,128]{2,1,0:T(8,128)}, f32[24,72,128]{2,1,0:T(8,128)}, f32[24,72,128]{2,1,0:T(8,128)}, f32[24,72,128]{2,1,0:T(8,128)}, f32[24,72,128]{2,1,0:T(8,128)}) custom-call(s32[2]{0:T(128)} %pad_add_fusion.refs_0_, f32[24,72,128]{2,1,0:T(8,128)} %collective-permute-done.5.refs_1_, f32[24,72,128]{2,1,0:T(8,128)} %copy-done.16, ...), custom_call_target="tpu_custom_call" | custom-call | flops 16986931200 | bytes 17694720 | tf_op jit(solution)/shard_map/pallas_call | solution.py:278
  261.6 2.5 add.170
  264.0 2.5 add.169
  266.5 1.3 collective-permute-start.26
  268.4 15.2 %shard_map.36 = (f32[4,12,72,128]{3,2,1,0:T(8,128)}, f32[4,12,72,128]{3,2,1,0:T(8,128)}, f32[24,72,128]{2,1,0:T(8,128)}, f32[24,72,128]{2,1,0:T(8,128)}, f32[24,72,128]{2,1,0:T(8,128)}, /*index=5*/f32[24,72,128]{2,1,0:T(8,128)}) custom-call(s32[2]{0:T(128)} %pad_add_fusion.refs_0_, f32[24,72,128]{2,1,0:T(8,128)} %copy-done.6, f32[24,72,128]{2,1,0:T(8,128)} %copy-done.7, ...), custom_call_target="tpu_custom_call" | custom-call | flops 16986931200 | bytes 17694720 | tf_op jit(solution)/shard_map/pallas_call | solution.py:278
  283.6 3.0 collective-permute-start.34
  288.3 2.8 add_add_fusion.2
  291.1 1.3 collective-permute-start.33
  293.6 2.2 add.181
  296.9 2.9 collective-permute-start.35
  299.8 3.4 collective-permute-start.36
  303.2 2.9 collective-permute-done.27
  306.1 3.9 %collective-permute-start.37 = (f32[12,72,128]{2,1,0:T(8,128)}, f32[12,72,128]{2,1,0:T(8,128)}, u32[]{:S(2)}, u32[]{:S(2)}) collective-permute-start(f32[12,72,128]{2,1,0:T(8,128)} %get-tuple-element.139), channel_id=1, source_target_pairs={{2,6},{4,0},{3,7},{5,1},{10,14},{12,8},{11,15},{13,9},{18,22},{20,... | collective-permute-start | bytes 1327112 | tf_op jit(solution)/shard_map/ppermute | solution.py:374
  310.1 1.5 add.171
  312.0 2.3 add_add_fusion.1
  314.9 2.3 bitcast_select_fusion.1
  317.2 1.3 collective-permute-start.38
  318.5 8.4 %collective-permute-start.40 = (f32[24,72,128]{2,1,0:T(8,128)S(1)}, f32[24,72,128]{2,1,0:T(8,128)S(1)}, u32[]{:S(2)}, u32[]{:S(2)}) collective-permute-start(f32[24,72,128]{2,1,0:T(8,128)S(1)} %add_add_fusion.1), channel_id=1, source_target_pairs={{4,2},{6,4},{5,3},{7,5},{12,10},{14,12},{13,11},{15,13},{20,18},{2... | collective-permute-start | bytes 2654216 | tf_op jit(solution)/shard_map/ppermute | solution.py:374
  328.6 1.4 collective-permute-start.32
  330.0 12.3 %collective-permute-done.38 = f32[24,72,128]{2,1,0:T(8,128)S(1)} collective-permute-done((f32[24,72,128]{2,1,0:T(8,128)S(1)}, f32[24,72,128]{2,1,0:T(8,128)S(1)}, u32[]{:S(2)}, u32[]{:S(2)}) %collective-permute-start.38) | collective-permute-done | bytes 884768 | tf_op jit(solution)/shard_map/ppermute | solution.py:374
  342.3 1.9 collective-permute-done.40
  344.2 1.5 add_select_fusion
  345.7 3.1 collective-permute-start.41
  348.8 3.1 collective-permute-start.39
  352.0 13.5 %collective-permute-done.41 = f32[24,72,128]{2,1,0:T(8,128)} collective-permute-done((f32[24,72,128]{2,1,0:T(8,128)S(1)}, f32[24,72,128]{2,1,0:T(8,128)}, u32[]{:S(2)}, u32[]{:S(2)}) %collective-permute-start.41) | collective-permute-done | bytes 884768 | tf_op jit(solution)/shard_map/ppermute | solution.py:374
  365.4 2.6 collective-permute-done.39
  368.1 2.5 add_add_fusion
  371.4 4.8 %collective-permute-start.42 = (f32[12,72,128]{2,1,0:T(8,128)}, f32[12,72,128]{2,1,0:T(8,128)}, u32[]{:S(2)}, u32[]{:S(2)}) collective-permute-start(f32[12,72,128]{2,1,0:T(8,128)} %constant_dynamic-slice_fusion), channel_id=1, source_target_pairs={{0,1},{1,0},{2,3},{3,2},{4,5},{5,4},{6,7},{7,6},{8,9},{9,8},{10,11... | collective-permute-start | bytes 1327112 | tf_op jit(solution)/shard_map/ppermute | solution.py:370
  376.2 1.8 collective-permute-done.42
  379.2 5.8 %shard_map.37 = f32[12,8,9216]{2,1,0:T(8,128)} custom-call(f32[3456,128]{1,0:T(8,128)S(1)} %bitcast.28, f32[3456,128]{1,0:T(8,128)S(1)} %bitcast.29), custom_call_target="tpu_custom_call" | custom-call | tf_op jit(solution)/shard_map/pallas_call | solution.py:358
  (110 shorter events, 30.4 us)
Async XLA Ops:
  0.0 2.0 copy-start
  6.7 62.0 %all-to-all-start = ((f32[4,12,72,128]{3,2,1,0:T(8,128)}), f32[4,12,72,128]{3,2,1,0:T(8,128)S(1)}, u32[]{:S(2)}, u32[]{:S(2)}) async-start(f32[4,12,72,128]{3,2,1,0:T(8,128)} %bitcast.6), calls=%async_computation | async-start | bytes 3538944 | tf_op jit(solution)/shard_map/all_to_all | solution.py:474
  12.4 2.7 collective-permute-start
  16.3 88.3 %copy-start.6 = (f32[24,72,128]{2,1,0:T(8,128)}, f32[24,72,128]{2,1,0:T(8,128)S(1)}, u32[]{:S(2)}) copy-start(f32[24,72,128]{2,1,0:T(8,128)S(1)} %pad_maximum_fusion.1.refs_1_) | copy-start | bytes 2654212
  16.3 21.0 %collective-permute-start.1 = (f32[24,72,128]{2,1,0:T(8,128)S(1)}, f32[24,72,128]{2,1,0:T(8,128)}, u32[]{:S(2)}, u32[]{:S(2)}) collective-permute-start(f32[24,72,128]{2,1,0:T(8,128)S(1)} %pad_maximum_fusion.1.refs_1_), channel_id=1, source_target_pairs={{0,8},{8,0},{16,24},{24,16},{1,9},{9,1},{17,25},{25,17},{2,10},{10... | collective-permute-start | bytes 2654216 | tf_op jit(solution)/shard_map/ppermute | solution.py:370
  17.6 51.1 %collective-permute-start.3 = (f32[24,72,128]{2,1,0:T(8,128)S(1)}, f32[24,72,128]{2,1,0:T(8,128)}, u32[]{:S(2)}, u32[]{:S(2)}) collective-permute-start(f32[24,72,128]{2,1,0:T(8,128)S(1)} %pad_maximum_fusion.1.refs_1_), channel_id=1, source_target_pairs={{0,2},{2,4},{4,6},{1,3},{3,5},{5,7},{8,10},{10,12},{12,14},{9,11},... | collective-permute-start | bytes 2654216 | tf_op jit(solution)/shard_map/ppermute | solution.py:374
  20.7 48.0 %collective-permute-start.4 = (f32[24,72,128]{2,1,0:T(8,128)S(1)}, f32[24,72,128]{2,1,0:T(8,128)S(1)}, u32[]{:S(2)}, u32[]{:S(2)}) collective-permute-start(f32[24,72,128]{2,1,0:T(8,128)S(1)} %pad_maximum_fusion.1.refs_1_), channel_id=1, source_target_pairs={{2,0},{4,2},{6,4},{3,1},{5,3},{7,5},{10,8},{12,10},{14,12},{11,9},... | collective-permute-start | bytes 2654216 | tf_op jit(solution)/shard_map/ppermute | solution.py:374
  22.9 45.8 %collective-permute-start.5 = (f32[24,72,128]{2,1,0:T(8,128)S(1)}, f32[24,72,128]{2,1,0:T(8,128)}, u32[]{:S(2)}, u32[]{:S(2)}) collective-permute-start(f32[24,72,128]{2,1,0:T(8,128)S(1)} %pad_maximum_fusion.1.refs_1_), channel_id=1, source_target_pairs={{0,16},{8,24},{16,0},{24,8},{1,17},{9,25},{17,1},{25,9},{2,18},{10... | collective-permute-start | bytes 2654216 | tf_op jit(solution)/shard_map/ppermute | solution.py:370
  37.3 31.3 %collective-permute-start.2 = (f32[24,72,128]{2,1,0:T(8,128)}, f32[24,72,128]{2,1,0:T(8,128)}, u32[]{:S(2)}, u32[]{:S(2)}) collective-permute-start(f32[24,72,128]{2,1,0:T(8,128)} %collective-permute-done.1.refs_1_), channel_id=1, source_target_pairs={{0,16},{8,24},{16,0},{24,8},{1,17},{9,25},{17,1},{25,9},{2,18},{10... | collective-permute-start | bytes 2654216 | tf_op jit(solution)/shard_map/ppermute | solution.py:370
  68.7 35.9 %copy-start.1 = (f32[4,12,72,128]{3,2,1,0:T(8,128)}, f32[4,12,72,128]{3,2,1,0:T(8,128)S(1)}, u32[]{:S(2)}) copy-start(f32[4,12,72,128]{3,2,1,0:T(8,128)S(1)} %all-to-all-done.refs_5_) | copy-start | bytes 5308420
  68.7 21.4 %collective-permute-start.7 = (f32[24,72,128]{2,1,0:T(8,128)}, f32[24,72,128]{2,1,0:T(8,128)S(1)}, u32[]{:S(2)}, u32[]{:S(2)}) collective-permute-start(f32[24,72,128]{2,1,0:T(8,128)} %collective-permute-done.3), channel_id=1, source_target_pairs={{2,4},{4,6},{3,5},{5,7},{10,12},{12,14},{11,13},{13,15},{18,20},{2... | collective-permute-start | bytes 2654216 | tf_op jit(solution)/shard_map/ppermute | solution.py:374
  70.6 20.2 %collective-permute-start.8 = (f32[24,72,128]{2,1,0:T(8,128)S(1)}, f32[24,72,128]{2,1,0:T(8,128)S(1)}, u32[]{:S(2)}, u32[]{:S(2)}) collective-permute-start(f32[24,72,128]{2,1,0:T(8,128)S(1)} %collective-permute-done.4), channel_id=1, source_target_pairs={{2,0},{4,2},{3,1},{5,3},{10,8},{12,10},{11,9},{13,11},{18,16},{20,... | collective-permute-start | bytes 2654216 | tf_op jit(solution)/shard_map/ppermute | solution.py:374
  75.4 15.5 %copy-start.7 = (f32[24,72,128]{2,1,0:T(8,128)}, f32[24,72,128]{2,1,0:T(8,128)S(1)}, u32[]{:S(2)}) copy-start(f32[24,72,128]{2,1,0:T(8,128)S(1)} %broadcast_select_fusion.1.refs_2_) | copy-start | bytes 2654212
  75.4 18.8 %collective-permute-start.6 = (f32[24,72,128]{2,1,0:T(8,128)S(1)}, f32[24,72,128]{2,1,0:T(8,128)S(1)}, u32[]{:S(2)}, u32[]{:S(2)}) collective-permute-start(f32[24,72,128]{2,1,0:T(8,128)S(1)} %broadcast_select_fusion.1.refs_2_), channel_id=1, source_target_pairs={{0,16},{8,24},{16,0},{24,8},{1,17},{9,25},{17,1},{25,9},{2,18},{10... | collective-permute-start | bytes 2654216 | tf_op jit(solution)/shard_map/ppermute | solution.py:370
  76.7 18.4 %collective-permute-start.9 = (f32[24,72,128]{2,1,0:T(8,128)S(1)}, f32[24,72,128]{2,1,0:T(8,128)S(1)}, u32[]{:S(2)}, u32[]{:S(2)}) collective-permute-start(f32[24,72,128]{2,1,0:T(8,128)S(1)} %broadcast_select_fusion.1.refs_2_), channel_id=1, source_target_pairs={{0,8},{8,0},{16,24},{24,16},{1,9},{9,1},{17,25},{25,17},{2,10},{10... | collective-permute-start | bytes 2654216 | tf_op jit(solution)/shard_map/ppermute | solution.py:370
  77.9 45.8 %collective-permute-start.18 = (f32[4,12,72,128]{3,2,1,0:T(8,128)S(1)}, f32[4,12,72,128]{3,2,1,0:T(8,128)}, u32[]{:S(2)}, u32[]{:S(2)}) collective-permute-start(f32[4,12,72,128]{3,2,1,0:T(8,128)S(1)} %all-to-all-done.refs_5_), channel_id=1, source_target_pairs={{0,1},{1,0},{2,3},{3,2},{4,5},{5,4},{6,7},{7,6},{8,9},{9,8},{10,11... | collective-permute-start | bytes 5308424 | tf_op jit(solution)/shard_map/ppermute | solution.py:370
  95.1 2.2 copy-start.18
  95.2 17.2 %collective-permute-start.10 = (f32[24,72,128]{2,1,0:T(8,128)}, f32[24,72,128]{2,1,0:T(8,128)}, u32[]{:S(2)}, u32[]{:S(2)}) collective-permute-start(f32[24,72,128]{2,1,0:T(8,128)} %add.162.refs_3_), channel_id=1, source_target_pairs={{4,6},{2,0},{5,7},{3,1},{12,14},{10,8},{13,15},{11,9},{20,22},{18,... | collective-permute-start | bytes 2654216 | tf_op jit(solution)/shard_map/ppermute | solution.py:374
  97.4 17.8 %collective-permute-start.11 = (f32[24,72,128]{2,1,0:T(8,128)}, f32[24,72,128]{2,1,0:T(8,128)}, u32[]{:S(2)}, u32[]{:S(2)}) collective-permute-start(f32[24,72,128]{2,1,0:T(8,128)} %add.162.refs_3_), channel_id=1, source_target_pairs={{0,8},{8,0},{16,24},{24,16},{1,9},{9,1},{17,25},{25,17},{2,10},{10... | collective-permute-start | bytes 2654216 | tf_op jit(solution)/shard_map/ppermute | solution.py:370
  98.6 17.6 %collective-permute-start.12 = (f32[24,72,128]{2,1,0:T(8,128)}, f32[24,72,128]{2,1,0:T(8,128)}, u32[]{:S(2)}, u32[]{:S(2)}) collective-permute-start(f32[24,72,128]{2,1,0:T(8,128)} %add.162.refs_3_), channel_id=1, source_target_pairs={{0,16},{8,24},{16,0},{24,8},{1,17},{9,25},{17,1},{25,9},{2,18},{10... | collective-permute-start | bytes 2654216 | tf_op jit(solution)/shard_map/ppermute | solution.py:370
  112.4 11.3 %copy-start.8 = (f32[24,72,128]{2,1,0:T(8,128)}, f32[24,72,128]{2,1,0:T(8,128)S(1)}, u32[]{:S(2)}) copy-start(f32[24,72,128]{2,1,0:T(8,128)S(1)} %broadcast_select_fusion.refs_4_) | copy-start | bytes 2654212
  116.1 23.0 %collective-permute-start.13 = (f32[24,72,128]{2,1,0:T(8,128)S(1)}, f32[24,72,128]{2,1,0:T(8,128)}, u32[]{:S(2)}, u32[]{:S(2)}) collective-permute-start(f32[24,72,128]{2,1,0:T(8,128)S(1)} %broadcast_select_fusion.refs_4_), channel_id=1, source_target_pairs={{0,8},{8,0},{16,24},{24,16},{1,9},{9,1},{17,25},{25,17},{2,10},{10... | collective-permute-start | bytes 2654216 | tf_op jit(solution)/shard_map/ppermute | solution.py:370
  116.4 22.7 %collective-permute-start.14 = (f32[24,72,128]{2,1,0:T(8,128)S(1)}, f32[24,72,128]{2,1,0:T(8,128)}, u32[]{:S(2)}, u32[]{:S(2)}) collective-permute-start(f32[24,72,128]{2,1,0:T(8,128)S(1)} %broadcast_select_fusion.refs_4_), channel_id=1, source_target_pairs={{0,16},{8,24},{16,0},{24,8},{1,17},{9,25},{17,1},{25,9},{2,18},{10... | collective-permute-start | bytes 2654216 | tf_op jit(solution)/shard_map/ppermute | solution.py:370
  117.9 78.5 %all-to-all-start.2 = ((f32[4,12,72,128]{3,2,1,0:T(8,128)}), f32[4,12,72,128]{3,2,1,0:T(8,128)}, u32[]{:S(2)}, u32[]{:S(2)}) async-start(f32[4,12,72,128]{3,2,1,0:T(8,128)} %bitcast.3), calls=%async_computation.2 | async-start | bytes 3538944 | tf_op jit(solution)/shard_map/all_to_all | solution.py:484
  123.7 15.4 %copy-start.17 = (f32[24,72,128]{2,1,0:T(8,128)S(1)}, f32[24,72,128]{2,1,0:T(8,128)}, u32[]{:S(2)}) copy-start(f32[24,72,128]{2,1,0:T(8,128)} %copy-done.16) | copy-start | bytes 2654212
  139.1 16.7 %collective-permute-start.15 = (f32[24,72,128]{2,1,0:T(8,128)S(1)}, f32[24,72,128]{2,1,0:T(8,128)S(1)}, u32[]{:S(2)}, u32[]{:S(2)}) collective-permute-start(f32[24,72,128]{2,1,0:T(8,128)S(1)} %copy-done.17), channel_id=1, source_target_pairs={{0,8},{8,0},{16,24},{24,16},{1,9},{9,1},{17,25},{25,17},{2,10},{10... | collective-permute-start | bytes 2654216 | tf_op jit(solution)/shard_map/ppermute | solution.py:370
  139.4 16.7 %collective-permute-start.16 = (f32[24,72,128]{2,1,0:T(8,128)}, f32[24,72,128]{2,1,0:T(8,128)S(1)}, u32[]{:S(2)}, u32[]{:S(2)}) collective-permute-start(f32[24,72,128]{2,1,0:T(8,128)} %collective-permute-done.11.refs_3_), channel_id=1, source_target_pairs={{0,16},{8,24},{16,0},{24,8},{1,17},{9,25},{17,1},{25,9},{2,18},{10... | collective-permute-start | bytes 2654216 | tf_op jit(solution)/shard_map/ppermute | solution.py:370
  155.9 15.5 %copy-start.19 = (f32[24,72,128]{2,1,0:T(8,128)}, f32[24,72,128]{2,1,0:T(8,128)S(1)}, u32[]{:S(2)}) copy-start(f32[24,72,128]{2,1,0:T(8,128)S(1)} %collective-permute-done.15.refs_2_) | copy-start | bytes 2654212
  155.9 18.1 %collective-permute-start.17 = (f32[24,72,128]{2,1,0:T(8,128)}, f32[24,72,128]{2,1,0:T(8,128)S(1)}, u32[]{:S(2)}, u32[]{:S(2)}) collective-permute-start(f32[24,72,128]{2,1,0:T(8,128)} %collective-permute-done.14.refs_4_), channel_id=1, source_target_pairs={{0,8},{8,0},{16,24},{24,16},{1,9},{9,1},{17,25},{25,17},{2,10},{10... | collective-permute-start | bytes 2654216 | tf_op jit(solution)/shard_map/ppermute | solution.py:370
  156.1 15.2 %copy-start.20 = (f32[24,72,128]{2,1,0:T(8,128)}, f32[24,72,128]{2,1,0:T(8,128)S(1)}, u32[]{:S(2)}) copy-start(f32[24,72,128]{2,1,0:T(8,128)S(1)} %collective-permute-done.16.refs_3_) | copy-start | bytes 2654212
  190.1 9.8 %collective-permute-start.19 = (f32[4,12,72,128]{3,2,1,0:T(8,128)}, f32[4,12,72,128]{3,2,1,0:T(8,128)S(1)}, u32[]{:S(2)}, u32[]{:S(2)}) collective-permute-start(f32[4,12,72,128]{3,2,1,0:T(8,128)} %get-tuple-element.86), channel_id=1, source_target_pairs={{0,1},{1,0},{2,3},{3,2},{4,5},{5,4},{6,7},{7,6},{8,9},{9,8},{10,11... | collective-permute-start | bytes 5308424 | tf_op jit(solution)/shard_map/ppermute | solution.py:370
  196.4 11.0 %collective-permute-start.20 = (f32[4,12,72,128]{3,2,1,0:T(8,128)}, f32[4,12,72,128]{3,2,1,0:T(8,128)S(1)}, u32[]{:S(2)}, u32[]{:S(2)}) collective-permute-start(f32[4,12,72,128]{3,2,1,0:T(8,128)} %all-to-all-done.2.refs_5_), channel_id=1, source_target_pairs={{0,1},{1,0},{2,3},{3,2},{4,5},{5,4},{6,7},{7,6},{8,9},{9,8},{10,11... | collective-permute-start | bytes 5308424 | tf_op jit(solution)/shard_map/ppermute | solution.py:370
  202.9 65.5 %all-to-all-start.1 = ((f32[4,12,72,128]{3,2,1,0:T(8,128)}), f32[4,12,72,128]{3,2,1,0:T(8,128)S(1)}, u32[]{:S(2)}, u32[]{:S(2)}) async-start(f32[4,12,72,128]{3,2,1,0:T(8,128)} %add.167), calls=%async_computation.1 | async-start | bytes 3538944 | tf_op jit(solution)/shard_map/all_to_all | solution.py:452
  207.4 1.3 copy-start.15
  223.8 20.5 %collective-permute-start.21 = (f32[24,72,128]{2,1,0:T(8,128)}, f32[24,72,128]{2,1,0:T(8,128)S(1)}, u32[]{:S(2)}, u32[]{:S(2)}) collective-permute-start(f32[24,72,128]{2,1,0:T(8,128)} %get-tuple-element.93), channel_id=1, source_target_pairs={{0,8},{8,0},{16,24},{24,16},{1,9},{9,1},{17,25},{25,17},{2,10},{10... | collective-permute-start | bytes 2654216 | tf_op jit(solution)/shard_map/ppermute | solution.py:370
  224.1 20.2 %collective-permute-start.22 = (f32[24,72,128]{2,1,0:T(8,128)}, f32[24,72,128]{2,1,0:T(8,128)S(1)}, u32[]{:S(2)}, u32[]{:S(2)}) collective-permute-start(f32[24,72,128]{2,1,0:T(8,128)} %get-tuple-element.94), channel_id=1, source_target_pairs={{0,16},{8,24},{16,0},{24,8},{1,17},{9,25},{17,1},{25,9},{2,18},{10... | collective-permute-start | bytes 2654216 | tf_op jit(solution)/shard_map/ppermute | solution.py:370
  245.3 21.2 %collective-permute-start.23 = (f32[24,72,128]{2,1,0:T(8,128)}, f32[24,72,128]{2,1,0:T(8,128)S(1)}, u32[]{:S(2)}, u32[]{:S(2)}) collective-permute-start(f32[24,72,128]{2,1,0:T(8,128)} %get-tuple-element.95), channel_id=1, source_target_pairs={{0,8},{8,0},{16,24},{24,16},{1,9},{9,1},{17,25},{25,17},{2,10},{10... | collective-permute-start | bytes 2654216 | tf_op jit(solution)/shard_map/ppermute | solution.py:370
  246.2 20.3 %collective-permute-start.24 = (f32[24,72,128]{2,1,0:T(8,128)}, f32[24,72,128]{2,1,0:T(8,128)S(1)}, u32[]{:S(2)}, u32[]{:S(2)}) collective-permute-start(f32[24,72,128]{2,1,0:T(8,128)} %get-tuple-element.97), channel_id=1, source_target_pairs={{0,16},{8,24},{16,0},{24,8},{1,17},{9,25},{17,1},{25,9},{2,18},{10... | collective-permute-start | bytes 2654216 | tf_op jit(solution)/shard_map/ppermute | solution.py:370
  266.5 1.3 copy-start.5
  266.5 17.1 %copy-start.11 = (f32[24,72,128]{2,1,0:T(8,128)}, f32[24,72,128]{2,1,0:T(8,128)S(1)}, u32[]{:S(2)}) copy-start(f32[24,72,128]{2,1,0:T(8,128)S(1)} %collective-permute-done.24) | copy-start | bytes 2654212
  266.5 20.1 %collective-permute-start.26 = (f32[24,72,128]{2,1,0:T(8,128)}, f32[24,72,128]{2,1,0:T(8,128)}, u32[]{:S(2)}, u32[]{:S(2)}) collective-permute-start(f32[24,72,128]{2,1,0:T(8,128)} %add.170), channel_id=1, source_target_pairs={{0,16},{8,24},{16,0},{24,8},{1,17},{9,25},{17,1},{25,9},{2,18},{10... | collective-permute-start | bytes 2654216 | tf_op jit(solution)/shard_map/ppermute | solution.py:370
  267.8 19.0 %collective-permute-start.25 = (f32[24,72,128]{2,1,0:T(8,128)}, f32[24,72,128]{2,1,0:T(8,128)}, u32[]{:S(2)}, u32[]{:S(2)}) collective-permute-start(f32[24,72,128]{2,1,0:T(8,128)} %add.169), channel_id=1, source_target_pairs={{0,8},{8,0},{16,24},{24,16},{1,9},{9,1},{17,25},{25,17},{2,10},{10... | collective-permute-start | bytes 2654216 | tf_op jit(solution)/shard_map/ppermute | solution.py:370
  283.6 8.8 %collective-permute-start.34 = (f32[4,12,72,128]{3,2,1,0:T(8,128)}, f32[4,12,72,128]{3,2,1,0:T(8,128)S(1)}, u32[]{:S(2)}, u32[]{:S(2)}) collective-permute-start(f32[4,12,72,128]{3,2,1,0:T(8,128)} %get-tuple-element.131), channel_id=1, source_target_pairs={{0,1},{1,0},{2,3},{3,2},{4,5},{5,4},{6,7},{7,6},{8,9},{9,8},{10,11... | collective-permute-start | bytes 5308424 | tf_op jit(solution)/shard_map/ppermute | solution.py:370
  286.9 24.7 %collective-permute-start.28 = (f32[24,72,128]{2,1,0:T(8,128)}, f32[24,72,128]{2,1,0:T(8,128)}, u32[]{:S(2)}, u32[]{:S(2)}) collective-permute-start(f32[24,72,128]{2,1,0:T(8,128)} %get-tuple-element.120), channel_id=1, source_target_pairs={{0,16},{8,24},{16,0},{24,8},{1,17},{9,25},{17,1},{25,9},{2,18},{10... | collective-permute-start | bytes 2654216 | tf_op jit(solution)/shard_map/ppermute | solution.py:370
  288.0 18.1 %collective-permute-start.27 = (f32[24,72,128]{2,1,0:T(8,128)}, f32[24,72,128]{2,1,0:T(8,128)}, u32[]{:S(2)}, u32[]{:S(2)}) collective-permute-start(f32[24,72,128]{2,1,0:T(8,128)} %get-tuple-element.118), channel_id=1, source_target_pairs={{0,8},{8,0},{16,24},{24,16},{1,9},{9,1},{17,25},{25,17},{2,10},{10... | collective-permute-start | bytes 2654216 | tf_op jit(solution)/shard_map/ppermute | solution.py:370
  291.1 20.7 %collective-permute-start.33 = (f32[24,72,128]{2,1,0:T(8,128)}, f32[24,72,128]{2,1,0:T(8,128)}, u32[]{:S(2)}, u32[]{:S(2)}) collective-permute-start(f32[24,72,128]{2,1,0:T(8,128)} %add_add_fusion.2), channel_id=1, source_target_pairs={{0,2},{6,4},{1,3},{7,5},{8,10},{14,12},{9,11},{15,13},{16,18},{22,... | collective-permute-start | bytes 2654216 | tf_op jit(solution)/shard_map/ppermute | solution.py:374
  292.4 1.2 copy-start.4
  296.9 17.4 %collective-permute-start.35 = (f32[12,72,128]{2,1,0:T(8,128)}, f32[12,72,128]{2,1,0:T(8,128)}, u32[]{:S(2)}, u32[]{:S(2)}) collective-permute-start(f32[12,72,128]{2,1,0:T(8,128)} %get-tuple-element.141), channel_id=1, source_target_pairs={{2,0},{4,2},{3,1},{5,3},{10,8},{12,10},{11,9},{13,11},{18,16},{20,... | collective-permute-start | bytes 1327112 | tf_op jit(solution)/shard_map/ppermute | solution.py:374
  299.8 14.5 %collective-permute-start.36 = (f32[12,72,128]{2,1,0:T(8,128)}, f32[12,72,128]{2,1,0:T(8,128)}, u32[]{:S(2)}, u32[]{:S(2)}) collective-permute-start(f32[12,72,128]{2,1,0:T(8,128)} %get-tuple-element.140), channel_id=1, source_target_pairs={{2,4},{4,6},{3,5},{5,7},{10,12},{12,14},{11,13},{13,15},{18,20},{2... | collective-permute-start | bytes 1327112 | tf_op jit(solution)/shard_map/ppermute | solution.py:374
  306.1 8.8 %collective-permute-start.37 = (f32[12,72,128]{2,1,0:T(8,128)}, f32[12,72,128]{2,1,0:T(8,128)}, u32[]{:S(2)}, u32[]{:S(2)}) collective-permute-start(f32[12,72,128]{2,1,0:T(8,128)} %get-tuple-element.139), channel_id=1, source_target_pairs={{2,6},{4,0},{3,7},{5,1},{10,14},{12,8},{11,15},{13,9},{18,22},{20,... | collective-permute-start | bytes 1327112 | tf_op jit(solution)/shard_map/ppermute | solution.py:374
  311.6 17.0 %collective-permute-start.30 = (f32[24,72,128]{2,1,0:T(8,128)S(1)}, f32[24,72,128]{2,1,0:T(8,128)S(1)}, u32[]{:S(2)}, u32[]{:S(2)}) collective-permute-start(f32[24,72,128]{2,1,0:T(8,128)S(1)} %add.171), channel_id=1, source_target_pairs={{0,16},{8,24},{16,0},{24,8},{1,17},{9,25},{17,1},{25,9},{2,18},{10... | collective-permute-start | bytes 2654216 | tf_op jit(solution)/shard_map/ppermute | solution.py:370
  311.7 16.9 %collective-permute-start.29 = (f32[24,72,128]{2,1,0:T(8,128)}, f32[24,72,128]{2,1,0:T(8,128)S(1)}, u32[]{:S(2)}, u32[]{:S(2)}) collective-permute-start(f32[24,72,128]{2,1,0:T(8,128)} %get-tuple-element.121), channel_id=1, source_target_pairs={{0,8},{8,0},{16,24},{24,16},{1,9},{9,1},{17,25},{25,17},{2,10},{10... | collective-permute-start | bytes 2654216 | tf_op jit(solution)/shard_map/ppermute | solution.py:370
  312.0 14.9 %copy-start.10 = (f32[24,72,128]{2,1,0:T(8,128)S(1)}, f32[24,72,128]{2,1,0:T(8,128)}, u32[]{:S(2)}) copy-start(f32[24,72,128]{2,1,0:T(8,128)} %get-tuple-element.111) | copy-start | bytes 2654212
  312.0 14.9 %copy-start.12 = (f32[24,72,128]{2,1,0:T(8,128)S(1)}, f32[24,72,128]{2,1,0:T(8,128)}, u32[]{:S(2)}) copy-start(f32[24,72,128]{2,1,0:T(8,128)} %copy-done.11) | copy-start | bytes 2654212
  314.2 29.9 %copy-start.9 = (f32[24,72,128]{2,1,0:T(8,128)S(1)}, f32[24,72,128]{2,1,0:T(8,128)}, u32[]{:S(2)}) copy-start(f32[24,72,128]{2,1,0:T(8,128)} %get-tuple-element.127) | copy-start | bytes 2654212
  317.2 25.0 %collective-permute-start.38 = (f32[24,72,128]{2,1,0:T(8,128)S(1)}, f32[24,72,128]{2,1,0:T(8,128)S(1)}, u32[]{:S(2)}, u32[]{:S(2)}) collective-permute-start(f32[24,72,128]{2,1,0:T(8,128)S(1)} %add_add_fusion.1), channel_id=1, source_target_pairs={{0,2},{2,4},{1,3},{3,5},{8,10},{10,12},{9,11},{11,13},{16,18},{18,... | collective-permute-start | bytes 2654216 | tf_op jit(solution)/shard_map/ppermute | solution.py:374
  318.5 25.7 %collective-permute-start.40 = (f32[24,72,128]{2,1,0:T(8,128)S(1)}, f32[24,72,128]{2,1,0:T(8,128)S(1)}, u32[]{:S(2)}, u32[]{:S(2)}) collective-permute-start(f32[24,72,128]{2,1,0:T(8,128)S(1)} %add_add_fusion.1), channel_id=1, source_target_pairs={{4,2},{6,4},{5,3},{7,5},{12,10},{14,12},{13,11},{15,13},{20,18},{2... | collective-permute-start | bytes 2654216 | tf_op jit(solution)/shard_map/ppermute | solution.py:374
  328.6 23.3 %collective-permute-start.32 = (f32[24,72,128]{2,1,0:T(8,128)}, f32[24,72,128]{2,1,0:T(8,128)}, u32[]{:S(2)}, u32[]{:S(2)}) collective-permute-start(f32[24,72,128]{2,1,0:T(8,128)} %get-tuple-element.126), channel_id=1, source_target_pairs={{0,16},{8,24},{16,0},{24,8},{1,17},{9,25},{17,1},{25,9},{2,18},{10... | collective-permute-start | bytes 2654216 | tf_op jit(solution)/shard_map/ppermute | solution.py:370
  330.0 21.9 %collective-permute-start.31 = (f32[24,72,128]{2,1,0:T(8,128)}, f32[24,72,128]{2,1,0:T(8,128)}, u32[]{:S(2)}, u32[]{:S(2)}) collective-permute-start(f32[24,72,128]{2,1,0:T(8,128)} %add.168), channel_id=1, source_target_pairs={{0,8},{8,0},{16,24},{24,16},{1,9},{9,1},{17,25},{25,17},{2,10},{10... | collective-permute-start | bytes 2654216 | tf_op jit(solution)/shard_map/ppermute | solution.py:370
  345.7 19.7 %collective-permute-start.41 = (f32[24,72,128]{2,1,0:T(8,128)S(1)}, f32[24,72,128]{2,1,0:T(8,128)}, u32[]{:S(2)}, u32[]{:S(2)}) collective-permute-start(f32[24,72,128]{2,1,0:T(8,128)S(1)} %get-tuple-element.136), channel_id=1, source_target_pairs={{2,0},{4,2},{6,4},{3,1},{5,3},{7,5},{10,8},{12,10},{14,12},{11,9},... | collective-permute-start | bytes 2654216 | tf_op jit(solution)/shard_map/ppermute | solution.py:374
  348.8 19.3 %collective-permute-start.39 = (f32[24,72,128]{2,1,0:T(8,128)S(1)}, f32[24,72,128]{2,1,0:T(8,128)}, u32[]{:S(2)}, u32[]{:S(2)}) collective-permute-start(f32[24,72,128]{2,1,0:T(8,128)S(1)} %get-tuple-element.135), channel_id=1, source_target_pairs={{0,2},{2,4},{4,6},{1,3},{3,5},{5,7},{8,10},{10,12},{12,14},{9,11},... | collective-permute-start | bytes 2654216 | tf_op jit(solution)/shard_map/ppermute | solution.py:374
  368.1 10.9 %copy-start.2 = (f32[12,72,128]{2,1,0:T(8,128)S(1)}, f32[12,72,128]{2,1,0:T(8,128)}, u32[]{:S(2)}) copy-start(f32[12,72,128]{2,1,0:T(8,128)} %get-tuple-element.133) | copy-start | bytes 1327108
  368.1 10.9 %copy-start.3 = (f32[12,72,128]{2,1,0:T(8,128)S(1)}, f32[12,72,128]{2,1,0:T(8,128)}, u32[]{:S(2)}) copy-start(f32[12,72,128]{2,1,0:T(8,128)} %get-tuple-element.134) | copy-start | bytes 1327108
  371.4 6.5 %collective-permute-start.42 = (f32[12,72,128]{2,1,0:T(8,128)}, f32[12,72,128]{2,1,0:T(8,128)}, u32[]{:S(2)}, u32[]{:S(2)}) collective-permute-start(f32[12,72,128]{2,1,0:T(8,128)} %constant_dynamic-slice_fusion), channel_id=1, source_target_pairs={{0,1},{1,0},{2,3},{3,2},{4,5},{5,4},{6,7},{7,6},{8,9},{9,8},{10,11... | collective-permute-start | bytes 1327112 | tf_op jit(solution)/shard_map/ppermute | solution.py:370
  (4 other events, 3.8 us)

commit v9 on v8

--- a/solution.py
+++ b/solution.py
@@ -283,7 +283,7 @@
         out_shape=kinds + pieces,
         scratch_shapes=[pltpu.VMEM(block, F32)] * 4
         + [
-            pltpu.VMEM((count * (count + GAP), LANES), F32),
+            pltpu.VMEM(((count + 1) * (count + GAP), LANES), F32),
             pltpu.VMEM(tables[0].shape, BF16),
             pltpu.VMEM(tables[1].shape, F32),
             pltpu.SemaphoreType.DMA((8, zs)),
@@ -311,58 +311,48 @@
     return tile % 3 * (rows // 3) + tile // 3
 
 
-def pack_kernel(sets, planes, rows, flat, *packed):
+def pack_kernel(planes, rows, flat, packed):
     plane = pl.program_id(0)
     for tile in range(rows):
         row = plane * rows + piece_row(tile, rows)
-        for runs, out in zip(sets, packed):
-            done = 0
-            for first, size in runs:
-                value = flat[0, first : first + size, tile * LANES : (tile + 1) * LANES]
-                out[pl.ds(row + done * planes * rows, size, stride=planes * rows), :] = value
-                done += size
-
-
-def pack(fields, sets):
+        value = flat[0, :, tile * LANES : (tile + 1) * LANES]
+        packed[pl.ds(row, flat.shape[1], stride=planes * rows), :] = value
+
+
+def pack(fields):
     planes, number, flat = fields.shape
     rows = flat // LANES
-    size = sum(run[1] for run in sets[0])
-    out = (size * planes * rows, LANES)
+    out = (number * planes * rows, LANES)
     packed = pl.pallas_call(
-        functools.partial(pack_kernel, sets, planes, rows),
+        functools.partial(pack_kernel, planes, rows),
         grid=(planes,),
         in_specs=[pl.BlockSpec((1, number, flat), lambda i: (i, 0, 0))],
-        out_specs=[pl.BlockSpec(out, lambda i: (0, 0))] * len(sets),
-        out_shape=[jax.ShapeDtypeStruct(out, F32)] * len(sets),
+        out_specs=pl.BlockSpec(out, lambda i: (0, 0)),
+        out_shape=jax.ShapeDtypeStruct(out, F32),
         compiler_params=pltpu.CompilerParams(vmem_limit_bytes=32 * 1024 * 1024),
     )(fields)
-    return [p.reshape(size, planes, rows, LANES) for p in packed]
-
-
-def unpack_kernel(order, planes, rows, *refs):
-    packed, flat = refs[:-1], refs[-1]
+    return packed.reshape(number, planes, rows, LANES)
+
+
+def unpack_kernel(planes, rows, packed, flat):
     plane = pl.program_id(0)
     for tile in range(rows):
         row = plane * rows + piece_row(tile, rows)
-        runs = [
-            packed[k][pl.ds(row + first * planes * rows, size, stride=planes * rows), :] for k, first, size in order
-        ]
-        value = runs[0] if len(runs) == 1 else jnp.concatenate(runs, axis=0)
+        value = packed[pl.ds(row, flat.shape[1], stride=planes * rows), :]
         flat[0, :, tile * LANES : (tile + 1) * LANES] = -ALPHA * value
 
 
-def unpack(fields, order):
-    planes, rows = fields[0].shape[1:3]
-    number = sum(run[2] for run in order)
-    flats = [f.reshape(f.shape[0] * planes * rows, LANES) for f in fields]
+def unpack(fields):
+    number, planes, rows, _ = fields.shape
+    whole = (number * planes * rows, LANES)
     return pl.pallas_call(
-        functools.partial(unpack_kernel, order, planes, rows),
+        functools.partial(unpack_kernel, planes, rows),
         grid=(planes,),
-        in_specs=[pl.BlockSpec(f.shape, lambda i: (0, 0), pipeline_mode=pl.Buffered(1)) for f in flats],
+        in_specs=[pl.BlockSpec(whole, lambda i: (0, 0), pipeline_mode=pl.Buffered(1))],
         out_specs=pl.BlockSpec((1, number, rows * LANES), lambda i: (i, 0, 0)),
         out_shape=jax.ShapeDtypeStruct((planes, number, rows * LANES), F32),
         compiler_params=pltpu.CompilerParams(vmem_limit_bytes=32 * 1024 * 1024),
-    )(*flats)
+    )(fields.reshape(whole))
 
 
 def swap(value, axis, flip):
@@ -415,12 +405,14 @@
     place = jnp.stack([lax.axis_index("z"), core]).astype(jnp.int32)
     tables = make_tables(count)
     square = bands == ROUNDS == 4 and zs == 4 and n_local == 8
-    runs = [((2, 4),), ((0, 1), (6, 2), (1, 1))] if square else [((k * zs, zs),) for k in range(n_local // zs)]
-    sets = pack(orbitals.swapaxes(0, 1), runs)
+    packed = pack(orbitals.swapaxes(0, 1))
+    if square:
+        sets = [packed[2:6], jnp.concatenate([packed[0:1], packed[6:8], packed[1:2]], axis=0)]
+    else:
+        sets = [packed[k : k + zs] for k in range(0, n_local, zs)]
     tail = sets[0].shape[2:]
-    members, step = (sets[1], zs - 1) if square else (sets[0], 1)
-    keep = lax.dynamic_index_in_dim(members, core * step, 0, keepdims=False)
-    come = swap(lax.dynamic_index_in_dim(members, (1 - core) * step, 0, keepdims=False), "core", 1)
+    keep = lax.dynamic_index_in_dim(packed, core, 0, keepdims=False)
+    come = swap(lax.dynamic_index_in_dim(packed, 1 - core, 0, keepdims=False), "core", 1)
     slab = jnp.concatenate([jnp.where(core == 0, keep, come), jnp.where(core == 0, come, keep)], axis=0)
     if square:
         return square_local(place, tables, sets, slab)
@@ -441,7 +433,7 @@
     owner = lax.psum_scatter(owner, ("band", "z"), scatter_dimension=0, tiled=True)
     back = [send_back(core_sum(*sums)) for sums in sums_out]
     back[0] = back[0].at[:PAIR].add(jnp.stack(by_member(owner)))
-    return unpack(back, [(k, 0, zs) for k in range(len(back))]).swapaxes(0, 1)
+    return unpack(jnp.concatenate(back, axis=0)).swapaxes(0, 1)
 
 
 def core_sum(keep, give):
@@ -515,8 +507,7 @@
     after = jnp.where(z == 0, near, own[3] + side3 + far3 + after)
     after, before = along(after, RIGHT), along(near + before, LEFT)
     owner = by_member(own[0] + side0 + far0 + after + before)
-    fields = [back[0], jnp.stack(owner + inner)]
-    return unpack(fields, [(1, 0, 2), (0, 0, 4), (1, 2, 2)]).swapaxes(0, 1)
+    return unpack(jnp.concatenate([jnp.stack(owner), back[0], jnp.stack(inner)], axis=0)).swapaxes(0, 1)
 
 
 def solution(mesh):

time: 386 us -> 381 us (0.987); the launches traced: 385 us -> 375 us
  waiting for transfers between devices: 117 us -> 105 us
    ppermute x30, waiting for transfers between devices: 39 us -> 31.2 us  [swap(): return lax.ppermute(value, axis, [(i, i ^ flip) for i in range(size)])]
    ppermute x30, starting transfers between devices: 36 us -> 40.5 us  [swap(): return lax.ppermute(value, axis, [(i, i ^ flip) for i in range(size)])]
    ppermute x13, waiting for transfers between devices: 78 us -> 73.5 us  [along(): return lax.ppermute(value, 'z', pairs)]
  transfers between devices with their start and end apart: 46 -> 46, of which waited for: 23 -> 20; matrix products, arithmetic and copies ran while one was open for 8% -> 10% of each run, Pallas kernels for 32% -> 33%
where the time goes in v9:
time: 381 us; the launch traced here: 375 us
  Pallas kernels  130 us (34%)
  waiting for transfers between devices  105 us (28%)
  starting transfers between devices  92.7 us (24%)
  other arithmetic  37.6 us (10%)
  local copies, waits for them, and re-layouts  9.42 us (2%)
    pallas_call x8, Pallas kernels, pair_solve(): pl.pallas_call(functools.partial(pair_kernel, count, (zs, planes), layout...  122 us
    ppermute x13, waiting for transfers between devices, along(): return lax.ppermute(value, 'z', pairs)  73.5 us
    ppermute x30, starting transfers between devices, swap(): return lax.ppermute(value, axis, [(i, i ^ flip) for i in range(size)])  40.5 us
    ppermute x13, starting transfers between devices, along(): return lax.ppermute(value, 'z', pairs)  38.4 us
    ppermute x30, waiting for transfers between devices, swap(): return lax.ppermute(value, axis, [(i, i ^ flip) for i in range(size)])  31.2 us
  transfers between devices with their start and end apart: 46, of which 20 were waited for; matrix products, arithmetic and copies ran while one was open for 10% of the time, Pallas kernels for 33%

profile of v9, /device:TPU:17, one launch (start us, length us, event | category | flops | bytes accessed | tf_op | source)
XLA Modules:
  0.0 375.4 jit_solution(17434702685461521835)
XLA Ops:
  0.0 2.0 copy-done
  2.0 2.2 shard_map.28
  4.2 1.3 slice.32
  5.5 4.6 %all-to-all-start = ((f32[4,12,72,128]{3,2,1,0:T(8,128)}), f32[4,12,72,128]{3,2,1,0:T(8,128)}, u32[]{:S(2)}, u32[]{:S(2)}) async-start(f32[4,12,72,128]{3,2,1,0:T(8,128)} %bitcast.36), calls=%async_computation | async-start | bytes 3538944 | tf_op jit(solution)/shard_map/all_to_all | solution.py:466
  12.2 1.8 collective-permute-done
  18.5 3.1 collective-permute-start.1
  21.5 2.2 collective-permute-start.2
  23.7 13.4 %collective-permute-done.3.refs_1_ = f32[24,72,128]{2,1,0:T(8,128)} collective-permute-done((f32[24,72,128]{2,1,0:T(8,128)}, f32[24,72,128]{2,1,0:T(8,128)}, u32[]{:S(2)}, u32[]{:S(2)}) %collective-permute-start.3) | collective-permute-done | bytes 884768 | tf_op jit(solution)/shard_map/ppermute | solution.py:360
  38.4 29.0 %collective-permute-done.1 = f32[24,72,128]{2,1,0:T(8,128)} collective-permute-done((f32[24,72,128]{2,1,0:T(8,128)}, f32[24,72,128]{2,1,0:T(8,128)}, u32[]{:S(2)}, u32[]{:S(2)}) %collective-permute-start.1) | collective-permute-done | bytes 884768 | tf_op jit(solution)/shard_map/ppermute | solution.py:364
  67.5 1.9 collective-permute-start.6
  69.4 3.5 collective-permute-start.7
  76.7 3.1 collective-permute-start.18
  79.8 9.1 %collective-permute-done.6 = f32[24,72,128]{2,1,0:T(8,128)S(1)} collective-permute-done((f32[24,72,128]{2,1,0:T(8,128)}, f32[24,72,128]{2,1,0:T(8,128)S(1)}, u32[]{:S(2)}, u32[]{:S(2)}) %collective-permute-start.6) | collective-permute-done | bytes 884768 | tf_op jit(solution)/shard_map/ppermute | solution.py:364
  90.9 2.0 collective-permute-done.8.refs_2_
  93.9 2.2 collective-permute-start.10
  97.6 4.8 %fusion.refs_8_.refs_9_.refs_10_ = f32[48,96,256]{2,1,0:T(8,128)} fusion(s32[256]{0:T(256)S(1)} %get-tuple-element.142, s32[256]{0:T(256)S(1)} %get-tuple-element.143, s32[96]{0:T(128)S(1)} %iota_add_fusion, s32[256]{0:T(256)S(1)} %get-tuple-element.141, s32[48]{0:T(128)S(1)} %iota_multiply_fusion, pred[96]{0:T(512)(128)(4,1)S(1)} %iota_compare_fusion, ...), kind=kLoop, calls=%fused_computation.4 | loop fusion | flops 31850496 | bytes 4722592 | tf_op jit(solution)/shard_map/div | solution.py:75
  104.1 2.6 pad_maximum_fusion
  106.7 4.3 %collective-permute-done.10 = f32[24,72,128]{2,1,0:T(8,128)} collective-permute-done((f32[24,72,128]{2,1,0:T(8,128)}, f32[24,72,128]{2,1,0:T(8,128)}, u32[]{:S(2)}, u32[]{:S(2)}) %collective-permute-start.10) | collective-permute-done | bytes 884768 | tf_op jit(solution)/shard_map/ppermute | solution.py:364
  112.3 1.6 collective-permute-done.11.refs_3_
  116.3 4.7 %all-to-all-start.1 = ((f32[4,12,72,128]{3,2,1,0:T(8,128)}), f32[4,12,72,128]{3,2,1,0:T(8,128)S(1)}, u32[]{:S(2)}, u32[]{:S(2)}) async-start(f32[4,12,72,128]{3,2,1,0:T(8,128)} %pad_maximum_fusion), calls=%async_computation.1 | async-start | bytes 3538944 | tf_op jit(solution)/shard_map/all_to_all | solution.py:476
  121.0 15.4 %shard_map.29 = (f32[96,72,128]{2,1,0:T(8,128)}, f32[96,72,128]{2,1,0:T(8,128)}) custom-call(s32[2]{0:T(128)} %pad_add_fusion.refs_0_, f32[24,72,128]{2,1,0:T(8,128)} %pad_maximum_fusion.1.refs_1_, f32[24,72,128]{2,1,0:T(8,128)} %copy-done.7, f32[24,72,128]{2,1,0:T(8,128)} %add.164.refs_3_, f32[24,72,128]{2,1,0:T(8,128)} %copy-done.8, ...), custom_call_target="tpu_custom_call" | custom-call | flops 16986931200 | bytes 17694720 | tf_op jit(solution)/shard_map/pallas_call | solution.py:278
  136.9 15.3 %shard_map.30 = (f32[96,72,128]{2,1,0:T(8,128)}, f32[96,72,128]{2,1,0:T(8,128)}) custom-call(s32[2]{0:T(128)} %pad_add_fusion.refs_0_, f32[24,72,128]{2,1,0:T(8,128)} %collective-permute-done.3.refs_1_, f32[24,72,128]{2,1,0:T(8,128)} %copy-done.15, f32[24,72,128]{2,1,0:T(8,128)} %collective-permute-done.11.refs_3_, ...), custom_call_target="tpu_custom_call" | custom-call | flops 16986931200 | bytes 17694720 | tf_op jit(solution)/shard_map/pallas_call | solution.py:278
  152.2 1.4 collective-permute-start.17
  153.7 15.3 %shard_map.31 = (f32[96,72,128]{2,1,0:T(8,128)}, f32[96,72,128]{2,1,0:T(8,128)}) custom-call(s32[2]{0:T(128)} %pad_add_fusion.refs_0_, f32[24,72,128]{2,1,0:T(8,128)} %collective-permute-done.4.refs_1_, f32[24,72,128]{2,1,0:T(8,128)} %copy-done.13, f32[24,72,128]{2,1,0:T(8,128)} %collective-permute-done.12.refs_3_, ...), custom_call_target="tpu_custom_call" | custom-call | flops 16986931200 | bytes 17694720 | tf_op jit(solution)/shard_map/pallas_call | solution.py:278
  169.0 1.3 collective-permute-done.17.refs_4_
  171.2 15.3 %shard_map.32 = (f32[4,12,72,128]{3,2,1,0:T(8,128)}, f32[4,12,72,128]{3,2,1,0:T(8,128)}, f32[96,72,128]{2,1,0:T(8,128)}) custom-call(s32[2]{0:T(128)} %pad_add_fusion.refs_0_, f32[24,72,128]{2,1,0:T(8,128)} %collective-permute-done.5.refs_1_, f32[24,72,128]{2,1,0:T(8,128)} %collective-permute-done.15.refs_2_, f32[24,72,128]{2,1,0:T(8,128)} %copy-done.16, ...), custom_call_target="tpu_custom_call" | custom-call | flops 16986931200 | bytes 17694720 | tf_op jit(solution)/shard_map/pallas_call | solution.py:278
  186.5 7.6 %collective-permute-start.19 = (f32[4,12,72,128]{3,2,1,0:T(8,128)S(1)}, f32[4,12,72,128]{3,2,1,0:T(8,128)}, u32[]{:S(2)}, u32[]{:S(2)}) collective-permute-start(f32[4,12,72,128]{3,2,1,0:T(8,128)S(1)} %all-to-all-done.1.refs_5_), channel_id=1, source_target_pairs={{0,1},{1,0},{2,3},{3,2},{4,5},{5,4},{6,7},{7,6},{8,9},{9,8},{10,11... | collective-permute-start | bytes 5308424 | tf_op jit(solution)/shard_map/ppermute | solution.py:360
  194.2 5.0 %collective-permute-done.19.refs_6_ = f32[4,12,72,128]{3,2,1,0:T(8,128)} collective-permute-done((f32[4,12,72,128]{3,2,1,0:T(8,128)S(1)}, f32[4,12,72,128]{3,2,1,0:T(8,128)}, u32[]{:S(2)}, u32[]{:S(2)}) %collective-permute-start.19) | collective-permute-done | bytes 1769504 | tf_op jit(solution)/shard_map/ppermute | solution.py:360
  199.2 15.3 %shard_map.33 = (f32[96,72,128]{2,1,0:T(8,128)}, f32[24,72,128]{2,1,0:T(8,128)}, f32[24,72,128]{2,1,0:T(8,128)}, f32[24,72,128]{2,1,0:T(8,128)}, f32[24,72,128]{2,1,0:T(8,128)}) custom-call(s32[2]{0:T(128)} %pad_add_fusion.refs_0_, f32[24,72,128]{2,1,0:T(8,128)} %collective-permute-done.5.refs_1_, f32[24,72,128]{2,1,0:T(8,128)} %collective-permute-done.15.refs_2_, ...), custom_call_target="tpu_custom_call" | custom-call | flops 16986931200 | bytes 17694720 | tf_op jit(solution)/shard_map/pallas_call | solution.py:278
  214.4 1.5 collective-permute-start.20
  217.1 2.9 add.169
  220.1 4.5 %all-to-all-start.2 = ((f32[4,12,72,128]{3,2,1,0:T(8,128)}), f32[4,12,72,128]{3,2,1,0:T(8,128)S(1)}, u32[]{:S(2)}, u32[]{:S(2)}) async-start(f32[4,12,72,128]{3,2,1,0:T(8,128)} %add.169), calls=%async_computation.2 | async-start | bytes 3538944 | tf_op jit(solution)/shard_map/all_to_all | solution.py:444
  224.6 15.3 %shard_map.34 = (f32[96,72,128]{2,1,0:T(8,128)}, f32[24,72,128]{2,1,0:T(8,128)}, f32[24,72,128]{2,1,0:T(8,128)}, f32[24,72,128]{2,1,0:T(8,128)}, f32[24,72,128]{2,1,0:T(8,128)}) custom-call(s32[2]{0:T(128)} %pad_add_fusion.refs_0_, f32[24,72,128]{2,1,0:T(8,128)} %collective-permute-done.3.refs_1_, f32[24,72,128]{2,1,0:T(8,128)} %copy-done.15, ...), custom_call_target="tpu_custom_call" | custom-call | flops 16986931200 | bytes 17694720 | tf_op jit(solution)/shard_map/pallas_call | solution.py:278
  240.3 2.5 add.171
  242.7 15.3 %shard_map.35 = (f32[96,72,128]{2,1,0:T(8,128)}, f32[24,72,128]{2,1,0:T(8,128)}, f32[24,72,128]{2,1,0:T(8,128)}, f32[24,72,128]{2,1,0:T(8,128)}, f32[24,72,128]{2,1,0:T(8,128)}) custom-call(s32[2]{0:T(128)} %pad_add_fusion.refs_0_, f32[24,72,128]{2,1,0:T(8,128)} %collective-permute-done.4.refs_1_, f32[24,72,128]{2,1,0:T(8,128)} %copy-done.13, ...), custom_call_target="tpu_custom_call" | custom-call | flops 16986931200 | bytes 17694720 | tf_op jit(solution)/shard_map/pallas_call | solution.py:278
  258.1 2.5 add.172
  260.6 1.5 collective-permute-start.25
  263.3 15.3 %shard_map.36 = (f32[4,12,72,128]{3,2,1,0:T(8,128)}, f32[4,12,72,128]{3,2,1,0:T(8,128)}, f32[24,72,128]{2,1,0:T(8,128)}, f32[24,72,128]{2,1,0:T(8,128)}, f32[24,72,128]{2,1,0:T(8,128)}, /*index=5*/f32[24,72,128]{2,1,0:T(8,128)}) custom-call(s32[2]{0:T(128)} %pad_add_fusion.refs_0_, f32[24,72,128]{2,1,0:T(8,128)} %pad_maximum_fusion.1.refs_1_, ...), custom_call_target="tpu_custom_call" | custom-call | flops 16986931200 | bytes 17694720 | tf_op jit(solution)/shard_map/pallas_call | solution.py:278
  278.6 2.7 collective-permute-start.34
  282.7 2.7 add_add_fusion.2
  285.4 1.3 collective-permute-start.33
  287.9 2.2 add.183
  291.2 2.9 collective-permute-start.35
  294.1 3.4 collective-permute-start.36
  297.5 2.1 collective-permute-done.27
  299.7 4.3 %collective-permute-start.37 = (f32[12,72,128]{2,1,0:T(8,128)}, f32[12,72,128]{2,1,0:T(8,128)}, u32[]{:S(2)}, u32[]{:S(2)}) collective-permute-start(f32[12,72,128]{2,1,0:T(8,128)} %get-tuple-element.137), channel_id=1, source_target_pairs={{2,6},{4,0},{3,7},{5,1},{10,14},{12,8},{11,15},{13,9},{18,22},{20,... | collective-permute-start | bytes 1327112 | tf_op jit(solution)/shard_map/ppermute | solution.py:364
  304.1 1.5 add.173
  305.7 2.3 add_add_fusion.1
  308.0 1.8 collective-permute-done.37
  309.9 2.3 bitcast_select_fusion
  312.2 1.3 collective-permute-start.38
  313.4 7.0 %collective-permute-start.40 = (f32[24,72,128]{2,1,0:T(8,128)S(1)}, f32[24,72,128]{2,1,0:T(8,128)S(1)}, u32[]{:S(2)}, u32[]{:S(2)}) collective-permute-start(f32[24,72,128]{2,1,0:T(8,128)S(1)} %add_add_fusion.1), channel_id=1, source_target_pairs={{4,2},{6,4},{5,3},{7,5},{12,10},{14,12},{13,11},{15,13},{20,18},{2... | collective-permute-start | bytes 2654216 | tf_op jit(solution)/shard_map/ppermute | solution.py:364
  322.9 1.5 collective-permute-start.31
  324.4 10.7 %collective-permute-done.38 = f32[24,72,128]{2,1,0:T(8,128)S(1)} collective-permute-done((f32[24,72,128]{2,1,0:T(8,128)S(1)}, f32[24,72,128]{2,1,0:T(8,128)S(1)}, u32[]{:S(2)}, u32[]{:S(2)}) %collective-permute-start.38) | collective-permute-done | bytes 884768 | tf_op jit(solution)/shard_map/ppermute | solution.py:364
  335.1 1.9 collective-permute-done.40
  337.0 1.5 add_select_fusion
  338.5 1.9 collective-permute-start.39
  340.4 3.4 collective-permute-start.41
  343.8 13.7 %collective-permute-done.39 = f32[24,72,128]{2,1,0:T(8,128)} collective-permute-done((f32[24,72,128]{2,1,0:T(8,128)S(1)}, f32[24,72,128]{2,1,0:T(8,128)}, u32[]{:S(2)}, u32[]{:S(2)}) %collective-permute-start.39) | collective-permute-done | bytes 884768 | tf_op jit(solution)/shard_map/ppermute | solution.py:364
  357.5 1.9 collective-permute-done.41
  359.4 2.4 add_add_fusion
  362.7 5.1 %collective-permute-start.42 = (f32[12,72,128]{2,1,0:T(8,128)}, f32[12,72,128]{2,1,0:T(8,128)S(1)}, u32[]{:S(2)}, u32[]{:S(2)}) collective-permute-start(f32[12,72,128]{2,1,0:T(8,128)} %constant_dynamic-slice_fusion), channel_id=1, source_target_pairs={{0,1},{1,0},{2,3},{3,2},{4,5},{5,4},{6,7},{7,6},{8,9},{9,8},{10,11... | collective-permute-start | bytes 1327112 | tf_op jit(solution)/shard_map/ppermute | solution.py:360
  367.7 1.6 collective-permute-done.42
  369.7 5.7 %shard_map.37 = f32[12,8,9216]{2,1,0:T(8,128)} custom-call(f32[6912,128]{1,0:T(8,128)S(1)} %bitcast.34), custom_call_target="tpu_custom_call" | custom-call | tf_op jit(solution)/shard_map/pallas_call | solution.py:348
  (109 shorter events, 33.2 us)
Async XLA Ops:
  0.0 2.0 copy-start
  5.5 61.9 %all-to-all-start = ((f32[4,12,72,128]{3,2,1,0:T(8,128)}), f32[4,12,72,128]{3,2,1,0:T(8,128)}, u32[]{:S(2)}, u32[]{:S(2)}) async-start(f32[4,12,72,128]{3,2,1,0:T(8,128)} %bitcast.36), calls=%async_computation | async-start | bytes 3538944 | tf_op jit(solution)/shard_map/all_to_all | solution.py:466
  11.0 3.0 collective-permute-start
  16.0 21.2 %collective-permute-start.3 = (f32[24,72,128]{2,1,0:T(8,128)}, f32[24,72,128]{2,1,0:T(8,128)}, u32[]{:S(2)}, u32[]{:S(2)}) collective-permute-start(f32[24,72,128]{2,1,0:T(8,128)} %pad_maximum_fusion.1.refs_1_), channel_id=1, source_target_pairs={{0,8},{8,0},{16,24},{24,16},{1,9},{9,1},{17,25},{25,17},{2,10},{10... | collective-permute-start | bytes 2654216 | tf_op jit(solution)/shard_map/ppermute | solution.py:360
  17.2 21.2 %collective-permute-start.4 = (f32[24,72,128]{2,1,0:T(8,128)}, f32[24,72,128]{2,1,0:T(8,128)}, u32[]{:S(2)}, u32[]{:S(2)}) collective-permute-start(f32[24,72,128]{2,1,0:T(8,128)} %pad_maximum_fusion.1.refs_1_), channel_id=1, source_target_pairs={{0,16},{8,24},{16,0},{24,8},{1,17},{9,25},{17,1},{25,9},{2,18},{10... | collective-permute-start | bytes 2654216 | tf_op jit(solution)/shard_map/ppermute | solution.py:360
  18.5 49.0 %collective-permute-start.1 = (f32[24,72,128]{2,1,0:T(8,128)}, f32[24,72,128]{2,1,0:T(8,128)}, u32[]{:S(2)}, u32[]{:S(2)}) collective-permute-start(f32[24,72,128]{2,1,0:T(8,128)} %pad_maximum_fusion.1.refs_1_), channel_id=1, source_target_pairs={{0,2},{2,4},{4,6},{1,3},{3,5},{5,7},{8,10},{10,12},{12,14},{9,11},... | collective-permute-start | bytes 2654216 | tf_op jit(solution)/shard_map/ppermute | solution.py:364
  21.5 45.9 %collective-permute-start.2 = (f32[24,72,128]{2,1,0:T(8,128)}, f32[24,72,128]{2,1,0:T(8,128)}, u32[]{:S(2)}, u32[]{:S(2)}) collective-permute-start(f32[24,72,128]{2,1,0:T(8,128)} %pad_maximum_fusion.1.refs_1_), channel_id=1, source_target_pairs={{2,0},{4,2},{6,4},{3,1},{5,3},{7,5},{10,8},{12,10},{14,12},{11,9},... | collective-permute-start | bytes 2654216 | tf_op jit(solution)/shard_map/ppermute | solution.py:364
  37.2 30.3 %collective-permute-start.5 = (f32[24,72,128]{2,1,0:T(8,128)}, f32[24,72,128]{2,1,0:T(8,128)}, u32[]{:S(2)}, u32[]{:S(2)}) collective-permute-start(f32[24,72,128]{2,1,0:T(8,128)} %collective-permute-done.3.refs_1_), channel_id=1, source_target_pairs={{0,16},{8,24},{16,0},{24,8},{1,17},{9,25},{17,1},{25,9},{2,18},{10... | collective-permute-start | bytes 2654216 | tf_op jit(solution)/shard_map/ppermute | solution.py:360
  67.5 21.4 %collective-permute-start.6 = (f32[24,72,128]{2,1,0:T(8,128)}, f32[24,72,128]{2,1,0:T(8,128)S(1)}, u32[]{:S(2)}, u32[]{:S(2)}) collective-permute-start(f32[24,72,128]{2,1,0:T(8,128)} %collective-permute-done.1), channel_id=1, source_target_pairs={{2,4},{4,6},{3,5},{5,7},{10,12},{12,14},{11,13},{13,15},{18,20},{2... | collective-permute-start | bytes 2654216 | tf_op jit(solution)/shard_map/ppermute | solution.py:364
  69.4 20.5 %collective-permute-start.7 = (f32[24,72,128]{2,1,0:T(8,128)}, f32[24,72,128]{2,1,0:T(8,128)S(1)}, u32[]{:S(2)}, u32[]{:S(2)}) collective-permute-start(f32[24,72,128]{2,1,0:T(8,128)} %collective-permute-done.2), channel_id=1, source_target_pairs={{2,0},{4,2},{3,1},{5,3},{10,8},{12,10},{11,9},{13,11},{18,16},{20,... | collective-permute-start | bytes 2654216 | tf_op jit(solution)/shard_map/ppermute | solution.py:364
  74.1 28.3 %copy-start.7 = (f32[24,72,128]{2,1,0:T(8,128)}, f32[24,72,128]{2,1,0:T(8,128)S(1)}, u32[]{:S(2)}) copy-start(f32[24,72,128]{2,1,0:T(8,128)S(1)} %broadcast_select_fusion.1.refs_2_) | copy-start | bytes 2654212
  74.2 18.8 %collective-permute-start.8 = (f32[24,72,128]{2,1,0:T(8,128)S(1)}, f32[24,72,128]{2,1,0:T(8,128)S(1)}, u32[]{:S(2)}, u32[]{:S(2)}) collective-permute-start(f32[24,72,128]{2,1,0:T(8,128)S(1)} %broadcast_select_fusion.1.refs_2_), channel_id=1, source_target_pairs={{0,8},{8,0},{16,24},{24,16},{1,9},{9,1},{17,25},{25,17},{2,10},{10... | collective-permute-start | bytes 2654216 | tf_op jit(solution)/shard_map/ppermute | solution.py:360
  75.4 18.4 %collective-permute-start.9 = (f32[24,72,128]{2,1,0:T(8,128)S(1)}, f32[24,72,128]{2,1,0:T(8,128)S(1)}, u32[]{:S(2)}, u32[]{:S(2)}) collective-permute-start(f32[24,72,128]{2,1,0:T(8,128)S(1)} %broadcast_select_fusion.1.refs_2_), channel_id=1, source_target_pairs={{0,16},{8,24},{16,0},{24,8},{1,17},{9,25},{17,1},{25,9},{2,18},{10... | collective-permute-start | bytes 2654216 | tf_op jit(solution)/shard_map/ppermute | solution.py:360
  76.7 44.3 %collective-permute-start.18 = (f32[4,12,72,128]{3,2,1,0:T(8,128)}, f32[4,12,72,128]{3,2,1,0:T(8,128)}, u32[]{:S(2)}, u32[]{:S(2)}) collective-permute-start(f32[4,12,72,128]{3,2,1,0:T(8,128)} %all-to-all-done.refs_5_), channel_id=1, source_target_pairs={{0,1},{1,0},{2,3},{3,2},{4,5},{5,4},{6,7},{7,6},{8,9},{9,8},{10,11... | collective-permute-start | bytes 5308424 | tf_op jit(solution)/shard_map/ppermute | solution.py:360
  92.9 9.5 %copy-start.15 = (f32[24,72,128]{2,1,0:T(8,128)}, f32[24,72,128]{2,1,0:T(8,128)S(1)}, u32[]{:S(2)}) copy-start(f32[24,72,128]{2,1,0:T(8,128)S(1)} %collective-permute-done.8.refs_2_) | copy-start | bytes 2654212
  93.9 8.6 %copy-start.13 = (f32[24,72,128]{2,1,0:T(8,128)}, f32[24,72,128]{2,1,0:T(8,128)S(1)}, u32[]{:S(2)}) copy-start(f32[24,72,128]{2,1,0:T(8,128)S(1)} %collective-permute-done.9.refs_2_) | copy-start | bytes 2654212
  93.9 17.2 %collective-permute-start.10 = (f32[24,72,128]{2,1,0:T(8,128)}, f32[24,72,128]{2,1,0:T(8,128)}, u32[]{:S(2)}, u32[]{:S(2)}) collective-permute-start(f32[24,72,128]{2,1,0:T(8,128)} %add.164.refs_3_), channel_id=1, source_target_pairs={{4,6},{2,0},{5,7},{3,1},{12,14},{10,8},{13,15},{11,9},{20,22},{18,... | collective-permute-start | bytes 2654216 | tf_op jit(solution)/shard_map/ppermute | solution.py:364
  96.1 17.8 %collective-permute-start.11 = (f32[24,72,128]{2,1,0:T(8,128)}, f32[24,72,128]{2,1,0:T(8,128)}, u32[]{:S(2)}, u32[]{:S(2)}) collective-permute-start(f32[24,72,128]{2,1,0:T(8,128)} %add.164.refs_3_), channel_id=1, source_target_pairs={{0,8},{8,0},{16,24},{24,16},{1,9},{9,1},{17,25},{25,17},{2,10},{10... | collective-permute-start | bytes 2654216 | tf_op jit(solution)/shard_map/ppermute | solution.py:360
  96.4 17.6 %collective-permute-start.12 = (f32[24,72,128]{2,1,0:T(8,128)}, f32[24,72,128]{2,1,0:T(8,128)}, u32[]{:S(2)}, u32[]{:S(2)}) collective-permute-start(f32[24,72,128]{2,1,0:T(8,128)} %add.164.refs_3_), channel_id=1, source_target_pairs={{0,16},{8,24},{16,0},{24,8},{1,17},{9,25},{17,1},{25,9},{2,18},{10... | collective-permute-start | bytes 2654216 | tf_op jit(solution)/shard_map/ppermute | solution.py:360
  112.3 8.7 %copy-start.8 = (f32[24,72,128]{2,1,0:T(8,128)}, f32[24,72,128]{2,1,0:T(8,128)S(1)}, u32[]{:S(2)}) copy-start(f32[24,72,128]{2,1,0:T(8,128)S(1)} %broadcast_select_fusion.refs_4_) | copy-start | bytes 2654212
  114.0 22.5 %collective-permute-start.13 = (f32[24,72,128]{2,1,0:T(8,128)S(1)}, f32[24,72,128]{2,1,0:T(8,128)}, u32[]{:S(2)}, u32[]{:S(2)}) collective-permute-start(f32[24,72,128]{2,1,0:T(8,128)S(1)} %broadcast_select_fusion.refs_4_), channel_id=1, source_target_pairs={{0,8},{8,0},{16,24},{24,16},{1,9},{9,1},{17,25},{25,17},{2,10},{10... | collective-permute-start | bytes 2654216 | tf_op jit(solution)/shard_map/ppermute | solution.py:360
  115.1 21.4 %collective-permute-start.14 = (f32[24,72,128]{2,1,0:T(8,128)S(1)}, f32[24,72,128]{2,1,0:T(8,128)}, u32[]{:S(2)}, u32[]{:S(2)}) collective-permute-start(f32[24,72,128]{2,1,0:T(8,128)S(1)} %broadcast_select_fusion.refs_4_), channel_id=1, source_target_pairs={{0,16},{8,24},{16,0},{24,8},{1,17},{9,25},{17,1},{25,9},{2,18},{10... | collective-permute-start | bytes 2654216 | tf_op jit(solution)/shard_map/ppermute | solution.py:360
  116.3 70.1 %all-to-all-start.1 = ((f32[4,12,72,128]{3,2,1,0:T(8,128)}), f32[4,12,72,128]{3,2,1,0:T(8,128)S(1)}, u32[]{:S(2)}, u32[]{:S(2)}) async-start(f32[4,12,72,128]{3,2,1,0:T(8,128)} %pad_maximum_fusion), calls=%async_computation.1 | async-start | bytes 3538944 | tf_op jit(solution)/shard_map/all_to_all | solution.py:476
  121.0 15.8 %copy-start.14 = (f32[24,72,128]{2,1,0:T(8,128)S(1)}, f32[24,72,128]{2,1,0:T(8,128)}, u32[]{:S(2)}) copy-start(f32[24,72,128]{2,1,0:T(8,128)} %copy-done.13) | copy-start | bytes 2654212
  136.5 15.7 %collective-permute-start.16 = (f32[24,72,128]{2,1,0:T(8,128)}, f32[24,72,128]{2,1,0:T(8,128)S(1)}, u32[]{:S(2)}, u32[]{:S(2)}) collective-permute-start(f32[24,72,128]{2,1,0:T(8,128)} %collective-permute-done.11.refs_3_), channel_id=1, source_target_pairs={{0,16},{8,24},{16,0},{24,8},{1,17},{9,25},{17,1},{25,9},{2,18},{10... | collective-permute-start | bytes 2654216 | tf_op jit(solution)/shard_map/ppermute | solution.py:360
  136.8 15.4 %collective-permute-start.15 = (f32[24,72,128]{2,1,0:T(8,128)S(1)}, f32[24,72,128]{2,1,0:T(8,128)}, u32[]{:S(2)}, u32[]{:S(2)}) collective-permute-start(f32[24,72,128]{2,1,0:T(8,128)S(1)} %copy-done.14), channel_id=1, source_target_pairs={{0,8},{8,0},{16,24},{24,16},{1,9},{9,1},{17,25},{25,17},{2,10},{10... | collective-permute-start | bytes 2654216 | tf_op jit(solution)/shard_map/ppermute | solution.py:360
  152.2 16.8 %copy-start.16 = (f32[24,72,128]{2,1,0:T(8,128)}, f32[24,72,128]{2,1,0:T(8,128)S(1)}, u32[]{:S(2)}) copy-start(f32[24,72,128]{2,1,0:T(8,128)S(1)} %collective-permute-done.16.refs_3_) | copy-start | bytes 2654212
  152.2 18.1 %collective-permute-start.17 = (f32[24,72,128]{2,1,0:T(8,128)}, f32[24,72,128]{2,1,0:T(8,128)S(1)}, u32[]{:S(2)}, u32[]{:S(2)}) collective-permute-start(f32[24,72,128]{2,1,0:T(8,128)} %collective-permute-done.14.refs_4_), channel_id=1, source_target_pairs={{0,8},{8,0},{16,24},{24,16},{1,9},{9,1},{17,25},{25,17},{2,10},{10... | collective-permute-start | bytes 2654216 | tf_op jit(solution)/shard_map/ppermute | solution.py:360
  170.3 0.9 copy-start.17
  186.5 12.7 %copy-start.1 = (f32[4,12,72,128]{3,2,1,0:T(8,128)}, f32[4,12,72,128]{3,2,1,0:T(8,128)S(1)}, u32[]{:S(2)}) copy-start(f32[4,12,72,128]{3,2,1,0:T(8,128)S(1)} %all-to-all-done.1.refs_5_) | copy-start | bytes 5308420
  186.5 12.7 %collective-permute-start.19 = (f32[4,12,72,128]{3,2,1,0:T(8,128)S(1)}, f32[4,12,72,128]{3,2,1,0:T(8,128)}, u32[]{:S(2)}, u32[]{:S(2)}) collective-permute-start(f32[4,12,72,128]{3,2,1,0:T(8,128)S(1)} %all-to-all-done.1.refs_5_), channel_id=1, source_target_pairs={{0,1},{1,0},{2,3},{3,2},{4,5},{5,4},{6,7},{7,6},{8,9},{9,8},{10,11... | collective-permute-start | bytes 5308424 | tf_op jit(solution)/shard_map/ppermute | solution.py:360
  194.1 23.1 %copy-start.5 = (f32[4,12,72,128]{3,2,1,0:T(8,128)S(1)}, f32[4,12,72,128]{3,2,1,0:T(8,128)}, u32[]{:S(2)}) copy-start(f32[4,12,72,128]{3,2,1,0:T(8,128)} %get-tuple-element.92) | copy-start | bytes 5308420
  194.1 23.0 %collective-permute-start.24 = (f32[4,12,72,128]{3,2,1,0:T(8,128)}, f32[4,12,72,128]{3,2,1,0:T(8,128)}, u32[]{:S(2)}, u32[]{:S(2)}) collective-permute-start(f32[4,12,72,128]{3,2,1,0:T(8,128)} %get-tuple-element.93), channel_id=1, source_target_pairs={{0,1},{1,0},{2,3},{3,2},{4,5},{5,4},{6,7},{7,6},{8,9},{9,8},{10,11... | collective-permute-start | bytes 5308424 | tf_op jit(solution)/shard_map/ppermute | solution.py:360
  214.4 25.4 %collective-permute-start.20 = (f32[24,72,128]{2,1,0:T(8,128)}, f32[24,72,128]{2,1,0:T(8,128)}, u32[]{:S(2)}, u32[]{:S(2)}) collective-permute-start(f32[24,72,128]{2,1,0:T(8,128)} %get-tuple-element.87), channel_id=1, source_target_pairs={{0,8},{8,0},{16,24},{24,16},{1,9},{9,1},{17,25},{25,17},{2,10},{10... | collective-permute-start | bytes 2654216 | tf_op jit(solution)/shard_map/ppermute | solution.py:360
  215.9 24.0 %collective-permute-start.21 = (f32[24,72,128]{2,1,0:T(8,128)}, f32[24,72,128]{2,1,0:T(8,128)}, u32[]{:S(2)}, u32[]{:S(2)}) collective-permute-start(f32[24,72,128]{2,1,0:T(8,128)} %get-tuple-element.88), channel_id=1, source_target_pairs={{0,16},{8,24},{16,0},{24,8},{1,17},{9,25},{17,1},{25,9},{2,18},{10... | collective-permute-start | bytes 2654216 | tf_op jit(solution)/shard_map/ppermute | solution.py:360
  220.1 43.2 %all-to-all-start.2 = ((f32[4,12,72,128]{3,2,1,0:T(8,128)}), f32[4,12,72,128]{3,2,1,0:T(8,128)S(1)}, u32[]{:S(2)}, u32[]{:S(2)}) async-start(f32[4,12,72,128]{3,2,1,0:T(8,128)} %add.169), calls=%async_computation.2 | async-start | bytes 3538944 | tf_op jit(solution)/shard_map/all_to_all | solution.py:444
  239.9 20.7 %collective-permute-start.23 = (f32[24,72,128]{2,1,0:T(8,128)}, f32[24,72,128]{2,1,0:T(8,128)S(1)}, u32[]{:S(2)}, u32[]{:S(2)}) collective-permute-start(f32[24,72,128]{2,1,0:T(8,128)} %get-tuple-element.91), channel_id=1, source_target_pairs={{0,16},{8,24},{16,0},{24,8},{1,17},{9,25},{17,1},{25,9},{2,18},{10... | collective-permute-start | bytes 2654216 | tf_op jit(solution)/shard_map/ppermute | solution.py:360
  240.2 20.4 %collective-permute-start.22 = (f32[24,72,128]{2,1,0:T(8,128)}, f32[24,72,128]{2,1,0:T(8,128)S(1)}, u32[]{:S(2)}, u32[]{:S(2)}) collective-permute-start(f32[24,72,128]{2,1,0:T(8,128)} %get-tuple-element.89), channel_id=1, source_target_pairs={{0,8},{8,0},{16,24},{24,16},{1,9},{9,1},{17,25},{25,17},{2,10},{10... | collective-permute-start | bytes 2654216 | tf_op jit(solution)/shard_map/ppermute | solution.py:360
  260.6 18.0 %copy-start.11 = (f32[24,72,128]{2,1,0:T(8,128)}, f32[24,72,128]{2,1,0:T(8,128)S(1)}, u32[]{:S(2)}) copy-start(f32[24,72,128]{2,1,0:T(8,128)S(1)} %collective-permute-done.23) | copy-start | bytes 2654212
  260.6 18.0 %copy-start.6 = (f32[24,72,128]{2,1,0:T(8,128)}, f32[24,72,128]{2,1,0:T(8,128)S(1)}, u32[]{:S(2)}) copy-start(f32[24,72,128]{2,1,0:T(8,128)S(1)} %collective-permute-done.22) | copy-start | bytes 2654212
  260.6 20.7 %collective-permute-start.25 = (f32[24,72,128]{2,1,0:T(8,128)}, f32[24,72,128]{2,1,0:T(8,128)}, u32[]{:S(2)}, u32[]{:S(2)}) collective-permute-start(f32[24,72,128]{2,1,0:T(8,128)} %add.171), channel_id=1, source_target_pairs={{0,8},{8,0},{16,24},{24,16},{1,9},{9,1},{17,25},{25,17},{2,10},{10... | collective-permute-start | bytes 2654216 | tf_op jit(solution)/shard_map/ppermute | solution.py:360
  262.0 19.3 %collective-permute-start.26 = (f32[24,72,128]{2,1,0:T(8,128)}, f32[24,72,128]{2,1,0:T(8,128)}, u32[]{:S(2)}, u32[]{:S(2)}) collective-permute-start(f32[24,72,128]{2,1,0:T(8,128)} %add.172), channel_id=1, source_target_pairs={{0,16},{8,24},{16,0},{24,8},{1,17},{9,25},{17,1},{25,9},{2,18},{10... | collective-permute-start | bytes 2654216 | tf_op jit(solution)/shard_map/ppermute | solution.py:360
  278.6 8.1 %collective-permute-start.34 = (f32[4,12,72,128]{3,2,1,0:T(8,128)}, f32[4,12,72,128]{3,2,1,0:T(8,128)S(1)}, u32[]{:S(2)}, u32[]{:S(2)}) collective-permute-start(f32[4,12,72,128]{3,2,1,0:T(8,128)} %get-tuple-element.127), channel_id=1, source_target_pairs={{0,1},{1,0},{2,3},{3,2},{4,5},{5,4},{6,7},{7,6},{8,9},{9,8},{10,11... | collective-permute-start | bytes 5308424 | tf_op jit(solution)/shard_map/ppermute | solution.py:360
  281.3 18.3 %collective-permute-start.27 = (f32[24,72,128]{2,1,0:T(8,128)}, f32[24,72,128]{2,1,0:T(8,128)}, u32[]{:S(2)}, u32[]{:S(2)}) collective-permute-start(f32[24,72,128]{2,1,0:T(8,128)} %get-tuple-element.114), channel_id=1, source_target_pairs={{0,8},{8,0},{16,24},{24,16},{1,9},{9,1},{17,25},{25,17},{2,10},{10... | collective-permute-start | bytes 2654216 | tf_op jit(solution)/shard_map/ppermute | solution.py:360
  281.4 22.5 %collective-permute-start.28 = (f32[24,72,128]{2,1,0:T(8,128)}, f32[24,72,128]{2,1,0:T(8,128)}, u32[]{:S(2)}, u32[]{:S(2)}) collective-permute-start(f32[24,72,128]{2,1,0:T(8,128)} %get-tuple-element.116), channel_id=1, source_target_pairs={{0,16},{8,24},{16,0},{24,8},{1,17},{9,25},{17,1},{25,9},{2,18},{10... | collective-permute-start | bytes 2654216 | tf_op jit(solution)/shard_map/ppermute | solution.py:360
  285.4 20.2 %collective-permute-start.33 = (f32[24,72,128]{2,1,0:T(8,128)}, f32[24,72,128]{2,1,0:T(8,128)}, u32[]{:S(2)}, u32[]{:S(2)}) collective-permute-start(f32[24,72,128]{2,1,0:T(8,128)} %add_add_fusion.2), channel_id=1, source_target_pairs={{0,2},{6,4},{1,3},{7,5},{8,10},{14,12},{9,11},{15,13},{16,18},{22,... | collective-permute-start | bytes 2654216 | tf_op jit(solution)/shard_map/ppermute | solution.py:364
  286.7 1.2 copy-start.4
  291.2 16.8 %collective-permute-start.35 = (f32[12,72,128]{2,1,0:T(8,128)}, f32[12,72,128]{2,1,0:T(8,128)}, u32[]{:S(2)}, u32[]{:S(2)}) collective-permute-start(f32[12,72,128]{2,1,0:T(8,128)} %get-tuple-element.139), channel_id=1, source_target_pairs={{2,0},{4,2},{3,1},{5,3},{10,8},{12,10},{11,9},{13,11},{18,16},{20,... | collective-permute-start | bytes 1327112 | tf_op jit(solution)/shard_map/ppermute | solution.py:364
  294.1 13.9 %collective-permute-start.36 = (f32[12,72,128]{2,1,0:T(8,128)}, f32[12,72,128]{2,1,0:T(8,128)}, u32[]{:S(2)}, u32[]{:S(2)}) collective-permute-start(f32[12,72,128]{2,1,0:T(8,128)} %get-tuple-element.138), channel_id=1, source_target_pairs={{2,4},{4,6},{3,5},{5,7},{10,12},{12,14},{11,13},{13,15},{18,20},{2... | collective-permute-start | bytes 1327112 | tf_op jit(solution)/shard_map/ppermute | solution.py:364
  299.7 10.2 %collective-permute-start.37 = (f32[12,72,128]{2,1,0:T(8,128)}, f32[12,72,128]{2,1,0:T(8,128)}, u32[]{:S(2)}, u32[]{:S(2)}) collective-permute-start(f32[12,72,128]{2,1,0:T(8,128)} %get-tuple-element.137), channel_id=1, source_target_pairs={{2,6},{4,0},{3,7},{5,1},{10,14},{12,8},{11,15},{13,9},{18,22},{20,... | collective-permute-start | bytes 1327112 | tf_op jit(solution)/shard_map/ppermute | solution.py:364
  304.0 17.9 %collective-permute-start.29 = (f32[24,72,128]{2,1,0:T(8,128)}, f32[24,72,128]{2,1,0:T(8,128)S(1)}, u32[]{:S(2)}, u32[]{:S(2)}) collective-permute-start(f32[24,72,128]{2,1,0:T(8,128)} %get-tuple-element.117), channel_id=1, source_target_pairs={{0,8},{8,0},{16,24},{24,16},{1,9},{9,1},{17,25},{25,17},{2,10},{10... | collective-permute-start | bytes 2654216 | tf_op jit(solution)/shard_map/ppermute | solution.py:360
  305.6 17.2 %collective-permute-start.30 = (f32[24,72,128]{2,1,0:T(8,128)S(1)}, f32[24,72,128]{2,1,0:T(8,128)S(1)}, u32[]{:S(2)}, u32[]{:S(2)}) collective-permute-start(f32[24,72,128]{2,1,0:T(8,128)S(1)} %add.173), channel_id=1, source_target_pairs={{0,16},{8,24},{16,0},{24,8},{1,17},{9,25},{17,1},{25,9},{2,18},{10... | collective-permute-start | bytes 2654216 | tf_op jit(solution)/shard_map/ppermute | solution.py:360
  305.7 14.7 %copy-start.10 = (f32[24,72,128]{2,1,0:T(8,128)S(1)}, f32[24,72,128]{2,1,0:T(8,128)}, u32[]{:S(2)}) copy-start(f32[24,72,128]{2,1,0:T(8,128)} %get-tuple-element.107) | copy-start | bytes 2654212
  305.7 14.8 %copy-start.12 = (f32[24,72,128]{2,1,0:T(8,128)S(1)}, f32[24,72,128]{2,1,0:T(8,128)}, u32[]{:S(2)}) copy-start(f32[24,72,128]{2,1,0:T(8,128)} %copy-done.11) | copy-start | bytes 2654212
  308.0 29.0 %copy-start.9 = (f32[24,72,128]{2,1,0:T(8,128)S(1)}, f32[24,72,128]{2,1,0:T(8,128)}, u32[]{:S(2)}) copy-start(f32[24,72,128]{2,1,0:T(8,128)} %get-tuple-element.123) | copy-start | bytes 2654212
  312.2 22.9 %collective-permute-start.38 = (f32[24,72,128]{2,1,0:T(8,128)S(1)}, f32[24,72,128]{2,1,0:T(8,128)S(1)}, u32[]{:S(2)}, u32[]{:S(2)}) collective-permute-start(f32[24,72,128]{2,1,0:T(8,128)S(1)} %add_add_fusion.1), channel_id=1, source_target_pairs={{0,2},{2,4},{1,3},{3,5},{8,10},{10,12},{9,11},{11,13},{16,18},{18,... | collective-permute-start | bytes 2654216 | tf_op jit(solution)/shard_map/ppermute | solution.py:364
  313.4 23.5 %collective-permute-start.40 = (f32[24,72,128]{2,1,0:T(8,128)S(1)}, f32[24,72,128]{2,1,0:T(8,128)S(1)}, u32[]{:S(2)}, u32[]{:S(2)}) collective-permute-start(f32[24,72,128]{2,1,0:T(8,128)S(1)} %add_add_fusion.1), channel_id=1, source_target_pairs={{4,2},{6,4},{5,3},{7,5},{12,10},{14,12},{13,11},{15,13},{20,18},{2... | collective-permute-start | bytes 2654216 | tf_op jit(solution)/shard_map/ppermute | solution.py:364
  322.9 20.9 %collective-permute-start.31 = (f32[24,72,128]{2,1,0:T(8,128)}, f32[24,72,128]{2,1,0:T(8,128)}, u32[]{:S(2)}, u32[]{:S(2)}) collective-permute-start(f32[24,72,128]{2,1,0:T(8,128)} %add.170), channel_id=1, source_target_pairs={{0,8},{8,0},{16,24},{24,16},{1,9},{9,1},{17,25},{25,17},{2,10},{10... | collective-permute-start | bytes 2654216 | tf_op jit(solution)/shard_map/ppermute | solution.py:360
  324.4 19.4 %collective-permute-start.32 = (f32[24,72,128]{2,1,0:T(8,128)}, f32[24,72,128]{2,1,0:T(8,128)}, u32[]{:S(2)}, u32[]{:S(2)}) collective-permute-start(f32[24,72,128]{2,1,0:T(8,128)} %get-tuple-element.122), channel_id=1, source_target_pairs={{0,16},{8,24},{16,0},{24,8},{1,17},{9,25},{17,1},{25,9},{2,18},{10... | collective-permute-start | bytes 2654216 | tf_op jit(solution)/shard_map/ppermute | solution.py:360
  338.5 19.0 %collective-permute-start.39 = (f32[24,72,128]{2,1,0:T(8,128)S(1)}, f32[24,72,128]{2,1,0:T(8,128)}, u32[]{:S(2)}, u32[]{:S(2)}) collective-permute-start(f32[24,72,128]{2,1,0:T(8,128)S(1)} %get-tuple-element.135), channel_id=1, source_target_pairs={{0,2},{2,4},{4,6},{1,3},{3,5},{5,7},{8,10},{10,12},{12,14},{9,11},... | collective-permute-start | bytes 2654216 | tf_op jit(solution)/shard_map/ppermute | solution.py:364
  340.4 19.0 %collective-permute-start.41 = (f32[24,72,128]{2,1,0:T(8,128)S(1)}, f32[24,72,128]{2,1,0:T(8,128)}, u32[]{:S(2)}, u32[]{:S(2)}) collective-permute-start(f32[24,72,128]{2,1,0:T(8,128)S(1)} %get-tuple-element.136), channel_id=1, source_target_pairs={{2,0},{4,2},{6,4},{3,1},{5,3},{7,5},{10,8},{12,10},{14,12},{11,9},... | collective-permute-start | bytes 2654216 | tf_op jit(solution)/shard_map/ppermute | solution.py:364
  361.8 7.8 %copy-start.3 = (f32[12,72,128]{2,1,0:T(8,128)S(1)}, f32[12,72,128]{2,1,0:T(8,128)}, u32[]{:S(2)}) copy-start(f32[12,72,128]{2,1,0:T(8,128)} %get-tuple-element.134) | copy-start | bytes 1327108
  362.7 6.7 %collective-permute-start.42 = (f32[12,72,128]{2,1,0:T(8,128)}, f32[12,72,128]{2,1,0:T(8,128)S(1)}, u32[]{:S(2)}, u32[]{:S(2)}) collective-permute-start(f32[12,72,128]{2,1,0:T(8,128)} %constant_dynamic-slice_fusion), channel_id=1, source_target_pairs={{0,1},{1,0},{2,3},{3,2},{4,5},{5,4},{6,7},{7,6},{8,9},{9,8},{10,11... | collective-permute-start | bytes 1327112 | tf_op jit(solution)/shard_map/ppermute | solution.py:360
  367.7 1.9 copy-start.2
